TPU v7x, 32 devices: a whole 2x2x4 slice. The times are simulated.
32 devices in a mesh: energy: 8 (over y, x, core), orb: 4 (over z).
Axes of the slice: x: 2, y: 2, z: 4, core: 2. Of those that a mesh axis runs over, the one named last changes fastest.
Arguments:
- green: float32 [8, 2, 2048, 2048], P('energy', None, 'orb'), may hold values from -0.75 to 0.75
- sigma: float32 [8, 16, 2, 128, 128], P('energy', 'orb'), may hold values from -0.375 to 0.375
- neighbours: int32 [256, 16], P('orb'), may hold values from 0 to 255, as said below
- phonon_shift: int32 [6], replicated, may hold values from 1 to 4
- phonon_weight: float32 [2, 6], replicated, may hold values from 0.1 to 0.6
- dham: float32 [4096, 3, 8, 8], P('orb'), may hold values from -2 to 2
Outputs:
- scattering: float32 [8, 4096, 128], P('energy', 'orb')
Inputs may be any that keep to these rules, and one draw needn't show every extreme that they name: neighbours[a, k] is an atom other than a within 8 atoms of a; every atom has a neighbour exactly 8 atoms away.
All inputs are finite; a program needn't handle non-finite values.
Results may differ from a plain program's by a relative error of at most 0.0003.
Values sent between devices are 32-bit elements; how exact they have to be, the bound alone decides.
No kernel may reach another device: no remote copies, remote signals or barrier semaphores. Data moves between devices by JAX's collectives and lax.ppermute only.
A program may use at most 128 MiB of HBM per device.

v0:
```python
import jax
import jax.numpy as jnp
from jax import lax
from jax.sharding import PartitionSpec as P

W = 8
BS = 128
REACH = 8


HIGHEST = lax.Precision.HIGHEST


def with_halo(array, sides, width):
    for axis, dim in sides:
        peers, length = (lax.axis_size(axis), array.shape[dim])
        up = [(i, (i + 1) % peers) for i in range(peers - 1)]
        down = [(j, i) for i, j in up]
        last = lax.slice_in_dim(array, length - width, length, axis=dim)
        leading = lax.slice_in_dim(array, 0, width, axis=dim)
        before = lax.ppermute(last, axis, up)
        after = lax.ppermute(leading, axis, down)
        array = jnp.concatenate([before, array, after], axis=dim)
    return array


def multiply(left, right, form):
    return jnp.einsum(form, left, right, precision=HIGHEST)


def build_kernel(phonon_shift, phonon_weight, energies):
    rows_e = jnp.arange(energies, dtype=jnp.int32)[None, :, None]
    cols_f = jnp.arange(energies, dtype=jnp.int32)[None, None, :]
    shifts = phonon_shift[:, None, None]
    emission = (cols_f == rows_e + shifts).astype(jnp.float32)
    absorption = (cols_f == rows_e - shifts).astype(jnp.float32)
    terms = (
        phonon_weight[0][:, None, None] * emission + phonon_weight[1][:, None, None] * absorption
    )
    return jnp.sum(terms, axis=0)


def per_device(green, sigma, neighbours, phonon_shift, phonon_weight, dham):
    own_green = green[0]
    row_count = own_green.shape[1]
    atom_count = row_count // W
    degree = neighbours.shape[1]
    pair_count = atom_count * degree
    piece = lax.all_gather(sigma, "orb", axis=1, tiled=True)
    block_count = piece.shape[1]
    columns = own_green
    columns = columns.reshape(2, row_count, block_count, BS)
    form = "rmi,mij->rmj"
    real_part = multiply(columns[0], piece[0, :, 0], form) - multiply(
        columns[1], piece[0, :, 1], form
    )
    imag_part = multiply(columns[0], piece[0, :, 1], form) + multiply(
        columns[1], piece[0, :, 0], form
    )
    product = jnp.stack([real_part, imag_part]).reshape(2, row_count, block_count * BS)
    margin = REACH * W
    window = with_halo(own_green, (("orb", 1),), margin)
    window_start = lax.axis_index("orb") * row_count - margin
    local_cols = neighbours * W - window_start
    offsets = jnp.arange(W, dtype=jnp.int32)
    form = "rn,cn->rc"
    full_real = multiply(product[0], window[0], form) + multiply(product[1], window[1], form)
    full_imag = multiply(product[1], window[0], form) - multiply(product[0], window[1], form)
    full_blocks = jnp.stack([full_real, full_imag]).reshape(2, atom_count, W, -1)
    wanted = (local_cols[:, :, None] + offsets[None, None, :]).reshape(atom_count, degree * W)
    picked = jnp.take_along_axis(full_blocks, wanted[None, :, None, :], axis=3)
    blocks = picked.reshape(2, atom_count, W, degree, W).transpose(1, 3, 0, 2, 4)
    lesser = blocks.reshape(1, pair_count, 2 * W * W)
    energies = lax.axis_size("energy")
    kernel = build_kernel(phonon_shift, phonon_weight, energies)
    spread = jnp.einsum(
        "ef,fpx->epx",
        kernel,
        lax.all_to_all(lesser, "energy", split_axis=1, concat_axis=0, tiled=True),
        precision=HIGHEST,
    )
    smeared = lax.all_to_all(spread, "energy", split_axis=0, concat_axis=1, tiled=True)
    split = smeared[0].reshape(pair_count, 2, W, W)
    halfway = jnp.einsum("pcij,pzjk->pczik", dham, split, precision=HIGHEST)
    result = jnp.einsum("pczik,pclk->pzil", halfway, dham, precision=HIGHEST)
    return result.reshape(1, pair_count, 2 * W * W)


def solution(mesh):
    return jax.shard_map(
        per_device,
        mesh=mesh,
        in_specs=(
            P("energy", None, "orb", None),
            P("energy", "orb", None, None, None),
            P("orb", None),
            P(),
            P(),
            P("orb", None, None, None),
        ),
        out_specs=P("energy", "orb", None),
        check_vma=False,
    )
```

profile of v0, /device:TPU:0, one launch (start us, length us, event | category | flops | bytes accessed | tf_op | source)
XLA Modules:
  0.0 586.9 jit_solution(15013880067707772051)
XLA Ops:
  6.5 2.0 copy.69
  8.6 2.8 fusion.25
  11.4 5.0 collective-permute-start
  16.4 1.3 collective-permute-start.1
  17.7 8.2 %fusion.26 = (f32[1,1,512,2048]{3,2,1,0:T(8,128)}, f32[1,1,512,2048]{3,2,1,0:T(8,128)}) fusion(f32[1,2,512,2048]{3,2,1,0:T(8,128)} %param.6), kind=kLoop, calls=%fused_computation.45 | loop fusion | bytes 16777216 | tf_op jit(solution)/shard_map/slice | solution.py:55
  25.9 5.4 copy.105
  31.3 5.4 copy.106
  37.0 22.1 %collective-permute-done = f32[2,64,2048]{2,1,0:T(8,128)S(1)} collective-permute-done((f32[2,64,2048]{2,1,0:T(8,128)}, f32[2,64,2048]{2,1,0:T(8,128)S(1)}, u32[]{:S(2)}, u32[]{:S(2)}) %collective-permute-start) | collective-permute-done | bytes 1048608 | tf_op jit(solution)/shard_map/ppermute | solution.py:21
  59.1 17.5 %collective-permute-done.1 = f32[2,64,2048]{2,1,0:T(8,128)S(1)} collective-permute-done((f32[2,64,2048]{2,1,0:T(8,128)S(1)}, f32[2,64,2048]{2,1,0:T(8,128)S(1)}, u32[]{:S(2)}, u32[]{:S(2)}) %collective-permute-start.1) | collective-permute-done | bytes 1048608 | tf_op jit(solution)/shard_map/ppermute | solution.py:22
  76.6 9.0 %pad_maximum_fusion = f32[2,640,2048]{2,1,0:T(8,128)} fusion(f32[2,64,2048]{2,1,0:T(8,128)S(1)} %collective-permute-done.1, f32[2,512,2048]{2,1,0:T(8,128)} %bitcast.92, f32[2,64,2048]{2,1,0:T(8,128)S(1)} %collective-permute-done), kind=kLoop, calls=%fused_computation.3 | loop fusion | flops 5242880 | bytes 20971520 | tf_op jit(solution)/shard_map/concatenate | solution.py:23
  85.6 6.0 %fusion.15 = f32[16,128,512]{2,1,0:T(8,128)S(1)} fusion(f32[512,16,128]{0,2,1:T(8,128)} %bitcast.93, f32[1,16,2,128,128]{3,4,1,2,0:T(8,128)} %all-gather.2.cloned.1.call-done), kind=kOutput, calls=%fused_computation.23 | convolution fusion | flops 1610612736 | bytes 9437184 | tf_op jit(solution)/shard_map/rmi,mij->rmj/dot_general | solution.py:28
  91.7 6.6 %convolution_add_fusion = f32[16,128,512]{2,1,0:T(8,128)S(1)} fusion(f32[16,128,512]{2,1,0:T(8,128)S(1)} %fusion.15, f32[512,16,128]{0,2,1:T(8,128)} %bitcast.95, f32[1,16,2,128,128]{3,4,1,2,0:T(8,128)} %all-gather.2.cloned.1.call-done), kind=kOutput, calls=%fused_computation.12 | convolution fusion | flops 1611661312 | bytes 13631488 | tf_op jit(solution)/shard_map/rmi,mij->rmj/dot_general | solution.py:28
  98.4 20.2 %fusion.5 = f32[512,640]{1,0:T(8,128)S(1)} fusion(f32[512,2048]{0,1:T(8,128)S(1)} %bitcast.97, f32[2,640,2048]{2,1,0:T(8,128)S(1)} %bitcast.90), kind=kOutput, calls=%fused_computation.9 | convolution fusion | flops 8053063680 | bytes 10747904 | tf_op jit(solution)/shard_map/rn,cn->rc/dot_general | solution.py:28
  118.6 4.1 fusion.14
  122.7 4.4 convolution_subtract_fusion
  127.2 20.4 %fusion.4 = f32[512,640]{1,0:T(8,128)S(1)} fusion(f32[512,2048]{0,1:T(8,128)S(1)} %bitcast.99, f32[2,640,2048]{2,1,0:T(8,128)S(1)} %bitcast.90), kind=kOutput, calls=%fused_computation.8 | convolution fusion | flops 8053063680 | bytes 10747904 | tf_op jit(solution)/shard_map/rn,cn->rc/dot_general | solution.py:28
  147.6 20.6 %fusion.10 = f32[1,64,8,640]{3,2,1,0:T(8,128)S(1)} fusion(f32[512,640]{1,0:T(8,128)S(1)} %fusion.5, f32[512,2048]{0,1:T(8,128)S(1)} %bitcast.100, f32[2,640,2048]{2,1,0:T(8,128)S(1)} %bitcast.90), kind=kOutput, calls=%fused_computation.15 | convolution fusion | flops 8053391360 | bytes 12058624 | tf_op jit(solution)/shard_map/rn,cn->rc/dot_general | solution.py:28
  168.2 20.2 %fusion.12 = f32[1,64,8,640]{3,2,1,0:T(8,128)S(1)} fusion(f32[512,640]{1,0:T(8,128)S(1)} %fusion.4, f32[512,2048]{0,1:T(8,128)S(1)} %bitcast.98, f32[2,640,2048]{2,1,0:T(8,128)S(1)} %bitcast.90), kind=kOutput, calls=%fused_computation.17 | convolution fusion | flops 8053391360 | bytes 12058624 | tf_op jit(solution)/shard_map/rn,cn->rc/dot_general | solution.py:28
  188.5 35.3 %copy.77 = f32[2,64,8,640]{2,0,3,1:T(2,128)} copy(f32[2,64,8,640]{3,2,1,0:T(8,128)S(1)} %pad_maximum_fusion.1) | data formatting | bytes 5242880 | tf_op jit(solution)/shard_map/stack | solution.py:69
  223.9 126.1 %gather_fusion = f32[8192,2,8]{2,1,0:T(2,128)} fusion(f32[2,64,8,640]{2,0,3,1:T(2,128)} %copy.77, s32[8192]{0:T(1024)S(1)} %bitcast.88), kind=kCustom, calls=%fused_computation | custom fusion | bytes 1114112 | tf_op jit(solution)/shard_map/jit(take_along_axis)/gather | solution.py:71
  350.0 10.7 %copy.78 = f32[64,128,2,8]{0,1,3,2:T(8,128)S(1)} copy(f32[64,128,2,8]{3,2,1,0:T(2,128)} %bitcast.101) | data formatting | bytes 1048576 | tf_op jit(solution)/shard_map/jit(take_along_axis)/gather | solution.py:71
  360.8 2.7 copy.79
  363.5 4.8 reshape.223
  369.3 3.7 all-to-all-start
  373.2 9.5 %all-to-all-done = f32[1,1024,128]{2,0,1:T(1,128)S(1)} async-done(((f32[1,1024,128]{2,0,1:T(1,128)}), f32[1,1024,128]{2,0,1:T(1,128)S(1)}, u32[]{:S(2)}, u32[]{:S(2)}) %all-to-all-start) | async-done | bytes 524320 | tf_op jit(solution)/shard_map/all_to_all | solution.py:79
  384.5 3.5 all-to-all-start.1
  388.0 6.9 %copy.95 = f32[1024,3,8,8,1]{3,2,1,4,0:T(8,128)} copy(f32[1024,3,8,8,1]{0,3,2,1,4:T(8,128)S(1)} %bitcast.105) | data formatting | bytes 1572864 | tf_op args[5]
  394.9 2.8 all-to-all-done.1
  398.0 5.9 %copy.94 = f32[1024,2,8,8,1]{2,3,4,1,0:T(8,128)} copy(f32[1024,2,8,8,1]{0,3,2,1,4:T(8,128)S(1)} %bitcast.102) | data formatting | bytes 1048576 | tf_op jit(solution)/shard_map/reshape;squeeze | solution.py:83
  403.9 124.2 %fusion.27 = f32[1024,2,8,3,8]{4,2,3,1,0:T(8,128)S(1)} fusion(f32[1024,2,8,8,1]{2,3,4,1,0:T(8,128)} %copy.94, f32[1024,3,8,8,1]{3,2,1,4,0:T(8,128)} %copy.95), kind=kOutput, calls=%fused_computation.46 | convolution fusion | flops 37748736 | bytes 2883584 | tf_op jit(solution)/shard_map/pcij,pzjk->pczik/dot_general | solution.py:84
  528.1 45.6 %fusion.6 = f32[1024,2,8,8]{3,2,1,0:T(8,128)} fusion(f32[1024,3,8,8,1]{3,2,1,4,0:T(8,128)} %copy.95, f32[1024,2,8,3,8]{4,2,3,1,0:T(8,128)S(1)} %fusion.27), kind=kOutput, calls=%fused_computation.10 | convolution fusion | flops 37748736 | bytes 2883584 | tf_op jit(solution)/shard_map/pczik,pclk->pzil/dot_general | solution.py:85
  573.8 5.1 copy.88
  (41 shorter events, 4.8 us)
Async XLA Ops:
  6.5 79.1 %all-gather.2.cloned.1.call-start = ((), (), s32[]{:S(2)}) async-start(), calls=%async_computation.2 | async-start | bytes 2621440 | tf_op jit(solution)/shard_map/all_gather | solution.py:49
  11.4 47.7 %collective-permute-start = (f32[2,64,2048]{2,1,0:T(8,128)}, f32[2,64,2048]{2,1,0:T(8,128)S(1)}, u32[]{:S(2)}, u32[]{:S(2)}) collective-permute-start(f32[2,64,2048]{2,1,0:T(8,128)} %get-tuple-element.5), channel_id=1, source_target_pairs={{0,1},{1,2},{2,3},{4,5},{5,6},{6,7},{8,9},{9,10},{10,11},{12,13},{... | collective-permute-start | bytes 3145736 | tf_op jit(solution)/shard_map/ppermute | solution.py:21
  16.4 60.2 %collective-permute-start.1 = (f32[2,64,2048]{2,1,0:T(8,128)S(1)}, f32[2,64,2048]{2,1,0:T(8,128)S(1)}, u32[]{:S(2)}, u32[]{:S(2)}) collective-permute-start(f32[2,64,2048]{2,1,0:T(8,128)S(1)} %get-tuple-element.6), channel_id=1, source_target_pairs={{1,0},{2,1},{3,2},{5,4},{6,5},{7,6},{9,8},{10,9},{11,10},{13,12},{... | collective-permute-start | bytes 3145736 | tf_op jit(solution)/shard_map/ppermute | solution.py:22
  31.3 5.5 copy-start.4
  85.6 12.7 %slice-start = ((s8[10485760]{0:T(1024)(128)(4,1)}), s8[4194304]{0:T(1024)(128)(4,1)S(1)}, s32[]{:S(2)}) async-start(s8[10485760]{0:T(1024)(128)(4,1)} %bitcast.89), calls=%async_computation.3 | async-start | bytes 8388608
  85.6 12.7 %slice-start.1 = ((s8[10485760]{0:T(1024)(128)(4,1)}), s8[4194304]{0:T(1024)(128)(4,1)S(1)}, s32[]{:S(2)}) async-start(s8[10485760]{0:T(1024)(128)(4,1)} %bitcast.89), calls=%async_computation.4 | async-start | bytes 8388608
  91.7 6.7 %slice-start.2 = ((s8[10485760]{0:T(1024)(128)(4,1)}), s8[2097152]{0:T(1024)(128)(4,1)S(1)}, s32[]{:S(2)}) async-start(s8[10485760]{0:T(1024)(128)(4,1)} %bitcast.89), calls=%async_computation.5 | async-start | bytes 4194304
  98.3 20.2 %copy-start = (f32[1,1,512,2048]{2,3,1,0:T(8,128)S(1)}, f32[1,1,512,2048]{2,3,1,0:T(8,128)}, u32[]{:S(2)}) copy-start(f32[1,1,512,2048]{2,3,1,0:T(8,128)} %copy.105) | copy-start | bytes 12582916
  98.3 20.2 %copy-start.2 = (f32[1,16,2,128,128]{3,4,1,2,0:T(8,128)S(1)}, f32[1,16,2,128,128]{3,4,1,2,0:T(8,128)}, u32[]{:S(2)}) copy-start(f32[1,16,2,128,128]{3,4,1,2,0:T(8,128)} %all-gather.2.cloned.1.call-done) | copy-start | bytes 6291460
  118.6 4.2 copy-start.1
  363.5 9.5 %copy-start.5 = (f32[2,6]{1,0:T(2,128)S(1)}, f32[2,6]{1,0:T(2,128)}, u32[]{:S(2)}) copy-start(f32[2,6]{1,0:T(2,128)} %param.10) | copy-start | bytes 148
  363.5 9.6 %copy-start.6 = (s32[6]{0:T(128)S(1)}, s32[6]{0:T(128)}, u32[]{:S(2)}) copy-start(s32[6]{0:T(128)} %param.9) | copy-start | bytes 76
  363.5 24.5 %copy-start.3 = (f32[1024,3,8,8]{0,3,2,1:T(8,128)S(1)}, f32[1024,3,8,8]{0,3,2,1:T(8,128)}, u32[]{:S(2)}) copy-start(f32[1024,3,8,8]{0,3,2,1:T(8,128)} %param.11) | copy-start | bytes 2359300
  369.3 13.5 %all-to-all-start = ((f32[1,1024,128]{2,0,1:T(1,128)}), f32[1,1024,128]{2,0,1:T(1,128)S(1)}, u32[]{:S(2)}, u32[]{:S(2)}) async-start(f32[1,1024,128]{2,0,1:T(1,128)} %copy.80), calls=%async_computation | async-start | bytes 1048576 | tf_op jit(solution)/shard_map/all_to_all | solution.py:79
  384.5 13.2 %all-to-all-start.1 = ((f32[8,128,128]{2,1,0:T(8,128)}), f32[8,128,128]{2,1,0:T(8,128)S(1)}, u32[]{:S(2)}, u32[]{:S(2)}) async-start(f32[8,128,128]{2,1,0:T(8,128)} %copy.82), calls=%async_computation.1 | async-start | bytes 1048576 | tf_op jit(solution)/shard_map/all_to_all | solution.py:82
Sparse Core Ops, SparseCore 0:
  8.9 66.3 all-gather.1
where the time goes:
time: 594 us; the launch traced here: 587 us
  matrix products  273 us (46%)
  local copies, waits for them, and re-layouts  225 us (38%)
  waiting for transfers between devices  52 us (9%)
  between operations  13.9 us (2%)
  starting transfers between devices  13.5 us (2%)
  other arithmetic  9.6 us (2%)
    gather x3, local copies, waits for them, and re-layouts, per_device(): picked = jnp.take_along_axis(full_blocks, wanted[None, :, None, :], axis=3)  137 us
    dot_general x1, matrix products, per_device(): halfway = jnp.einsum('pcij,pzjk->pczik', dham, split, precision=HIGHEST)  124 us
    dot_general x8, matrix products, multiply(): return jnp.einsum(form, left, right, precision=HIGHEST)  103 us
    dot_general x1, matrix products, per_device(): result = jnp.einsum('pczik,pclk->pzil', halfway, dham, precision=HIGHEST)  45.6 us
    another operation x1, local copies, waits for them, and re-layouts, per_device(): jnp.stack([full_real, full_imag]).reshape(2, atom_count, W, -1)  35.3 us
    ppermute x1, waiting for transfers between devices, with_halo(): before = lax.ppermute(last, axis, up)  22.1 us
    unnamed x24, local copies, waits for them, and re-layouts  19.7 us
    ppermute x1, waiting for transfers between devices, with_halo(): after = lax.ppermute(leading, axis, down)  17.5 us
  transfers between devices with their start and end apart: 5, of which 4 were waited for; matrix products, arithmetic and copies ran while one was open for 6% of the time, Pallas kernels for 0%

commit v1 on v0

v1 whole, which is shorter than its diff:
```python
import functools

import jax
import jax.numpy as jnp
from jax import lax
from jax.experimental import pallas as pl
from jax.experimental.pallas import tpu as pltpu
from jax.sharding import PartitionSpec as P

W = 8
BS = 128
REACH = 8
MARGIN = REACH * W
HALF = MARGIN // 2
TILE = 128
LANES = 128
F32, BF16 = jnp.float32, jnp.bfloat16

NT = (((1,), (1,)), ((), ()))
NN = (((1,), (0,)), ((), ()))


def halves(x):
    hi = x.astype(BF16)
    return hi, (x - hi.astype(F32)).astype(BF16)


def dot(a, b, dims):
    return lax.dot_general(a, b, dims, preferred_element_type=F32)


def dot3(a, b, dims):
    return dot(a[0], b[0], dims) + dot(a[0], b[1], dims) + dot(a[1], b[0], dims)


def one_block(real, imag, self_real, self_imag, hi_ref, lo_ref, acc_ref, tiles, pad):
    rows = real.shape[0]
    hi, lo = halves(jnp.concatenate([real, imag], axis=1))
    hi_ref[pad : pad + rows, :] = hi
    lo_ref[pad : pad + rows, :] = lo
    weight = halves(
        jnp.concatenate(
            [
                jnp.concatenate([self_real, self_imag], axis=1),
                jnp.concatenate([-self_imag, self_real], axis=1),
            ],
            axis=0,
        )
    )
    for t, (row, window, width) in enumerate(tiles):
        left = (hi_ref[row : row + TILE, :], lo_ref[row : row + TILE, :])
        product = dot3(left, weight, NN)
        turned = jnp.concatenate([product[:, BS:], -product[:, :BS]], axis=1)
        both = halves(jnp.concatenate([product, turned], axis=0))
        near = (hi_ref[window : window + width, :], lo_ref[window : window + width, :])
        acc_ref[t] = acc_ref[t] + dot3(both, near, NT)


def main_tiles(rows):
    return [(MARGIN + t * TILE, t * TILE, TILE + 2 * MARGIN) for t in range(rows // TILE)]


def lesser_kernel(count, first, idx_ref, green_ref, sigma_ref, *rest):
    if first:
        acc_ref, buf, hi_ref, lo_ref, sem = rest
    else:
        before_ref, acc_ref, buf, hi_ref, lo_ref, sem = rest
    rows = green_ref.shape[2]

    def fetch(s):
        col = pl.multiple_of(idx_ref[1, s] * BS, BS)
        return pltpu.make_async_copy(
            green_ref.at[0, :, :, pl.ds(col, BS)], buf.at[s], sem.at[s]
        )

    for s in range(count):
        fetch(s).start()
    acc_ref[...] = jnp.zeros_like(acc_ref) if first else before_ref[...]
    for ref in (hi_ref, lo_ref):
        ref[:MARGIN, :] = jnp.zeros((MARGIN, 2 * BS), BF16)
        ref[MARGIN + rows :, :] = jnp.zeros((MARGIN, 2 * BS), BF16)

    def step(s, carry):
        fetch(s).wait()
        at = idx_ref[0, s]
        one_block(
            buf[s, 0], buf[s, 1], sigma_ref[0, at, 0], sigma_ref[0, at, 1],
            hi_ref, lo_ref, acc_ref, main_tiles(rows), MARGIN,
        )
        return carry

    lax.fori_loop(0, count, step, 0)


def lesser_part(green, sigma, index, before):
    rows, count = green.shape[2], index.shape[1]
    tiles = rows // TILE
    first = before is None
    acc = jax.ShapeDtypeStruct((tiles, 2 * TILE, TILE + 2 * MARGIN), F32)
    vmem = pl.BlockSpec(memory_space=pltpu.VMEM)
    return pl.pallas_call(
        functools.partial(lesser_kernel, count, first),
        out_shape=acc,
        in_specs=[
            pl.BlockSpec(memory_space=pltpu.SMEM),
            pl.BlockSpec(memory_space=pl.ANY),
            vmem,
        ]
        + ([] if first else [vmem]),
        out_specs=vmem,
        scratch_shapes=[
            pltpu.VMEM((count, 2, rows, BS), F32),
            pltpu.VMEM((rows + 2 * MARGIN, 2 * BS), BF16),
            pltpu.VMEM((rows + 2 * MARGIN, 2 * BS), BF16),
            pltpu.SemaphoreType.DMA((count,)),
        ],
        input_output_aliases={} if first else {3: 0},
        compiler_params=pltpu.CompilerParams(vmem_limit_bytes=24 << 20),
        cost_estimate=pl.CostEstimate(
            flops=count * 6 * rows * 2 * BS * (2 * BS + 4 * TILE),
            bytes_accessed=count * rows * BS * 8 + 8 * tiles * TILE * 512,
            transcendentals=0,
        ),
        name="lesser_own" if first else "lesser_more",
    )(index, green, sigma, *([] if first else [before]))


def edge_kernel(
    blocks, flag_ref, green_ref, a_ref, b_ref, c_ref, sig0_ref, sig1_ref,
    left_ref, right_ref, own_ref, buf, hi_ref, lo_ref, acc_ref, sem,
):
    rows = green_ref.shape[2]
    tiles = [(0, 0, TILE), (TILE, TILE, TILE)]
    size = 2 * TILE

    def fetch(s):
        cols = pl.ds(pl.multiple_of(s * BS, BS), BS)
        slot = lax.rem(s, 2)
        parts = [
            (a_ref.at[:, :, cols], 0),
            (b_ref.at[:, :, cols], HALF),
            (green_ref.at[0, :, pl.ds(0, MARGIN), cols], MARGIN),
            (green_ref.at[0, :, pl.ds(rows - MARGIN, MARGIN), cols], TILE),
            (c_ref.at[:, :, cols], TILE + MARGIN),
            (a_ref.at[:, :, cols], TILE + MARGIN + HALF),
        ]
        return [
            pltpu.make_async_copy(
                src, buf.at[slot, :, pl.ds(at, src.shape[1]), :], sem.at[slot, k]
            )
            for k, (src, at) in enumerate(parts)
        ]

    acc_ref[...] = jnp.zeros_like(acc_ref)

    @pl.when(flag_ref[0] == 1)
    def _():
        for copy in fetch(0):
            copy.start()
        row = lax.broadcasted_iota(jnp.int32, (size, BS), 0)
        keep = (row >= HALF) | (flag_ref[1] == 1)
        keep &= (row < TILE) | (row >= TILE + MARGIN) | (row < TILE + flag_ref[3])
        keep &= (row < size - HALF) | (flag_ref[2] == 1)

        def step(s, carry):
            for copy in fetch(s):
                copy.wait()

            @pl.when(s + 1 < blocks)
            def _():
                for copy in fetch(s + 1):
                    copy.start()

            slot = lax.rem(s, 2)
            real = jnp.where(keep, buf[slot, 0], 0.0)
            imag = jnp.where(keep, buf[slot, 1], 0.0)
            owner, local = s // flag_ref[4], lax.rem(s, flag_ref[4])
            piece = flag_ref[4] // 2
            at = owner * piece + lax.rem(local, piece)
            low = local < piece
            self_real = jnp.where(low, sig0_ref[0, at, 0], sig1_ref[0, at, 0])
            self_imag = jnp.where(low, sig0_ref[0, at, 1], sig1_ref[0, at, 1])
            one_block(real, imag, self_real, self_imag, hi_ref, lo_ref, acc_ref, tiles, 0)
            return carry

        lax.fori_loop(0, blocks, step, 0)

    lane = lax.broadcasted_iota(jnp.int32, (MARGIN, LANES), 1)
    low = lane < MARGIN
    for part in range(2):
        base = part * TILE
        outer_l = acc_ref[0, base : base + MARGIN, :]
        inner_l = acc_ref[0, base + MARGIN : base + TILE, :]
        inner_r = acc_ref[1, base : base + MARGIN, :]
        outer_r = acc_ref[1, base + MARGIN : base + TILE, :]
        left_ref[part] = jnp.where(low, 0.0, outer_l)
        right_ref[part] = jnp.where(low, outer_r, 0.0)
        own_ref[0, part] = jnp.where(low, inner_l, 0.0)
        own_ref[1, part] = jnp.where(low, 0.0, inner_r)


def edge_part(flags, green, a, b, c, sig0, sig1):
    blocks = sig0.shape[1] + sig1.shape[1]
    vmem = pl.BlockSpec(memory_space=pltpu.VMEM)
    hbm = pl.BlockSpec(memory_space=pl.ANY)
    side = jax.ShapeDtypeStruct((2, MARGIN, LANES), F32)
    size = 2 * TILE
    return pl.pallas_call(
        functools.partial(edge_kernel, blocks),
        out_shape=(side, side, jax.ShapeDtypeStruct((2, 2, MARGIN, LANES), F32)),
        in_specs=[pl.BlockSpec(memory_space=pltpu.SMEM), hbm, hbm, hbm, hbm, vmem, vmem],
        out_specs=(vmem, vmem, vmem),
        scratch_shapes=[
            pltpu.VMEM((2, 2, size, BS), F32),
            pltpu.VMEM((size, 2 * BS), BF16),
            pltpu.VMEM((size, 2 * BS), BF16),
            pltpu.VMEM((2, 2 * TILE, TILE), F32),
            pltpu.SemaphoreType.DMA((2, 6)),
        ],
        compiler_params=pltpu.CompilerParams(vmem_limit_bytes=16 << 20),
        cost_estimate=pl.CostEstimate(
            flops=blocks * 6 * size * 2 * BS * (2 * BS + 2 * TILE),
            bytes_accessed=blocks * size * BS * 8 + blocks * BS * BS * 8,
            transcendentals=0,
        ),
        name="edges",
    )(flags, green, a, b, c, sig0, sig1)


def band_kernel(acc_ref, own_ref, from_left_ref, from_right_ref, out_ref, rows_ref):
    tiles = acc_ref.shape[0]
    group = out_ref.shape[2]
    per_tile = TILE // W
    for t in range(tiles):
        for part in range(2):
            base = part * TILE
            x = acc_ref[t, base : base + TILE, :]
            rows_ref[t, part] = x
            if t == 0:
                extra = own_ref[0, part] + from_left_ref[part]
                rows_ref[t, part, :MARGIN, :LANES] = x[:MARGIN, :LANES] + extra
            if t == tiles - 1:
                extra = own_ref[1, part] + from_right_ref[part]
                rows_ref[t, part, MARGIN:, LANES:] = x[MARGIN:, LANES:] + extra
    low = lax.broadcasted_iota(jnp.int32, (W, LANES), 1) < MARGIN
    width = TILE + 2 * MARGIN
    for a in range(per_tile):
        for t in range(tiles):
            atom = t * per_tile + a
            for part in range(2):
                x = rows_ref[t, part, a * W : (a + 1) * W, :]
                before = pltpu.roll(x, (width - a * W) % width, 1)[:, :LANES]
                after = pltpu.roll(x, (width - (a + 1) * W) % width, 1)[:, :LANES]
                out_ref[atom // group, part, atom % group] = jnp.where(low, before, after)


def band(acc, own, from_left, from_right, energies):
    tiles = acc.shape[0]
    atoms = tiles * TILE // W
    vmem = pl.BlockSpec(memory_space=pltpu.VMEM)
    return pl.pallas_call(
        band_kernel,
        out_shape=jax.ShapeDtypeStruct((energies, 2, atoms // energies, W, LANES), F32),
        in_specs=[vmem] * 4,
        out_specs=vmem,
        scratch_shapes=[pltpu.VMEM((tiles, 2, TILE, TILE + 2 * MARGIN), F32)],
        compiler_params=pltpu.CompilerParams(vmem_limit_bytes=16 << 20),
        name="band",
    )(acc, own, from_left, from_right)


def picks_kernel(where_ref, out_ref):
    rows = out_ref.shape[0]
    padded = where_ref.shape[1]
    entry = lax.broadcasted_iota(jnp.int32, (rows, padded), 0)
    first = where_ref[...] * W
    for j in range(W):
        hit = entry == first + j
        out_ref[:, j * padded : (j + 1) * padded] = jnp.where(hit, 1.0, 0.0).astype(BF16)


def picks(where, rows):
    padded = where.shape[1]
    vmem = pl.BlockSpec(memory_space=pltpu.VMEM)
    return pl.pallas_call(
        picks_kernel,
        out_shape=jax.ShapeDtypeStruct((rows, W * padded), BF16),
        in_specs=[vmem],
        out_specs=vmem,
        compiler_params=pltpu.CompilerParams(vmem_limit_bytes=16 << 20),
        name="picks",
    )(where)


def scatter_kernel(recv_ref, pick_ref, mix_ref, dham_ref, out_ref, smeared_ref, result_ref):
    energies, _, group, _, _ = recv_ref.shape
    padded = dham_ref.shape[1]
    pairs = out_ref.shape[1]
    columns = [
        recv_ref[:, :, a, :, :].reshape(energies * 2 * W, LANES) for a in range(group)
    ]
    received = halves(jnp.concatenate(columns, axis=1))
    mixed = halves(dot3(halves(mix_ref[...]), received, NN))
    smeared_ref[...] = dot(mixed[0], pick_ref[...], NN) + dot(mixed[1], pick_ref[...], NN)

    def block(part, j, k):
        row = (part * W + j) * energies
        return smeared_ref[row : row + energies, k * padded : (k + 1) * padded]

    def factor(c, i, j):
        row = (c * W + i) * W + j
        return dham_ref[row : row + 1, :]

    for part in range(2):
        for i in range(W):
            total = [None] * W
            for c in range(3):
                for k in range(W):
                    t = None
                    for j in range(W):
                        term = factor(c, i, j) * block(part, j, k)
                        t = term if t is None else t + term
                    for l in range(W):
                        term = t * factor(c, l, k)
                        total[l] = term if total[l] is None else total[l] + term
            for l in range(W):
                row = ((part * W + i) * W + l) * energies
                result_ref[row : row + energies, :] = total[l]
    for e in range(energies):
        one = result_ref[pl.ds(e, 2 * W * W, stride=energies), :]
        out_ref[e] = one.T[:pairs, :]


def scatter(recv, pick, mix, dham, pairs):
    energies, _, group, _, _ = recv.shape
    padded = dham.shape[1]
    vmem = pl.BlockSpec(memory_space=pltpu.VMEM)
    return pl.pallas_call(
        scatter_kernel,
        out_shape=jax.ShapeDtypeStruct((energies, pairs, 2 * W * W), F32),
        in_specs=[vmem] * 4,
        out_specs=vmem,
        scratch_shapes=[
            pltpu.VMEM((2 * W * energies, W * padded), F32),
            pltpu.VMEM((2 * W * W * energies, padded), F32),
        ],
        compiler_params=pltpu.CompilerParams(vmem_limit_bytes=24 << 20),
        name="scatter",
    )(recv, pick, mix, dham)


def build_kernel(phonon_shift, phonon_weight, energies):
    rows_e = jnp.arange(energies, dtype=jnp.int32)[None, :, None]
    cols_f = jnp.arange(energies, dtype=jnp.int32)[None, None, :]
    shifts = phonon_shift[:, None, None]
    emission = (cols_f == rows_e + shifts).astype(F32)
    absorption = (cols_f == rows_e - shifts).astype(F32)
    terms = (
        phonon_weight[0][:, None, None] * emission + phonon_weight[1][:, None, None] * absorption
    )
    return jnp.sum(terms, axis=0)


def build_mix(phonon_shift, phonon_weight, energies):
    kernel = build_kernel(phonon_shift, phonon_weight, energies)
    same = jnp.eye(2 * W, dtype=F32)
    mix = same[:, None, None, :] * kernel[None, :, :, None]
    return mix.reshape(2 * W * energies, energies * 2 * W)


def send(x, pairs):
    return lax.ppermute(x, "orb", pairs)


def per_device(green, sigma, neighbours, phonon_shift, phonon_weight, dham):
    energies = lax.axis_size("energy")
    peers = lax.axis_size("orb")
    e, z = lax.axis_index("energy"), lax.axis_index("orb")
    rows = green.shape[2]
    atoms = rows // W
    degree = neighbours.shape[1]
    group = atoms // energies
    pairs = group * degree
    padded = -(-pairs // LANES) * LANES
    held = sigma.shape[1]
    piece = held // 2

    sig = [
        lax.all_gather(sigma[:, h * piece : (h + 1) * piece], "orb", axis=1, tiled=True)
        for h in range(2)
    ]

    far = peers >= 4
    up = [(i, i + 1) for i in range(peers - 1)]
    down = [(i + 1, i) for i in range(peers - 1)]
    near_right = send(green[0, :, rows - HALF :], up[:-1] if far else up)
    near_left = send(green[0, :, :HALF], down[1:] if far else down)
    if far:
        more = jnp.where(
            z == 0, green[0, :, rows - MARGIN : rows - HALF], green[0, :, HALF:MARGIN]
        )
        other = send(more, [(0, 1), (peers - 1, peers - 2)])
        from_left, from_right = z == 1, z == peers - 2
        active = (z > 0) & (z < peers - 1)
    else:
        other = jnp.zeros_like(near_left)
        from_left = from_right = jnp.zeros((), bool)
        active = jnp.ones((), bool)
    limit = jnp.where(from_right, MARGIN, HALF)
    flags = jnp.stack(
        [x.astype(jnp.int32) for x in (active, from_left, from_right, limit)]
        + [jnp.int32(held)]
    )

    slot = jnp.arange(held, dtype=jnp.int32)
    acc = lesser_part(green, sigma, jnp.stack([slot, z * held + slot]), None)
    slot = jnp.arange((peers - 1) * piece, dtype=jnp.int32)
    owner = lax.rem(z + 1 + slot // piece, peers)
    at = slot % piece
    for h in range(2):
        index = jnp.stack([owner * piece + at, owner * held + h * piece + at])
        acc = lesser_part(green, sig[h], index, acc)
    to_left, to_right, own = edge_part(
        flags, green, other, near_right, near_left, sig[0], sig[1]
    )
    back_right = send(to_left, down)
    back_left = send(to_right, up)
    lesser = band(acc, own, back_left, back_right, energies)

    mine = lax.dynamic_slice_in_dim(neighbours, e * group, group, axis=0)
    first = z * atoms + e * group
    offset = mine - (first + jnp.arange(group, dtype=jnp.int32))[:, None]
    column = jnp.where(offset < 0, offset + REACH, offset + REACH - 1)
    where = column + 2 * REACH * jnp.arange(group, dtype=jnp.int32)[:, None]
    where = jnp.pad(where.reshape(1, pairs), ((0, 0), (0, padded - pairs)), constant_values=-1)
    pick = picks(where, group * LANES)
    mix = build_mix(phonon_shift, phonon_weight, energies)
    factors = lax.dynamic_slice_in_dim(
        dham.transpose(1, 2, 3, 0).reshape(3 * W * W, -1), e * pairs, pairs, axis=1
    )
    factors = jnp.pad(factors, ((0, 0), (0, padded - pairs)))

    recv = lax.all_to_all(lesser, "energy", split_axis=0, concat_axis=0, tiled=True)
    spread = scatter(recv, pick, mix, factors, pairs)
    result = lax.all_to_all(spread, "energy", split_axis=0, concat_axis=0, tiled=True)
    return result.reshape(1, atoms * degree, 2 * W * W)


def solution(mesh):
    return jax.shard_map(
        per_device,
        mesh=mesh,
        in_specs=(
            P("energy", None, "orb", None),
            P("energy", "orb", None, None, None),
            P("orb", None),
            P(),
            P(),
            P("orb", None, None, None),
        ),
        out_specs=P("energy", "orb", None),
        check_vma=False,
    )
```

time: 594 us -> 169 us (0.28); the launches traced: 587 us -> 168 us
  matrix products: 273 us -> 0 us
  local copies, waits for them, and re-layouts: 225 us -> 22.7 us
  Pallas kernels: 0 us -> 23.8 us
  starting transfers between devices: 13.5 us -> 32.6 us
  blocking collectives: 0 us -> 12.2 us
  waiting for transfers between devices: 52 us -> 58.9 us
    dot_general x11 -> x0, matrix products: 273 us -> none  [the longest x1 124 us: per_device(): halfway = jnp.einsum('pcij,pzjk->pczik', dham, split, precision=HIGHEST)]
    gather x3 -> x0, local copies, waits for them, and re-layouts: 137 us -> none  [per_device(): picked = jnp.take_along_axis(full_blocks, wanted[None, :, None, :], axis=3)]
    another operation x3 -> x1, local copies, waits for them, and re-layouts: 41.4 us -> 0.09 us  [per_device(): jnp.stack([x.astype(jnp.int32) for x in (active, from_left, from_right, l...]
    all_gather x1 -> x2, waiting for transfers between devices: 0.01 us -> 29.8 us  [per_device(): lax.all_gather(sigma[:, h * piece:(h + 1) * piece], 'orb', axis=1, tiled=...]
    pallas_call x0 -> x7, Pallas kernels: none -> 23.8 us  [the longest x3 19.3 us: lesser_part(): pl.pallas_call(functools.partial(lesser_kernel, count, first), out_shape=...]
    ppermute x2 -> x5, starting transfers between devices: 6.27 us -> 28.9 us  [send(): return lax.ppermute(x, 'orb', pairs)]
    ppermute x2 -> x5, waiting for transfers between devices: 39.6 us -> 22.1 us  [send(): return lax.ppermute(x, 'orb', pairs)]
    all_to_all x0 -> x1, blocking collectives: none -> 12.2 us  [per_device(): lax.all_to_all(spread, 'energy', split_axis=0, concat_axis=0, tiled=True)]
  transfers between devices with their start and end apart: 5 -> 8, of which waited for: 4 -> 4; matrix products, arithmetic and copies ran while one was open for 6% -> 5% of each run, Pallas kernels for 0% -> 12%
where the time goes in v1:
time: 169 us; the launch traced here: 168 us
  waiting for transfers between devices  58.9 us (35%)
  starting transfers between devices  32.6 us (19%)
  Pallas kernels  23.8 us (14%)
  local copies, waits for them, and re-layouts  22.7 us (13%)
  between operations  13.6 us (8%)
  blocking collectives  12.2 us (7%)
  other arithmetic  4.63 us (3%)
    all_gather x2, waiting for transfers between devices, per_device(): lax.all_gather(sigma[:, h * piece:(h + 1) * piece], 'orb', axis=1, tiled=...  29.8 us
    ppermute x5, starting transfers between devices, send(): return lax.ppermute(x, 'orb', pairs)  28.9 us
    ppermute x5, waiting for transfers between devices, send(): return lax.ppermute(x, 'orb', pairs)  22.1 us
    pallas_call x3, Pallas kernels, lesser_part(): pl.pallas_call(functools.partial(lesser_kernel, count, first), out_shape=...  19.3 us
    unnamed x28, local copies, waits for them, and re-layouts  17.2 us
    all_to_all x1, blocking collectives, per_device(): lax.all_to_all(spread, 'energy', split_axis=0, concat_axis=0, tiled=True)  12.2 us
    all_to_all x1, waiting for transfers between devices, per_device(): lax.all_to_all(lesser, 'energy', split_axis=0, concat_axis=0, tiled=True)  6.94 us
    all_to_all x1, starting transfers between devices, per_device(): lax.all_to_all(lesser, 'energy', split_axis=0, concat_axis=0, tiled=True)  3.65 us
  transfers between devices with their start and end apart: 8, of which 4 were waited for; matrix products, arithmetic and copies ran while one was open for 5% of the time, Pallas kernels for 12%

profile of v1, /device:TPU:0, one launch (start us, length us, event | category | flops | bytes accessed | tf_op | source)
XLA Modules:
  0.0 168.4 jit_solution(7120523126200598220)
XLA Ops:
  6.5 1.9 %fusion.3 = (f32[1,2,2,128,128]{4,3,2,0,1:T(8,128)}, f32[1,2,2,128,128]{4,3,2,0,1:T(8,128)}) fusion(f32[1,4,2,128,128]{4,3,2,0,1:T(8,128)} %bitcast.24), kind=kLoop, calls=%fused_computation.34 | loop fusion | bytes 1048576 | tf_op jit(solution)/shard_map/slice | solution.py:389
  8.6 2.7 %slice_bitcast_fusion = (f32[2,32,2048]{2,1,0:T(8,128)}, f32[2,32,2048]{2,1,0:T(8,128)}, f32[2,32,2048]{2,1,0:T(8,128)}) fusion(f32[1,2,512,2048]{3,2,1,0:T(8,128)} %green_ref.7, pred[]{:T(512)S(6)} %eq.46), kind=kLoop, calls=%fused_computation | loop fusion | flops 131072 | bytes 3670017 | tf_op jit(solution)/shard_map/squeeze | solution.py:397
  11.3 4.9 %collective-permute-start = (f32[2,32,2048]{2,1,0:T(8,128)}, f32[2,32,2048]{2,1,0:T(8,128)S(1)}, u32[]{:S(2)}, u32[]{:S(2)}) collective-permute-start(f32[2,32,2048]{2,1,0:T(8,128)} %get-tuple-element.12), channel_id=1, source_target_pairs={{0,1},{3,2},{4,5},{7,6},{8,9},{11,10},{12,13},{15,14},{16,17},{19,... | collective-permute-start | bytes 1572872 | tf_op jit(solution)/shard_map/ppermute | solution.py:372
  16.3 2.1 %collective-permute-start.1 = (f32[2,32,2048]{2,1,0:T(8,128)}, f32[2,32,2048]{2,1,0:T(8,128)}, u32[]{:S(2)}, u32[]{:S(2)}) collective-permute-start(f32[2,32,2048]{2,1,0:T(8,128)} %get-tuple-element.13), channel_id=1, source_target_pairs={{0,1},{1,2},{4,5},{5,6},{8,9},{9,10},{12,13},{13,14},{16,17},{17,1... | collective-permute-start | bytes 1572872 | tf_op jit(solution)/shard_map/ppermute | solution.py:372
  18.4 1.5 collective-permute-start.2
  19.9 0.8 constant_dynamic-slice_fusion.1
  21.7 0.7 iota_add_fusion
  22.4 0.8 slice_bitcast_fusion.3
  23.3 3.4 %copy-done.1 = f32[1,2,512,2048]{3,2,1,0:T(8,128)S(1)} copy-done((f32[1,2,512,2048]{3,2,1,0:T(8,128)S(1)}, f32[1,2,512,2048]{3,2,1,0:T(8,128)}, u32[]{:S(2)}) %copy-start.1) | copy-done | bytes 8388632
  26.7 1.1 copy-done.6
  27.7 5.0 %lesser_own.1.rest_0_ = f32[4,256,256]{2,1,0:T(8,128)S(1)} custom-call(s32[2,4]{1,0:T(2,128)S(1)} %pad_add_fusion.2.idx_ref, f32[1,2,512,2048]{3,2,1,0:T(8,128)S(1)} %copy-done.1, f32[1,4,2,128,128]{4,3,2,1,0:T(8,128)S(1)} %copy-done.6), custom_call_target="tpu_custom_call" | custom-call | flops 2415919104 | bytes 4194304 | tf_op jit(solution)/shard_map/lesser_own/pallas_call | solution.py:101
  32.7 1.0 copy-done.4
  33.7 4.1 %collective-permute-done.a_ref = f32[2,32,2048]{2,1,0:T(8,128)S(1)} collective-permute-done((f32[2,32,2048]{2,1,0:T(8,128)}, f32[2,32,2048]{2,1,0:T(8,128)S(1)}, u32[]{:S(2)}, u32[]{:S(2)}) %collective-permute-start) | collective-permute-done | bytes 524320 | tf_op jit(solution)/shard_map/ppermute | solution.py:372
  37.8 18.0 %collective-permute-done.1.b_ref = f32[2,32,2048]{2,1,0:T(8,128)} collective-permute-done((f32[2,32,2048]{2,1,0:T(8,128)}, f32[2,32,2048]{2,1,0:T(8,128)}, u32[]{:S(2)}, u32[]{:S(2)}) %collective-permute-start.1) | collective-permute-done | bytes 524320 | tf_op jit(solution)/shard_map/ppermute | solution.py:372
  55.8 29.8 %all-gather.5.cloned.1.call-done = f32[1,8,2,128,128]{4,3,2,0,1:T(8,128)} async-done(((f32[1,2,2,128,128]{4,3,2,0,1:T(8,128)}), f32[1,8,2,128,128]{4,3,2,0,1:T(8,128)}) %all-gather.5.cloned.1.call-update) | async-done | bytes 1048592 | tf_op jit(solution)/shard_map/all_gather | solution.py:389
  85.6 3.4 %copy-done.2 = f32[1,2,512,2048]{3,2,1,0:T(8,128)S(1)} copy-done((f32[1,2,512,2048]{3,2,1,0:T(8,128)S(1)}, f32[1,2,512,2048]{3,2,1,0:T(8,128)}, u32[]{:S(2)}) %copy-start.2) | copy-done | bytes 8388632
  89.0 1.2 copy-done.8
  90.2 1.2 copy-done.10
  92.1 19.1 %collective-permute-start.3 = (f32[2,64,128]{2,1,0:T(8,128)S(1)}, f32[2,64,128]{2,1,0:T(8,128)S(1)}, u32[]{:S(2)}, u32[]{:S(2)}) collective-permute-start(f32[2,64,128]{2,1,0:T(8,128)S(1)} %get-tuple-element.9), channel_id=1, source_target_pairs={{0,1},{1,2},{2,3},{4,5},{5,6},{6,7},{8,9},{9,10},{10,11},{12,13},{... | collective-permute-start | bytes 196616 | tf_op jit(solution)/shard_map/ppermute | solution.py:372
  111.2 1.3 collective-permute-start.4
  112.5 3.4 %copy-done.3 = f32[1,2,512,2048]{3,2,1,0:T(8,128)S(1)} copy-done((f32[1,2,512,2048]{3,2,1,0:T(8,128)S(1)}, f32[1,2,512,2048]{3,2,1,0:T(8,128)}, u32[]{:S(2)}) %copy-start.3) | copy-done | bytes 8388632
  115.9 7.2 %lesser_more.2.rest_0_ = f32[4,256,256]{2,1,0:T(8,128)S(1)} custom-call(s32[2,6]{1,0:T(2,128)S(1)} %get-tuple-element.20.idx_ref, f32[1,2,512,2048]{3,2,1,0:T(8,128)S(1)} %copy-done.3, f32[1,8,2,128,128]{4,3,2,1,0:T(8,128)S(1)} %bitcast.28, f32[4,256,256]{2,1,0:T(8,128)S(1)} %copy-done.5), custom_call_target="tpu_custom_call", output_to_operand_aliasing={{}: (3, {})} | custom-call | flops 3623878656 | bytes 5242880 | tf_op jit(solution)/shard_map/lesser_more/pallas_call | solution.py:101
  123.1 7.2 %lesser_more.3.acc_ref = f32[4,256,256]{2,1,0:T(8,128)S(1)} custom-call(s32[2,6]{1,0:T(2,128)S(1)} %get-tuple-element.21.idx_ref, f32[1,2,512,2048]{3,2,1,0:T(8,128)S(1)} %copy-done.3, f32[1,8,2,128,128]{4,3,2,1,0:T(8,128)S(1)} %bitcast.26, f32[4,256,256]{2,1,0:T(8,128)S(1)} %lesser_more.2.rest_0_), custom_call_target="tpu_custom_call", output_to_operand_aliasing={{}: (3, {})} | custom-call | flops 3623878656 | bytes 5242880 | tf_op jit(solution)/shard_map/lesser_more/pallas_call | solution.py:101
  130.9 0.8 copy-done.7
  131.7 3.7 %all-to-all-start = ((f32[8,2,8,8,128]{4,3,2,1,0:T(8,128)}), f32[8,2,8,8,128]{4,3,2,1,0:T(8,128)S(1)}, u32[]{:S(2)}, u32[]{:S(2)}) async-start(f32[8,2,8,8,128]{4,3,2,1,0:T(8,128)} %copy-done.7), calls=%async_computation | async-start | bytes 1048576 | tf_op jit(solution)/shard_map/all_to_all | solution.py:443
  135.4 0.9 broadcast_multiply_fusion
  136.3 1.8 %mul.99.mix_ref = f32[128,128]{1,0:T(8,128)} reshape(f32[16,8,8,16]{3,2,1,0:T(8,128)} %broadcast_multiply_fusion) | data formatting | bytes 131072 | tf_op jit(solution)/shard_map/mul | solution.py:367
  138.2 6.9 %all-to-all-done.recv_ref = f32[8,2,8,8,128]{4,3,2,1,0:T(8,128)S(1)} async-done(((f32[8,2,8,8,128]{4,3,2,1,0:T(8,128)}), f32[8,2,8,8,128]{4,3,2,1,0:T(8,128)S(1)}, u32[]{:S(2)}, u32[]{:S(2)}) %all-to-all-start) | async-done | bytes 524320 | tf_op jit(solution)/shard_map/all_to_all | solution.py:443
  145.1 0.8 copy-done.12
  145.9 2.6 %scatter.1 = f32[8,128,128]{2,1,0:T(8,128)S(1)} custom-call(f32[8,2,8,8,128]{4,3,2,1,0:T(8,128)S(1)} %all-to-all-done.recv_ref, bf16[1024,1024]{1,0:T(8,128)(2,1)S(1)} %picks.1.pick_ref, f32[128,128]{1,0:T(8,128)S(1)} %copy-done.12, f32[192,128]{1,0:T(8,128)S(1)} %constant_dynamic-slice_fusion.dham_ref), custom_call_target="tpu_custom_call" | custom-call | tf_op jit(solution)/shard_map/scatter/pallas_call | solution.py:338
  148.6 12.2 %all_to_all.10 = f32[8,128,128]{2,1,0:T(8,128)S(1)} all-to-all(f32[8,128,128]{2,1,0:T(8,128)S(1)} %scatter.1), channel_id=1, replica_groups=mesh['energy'=8,'orb'=4] {'energy'}, dimensions={0} | all-to-all | bytes 1048576 | tf_op jit(solution)/shard_map/all_to_all | solution.py:445
  160.7 0.8 copy.35
  (42 shorter events, 2.5 us)
Async XLA Ops:
  6.5 131.6 %copy-start = (f32[1024,3,8,8]{0,3,2,1:T(8,128)S(1)}, f32[1024,3,8,8]{0,3,2,1:T(8,128)}, u32[]{:S(2)}) copy-start(f32[1024,3,8,8]{0,3,2,1:T(8,128)} %param.11) | copy-start | bytes 2359300
  6.5 49.3 %all-gather.3.cloned.1.call-start = ((), (), s32[]{:S(2)}) async-start(), calls=%async_computation.2 | async-start | bytes 1310720 | tf_op jit(solution)/shard_map/all_gather | solution.py:389
  8.5 77.1 %all-gather.5.cloned.1.call-start = ((), (), s32[]{:S(2)}) async-start(), calls=%async_computation.3 | async-start | bytes 1310720 | tf_op jit(solution)/shard_map/all_gather | solution.py:389
  11.3 26.5 %collective-permute-start = (f32[2,32,2048]{2,1,0:T(8,128)}, f32[2,32,2048]{2,1,0:T(8,128)S(1)}, u32[]{:S(2)}, u32[]{:S(2)}) collective-permute-start(f32[2,32,2048]{2,1,0:T(8,128)} %get-tuple-element.12), channel_id=1, source_target_pairs={{0,1},{3,2},{4,5},{7,6},{8,9},{11,10},{12,13},{15,14},{16,17},{19,... | collective-permute-start | bytes 1572872 | tf_op jit(solution)/shard_map/ppermute | solution.py:372
  16.3 39.5 %collective-permute-start.1 = (f32[2,32,2048]{2,1,0:T(8,128)}, f32[2,32,2048]{2,1,0:T(8,128)}, u32[]{:S(2)}, u32[]{:S(2)}) collective-permute-start(f32[2,32,2048]{2,1,0:T(8,128)} %get-tuple-element.13), channel_id=1, source_target_pairs={{0,1},{1,2},{4,5},{5,6},{8,9},{9,10},{12,13},{13,14},{16,17},{17,1... | collective-permute-start | bytes 1572872 | tf_op jit(solution)/shard_map/ppermute | solution.py:372
  18.4 37.4 %collective-permute-start.2 = (f32[2,32,2048]{2,1,0:T(8,128)}, f32[2,32,2048]{2,1,0:T(8,128)}, u32[]{:S(2)}, u32[]{:S(2)}) collective-permute-start(f32[2,32,2048]{2,1,0:T(8,128)} %get-tuple-element.11), channel_id=1, source_target_pairs={{2,1},{3,2},{6,5},{7,6},{10,9},{11,10},{14,13},{15,14},{18,17},{19... | collective-permute-start | bytes 1572872 | tf_op jit(solution)/shard_map/ppermute | solution.py:372
  23.3 3.4 %copy-start.1 = (f32[1,2,512,2048]{3,2,1,0:T(8,128)S(1)}, f32[1,2,512,2048]{3,2,1,0:T(8,128)}, u32[]{:S(2)}) copy-start(f32[1,2,512,2048]{3,2,1,0:T(8,128)} %green_ref.7) | copy-start | bytes 25165828
  26.7 1.1 copy-start.6
  32.7 1.0 copy-start.4
  85.6 3.4 %copy-start.2 = (f32[1,2,512,2048]{3,2,1,0:T(8,128)S(1)}, f32[1,2,512,2048]{3,2,1,0:T(8,128)}, u32[]{:S(2)}) copy-start(f32[1,2,512,2048]{3,2,1,0:T(8,128)} %green_ref.7) | copy-start | bytes 25165828
  89.0 1.2 copy-start.8
  90.2 1.2 copy-start.10
  91.4 21.1 %copy-start.5 = (f32[4,256,256]{2,1,0:T(8,128)S(1)}, f32[4,256,256]{2,1,0:T(8,128)}, u32[]{:S(2)}) copy-start(f32[4,256,256]{2,1,0:T(8,128)} %copy-done.4) | copy-start | bytes 3145732
  91.4 21.1 %copy-start.11 = (f32[1,8,2,128,128]{4,3,2,0,1:T(8,128)S(1)}, f32[1,8,2,128,128]{4,3,2,0,1:T(8,128)}, u32[]{:S(2)}) copy-start(f32[1,8,2,128,128]{4,3,2,0,1:T(8,128)} %all-gather.5.cloned.1.call-done) | copy-start | bytes 3145732
  91.5 31.7 %copy-start.9 = (f32[1,8,2,128,128]{4,3,2,0,1:T(8,128)S(1)}, f32[1,8,2,128,128]{4,3,2,0,1:T(8,128)}, u32[]{:S(2)}) copy-start(f32[1,8,2,128,128]{4,3,2,0,1:T(8,128)} %all-gather.3.cloned.1.call-done) | copy-start | bytes 3145732
  92.1 38.2 %collective-permute-start.3 = (f32[2,64,128]{2,1,0:T(8,128)S(1)}, f32[2,64,128]{2,1,0:T(8,128)S(1)}, u32[]{:S(2)}, u32[]{:S(2)}) collective-permute-start(f32[2,64,128]{2,1,0:T(8,128)S(1)} %get-tuple-element.9), channel_id=1, source_target_pairs={{0,1},{1,2},{2,3},{4,5},{5,6},{6,7},{8,9},{9,10},{10,11},{12,13},{... | collective-permute-start | bytes 196616 | tf_op jit(solution)/shard_map/ppermute | solution.py:372
  111.2 19.1 %collective-permute-start.4 = (f32[2,64,128]{2,1,0:T(8,128)S(1)}, f32[2,64,128]{2,1,0:T(8,128)S(1)}, u32[]{:S(2)}, u32[]{:S(2)}) collective-permute-start(f32[2,64,128]{2,1,0:T(8,128)S(1)} %get-tuple-element.10), channel_id=1, source_target_pairs={{1,0},{2,1},{3,2},{5,4},{6,5},{7,6},{9,8},{10,9},{11,10},{13,12},{... | collective-permute-start | bytes 196616 | tf_op jit(solution)/shard_map/ppermute | solution.py:372
  112.5 3.4 %copy-start.3 = (f32[1,2,512,2048]{3,2,1,0:T(8,128)S(1)}, f32[1,2,512,2048]{3,2,1,0:T(8,128)}, u32[]{:S(2)}) copy-start(f32[1,2,512,2048]{3,2,1,0:T(8,128)} %green_ref.7) | copy-start | bytes 25165828
  130.9 0.8 copy-start.7
  131.7 13.4 %all-to-all-start = ((f32[8,2,8,8,128]{4,3,2,1,0:T(8,128)}), f32[8,2,8,8,128]{4,3,2,1,0:T(8,128)S(1)}, u32[]{:S(2)}, u32[]{:S(2)}) async-start(f32[8,2,8,8,128]{4,3,2,1,0:T(8,128)} %copy-done.7), calls=%async_computation | async-start | bytes 1048576 | tf_op jit(solution)/shard_map/all_to_all | solution.py:443
  145.1 0.8 copy-start.12
Sparse Core Ops, SparseCore 0:
  8.9 44.6 all-gather.2
  55.2 30.3 all-gather.4

commit v2 on v1

--- a/solution.py
+++ b/solution.py
@@ -33,198 +33,231 @@
     return dot(a[0], b[0], dims) + dot(a[0], b[1], dims) + dot(a[1], b[0], dims)
 
 
-def one_block(real, imag, self_real, self_imag, hi_ref, lo_ref, acc_ref, tiles, pad):
-    rows = real.shape[0]
-    hi, lo = halves(jnp.concatenate([real, imag], axis=1))
-    hi_ref[pad : pad + rows, :] = hi
-    lo_ref[pad : pad + rows, :] = lo
-    weight = halves(
-        jnp.concatenate(
-            [
-                jnp.concatenate([self_real, self_imag], axis=1),
-                jnp.concatenate([-self_imag, self_real], axis=1),
-            ],
-            axis=0,
+def blocks_at_once(held):
+    return 2 if held % 2 == 0 else 1
+
+
+def some_blocks(fields, weights, hi_ref, lo_ref, acc_ref, edges):
+    rows = fields[0][0].shape[0]
+    wide = 2 * BS
+    hi, lo = halves(jnp.concatenate([x for pair in fields for x in pair], axis=1))
+    hi_ref[MARGIN : MARGIN + rows, :] = hi
+    lo_ref[MARGIN : MARGIN + rows, :] = lo
+    split = []
+    for real, imag in weights:
+        top = jnp.concatenate([real, imag], axis=1)
+        split.append(halves(jnp.concatenate([top, jnp.concatenate([-imag, real], axis=1)], axis=0)))
+    tiles = rows // TILE
+    for t in range(tiles):
+        row, window = MARGIN + t * TILE, t * TILE
+        both = []
+        for n, weight in enumerate(split):
+            cols = slice(n * wide, (n + 1) * wide)
+            left = (hi_ref[row : row + TILE, cols], lo_ref[row : row + TILE, cols])
+            product = dot3(left, weight, NN)
+            turned = jnp.concatenate([product[:, BS:], -product[:, :BS]], axis=1)
+            both.append(halves(jnp.concatenate([product, turned], axis=0)))
+            if edges is not None:
+                for ref, part in zip(edges, both[-1]):
+                    if t == 0:
+                        ref[n, :MARGIN, :] = part[:MARGIN]
+                    if t == tiles - 1:
+                        ref[n, 3 * MARGIN :, :] = part[TILE - MARGIN : TILE]
+        both = [jnp.concatenate(parts, axis=1) for parts in zip(*both)]
+        upto = window + TILE + 2 * MARGIN
+        acc_ref[t] = acc_ref[t] + dot3(both, (hi_ref[window:upto, :], lo_ref[window:upto, :]), NT)
+    if edges is not None:
+        for n, weight in enumerate(split):
+            cols = slice(n * wide, (n + 1) * wide)
+            outer = [
+                jnp.concatenate(
+                    [ref[MARGIN : 2 * MARGIN, cols], ref[rows : rows + MARGIN, cols]], axis=0
+                )
+                for ref in (hi_ref, lo_ref)
+            ]
+            for ref, part in zip(edges, halves(dot3(outer, weight, NT))):
+                ref[n, MARGIN : 3 * MARGIN, :] = part
+
+
+def lesser_kernel(shards, first, idx_ref, green_ref, *rest):
+    sigmas, rest = rest[:shards], rest[shards:]
+    if not first:
+        before_ref, rest = rest[0], rest[1:]
+    acc_ref, keep_hi_ref, keep_lo_ref, buf, hi_ref, lo_ref, sem = rest
+    rows, held = green_ref.shape[2], sigmas[0].shape[1]
+    once = blocks_at_once(held)
+
+    def fetch(shard, s):
+        col = pl.multiple_of((idx_ref[shard] * held + s) * BS, BS)
+        at = shard * held + s
+        return pltpu.make_async_copy(
+            green_ref.at[0, :, :, pl.ds(col, BS)], buf.at[at], sem.at[at]
         )
-    )
-    for t, (row, window, width) in enumerate(tiles):
-        left = (hi_ref[row : row + TILE, :], lo_ref[row : row + TILE, :])
-        product = dot3(left, weight, NN)
-        turned = jnp.concatenate([product[:, BS:], -product[:, :BS]], axis=1)
-        both = halves(jnp.concatenate([product, turned], axis=0))
-        near = (hi_ref[window : window + width, :], lo_ref[window : window + width, :])
-        acc_ref[t] = acc_ref[t] + dot3(both, near, NT)
-
-
-def main_tiles(rows):
-    return [(MARGIN + t * TILE, t * TILE, TILE + 2 * MARGIN) for t in range(rows // TILE)]
-
-
-def lesser_kernel(count, first, idx_ref, green_ref, sigma_ref, *rest):
-    if first:
-        acc_ref, buf, hi_ref, lo_ref, sem = rest
-    else:
-        before_ref, acc_ref, buf, hi_ref, lo_ref, sem = rest
-    rows = green_ref.shape[2]
-
-    def fetch(s):
-        col = pl.multiple_of(idx_ref[1, s] * BS, BS)
-        return pltpu.make_async_copy(
-            green_ref.at[0, :, :, pl.ds(col, BS)], buf.at[s], sem.at[s]
-        )
-
-    for s in range(count):
-        fetch(s).start()
+
+    def valid(shard):
+        return idx_ref[shards + shard] == 1
+
+    for shard in range(shards):
+
+        @pl.when(valid(shard))
+        def _():
+            for s in range(held):
+                fetch(shard, s).start()
+
     acc_ref[...] = jnp.zeros_like(acc_ref) if first else before_ref[...]
     for ref in (hi_ref, lo_ref):
-        ref[:MARGIN, :] = jnp.zeros((MARGIN, 2 * BS), BF16)
-        ref[MARGIN + rows :, :] = jnp.zeros((MARGIN, 2 * BS), BF16)
-
-    def step(s, carry):
-        fetch(s).wait()
-        at = idx_ref[0, s]
-        one_block(
-            buf[s, 0], buf[s, 1], sigma_ref[0, at, 0], sigma_ref[0, at, 1],
-            hi_ref, lo_ref, acc_ref, main_tiles(rows), MARGIN,
-        )
-        return carry
-
-    lax.fori_loop(0, count, step, 0)
-
-
-def lesser_part(green, sigma, index, before):
-    rows, count = green.shape[2], index.shape[1]
-    tiles = rows // TILE
+        ref[:MARGIN, :] = jnp.zeros((MARGIN, ref.shape[1]), BF16)
+        ref[MARGIN + rows :, :] = jnp.zeros((MARGIN, ref.shape[1]), BF16)
+
+    for shard in range(shards):
+
+        @pl.when(valid(shard))
+        def _():
+            def step(g, carry):
+                fields, weights = [], []
+                for n in range(once):
+                    s = g * once + n
+                    fetch(shard, s).wait()
+                    at = shard * held + s
+                    fields.append((buf[at, 0], buf[at, 1]))
+                    weights.append((sigmas[shard][0, s, 0], sigmas[shard][0, s, 1]))
+                slots = pl.ds(shard * held + g * once, once)
+                some_blocks(
+                    fields, weights, hi_ref, lo_ref, acc_ref,
+                    (keep_hi_ref.at[slots], keep_lo_ref.at[slots]),
+                )
+                return carry
+
+            lax.fori_loop(0, held // once, step, 0)
+
+
+def lesser_part(green, sigmas, index, before):
+    rows, held, shards = green.shape[2], sigmas[0].shape[1], len(sigmas)
+    tiles, count = rows // TILE, held * shards
+    once = blocks_at_once(held)
     first = before is None
-    acc = jax.ShapeDtypeStruct((tiles, 2 * TILE, TILE + 2 * MARGIN), F32)
     vmem = pl.BlockSpec(memory_space=pltpu.VMEM)
+    keep = jax.ShapeDtypeStruct((count, 4 * MARGIN, 2 * BS), BF16)
     return pl.pallas_call(
-        functools.partial(lesser_kernel, count, first),
-        out_shape=acc,
+        functools.partial(lesser_kernel, shards, first),
+        out_shape=(
+            jax.ShapeDtypeStruct((tiles, 2 * TILE, TILE + 2 * MARGIN), F32),
+            keep,
+            keep,
+        ),
         in_specs=[
             pl.BlockSpec(memory_space=pltpu.SMEM),
-            pl.BlockSpec(memory_space=pl.ANY),
-            vmem,
+            pl.BlockSpec(memory_space=pltpu.HBM),
         ]
-        + ([] if first else [vmem]),
-        out_specs=vmem,
+        + [vmem] * (shards if first else shards + 1),
+        out_specs=(vmem, vmem, vmem),
         scratch_shapes=[
             pltpu.VMEM((count, 2, rows, BS), F32),
-            pltpu.VMEM((rows + 2 * MARGIN, 2 * BS), BF16),
-            pltpu.VMEM((rows + 2 * MARGIN, 2 * BS), BF16),
+            pltpu.VMEM((rows + 2 * MARGIN, once * 2 * BS), BF16),
+            pltpu.VMEM((rows + 2 * MARGIN, once * 2 * BS), BF16),
             pltpu.SemaphoreType.DMA((count,)),
         ],
-        input_output_aliases={} if first else {3: 0},
+        input_output_aliases={} if first else {2 + shards: 0},
         compiler_params=pltpu.CompilerParams(vmem_limit_bytes=24 << 20),
         cost_estimate=pl.CostEstimate(
-            flops=count * 6 * rows * 2 * BS * (2 * BS + 4 * TILE),
-            bytes_accessed=count * rows * BS * 8 + 8 * tiles * TILE * 512,
+            flops=held * 6 * rows * 2 * BS * (2 * BS + 4 * TILE),
+            bytes_accessed=held * rows * BS * 8 + 8 * tiles * TILE * 512,
             transcendentals=0,
         ),
         name="lesser_own" if first else "lesser_more",
-    )(index, green, sigma, *([] if first else [before]))
-
-
-def edge_kernel(
-    blocks, flag_ref, green_ref, a_ref, b_ref, c_ref, sig0_ref, sig1_ref,
-    left_ref, right_ref, own_ref, buf, hi_ref, lo_ref, acc_ref, sem,
-):
-    rows = green_ref.shape[2]
-    tiles = [(0, 0, TILE), (TILE, TILE, TILE)]
-    size = 2 * TILE
-
-    def fetch(s):
-        cols = pl.ds(pl.multiple_of(s * BS, BS), BS)
-        slot = lax.rem(s, 2)
-        parts = [
-            (a_ref.at[:, :, cols], 0),
-            (b_ref.at[:, :, cols], HALF),
-            (green_ref.at[0, :, pl.ds(0, MARGIN), cols], MARGIN),
-            (green_ref.at[0, :, pl.ds(rows - MARGIN, MARGIN), cols], TILE),
-            (c_ref.at[:, :, cols], TILE + MARGIN),
-            (a_ref.at[:, :, cols], TILE + MARGIN + HALF),
-        ]
-        return [
-            pltpu.make_async_copy(
-                src, buf.at[slot, :, pl.ds(at, src.shape[1]), :], sem.at[slot, k]
+    )(index, green, *sigmas, *([] if first else [before]))
+
+
+def edge_kernel(counts, idx_ref, a_ref, b_ref, c_ref, *rest):
+    parts = len(counts)
+    keeps, rest = rest[: 2 * parts], rest[2 * parts :]
+    left_ref, right_ref, own_ref, acc_ref = rest
+    base = 2 * sum(counts)
+    active, from_left, from_right = [idx_ref[base + k] == 1 for k in range(3)]
+    limit = idx_ref[base + 3]
+    acc_ref[...] = jnp.zeros_like(acc_ref)
+
+    def add(col, keep_hi, keep_lo):
+        cols = pl.ds(pl.multiple_of(col * BS, BS), BS)
+        more = [a_ref[part, :, cols] for part in range(2)]
+        near = [b_ref[part, :, cols] for part in range(2)]
+        after = [c_ref[part, :, cols] for part in range(2)]
+        sides = []
+        for part in range(2):
+            outer = jnp.where(from_left, more[part], 0.0)
+            beyond = jnp.where(from_right, more[part], 0.0)
+            sides.append(
+                (
+                    jnp.concatenate([outer, near[part]], axis=0),
+                    jnp.concatenate([after[part], beyond], axis=0),
+                )
             )
-            for k, (src, at) in enumerate(parts)
-        ]
-
-    acc_ref[...] = jnp.zeros_like(acc_ref)
-
-    @pl.when(flag_ref[0] == 1)
+        for side in range(2):
+            real, imag = sides[0][side], sides[1][side]
+            halo = jnp.concatenate(
+                [
+                    jnp.concatenate([real, imag], axis=1),
+                    jnp.concatenate([-imag, real], axis=1),
+                ],
+                axis=0,
+            )
+            rows = slice(side * TILE, (side + 1) * TILE)
+            acc_ref[side] = acc_ref[side] + dot3(
+                halves(halo), (keep_hi[rows, :], keep_lo[rows, :]), NT
+            )
+
+    @pl.when(active)
     def _():
-        for copy in fetch(0):
-            copy.start()
-        row = lax.broadcasted_iota(jnp.int32, (size, BS), 0)
-        keep = (row >= HALF) | (flag_ref[1] == 1)
-        keep &= (row < TILE) | (row >= TILE + MARGIN) | (row < TILE + flag_ref[3])
-        keep &= (row < size - HALF) | (flag_ref[2] == 1)
-
-        def step(s, carry):
-            for copy in fetch(s):
-                copy.wait()
-
-            @pl.when(s + 1 < blocks)
-            def _():
-                for copy in fetch(s + 1):
-                    copy.start()
-
-            slot = lax.rem(s, 2)
-            real = jnp.where(keep, buf[slot, 0], 0.0)
-            imag = jnp.where(keep, buf[slot, 1], 0.0)
-            owner, local = s // flag_ref[4], lax.rem(s, flag_ref[4])
-            piece = flag_ref[4] // 2
-            at = owner * piece + lax.rem(local, piece)
-            low = local < piece
-            self_real = jnp.where(low, sig0_ref[0, at, 0], sig1_ref[0, at, 0])
-            self_imag = jnp.where(low, sig0_ref[0, at, 1], sig1_ref[0, at, 1])
-            one_block(real, imag, self_real, self_imag, hi_ref, lo_ref, acc_ref, tiles, 0)
-            return carry
-
-        lax.fori_loop(0, blocks, step, 0)
+        shard = 0
+        for part, count in enumerate(counts):
+            hi, lo = keeps[2 * part], keeps[2 * part + 1]
+            held = hi.shape[0] // count
+            for k in range(count):
+                number, valid = idx_ref[2 * shard], idx_ref[2 * shard + 1]
+                shard += 1
+
+                @pl.when(valid == 1)
+                def _():
+                    def step(s, carry):
+                        at = k * held + s
+                        add(number * held + s, hi.at[at], lo.at[at])
+                        return carry
+
+                    lax.fori_loop(0, held, step, 0)
 
     lane = lax.broadcasted_iota(jnp.int32, (MARGIN, LANES), 1)
+    row = lax.broadcasted_iota(jnp.int32, (MARGIN, LANES), 0)
     low = lane < MARGIN
-    for part in range(2):
-        base = part * TILE
-        outer_l = acc_ref[0, base : base + MARGIN, :]
-        inner_l = acc_ref[0, base + MARGIN : base + TILE, :]
-        inner_r = acc_ref[1, base : base + MARGIN, :]
-        outer_r = acc_ref[1, base + MARGIN : base + TILE, :]
-        left_ref[part] = jnp.where(low, 0.0, outer_l)
-        right_ref[part] = jnp.where(low, outer_r, 0.0)
-        own_ref[0, part] = jnp.where(low, inner_l, 0.0)
-        own_ref[1, part] = jnp.where(low, 0.0, inner_r)
-
-
-def edge_part(flags, green, a, b, c, sig0, sig1):
-    blocks = sig0.shape[1] + sig1.shape[1]
+    left, right = acc_ref[0], acc_ref[1]
+    turned_left, turned_right = left.T[:MARGIN], right.T[MARGIN:]
+    left_ref[0] = jnp.where(low, 0.0, left[:MARGIN])
+    left_ref[1] = jnp.where(low, 0.0, -left[MARGIN:])
+    right_ref[0] = jnp.where(lane < limit, right[:MARGIN], 0.0)
+    right_ref[1] = jnp.where(lane < limit, -right[MARGIN:], 0.0)
+    own_ref[0, 0] = jnp.where(low, turned_left, 0.0)
+    own_ref[0, 1] = jnp.where(low, pltpu.roll(turned_left, MARGIN, 1), 0.0)
+    mine = jnp.logical_and(row < limit, lane >= MARGIN)
+    own_ref[1, 0] = jnp.where(mine, pltpu.roll(turned_right, MARGIN, 1), 0.0)
+    own_ref[1, 1] = jnp.where(mine, turned_right, 0.0)
+
+
+def edge_part(flags, a, b, c, keeps, counts):
     vmem = pl.BlockSpec(memory_space=pltpu.VMEM)
-    hbm = pl.BlockSpec(memory_space=pl.ANY)
     side = jax.ShapeDtypeStruct((2, MARGIN, LANES), F32)
-    size = 2 * TILE
     return pl.pallas_call(
-        functools.partial(edge_kernel, blocks),
+        functools.partial(edge_kernel, counts),
         out_shape=(side, side, jax.ShapeDtypeStruct((2, 2, MARGIN, LANES), F32)),
-        in_specs=[pl.BlockSpec(memory_space=pltpu.SMEM), hbm, hbm, hbm, hbm, vmem, vmem],
+        in_specs=[pl.BlockSpec(memory_space=pltpu.SMEM)] + [vmem] * (3 + len(keeps)),
         out_specs=(vmem, vmem, vmem),
-        scratch_shapes=[
-            pltpu.VMEM((2, 2, size, BS), F32),
-            pltpu.VMEM((size, 2 * BS), BF16),
-            pltpu.VMEM((size, 2 * BS), BF16),
-            pltpu.VMEM((2, 2 * TILE, TILE), F32),
-            pltpu.SemaphoreType.DMA((2, 6)),
-        ],
-        compiler_params=pltpu.CompilerParams(vmem_limit_bytes=16 << 20),
+        scratch_shapes=[pltpu.VMEM((2, TILE, TILE), F32)],
+        compiler_params=pltpu.CompilerParams(vmem_limit_bytes=24 << 20),
         cost_estimate=pl.CostEstimate(
-            flops=blocks * 6 * size * 2 * BS * (2 * BS + 2 * TILE),
-            bytes_accessed=blocks * size * BS * 8 + blocks * BS * BS * 8,
+            flops=a.shape[2] * 2 * 12 * TILE * 2 * TILE,
+            bytes_accessed=a.shape[2] * 2 * 4 * TILE * 4,
             transcendentals=0,
         ),
         name="edges",
-    )(flags, green, a, b, c, sig0, sig1)
+    )(flags, a, b, c, *keeps)
 
 
 def band_kernel(acc_ref, own_ref, from_left_ref, from_right_ref, out_ref, rows_ref):
@@ -383,12 +416,6 @@
     pairs = group * degree
     padded = -(-pairs // LANES) * LANES
     held = sigma.shape[1]
-    piece = held // 2
-
-    sig = [
-        lax.all_gather(sigma[:, h * piece : (h + 1) * piece], "orb", axis=1, tiled=True)
-        for h in range(2)
-    ]
 
     far = peers >= 4
     up = [(i, i + 1) for i in range(peers - 1)]
@@ -407,21 +434,25 @@
         from_left = from_right = jnp.zeros((), bool)
         active = jnp.ones((), bool)
     limit = jnp.where(from_right, MARGIN, HALF)
-    flags = jnp.stack(
-        [x.astype(jnp.int32) for x in (active, from_left, from_right, limit)]
-        + [jnp.int32(held)]
-    )
-
-    slot = jnp.arange(held, dtype=jnp.int32)
-    acc = lesser_part(green, sigma, jnp.stack([slot, z * held + slot]), None)
-    slot = jnp.arange((peers - 1) * piece, dtype=jnp.int32)
-    owner = lax.rem(z + 1 + slot // piece, peers)
-    at = slot % piece
-    for h in range(2):
-        index = jnp.stack([owner * piece + at, owner * held + h * piece + at])
-        acc = lesser_part(green, sig[h], index, acc)
+
+    one = jnp.ones((), jnp.int32)
+    acc, *keeps = lesser_part(green, [sigma], jnp.stack([z, one]), None)
+    counts, listed = [1], [z, one]
+    rightward = leftward = sigma
+    for k in range(1, peers):
+        rightward = send(rightward, up[k - 1 :])
+        leftward = send(leftward, down[: peers - k])
+        numbers = [jnp.maximum(z - k, 0), jnp.minimum(z + k, peers - 1)]
+        valid = [(z >= k).astype(jnp.int32), (z + k < peers).astype(jnp.int32)]
+        acc, *more_keeps = lesser_part(
+            green, [rightward, leftward], jnp.stack(numbers + valid), acc
+        )
+        keeps += more_keeps
+        counts.append(2)
+        listed += [numbers[0], valid[0], numbers[1], valid[1]]
+    listed += [x.astype(jnp.int32) for x in (active, from_left, from_right, limit)]
     to_left, to_right, own = edge_part(
-        flags, green, other, near_right, near_left, sig[0], sig[1]
+        jnp.stack(listed), other, near_right, near_left, keeps, tuple(counts)
     )
     back_right = send(to_left, down)
     back_left = send(to_right, up)

time: 169 us -> 105 us (0.62)
  waiting for transfers between devices: 58.9 us -> 19.7 us
  between operations: 13.6 us -> 0.22 us
  local copies, waits for them, and re-layouts: 22.7 us -> 10.5 us
  Pallas kernels: 23.8 us -> 25.8 us
    all_gather x2 -> x0, waiting for transfers between devices: 29.8 us -> none  [per_device(): lax.all_gather(sigma[:, h * piece:(h + 1) * piece], 'orb', axis=1, tiled=...]
    unnamed x28 -> x12, local copies, waits for them, and re-layouts: 17.2 us -> 6.92 us
    ppermute x5 -> x11, waiting for transfers between devices: 22.1 us -> 12.8 us  [send(): return lax.ppermute(x, 'orb', pairs)]
    pallas_call x4 -> x5, Pallas kernels: 20 us -> 22 us  [the longest x4 20.6 us: lesser_part(): pl.pallas_call(functools.partial(lesser_kernel, shards, first), out_shape...]
    slice x1 -> x0, local copies, waits for them, and re-layouts: 1.95 us -> none  [per_device(): sigma[:, h * piece:(h + 1) * piece]]
    ppermute x5 -> x11, starting transfers between devices: 28.9 us -> 27.6 us  [send(): return lax.ppermute(x, 'orb', pairs)]
  transfers between devices with their start and end apart: 8 -> 12, of which waited for: 4 -> 6; matrix products, arithmetic and copies ran while one was open for 5% -> 8% of each run, Pallas kernels for 12% -> 20%
where the time goes in v2:
time: 105 us
  starting transfers between devices  31.4 us (30%)
  Pallas kernels  25.8 us (25%)
  waiting for transfers between devices  19.7 us (19%)
  blocking collectives  12.2 us (12%)
  local copies, waits for them, and re-layouts  10.5 us (10%)
  other arithmetic  4.88 us (5%)
    ppermute x11, starting transfers between devices, send(): return lax.ppermute(x, 'orb', pairs)  27.6 us
    pallas_call x4, Pallas kernels, lesser_part(): pl.pallas_call(functools.partial(lesser_kernel, shards, first), out_shape...  20.6 us
    ppermute x11, waiting for transfers between devices, send(): return lax.ppermute(x, 'orb', pairs)  12.8 us
    all_to_all x1, blocking collectives, per_device(): lax.all_to_all(spread, 'energy', split_axis=0, concat_axis=0, tiled=True)  12.2 us
    all_to_all x1, waiting for transfers between devices, per_device(): lax.all_to_all(lesser, 'energy', split_axis=0, concat_axis=0, tiled=True)  6.93 us
    unnamed x12, local copies, waits for them, and re-layouts  6.92 us
    all_to_all x1, starting transfers between devices, per_device(): lax.all_to_all(lesser, 'energy', split_axis=0, concat_axis=0, tiled=True)  3.72 us
    squeeze x1, other arithmetic, per_device(): near_left = send(green[0, :, :HALF], down[1:] if far else down)  2.73 us
  transfers between devices with their start and end apart: 12, of which 6 were waited for; matrix products, arithmetic and copies ran while one was open for 8% of the time, Pallas kernels for 20%

profile of v2, /device:TPU:0, one launch (start us, length us, event | category | flops | bytes accessed | tf_op | source)
XLA Modules:
  0.0 104.6 jit_solution(17381714435503505742)
XLA Ops:
  0.0 5.9 %collective-permute-start = (f32[1,4,2,128,128]{4,3,2,1,0:T(8,128)}, f32[1,4,2,128,128]{4,3,2,1,0:T(8,128)}, u32[]{:S(2)}, u32[]{:S(2)}) collective-permute-start(f32[1,4,2,128,128]{4,3,2,1,0:T(8,128)} %rest_0_.1), channel_id=1, source_target_pairs={{0,1},{1,2},{2,3},{4,5},{5,6},{6,7},{8,9},{9,10},{10,11},{12,13},{... | collective-permute-start | bytes 1572872 | tf_op jit(solution)/shard_map/ppermute | solution.py:405
  5.9 1.3 %collective-permute-start.3 = (f32[1,4,2,128,128]{4,3,2,1,0:T(8,128)}, f32[1,4,2,128,128]{4,3,2,1,0:T(8,128)}, u32[]{:S(2)}, u32[]{:S(2)}) collective-permute-start(f32[1,4,2,128,128]{4,3,2,1,0:T(8,128)} %rest_0_.1), channel_id=1, source_target_pairs={{1,0},{2,1},{3,2},{5,4},{6,5},{7,6},{9,8},{10,9},{11,10},{13,12},{... | collective-permute-start | bytes 1572872 | tf_op jit(solution)/shard_map/ppermute | solution.py:405
  7.2 2.7 %slice_bitcast_fusion = (f32[2,32,2048]{2,1,0:T(8,128)}, f32[2,32,2048]{2,1,0:T(8,128)}, f32[2,32,2048]{2,1,0:T(8,128)}) fusion(f32[1,2,512,2048]{3,2,1,0:T(8,128)} %green_ref.7, pred[]{:T(512)S(6)} %eq.44), kind=kLoop, calls=%fused_computation | loop fusion | flops 131072 | bytes 3670017 | tf_op jit(solution)/shard_map/squeeze | solution.py:424
  9.9 4.6 %collective-permute-start.6 = (f32[2,32,2048]{2,1,0:T(8,128)}, f32[2,32,2048]{2,1,0:T(8,128)S(1)}, u32[]{:S(2)}, u32[]{:S(2)}) collective-permute-start(f32[2,32,2048]{2,1,0:T(8,128)} %get-tuple-element.36), channel_id=1, source_target_pairs={{0,1},{3,2},{4,5},{7,6},{8,9},{11,10},{12,13},{15,14},{16,17},{19,... | collective-permute-start | bytes 1572872 | tf_op jit(solution)/shard_map/ppermute | solution.py:405
  14.5 2.1 %collective-permute-start.7 = (f32[2,32,2048]{2,1,0:T(8,128)}, f32[2,32,2048]{2,1,0:T(8,128)}, u32[]{:S(2)}, u32[]{:S(2)}) collective-permute-start(f32[2,32,2048]{2,1,0:T(8,128)} %get-tuple-element.37), channel_id=1, source_target_pairs={{0,1},{1,2},{4,5},{5,6},{8,9},{9,10},{12,13},{13,14},{16,17},{17,1... | collective-permute-start | bytes 1572872 | tf_op jit(solution)/shard_map/ppermute | solution.py:405
  16.6 1.5 %collective-permute-start.8 = (f32[2,32,2048]{2,1,0:T(8,128)}, f32[2,32,2048]{2,1,0:T(8,128)}, u32[]{:S(2)}, u32[]{:S(2)}) collective-permute-start(f32[2,32,2048]{2,1,0:T(8,128)} %get-tuple-element.35), channel_id=1, source_target_pairs={{2,1},{3,2},{6,5},{7,6},{10,9},{11,10},{14,13},{15,14},{18,17},{19... | collective-permute-start | bytes 1572872 | tf_op jit(solution)/shard_map/ppermute | solution.py:405
  18.0 0.8 constant_dynamic-slice_fusion.1
  19.9 0.8 slice_bitcast_fusion.3
  21.5 1.3 %collective-permute-start.4 = (f32[1,4,2,128,128]{4,3,2,1,0:T(8,128)}, f32[1,4,2,128,128]{4,3,2,1,0:T(8,128)S(1)}, u32[]{:S(2)}, u32[]{:S(2)}) collective-permute-start(f32[1,4,2,128,128]{4,3,2,1,0:T(8,128)} %collective-permute-done.3.rest_1_), channel_id=1, source_target_pairs={{1,0},{2,1},{5,4},{6,5},{9,8},{10,9},{13,12},{14,13},{17,16},{18,1... | collective-permute-start | bytes 1572872 | tf_op jit(solution)/shard_map/ppermute | solution.py:405
  22.8 0.7 iota_add_fusion
  23.6 3.4 %copy-done.1 = f32[1,2,512,2048]{3,2,1,0:T(8,128)S(1)} copy-done((f32[1,2,512,2048]{3,2,1,0:T(8,128)S(1)}, f32[1,2,512,2048]{3,2,1,0:T(8,128)}, u32[]{:S(2)}) %copy-start.1) | copy-done | bytes 8388632
  26.9 1.0 copy-done.4
  28.0 4.9 %lesser_own.1 = (f32[4,256,256]{2,1,0:T(8,128)S(1)}, bf16[4,256,256]{2,1,0:T(8,128)(2,1)S(1)}, bf16[4,256,256]{2,1,0:T(8,128)(2,1)S(1)}) custom-call(s32[2]{0:T(128)S(1)} %pad_add_fusion.3.idx_ref, f32[1,2,512,2048]{3,2,1,0:T(8,128)S(1)} %copy-done.1, f32[1,4,2,128,128]{4,3,2,1,0:T(8,128)S(1)} %copy-done.4), custom_call_target="tpu_custom_call" | custom-call | flops 2415919104 | bytes 4194304 | tf_op jit(solution)/shard_map/lesser_own/pallas_call | solution.py:141
  33.5 4.2 %collective-permute-done.4.rest_1_ = f32[1,4,2,128,128]{4,3,2,1,0:T(8,128)S(1)} collective-permute-done((f32[1,4,2,128,128]{4,3,2,1,0:T(8,128)}, f32[1,4,2,128,128]{4,3,2,1,0:T(8,128)S(1)}, u32[]{:S(2)}, u32[]{:S(2)}) %collective-permute-start.4) | collective-permute-done | bytes 524320 | tf_op jit(solution)/shard_map/ppermute | solution.py:405
  37.7 1.3 %collective-permute-start.5 = (f32[1,4,2,128,128]{4,3,2,1,0:T(8,128)S(1)}, f32[1,4,2,128,128]{4,3,2,1,0:T(8,128)S(1)}, u32[]{:S(2)}, u32[]{:S(2)}) collective-permute-start(f32[1,4,2,128,128]{4,3,2,1,0:T(8,128)S(1)} %collective-permute-done.4.rest_1_), channel_id=1, source_target_pairs={{1,0},{5,4},{9,8},{13,12},{17,16},{21,20},{25,24},{29,28}} | collective-permute-start | bytes 1572872 | tf_op jit(solution)/shard_map/ppermute | solution.py:405
  39.1 5.6 %lesser_more.3 = (f32[4,256,256]{2,1,0:T(8,128)S(1)}, bf16[8,256,256]{2,1,0:T(8,128)(2,1)S(1)}, bf16[8,256,256]{2,1,0:T(8,128)(2,1)S(1)}) custom-call(s32[4]{0:T(128)S(1)} %pad_add_fusion.2.idx_ref, f32[1,2,512,2048]{3,2,1,0:T(8,128)S(1)} %copy-done.1, f32[1,4,2,128,128]{4,3,2,1,0:T(8,128)} %collective-permute-done.rest_0_, ...), custom_call_target="tpu_custom_call", output_to_operand_aliasing={{0}: (4, {})} | custom-call | flops 2415919104 | bytes 4194304 | tf_op jit(solution)/shard_map/lesser_more/pallas_call | solution.py:141
  44.7 5.2 %lesser_more.4 = (f32[4,256,256]{2,1,0:T(8,128)S(1)}, bf16[8,256,256]{2,1,0:T(8,128)(2,1)S(1)}, bf16[8,256,256]{2,1,0:T(8,128)(2,1)S(1)}) custom-call(s32[4]{0:T(128)S(1)} %pad_add_fusion.1.idx_ref, f32[1,2,512,2048]{3,2,1,0:T(8,128)S(1)} %copy-done.1, f32[1,4,2,128,128]{4,3,2,1,0:T(8,128)S(1)} %collective-permute-done.1.rest_0_, ...), custom_call_target="tpu_custom_call", output_to_operand_aliasing={{0}: (4, {})} | custom-call | flops 2415919104 | bytes 4194304 | tf_op jit(solution)/shard_map/lesser_more/pallas_call | solution.py:141
  49.9 6.7 %collective-permute-done.5.rest_1_ = f32[1,4,2,128,128]{4,3,2,1,0:T(8,128)S(1)} collective-permute-done((f32[1,4,2,128,128]{4,3,2,1,0:T(8,128)S(1)}, f32[1,4,2,128,128]{4,3,2,1,0:T(8,128)S(1)}, u32[]{:S(2)}, u32[]{:S(2)}) %collective-permute-start.5) | collective-permute-done | bytes 524320 | tf_op jit(solution)/shard_map/ppermute | solution.py:405
  56.6 5.0 %lesser_more.5 = (f32[4,256,256]{2,1,0:T(8,128)S(1)}, bf16[8,256,256]{2,1,0:T(8,128)(2,1)S(1)}, bf16[8,256,256]{2,1,0:T(8,128)(2,1)S(1)}) custom-call(s32[4]{0:T(128)S(1)} %pad_add_fusion.idx_ref, f32[1,2,512,2048]{3,2,1,0:T(8,128)S(1)} %copy-done.1, f32[1,4,2,128,128]{4,3,2,1,0:T(8,128)S(1)} %collective-permute-done.2.rest_0_, ...), custom_call_target="tpu_custom_call", output_to_operand_aliasing={{0}: (4, {})} | custom-call | flops 2415919104 | bytes 4194304 | tf_op jit(solution)/shard_map/lesser_more/pallas_call | solution.py:141
  61.6 1.4 %edges.1 = (f32[2,64,128]{2,1,0:T(8,128)S(1)}, f32[2,64,128]{2,1,0:T(8,128)S(1)}, f32[2,2,64,128]{3,2,1,0:T(8,128)S(1)}) custom-call(s32[18]{0:T(128)S(1)} %stack.136.idx_ref, f32[2,32,2048]{2,1,0:T(8,128)S(1)} %collective-permute-done.6.a_ref, f32[2,32,2048]{2,1,0:T(8,128)} %collective-permute-done.7.b_ref, f32[2,32,2048]{2,1,0:T(8,128)} %collective-permute-done.8.c_ref, ...), custom_call_target="tpu_custom_call" | custom-call | flops 1610612736 | bytes 8388608 | tf_op jit(solution)/shard_map/edges/pallas_call | solution.py:247
  63.0 1.3 %collective-permute-start.10 = (f32[2,64,128]{2,1,0:T(8,128)S(1)}, f32[2,64,128]{2,1,0:T(8,128)S(1)}, u32[]{:S(2)}, u32[]{:S(2)}) collective-permute-start(f32[2,64,128]{2,1,0:T(8,128)S(1)} %get-tuple-element.34), channel_id=1, source_target_pairs={{1,0},{2,1},{3,2},{5,4},{6,5},{7,6},{9,8},{10,9},{11,10},{13,12},{... | collective-permute-start | bytes 196616 | tf_op jit(solution)/shard_map/ppermute | solution.py:405
  64.3 7.1 %collective-permute-start.9 = (f32[2,64,128]{2,1,0:T(8,128)S(1)}, f32[2,64,128]{2,1,0:T(8,128)S(1)}, u32[]{:S(2)}, u32[]{:S(2)}) collective-permute-start(f32[2,64,128]{2,1,0:T(8,128)S(1)} %get-tuple-element.33), channel_id=1, source_target_pairs={{0,1},{1,2},{2,3},{4,5},{5,6},{6,7},{8,9},{9,10},{10,11},{12,13},{... | collective-permute-start | bytes 196616 | tf_op jit(solution)/shard_map/ppermute | solution.py:405
  71.8 1.6 %collective-permute-done.9.from_left_ref = f32[2,64,128]{2,1,0:T(8,128)S(1)} collective-permute-done((f32[2,64,128]{2,1,0:T(8,128)S(1)}, f32[2,64,128]{2,1,0:T(8,128)S(1)}, u32[]{:S(2)}, u32[]{:S(2)}) %collective-permute-start.9) | collective-permute-done | bytes 65568 | tf_op jit(solution)/shard_map/ppermute | solution.py:405
  73.9 0.8 copy-done.2
  74.7 3.7 %all-to-all-start = ((f32[8,2,8,8,128]{4,3,2,1,0:T(8,128)}), f32[8,2,8,8,128]{4,3,2,1,0:T(8,128)S(1)}, u32[]{:S(2)}, u32[]{:S(2)}) async-start(f32[8,2,8,8,128]{4,3,2,1,0:T(8,128)} %copy-done.2), calls=%async_computation | async-start | bytes 1048576 | tf_op jit(solution)/shard_map/all_to_all | solution.py:474
  78.4 0.9 broadcast_multiply_fusion
  79.4 1.9 %mul.67.mix_ref = f32[128,128]{1,0:T(8,128)} reshape(f32[16,8,8,16]{3,2,1,0:T(8,128)} %broadcast_multiply_fusion) | data formatting | bytes 131072 | tf_op jit(solution)/shard_map/mul | solution.py:400
  81.3 6.9 %all-to-all-done.recv_ref = f32[8,2,8,8,128]{4,3,2,1,0:T(8,128)S(1)} async-done(((f32[8,2,8,8,128]{4,3,2,1,0:T(8,128)}), f32[8,2,8,8,128]{4,3,2,1,0:T(8,128)S(1)}, u32[]{:S(2)}, u32[]{:S(2)}) %all-to-all-start) | async-done | bytes 524320 | tf_op jit(solution)/shard_map/all_to_all | solution.py:474
  88.2 0.8 copy-done.3
  89.0 2.6 %scatter.1 = f32[8,128,128]{2,1,0:T(8,128)S(1)} custom-call(f32[8,2,8,8,128]{4,3,2,1,0:T(8,128)S(1)} %all-to-all-done.recv_ref, bf16[1024,1024]{1,0:T(8,128)(2,1)S(1)} %picks.1.pick_ref, f32[128,128]{1,0:T(8,128)S(1)} %copy-done.3, f32[192,128]{1,0:T(8,128)S(1)} %constant_dynamic-slice_fusion.dham_ref), custom_call_target="tpu_custom_call" | custom-call | tf_op jit(solution)/shard_map/scatter/pallas_call | solution.py:371
  91.7 12.2 %all_to_all.10 = f32[8,128,128]{2,1,0:T(8,128)S(1)} all-to-all(f32[8,128,128]{2,1,0:T(8,128)S(1)} %scatter.1), channel_id=1, replica_groups=mesh['energy'=8,'orb'=4] {'energy'}, dimensions={0} | all-to-all | bytes 1048576 | tf_op jit(solution)/shard_map/all_to_all | solution.py:476
  103.8 0.8 copy.18
  (30 shorter events, 3.6 us)
Async XLA Ops:
  0.0 81.2 %copy-start = (f32[1024,3,8,8]{0,3,2,1:T(8,128)S(1)}, f32[1024,3,8,8]{0,3,2,1:T(8,128)}, u32[]{:S(2)}) copy-start(f32[1024,3,8,8]{0,3,2,1:T(8,128)} %param.11) | copy-start | bytes 2359300
  0.0 20.7 %collective-permute-start = (f32[1,4,2,128,128]{4,3,2,1,0:T(8,128)}, f32[1,4,2,128,128]{4,3,2,1,0:T(8,128)}, u32[]{:S(2)}, u32[]{:S(2)}) collective-permute-start(f32[1,4,2,128,128]{4,3,2,1,0:T(8,128)} %rest_0_.1), channel_id=1, source_target_pairs={{0,1},{1,2},{2,3},{4,5},{5,6},{6,7},{8,9},{9,10},{10,11},{12,13},{... | collective-permute-start | bytes 1572872 | tf_op jit(solution)/shard_map/ppermute | solution.py:405
  5.9 15.6 %collective-permute-start.3 = (f32[1,4,2,128,128]{4,3,2,1,0:T(8,128)}, f32[1,4,2,128,128]{4,3,2,1,0:T(8,128)}, u32[]{:S(2)}, u32[]{:S(2)}) collective-permute-start(f32[1,4,2,128,128]{4,3,2,1,0:T(8,128)} %rest_0_.1), channel_id=1, source_target_pairs={{1,0},{2,1},{3,2},{5,4},{6,5},{7,6},{9,8},{10,9},{11,10},{13,12},{... | collective-permute-start | bytes 1572872 | tf_op jit(solution)/shard_map/ppermute | solution.py:405
  9.9 51.7 %collective-permute-start.6 = (f32[2,32,2048]{2,1,0:T(8,128)}, f32[2,32,2048]{2,1,0:T(8,128)S(1)}, u32[]{:S(2)}, u32[]{:S(2)}) collective-permute-start(f32[2,32,2048]{2,1,0:T(8,128)} %get-tuple-element.36), channel_id=1, source_target_pairs={{0,1},{3,2},{4,5},{7,6},{8,9},{11,10},{12,13},{15,14},{16,17},{19,... | collective-permute-start | bytes 1572872 | tf_op jit(solution)/shard_map/ppermute | solution.py:405
  14.5 47.1 %collective-permute-start.7 = (f32[2,32,2048]{2,1,0:T(8,128)}, f32[2,32,2048]{2,1,0:T(8,128)}, u32[]{:S(2)}, u32[]{:S(2)}) collective-permute-start(f32[2,32,2048]{2,1,0:T(8,128)} %get-tuple-element.37), channel_id=1, source_target_pairs={{0,1},{1,2},{4,5},{5,6},{8,9},{9,10},{12,13},{13,14},{16,17},{17,1... | collective-permute-start | bytes 1572872 | tf_op jit(solution)/shard_map/ppermute | solution.py:405
  16.6 45.0 %collective-permute-start.8 = (f32[2,32,2048]{2,1,0:T(8,128)}, f32[2,32,2048]{2,1,0:T(8,128)}, u32[]{:S(2)}, u32[]{:S(2)}) collective-permute-start(f32[2,32,2048]{2,1,0:T(8,128)} %get-tuple-element.35), channel_id=1, source_target_pairs={{2,1},{3,2},{6,5},{7,6},{10,9},{11,10},{14,13},{15,14},{18,17},{19... | collective-permute-start | bytes 1572872 | tf_op jit(solution)/shard_map/ppermute | solution.py:405
  20.7 12.2 %collective-permute-start.1 = (f32[1,4,2,128,128]{4,3,2,1,0:T(8,128)}, f32[1,4,2,128,128]{4,3,2,1,0:T(8,128)S(1)}, u32[]{:S(2)}, u32[]{:S(2)}) collective-permute-start(f32[1,4,2,128,128]{4,3,2,1,0:T(8,128)} %collective-permute-done.rest_0_), channel_id=1, source_target_pairs={{1,2},{2,3},{5,6},{6,7},{9,10},{10,11},{13,14},{14,15},{17,18},{18... | collective-permute-start | bytes 1572872 | tf_op jit(solution)/shard_map/ppermute | solution.py:405
  21.5 16.3 %collective-permute-start.4 = (f32[1,4,2,128,128]{4,3,2,1,0:T(8,128)}, f32[1,4,2,128,128]{4,3,2,1,0:T(8,128)S(1)}, u32[]{:S(2)}, u32[]{:S(2)}) collective-permute-start(f32[1,4,2,128,128]{4,3,2,1,0:T(8,128)} %collective-permute-done.3.rest_1_), channel_id=1, source_target_pairs={{1,0},{2,1},{5,4},{6,5},{9,8},{10,9},{13,12},{14,13},{17,16},{18,1... | collective-permute-start | bytes 1572872 | tf_op jit(solution)/shard_map/ppermute | solution.py:405
  23.6 3.4 %copy-start.1 = (f32[1,2,512,2048]{3,2,1,0:T(8,128)S(1)}, f32[1,2,512,2048]{3,2,1,0:T(8,128)}, u32[]{:S(2)}) copy-start(f32[1,2,512,2048]{3,2,1,0:T(8,128)} %green_ref.7) | copy-start | bytes 25165828
  26.9 1.0 copy-start.4
  32.8 17.1 %collective-permute-start.2 = (f32[1,4,2,128,128]{4,3,2,1,0:T(8,128)S(1)}, f32[1,4,2,128,128]{4,3,2,1,0:T(8,128)S(1)}, u32[]{:S(2)}, u32[]{:S(2)}) collective-permute-start(f32[1,4,2,128,128]{4,3,2,1,0:T(8,128)S(1)} %collective-permute-done.1.rest_0_), channel_id=1, source_target_pairs={{2,3},{6,7},{10,11},{14,15},{18,19},{22,23},{26,27},{30,31}} | collective-permute-start | bytes 1572872 | tf_op jit(solution)/shard_map/ppermute | solution.py:405
  37.7 18.9 %collective-permute-start.5 = (f32[1,4,2,128,128]{4,3,2,1,0:T(8,128)S(1)}, f32[1,4,2,128,128]{4,3,2,1,0:T(8,128)S(1)}, u32[]{:S(2)}, u32[]{:S(2)}) collective-permute-start(f32[1,4,2,128,128]{4,3,2,1,0:T(8,128)S(1)} %collective-permute-done.4.rest_1_), channel_id=1, source_target_pairs={{1,0},{5,4},{9,8},{13,12},{17,16},{21,20},{25,24},{29,28}} | collective-permute-start | bytes 1572872 | tf_op jit(solution)/shard_map/ppermute | solution.py:405
  63.0 8.8 %collective-permute-start.10 = (f32[2,64,128]{2,1,0:T(8,128)S(1)}, f32[2,64,128]{2,1,0:T(8,128)S(1)}, u32[]{:S(2)}, u32[]{:S(2)}) collective-permute-start(f32[2,64,128]{2,1,0:T(8,128)S(1)} %get-tuple-element.34), channel_id=1, source_target_pairs={{1,0},{2,1},{3,2},{5,4},{6,5},{7,6},{9,8},{10,9},{11,10},{13,12},{... | collective-permute-start | bytes 196616 | tf_op jit(solution)/shard_map/ppermute | solution.py:405
  64.3 9.0 %collective-permute-start.9 = (f32[2,64,128]{2,1,0:T(8,128)S(1)}, f32[2,64,128]{2,1,0:T(8,128)S(1)}, u32[]{:S(2)}, u32[]{:S(2)}) collective-permute-start(f32[2,64,128]{2,1,0:T(8,128)S(1)} %get-tuple-element.33), channel_id=1, source_target_pairs={{0,1},{1,2},{2,3},{4,5},{5,6},{6,7},{8,9},{9,10},{10,11},{12,13},{... | collective-permute-start | bytes 196616 | tf_op jit(solution)/shard_map/ppermute | solution.py:405
  73.9 0.8 copy-start.2
  74.7 13.5 %all-to-all-start = ((f32[8,2,8,8,128]{4,3,2,1,0:T(8,128)}), f32[8,2,8,8,128]{4,3,2,1,0:T(8,128)S(1)}, u32[]{:S(2)}, u32[]{:S(2)}) async-start(f32[8,2,8,8,128]{4,3,2,1,0:T(8,128)} %copy-done.2), calls=%async_computation | async-start | bytes 1048576 | tf_op jit(solution)/shard_map/all_to_all | solution.py:474
  88.2 0.8 copy-start.3

commit v3 on v2

--- a/solution.py
+++ b/solution.py
@@ -30,7 +30,9 @@
 
 
 def dot3(a, b, dims):
-    return dot(a[0], b[0], dims) + dot(a[0], b[1], dims) + dot(a[1], b[0], dims)
+    left = jnp.concatenate([a[0], a[0], a[1]], axis=1)
+    right = jnp.concatenate([b[0], b[1], b[0]], axis=dims[0][1][0])
+    return dot(left, right, dims)
 
 
 def blocks_at_once(held):
@@ -55,8 +57,14 @@
             cols = slice(n * wide, (n + 1) * wide)
             left = (hi_ref[row : row + TILE, cols], lo_ref[row : row + TILE, cols])
             product = dot3(left, weight, NN)
-            turned = jnp.concatenate([product[:, BS:], -product[:, :BS]], axis=1)
-            both.append(halves(jnp.concatenate([product, turned], axis=0)))
+            both.append(
+                [
+                    jnp.concatenate(
+                        [x, jnp.concatenate([x[:, BS:], -x[:, :BS]], axis=1)], axis=0
+                    )
+                    for x in halves(product)
+                ]
+            )
             if edges is not None:
                 for ref, part in zip(edges, both[-1]):
                     if t == 0:
@@ -81,14 +89,15 @@
 
 def lesser_kernel(shards, first, idx_ref, green_ref, *rest):
     sigmas, rest = rest[:shards], rest[shards:]
-    if not first:
-        before_ref, rest = rest[0], rest[1:]
-    acc_ref, keep_hi_ref, keep_lo_ref, buf, hi_ref, lo_ref, sem = rest
+    if first:
+        acc_ref, keep_hi_ref, keep_lo_ref, *sent, buf, hi_ref, lo_ref, sem, self_ref, self_sem = rest
+    else:
+        before_ref, acc_ref, keep_hi_ref, keep_lo_ref, buf, hi_ref, lo_ref, sem = rest
     rows, held = green_ref.shape[2], sigmas[0].shape[1]
     once = blocks_at_once(held)
 
     def fetch(shard, s):
-        col = pl.multiple_of((idx_ref[shard] * held + s) * BS, BS)
+        col = pl.multiple_of((idx_ref[shard] + s) * BS, BS)
         at = shard * held + s
         return pltpu.make_async_copy(
             green_ref.at[0, :, :, pl.ds(col, BS)], buf.at[at], sem.at[at]
@@ -97,6 +106,10 @@
     def valid(shard):
         return idx_ref[shards + shard] == 1
 
+    if first:
+        load = pltpu.make_async_copy(sigmas[0], self_ref, self_sem.at[0])
+        load.start()
+        sigmas = [self_ref]
     for shard in range(shards):
 
         @pl.when(valid(shard))
@@ -104,10 +117,22 @@
             for s in range(held):
                 fetch(shard, s).start()
 
+    if first:
+        starts = [pl.multiple_of(idx_ref[2], HALF), rows - HALF, 0]
+        copies = [
+            pltpu.make_async_copy(
+                green_ref.at[0, :, pl.ds(row, HALF), :], out, self_sem.at[n + 1]
+            )
+            for n, (row, out) in enumerate(zip(starts, sent))
+        ]
+        for copy in copies:
+            copy.start()
     acc_ref[...] = jnp.zeros_like(acc_ref) if first else before_ref[...]
     for ref in (hi_ref, lo_ref):
         ref[:MARGIN, :] = jnp.zeros((MARGIN, ref.shape[1]), BF16)
         ref[MARGIN + rows :, :] = jnp.zeros((MARGIN, ref.shape[1]), BF16)
+    if first:
+        load.wait()
 
     for shard in range(shards):
 
@@ -130,6 +155,10 @@
 
             lax.fori_loop(0, held // once, step, 0)
 
+    if first:
+        for copy in copies:
+            copy.wait()
+
 
 def lesser_part(green, sigmas, index, before):
     rows, held, shards = green.shape[2], sigmas[0].shape[1], len(sigmas)
@@ -137,26 +166,29 @@
     once = blocks_at_once(held)
     first = before is None
     vmem = pl.BlockSpec(memory_space=pltpu.VMEM)
+    hbm = pl.BlockSpec(memory_space=pl.ANY)
     keep = jax.ShapeDtypeStruct((count, 4 * MARGIN, 2 * BS), BF16)
+    sent = jax.ShapeDtypeStruct((2, HALF, green.shape[3]), F32)
+    more = [sent] * 3 if first else []
+    extra = [pltpu.VMEM(sigmas[0].shape, F32), pltpu.SemaphoreType.DMA((4,))] if first else []
     return pl.pallas_call(
         functools.partial(lesser_kernel, shards, first),
-        out_shape=(
+        out_shape=[
             jax.ShapeDtypeStruct((tiles, 2 * TILE, TILE + 2 * MARGIN), F32),
             keep,
             keep,
-        ),
-        in_specs=[
-            pl.BlockSpec(memory_space=pltpu.SMEM),
-            pl.BlockSpec(memory_space=pltpu.HBM),
         ]
-        + [vmem] * (shards if first else shards + 1),
-        out_specs=(vmem, vmem, vmem),
+        + more,
+        in_specs=[pl.BlockSpec(memory_space=pltpu.SMEM), hbm]
+        + ([hbm] * shards if first else [vmem] * (shards + 1)),
+        out_specs=[vmem] * 3 + [hbm] * len(more),
         scratch_shapes=[
             pltpu.VMEM((count, 2, rows, BS), F32),
             pltpu.VMEM((rows + 2 * MARGIN, once * 2 * BS), BF16),
             pltpu.VMEM((rows + 2 * MARGIN, once * 2 * BS), BF16),
             pltpu.SemaphoreType.DMA((count,)),
-        ],
+        ]
+        + extra,
         input_output_aliases={} if first else {2 + shards: 0},
         compiler_params=pltpu.CompilerParams(vmem_limit_bytes=24 << 20),
         cost_estimate=pl.CostEstimate(
@@ -177,34 +209,36 @@
     limit = idx_ref[base + 3]
     acc_ref[...] = jnp.zeros_like(acc_ref)
 
-    def add(col, keep_hi, keep_lo):
-        cols = pl.ds(pl.multiple_of(col * BS, BS), BS)
-        more = [a_ref[part, :, cols] for part in range(2)]
-        near = [b_ref[part, :, cols] for part in range(2)]
-        after = [c_ref[part, :, cols] for part in range(2)]
-        sides = []
-        for part in range(2):
-            outer = jnp.where(from_left, more[part], 0.0)
-            beyond = jnp.where(from_right, more[part], 0.0)
-            sides.append(
-                (
-                    jnp.concatenate([outer, near[part]], axis=0),
-                    jnp.concatenate([after[part], beyond], axis=0),
-                )
-            )
+    def add(col, hi, lo, at, held):
+        cols = pl.ds(pl.multiple_of(col * BS, BS), held * BS)
+        wide = [
+            [ref[part, :, cols] for part in range(2)] for ref in (a_ref, b_ref, c_ref)
+        ]
         for side in range(2):
-            real, imag = sides[0][side], sides[1][side]
-            halo = jnp.concatenate(
-                [
-                    jnp.concatenate([real, imag], axis=1),
-                    jnp.concatenate([-imag, real], axis=1),
-                ],
-                axis=0,
-            )
+            fields = []
+            for part in range(2):
+                more = wide[0][part]
+                if side == 0:
+                    rows = [jnp.where(from_left, more, 0.0), wide[1][part]]
+                else:
+                    rows = [wide[2][part], jnp.where(from_right, more, 0.0)]
+                fields.append(halves(jnp.concatenate(rows, axis=0)))
+            halo = []
+            for real, imag in zip(*fields):
+                lanes = []
+                for s in range(held):
+                    one = slice(s * BS, (s + 1) * BS)
+                    lanes += [
+                        jnp.concatenate([real[:, one], -imag[:, one]], axis=0),
+                        jnp.concatenate([imag[:, one], real[:, one]], axis=0),
+                    ]
+                halo.append(jnp.concatenate(lanes, axis=1))
             rows = slice(side * TILE, (side + 1) * TILE)
-            acc_ref[side] = acc_ref[side] + dot3(
-                halves(halo), (keep_hi[rows, :], keep_lo[rows, :]), NT
-            )
+            kept = [
+                jnp.concatenate([ref[at + s, rows, :] for s in range(held)], axis=1)
+                for ref in (hi, lo)
+            ]
+            acc_ref[side] = acc_ref[side] + dot3(halo, kept, NT)
 
     @pl.when(active)
     def _():
@@ -213,17 +247,12 @@
             hi, lo = keeps[2 * part], keeps[2 * part + 1]
             held = hi.shape[0] // count
             for k in range(count):
-                number, valid = idx_ref[2 * shard], idx_ref[2 * shard + 1]
+                col, valid = idx_ref[2 * shard], idx_ref[2 * shard + 1]
                 shard += 1
 
                 @pl.when(valid == 1)
                 def _():
-                    def step(s, carry):
-                        at = k * held + s
-                        add(number * held + s, hi.at[at], lo.at[at])
-                        return carry
-
-                    lax.fori_loop(0, held, step, 0)
+                    add(col, hi, lo, k * held, held)
 
     lane = lax.broadcasted_iota(jnp.int32, (MARGIN, LANES), 1)
     row = lax.broadcasted_iota(jnp.int32, (MARGIN, LANES), 0)
@@ -420,12 +449,18 @@
     far = peers >= 4
     up = [(i, i + 1) for i in range(peers - 1)]
     down = [(i + 1, i) for i in range(peers - 1)]
-    near_right = send(green[0, :, rows - HALF :], up[:-1] if far else up)
-    near_left = send(green[0, :, :HALF], down[1:] if far else down)
+    one = jnp.ones((), jnp.int32)
+    sooner = jnp.where(z == 0, rows - MARGIN, HALF)
+    green = pltpu.with_memory_space_constraint(green, pltpu.HBM)
+    acc, *keeps, more, last, leading = lesser_part(
+        green,
+        [pltpu.with_memory_space_constraint(sigma, pltpu.HBM)],
+        jnp.stack([z * held, one, sooner]),
+        None,
+    )
+    near_right = send(last, up[:-1] if far else up)
+    near_left = send(leading, down[1:] if far else down)
     if far:
-        more = jnp.where(
-            z == 0, green[0, :, rows - MARGIN : rows - HALF], green[0, :, HALF:MARGIN]
-        )
         other = send(more, [(0, 1), (peers - 1, peers - 2)])
         from_left, from_right = z == 1, z == peers - 2
         active = (z > 0) & (z < peers - 1)
@@ -435,21 +470,24 @@
         active = jnp.ones((), bool)
     limit = jnp.where(from_right, MARGIN, HALF)
 
-    one = jnp.ones((), jnp.int32)
-    acc, *keeps = lesser_part(green, [sigma], jnp.stack([z, one]), None)
-    counts, listed = [1], [z, one]
-    rightward = leftward = sigma
+    counts, listed = [1], [z * held, one]
+    cuts = 2 if held % 2 == 0 else 1
+    piece = held // cuts
+    rightward = [sigma[:, h * piece : (h + 1) * piece] for h in range(cuts)]
+    leftward = list(rightward)
     for k in range(1, peers):
-        rightward = send(rightward, up[k - 1 :])
-        leftward = send(leftward, down[: peers - k])
-        numbers = [jnp.maximum(z - k, 0), jnp.minimum(z + k, peers - 1)]
+        numbers = [jnp.maximum(z - k, 0) * held, jnp.minimum(z + k, peers - 1) * held]
         valid = [(z >= k).astype(jnp.int32), (z + k < peers).astype(jnp.int32)]
-        acc, *more_keeps = lesser_part(
-            green, [rightward, leftward], jnp.stack(numbers + valid), acc
-        )
-        keeps += more_keeps
-        counts.append(2)
-        listed += [numbers[0], valid[0], numbers[1], valid[1]]
+        for h in range(cuts):
+            rightward[h] = send(rightward[h], up[k - 1 :])
+            leftward[h] = send(leftward[h], down[: peers - k])
+            firsts = [x + h * piece for x in numbers]
+            acc, *more_keeps = lesser_part(
+                green, [rightward[h], leftward[h]], jnp.stack(firsts + valid), acc
+            )
+            keeps += more_keeps
+            counts.append(2)
+            listed += [firsts[0], valid[0], firsts[1], valid[1]]
     listed += [x.astype(jnp.int32) for x in (active, from_left, from_right, limit)]
     to_left, to_right, own = edge_part(
         jnp.stack(listed), other, near_right, near_left, keeps, tuple(counts)

time: 105 us -> 133 us (1.27)
  Pallas kernels: 25.8 us -> 47.5 us
  starting transfers between devices: 31.4 us -> 45.7 us
  other arithmetic: 4.88 us -> 0.89 us
  local copies, waits for them, and re-layouts: 10.5 us -> 7.85 us
  waiting for transfers between devices: 19.7 us -> 18.1 us
    pallas_call x4 -> x7, Pallas kernels: 20.6 us -> 42.3 us  [lesser_part(): pl.pallas_call(functools.partial(lesser_kernel, shards, first), out_shape...]
    ppermute x11 -> x17, starting transfers between devices: 27.6 us -> 42 us  [send(): return lax.ppermute(x, 'orb', pairs)]
    ppermute x11 -> x17, waiting for transfers between devices: 12.8 us -> 8.7 us  [send(): return lax.ppermute(x, 'orb', pairs)]
    squeeze x1 -> x0, other arithmetic: 2.73 us -> none  [per_device(): near_left = send(green[0, :, :HALF], down[1:] if far else down)]
    all_to_all x1, waiting for transfers between devices: 6.93 us -> 9.38 us  [per_device(): lax.all_to_all(lesser, 'energy', split_axis=0, concat_axis=0, tiled=True)]
    slice x0 -> x1, local copies, waits for them, and re-layouts: none -> 1.94 us  [per_device(): rightward = [sigma[:, h * piece:(h + 1) * piece] for h in range(cuts)]]
    mul x1, local copies, waits for them, and re-layouts: 1.86 us -> 0.19 us  [build_mix(): mix = same[:, None, None, :] * kernel[None, :, :, None]]
    unnamed x12 -> x22, local copies, waits for them, and re-layouts: 6.92 us -> 5.43 us
  transfers between devices with their start and end apart: 12 -> 18, of which waited for: 6 -> 4; matrix products, arithmetic and copies ran while one was open for 8% -> 1% of each run, Pallas kernels for 20% -> 32%
where the time goes in v3:
time: 133 us
  Pallas kernels  47.5 us (36%)
  starting transfers between devices  45.7 us (34%)
  waiting for transfers between devices  18.1 us (14%)
  blocking collectives  12.2 us (9%)
  local copies, waits for them, and re-layouts  7.85 us (6%)
    pallas_call x7, Pallas kernels, lesser_part(): pl.pallas_call(functools.partial(lesser_kernel, shards, first), out_shape...  42.3 us
    ppermute x17, starting transfers between devices, send(): return lax.ppermute(x, 'orb', pairs)  42 us
    all_to_all x1, blocking collectives, per_device(): lax.all_to_all(spread, 'energy', split_axis=0, concat_axis=0, tiled=True)  12.2 us
    all_to_all x1, waiting for transfers between devices, per_device(): lax.all_to_all(lesser, 'energy', split_axis=0, concat_axis=0, tiled=True)  9.38 us
    ppermute x17, waiting for transfers between devices, send(): return lax.ppermute(x, 'orb', pairs)  8.7 us
    unnamed x22, local copies, waits for them, and re-layouts  5.43 us
    all_to_all x1, starting transfers between devices, per_device(): lax.all_to_all(lesser, 'energy', split_axis=0, concat_axis=0, tiled=True)  3.73 us
  transfers between devices with their start and end apart: 18, of which 4 were waited for; matrix products, arithmetic and copies ran while one was open for 1% of the time, Pallas kernels for 32%

profile of v3, /device:TPU:0, one launch (start us, length us, event | category | flops | bytes accessed | tf_op | source)
XLA Modules:
  0.0 132.6 jit_solution(12424406198725798356)
XLA Ops:
  0.0 1.9 %fusion.1 = (f32[1,2,2,128,128]{4,3,2,1,0:T(8,128)}, f32[1,2,2,128,128]{4,3,2,1,0:T(8,128)}) fusion(f32[1,4,2,128,128]{4,3,2,1,0:T(8,128)} %rest_0_.1), kind=kLoop, calls=%fused_computation.22 | loop fusion | bytes 1048576 | tf_op jit(solution)/shard_map/slice | solution.py:476
  1.9 5.6 %collective-permute-start.6 = (f32[1,2,2,128,128]{4,3,2,1,0:T(8,128)}, f32[1,2,2,128,128]{4,3,2,1,0:T(8,128)}, u32[]{:S(2)}, u32[]{:S(2)}) collective-permute-start(f32[1,2,2,128,128]{4,3,2,1,0:T(8,128)} %get-tuple-element.59), channel_id=1, source_target_pairs={{0,1},{1,2},{2,3},{4,5},{5,6},{6,7},{8,9},{9,10},{10,11},{12,13},{... | collective-permute-start | bytes 786440 | tf_op jit(solution)/shard_map/ppermute | solution.py:434
  7.6 1.3 collective-permute-start.9
  8.9 5.3 %collective-permute-start = (f32[1,2,2,128,128]{4,3,2,1,0:T(8,128)}, f32[1,2,2,128,128]{4,3,2,1,0:T(8,128)}, u32[]{:S(2)}, u32[]{:S(2)}) collective-permute-start(f32[1,2,2,128,128]{4,3,2,1,0:T(8,128)} %get-tuple-element.60), channel_id=1, source_target_pairs={{0,1},{1,2},{2,3},{4,5},{5,6},{6,7},{8,9},{9,10},{10,11},{12,13},{... | collective-permute-start | bytes 786440 | tf_op jit(solution)/shard_map/ppermute | solution.py:434
  14.1 1.3 collective-permute-start.3
  15.5 17.6 %lesser_own.1 = (f32[4,256,256]{2,1,0:T(8,128)S(1)}, bf16[4,256,256]{2,1,0:T(8,128)(2,1)S(1)}, bf16[4,256,256]{2,1,0:T(8,128)(2,1)S(1)}, f32[2,32,2048]{2,1,0:T(...) custom-call(s32[3]{0:T(128)S(1)} %pad_add_fusion.idx_ref, f32[1,2,512,2048]{3,2,1,0:T(8,128)} %green_ref.13, ...), custom_call_target="tpu_custom_call" | custom-call | flops 2415919104 | bytes 4194304 | tf_op jit(solution)/shard_map/lesser_own/pallas_call | solution.py:174
  34.7 4.6 %collective-permute-start.12 = (f32[2,32,2048]{2,1,0:T(8,128)}, f32[2,32,2048]{2,1,0:T(8,128)S(1)}, u32[]{:S(2)}, u32[]{:S(2)}) collective-permute-start(f32[2,32,2048]{2,1,0:T(8,128)} %get-tuple-element.39), channel_id=1, source_target_pairs={{0,1},{3,2},{4,5},{7,6},{8,9},{11,10},{12,13},{15,14},{16,17},{19,... | collective-permute-start | bytes 1572872 | tf_op jit(solution)/shard_map/ppermute | solution.py:434
  39.8 1.3 collective-permute-start.10
  41.1 1.4 %collective-permute-start.7 = (f32[1,2,2,128,128]{4,3,2,1,0:T(8,128)}, f32[1,2,2,128,128]{4,3,2,1,0:T(8,128)}, u32[]{:S(2)}, u32[]{:S(2)}) collective-permute-start(f32[1,2,2,128,128]{4,3,2,1,0:T(8,128)} %collective-permute-done.6.rest_0_), channel_id=1, source_target_pairs={{1,2},{2,3},{5,6},{6,7},{9,10},{10,11},{13,14},{14,15},{17,18},{18... | collective-permute-start | bytes 786440 | tf_op jit(solution)/shard_map/ppermute | solution.py:434
  42.7 1.4 %collective-permute-start.1 = (f32[1,2,2,128,128]{4,3,2,1,0:T(8,128)}, f32[1,2,2,128,128]{4,3,2,1,0:T(8,128)}, u32[]{:S(2)}, u32[]{:S(2)}) collective-permute-start(f32[1,2,2,128,128]{4,3,2,1,0:T(8,128)} %collective-permute-done.rest_0_), channel_id=1, source_target_pairs={{1,2},{2,3},{5,6},{6,7},{9,10},{10,11},{13,14},{14,15},{17,18},{18... | collective-permute-start | bytes 786440 | tf_op jit(solution)/shard_map/ppermute | solution.py:434
  44.0 1.3 collective-permute-start.4
  45.4 3.3 %collective-permute-done.10.rest_1_ = f32[1,2,2,128,128]{4,3,2,1,0:T(8,128)} collective-permute-done((f32[1,2,2,128,128]{4,3,2,1,0:T(8,128)}, f32[1,2,2,128,128]{4,3,2,1,0:T(8,128)}, u32[]{:S(2)}, u32[]{:S(2)}) %collective-permute-start.10) | collective-permute-done | bytes 262176 | tf_op jit(solution)/shard_map/ppermute | solution.py:434
  48.7 1.3 collective-permute-start.11
  50.0 1.4 %collective-permute-start.8 = (f32[1,2,2,128,128]{4,3,2,1,0:T(8,128)}, f32[1,2,2,128,128]{4,3,2,1,0:T(8,128)}, u32[]{:S(2)}, u32[]{:S(2)}) collective-permute-start(f32[1,2,2,128,128]{4,3,2,1,0:T(8,128)} %collective-permute-done.7.rest_0_), channel_id=1, source_target_pairs={{2,3},{6,7},{10,11},{14,15},{18,19},{22,23},{26,27},{30,31}} | collective-permute-start | bytes 786440 | tf_op jit(solution)/shard_map/ppermute | solution.py:434
  52.1 1.4 %copy-done.1 = bf16[1024,1024]{1,0:T(8,128)(2,1)} copy-done((bf16[1024,1024]{1,0:T(8,128)(2,1)}, bf16[1024,1024]{1,0:T(8,128)(2,1)S(1)}, u32[]{:S(2)}) %copy-start.1) | copy-done | bytes 2097176
  53.6 4.3 %lesser_more.6 = (f32[4,256,256]{2,1,0:T(8,128)S(1)}, bf16[4,256,256]{2,1,0:T(8,128)(2,1)S(1)}, bf16[4,256,256]{2,1,0:T(8,128)(2,1)S(1)}) custom-call(s32[4]{0:T(128)S(1)} %add_add_fusion.5.idx_ref, f32[1,2,512,2048]{3,2,1,0:T(8,128)} %green_ref.13, f32[1,2,2,128,128]{4,3,2,1,0:T(8,128)} %collective-permute-done.6.rest_0_, ...), custom_call_target="tpu_custom_call", output_to_operand_aliasing={{0}: (4, {})} | custom-call | flops 1207959552 | bytes 3145728 | tf_op jit(solution)/shard_map/lesser_more/pallas_call | solution.py:174
  57.9 7.2 %collective-permute-start.13 = (f32[2,32,2048]{2,1,0:T(8,128)S(1)}, f32[2,32,2048]{2,1,0:T(8,128)S(1)}, u32[]{:S(2)}, u32[]{:S(2)}) collective-permute-start(f32[2,32,2048]{2,1,0:T(8,128)S(1)} %copy-done.6), channel_id=1, source_target_pairs={{0,1},{1,2},{4,5},{5,6},{8,9},{9,10},{12,13},{13,14},{16,17},{17,1... | collective-permute-start | bytes 1572872 | tf_op jit(solution)/shard_map/ppermute | solution.py:434
  65.8 4.2 %lesser_more.7 = (f32[4,256,256]{2,1,0:T(8,128)S(1)}, bf16[4,256,256]{2,1,0:T(8,128)(2,1)S(1)}, bf16[4,256,256]{2,1,0:T(8,128)(2,1)S(1)}) custom-call(s32[4]{0:T(128)S(1)} %add_add_fusion.4.idx_ref, f32[1,2,512,2048]{3,2,1,0:T(8,128)} %green_ref.13, f32[1,2,2,128,128]{4,3,2,1,0:T(8,128)} %collective-permute-done.rest_0_, ...), custom_call_target="tpu_custom_call", output_to_operand_aliasing={{0}: (4, {})} | custom-call | flops 1207959552 | bytes 3145728 | tf_op jit(solution)/shard_map/lesser_more/pallas_call | solution.py:174
  70.7 1.3 collective-permute-start.5
  72.0 4.2 %lesser_more.8 = (f32[4,256,256]{2,1,0:T(8,128)S(1)}, bf16[4,256,256]{2,1,0:T(8,128)(2,1)S(1)}, bf16[4,256,256]{2,1,0:T(8,128)(2,1)S(1)}) custom-call(s32[4]{0:T(128)S(1)} %add_add_fusion.3.idx_ref, f32[1,2,512,2048]{3,2,1,0:T(8,128)} %green_ref.13, f32[1,2,2,128,128]{4,3,2,1,0:T(8,128)} %collective-permute-done.7.rest_0_, ...), custom_call_target="tpu_custom_call", output_to_operand_aliasing={{0}: (4, {})} | custom-call | flops 1207959552 | bytes 3145728 | tf_op jit(solution)/shard_map/lesser_more/pallas_call | solution.py:174
  76.2 4.2 %lesser_more.9 = (f32[4,256,256]{2,1,0:T(8,128)S(1)}, bf16[4,256,256]{2,1,0:T(8,128)(2,1)S(1)}, bf16[4,256,256]{2,1,0:T(8,128)(2,1)S(1)}) custom-call(s32[4]{0:T(128)S(1)} %add_add_fusion.2.idx_ref, f32[1,2,512,2048]{3,2,1,0:T(8,128)} %green_ref.13, f32[1,2,2,128,128]{4,3,2,1,0:T(8,128)} %collective-permute-done.1.rest_0_, ...), custom_call_target="tpu_custom_call", output_to_operand_aliasing={{0}: (4, {})} | custom-call | flops 1207959552 | bytes 3145728 | tf_op jit(solution)/shard_map/lesser_more/pallas_call | solution.py:174
  80.4 4.2 %lesser_more.10 = (f32[4,256,256]{2,1,0:T(8,128)S(1)}, bf16[4,256,256]{2,1,0:T(8,128)(2,1)S(1)}, bf16[4,256,256]{2,1,0:T(8,128)(2,1)S(1)}) custom-call(s32[4]{0:T(128)S(1)} %add_add_fusion.1.idx_ref, f32[1,2,512,2048]{3,2,1,0:T(8,128)} %green_ref.13, f32[1,2,2,128,128]{4,3,2,1,0:T(8,128)} %collective-permute-done.8.rest_0_, ...), custom_call_target="tpu_custom_call", output_to_operand_aliasing={{0}: (4, {})} | custom-call | flops 1207959552 | bytes 3145728 | tf_op jit(solution)/shard_map/lesser_more/pallas_call | solution.py:174
  84.6 3.7 %lesser_more.11 = (f32[4,256,256]{2,1,0:T(8,128)S(1)}, bf16[4,256,256]{2,1,0:T(8,128)(2,1)S(1)}, bf16[4,256,256]{2,1,0:T(8,128)(2,1)S(1)}) custom-call(s32[4]{0:T(128)S(1)} %add_add_fusion.idx_ref, f32[1,2,512,2048]{3,2,1,0:T(8,128)} %green_ref.13, f32[1,2,2,128,128]{4,3,2,1,0:T(8,128)S(1)} %collective-permute-done.2.rest_0_, ...), custom_call_target="tpu_custom_call", output_to_operand_aliasing={{0}: (4, {})} | custom-call | flops 1207959552 | bytes 3145728 | tf_op jit(solution)/shard_map/lesser_more/pallas_call | solution.py:174
  89.1 4.9 %collective-permute-start.15 = (f32[2,64,128]{2,1,0:T(8,128)S(1)}, f32[2,64,128]{2,1,0:T(8,128)S(1)}, u32[]{:S(2)}, u32[]{:S(2)}) collective-permute-start(f32[2,64,128]{2,1,0:T(8,128)S(1)} %get-tuple-element.57), channel_id=1, source_target_pairs={{0,1},{1,2},{2,3},{4,5},{5,6},{6,7},{8,9},{9,10},{10,11},{12,13},{... | collective-permute-start | bytes 196616 | tf_op jit(solution)/shard_map/ppermute | solution.py:434
  93.9 1.3 collective-permute-start.16
  95.8 4.9 %collective-permute-done.16.from_right_ref = f32[2,64,128]{2,1,0:T(8,128)S(1)} collective-permute-done((f32[2,64,128]{2,1,0:T(8,128)S(1)}, f32[2,64,128]{2,1,0:T(8,128)S(1)}, u32[]{:S(2)}, u32[]{:S(2)}) %collective-permute-start.16) | collective-permute-done | bytes 65568 | tf_op jit(solution)/shard_map/ppermute | solution.py:434
  100.7 1.4 %band.1 = f32[8,2,8,8,128]{4,3,2,1,0:T(8,128)} custom-call(f32[4,256,256]{2,1,0:T(8,128)S(1)} %get-tuple-element.38.acc_ref, f32[2,2,64,128]{3,2,1,0:T(8,128)S(1)} %get-tuple-element.56.own_ref, f32[2,64,128]{2,1,0:T(8,128)S(1)} %collective-permute-done.15.from_left_ref, f32[2,64,128]{2,1,0:T(8,128)S(1)} %collective-permute-done.16.from_right_ref), custom_call_target="tpu_custom_call" | custom-call | tf_op jit(solution)/shard_map/band/pallas_call | solution.py:323
  102.1 3.7 %all-to-all-start = ((f32[8,2,8,8,128]{4,3,2,1,0:T(8,128)}), f32[8,2,8,8,128]{4,3,2,1,0:T(8,128)S(1)}, u32[]{:S(2)}, u32[]{:S(2)}) async-start(f32[8,2,8,8,128]{4,3,2,1,0:T(8,128)} %band.1), calls=%async_computation | async-start | bytes 1048576 | tf_op jit(solution)/shard_map/all_to_all | solution.py:512
  106.2 9.4 %all-to-all-done.recv_ref = f32[8,2,8,8,128]{4,3,2,1,0:T(8,128)S(1)} async-done(((f32[8,2,8,8,128]{4,3,2,1,0:T(8,128)}), f32[8,2,8,8,128]{4,3,2,1,0:T(8,128)S(1)}, u32[]{:S(2)}, u32[]{:S(2)}) %all-to-all-start) | async-done | bytes 524320 | tf_op jit(solution)/shard_map/all_to_all | solution.py:512
  115.6 1.6 %copy-done.2 = bf16[1024,1024]{1,0:T(8,128)(2,1)S(1)} copy-done((bf16[1024,1024]{1,0:T(8,128)(2,1)S(1)}, bf16[1024,1024]{1,0:T(8,128)(2,1)}, u32[]{:S(2)}) %copy-start.2) | copy-done | bytes 2097176
  117.2 2.5 %scatter.1 = f32[8,128,128]{2,1,0:T(8,128)S(1)} custom-call(f32[8,2,8,8,128]{4,3,2,1,0:T(8,128)S(1)} %all-to-all-done.recv_ref, bf16[1024,1024]{1,0:T(8,128)(2,1)S(1)} %copy-done.2, f32[128,128]{1,0:T(8,128)S(1)} %mul.96.mix_ref, f32[192,128]{1,0:T(8,128)S(1)} %constant_dynamic-slice_fusion.dham_ref), custom_call_target="tpu_custom_call" | custom-call | tf_op jit(solution)/shard_map/scatter/pallas_call | solution.py:400
  119.7 12.2 %all_to_all.10 = f32[8,128,128]{2,1,0:T(8,128)S(1)} all-to-all(f32[8,128,128]{2,1,0:T(8,128)S(1)} %scatter.1), channel_id=1, replica_groups=mesh['energy'=8,'orb'=4] {'energy'}, dimensions={0} | all-to-all | bytes 1048576 | tf_op jit(solution)/shard_map/all_to_all | solution.py:514
  (58 shorter events, 7.1 us)
Async XLA Ops:
  0.0 106.2 %copy-start = (f32[1024,3,8,8]{0,3,2,1:T(8,128)S(1)}, f32[1024,3,8,8]{0,3,2,1:T(8,128)}, u32[]{:S(2)}) copy-start(f32[1024,3,8,8]{0,3,2,1:T(8,128)} %param.11) | copy-start | bytes 2359300
  0.0 39.3 %copy-start.7 = (s32[64,16]{0,1:T(8,128)S(1)}, s32[64,16]{0,1:T(8,128)}, u32[]{:S(2)}) copy-start(s32[64,16]{0,1:T(8,128)} %param.8) | copy-start | bytes 12292
  0.0 39.5 %copy-start.9 = (s32[6]{0:T(128)S(1)}, s32[6]{0:T(128)}, u32[]{:S(2)}) copy-start(s32[6]{0:T(128)} %param.9) | copy-start | bytes 76
  0.0 39.6 %copy-start.8 = (f32[2,6]{1,0:T(2,128)S(1)}, f32[2,6]{1,0:T(2,128)}, u32[]{:S(2)}) copy-start(f32[2,6]{1,0:T(2,128)} %param.10) | copy-start | bytes 148
  1.9 39.2 %collective-permute-start.6 = (f32[1,2,2,128,128]{4,3,2,1,0:T(8,128)}, f32[1,2,2,128,128]{4,3,2,1,0:T(8,128)}, u32[]{:S(2)}, u32[]{:S(2)}) collective-permute-start(f32[1,2,2,128,128]{4,3,2,1,0:T(8,128)} %get-tuple-element.59), channel_id=1, source_target_pairs={{0,1},{1,2},{2,3},{4,5},{5,6},{6,7},{8,9},{9,10},{10,11},{12,13},{... | collective-permute-start | bytes 786440 | tf_op jit(solution)/shard_map/ppermute | solution.py:434
  7.6 32.2 %collective-permute-start.9 = (f32[1,2,2,128,128]{4,3,2,1,0:T(8,128)}, f32[1,2,2,128,128]{4,3,2,1,0:T(8,128)}, u32[]{:S(2)}, u32[]{:S(2)}) collective-permute-start(f32[1,2,2,128,128]{4,3,2,1,0:T(8,128)} %get-tuple-element.59), channel_id=1, source_target_pairs={{1,0},{2,1},{3,2},{5,4},{6,5},{7,6},{9,8},{10,9},{11,10},{13,12},{... | collective-permute-start | bytes 786440 | tf_op jit(solution)/shard_map/ppermute | solution.py:434
  8.9 33.8 %collective-permute-start = (f32[1,2,2,128,128]{4,3,2,1,0:T(8,128)}, f32[1,2,2,128,128]{4,3,2,1,0:T(8,128)}, u32[]{:S(2)}, u32[]{:S(2)}) collective-permute-start(f32[1,2,2,128,128]{4,3,2,1,0:T(8,128)} %get-tuple-element.60), channel_id=1, source_target_pairs={{0,1},{1,2},{2,3},{4,5},{5,6},{6,7},{8,9},{9,10},{10,11},{12,13},{... | collective-permute-start | bytes 786440 | tf_op jit(solution)/shard_map/ppermute | solution.py:434
  14.1 29.9 %collective-permute-start.3 = (f32[1,2,2,128,128]{4,3,2,1,0:T(8,128)}, f32[1,2,2,128,128]{4,3,2,1,0:T(8,128)}, u32[]{:S(2)}, u32[]{:S(2)}) collective-permute-start(f32[1,2,2,128,128]{4,3,2,1,0:T(8,128)} %get-tuple-element.60), channel_id=1, source_target_pairs={{1,0},{2,1},{3,2},{5,4},{6,5},{7,6},{9,8},{10,9},{11,10},{13,12},{... | collective-permute-start | bytes 786440 | tf_op jit(solution)/shard_map/ppermute | solution.py:434
  33.1 0.8 copy-start.3
  33.9 0.8 copy-start.5
  34.7 53.6 %collective-permute-start.12 = (f32[2,32,2048]{2,1,0:T(8,128)}, f32[2,32,2048]{2,1,0:T(8,128)S(1)}, u32[]{:S(2)}, u32[]{:S(2)}) collective-permute-start(f32[2,32,2048]{2,1,0:T(8,128)} %get-tuple-element.39), channel_id=1, source_target_pairs={{0,1},{3,2},{4,5},{7,6},{8,9},{11,10},{12,13},{15,14},{16,17},{19,... | collective-permute-start | bytes 1572872 | tf_op jit(solution)/shard_map/ppermute | solution.py:434
  39.8 8.8 %collective-permute-start.10 = (f32[1,2,2,128,128]{4,3,2,1,0:T(8,128)}, f32[1,2,2,128,128]{4,3,2,1,0:T(8,128)}, u32[]{:S(2)}, u32[]{:S(2)}) collective-permute-start(f32[1,2,2,128,128]{4,3,2,1,0:T(8,128)} %collective-permute-done.9.rest_1_), channel_id=1, source_target_pairs={{1,0},{2,1},{5,4},{6,5},{9,8},{10,9},{13,12},{14,13},{17,16},{18,1... | collective-permute-start | bytes 786440 | tf_op jit(solution)/shard_map/ppermute | solution.py:434
  41.1 8.8 %collective-permute-start.7 = (f32[1,2,2,128,128]{4,3,2,1,0:T(8,128)}, f32[1,2,2,128,128]{4,3,2,1,0:T(8,128)}, u32[]{:S(2)}, u32[]{:S(2)}) collective-permute-start(f32[1,2,2,128,128]{4,3,2,1,0:T(8,128)} %collective-permute-done.6.rest_0_), channel_id=1, source_target_pairs={{1,2},{2,3},{5,6},{6,7},{9,10},{10,11},{13,14},{14,15},{17,18},{18... | collective-permute-start | bytes 786440 | tf_op jit(solution)/shard_map/ppermute | solution.py:434
  42.7 15.2 %collective-permute-start.1 = (f32[1,2,2,128,128]{4,3,2,1,0:T(8,128)}, f32[1,2,2,128,128]{4,3,2,1,0:T(8,128)}, u32[]{:S(2)}, u32[]{:S(2)}) collective-permute-start(f32[1,2,2,128,128]{4,3,2,1,0:T(8,128)} %collective-permute-done.rest_0_), channel_id=1, source_target_pairs={{1,2},{2,3},{5,6},{6,7},{9,10},{10,11},{13,14},{14,15},{17,18},{18... | collective-permute-start | bytes 786440 | tf_op jit(solution)/shard_map/ppermute | solution.py:434
  44.0 21.1 %collective-permute-start.4 = (f32[1,2,2,128,128]{4,3,2,1,0:T(8,128)}, f32[1,2,2,128,128]{4,3,2,1,0:T(8,128)}, u32[]{:S(2)}, u32[]{:S(2)}) collective-permute-start(f32[1,2,2,128,128]{4,3,2,1,0:T(8,128)} %collective-permute-done.3.rest_1_), channel_id=1, source_target_pairs={{1,0},{2,1},{5,4},{6,5},{9,8},{10,9},{13,12},{14,13},{17,16},{18,1... | collective-permute-start | bytes 786440 | tf_op jit(solution)/shard_map/ppermute | solution.py:434
  48.7 21.3 %collective-permute-start.11 = (f32[1,2,2,128,128]{4,3,2,1,0:T(8,128)}, f32[1,2,2,128,128]{4,3,2,1,0:T(8,128)}, u32[]{:S(2)}, u32[]{:S(2)}) collective-permute-start(f32[1,2,2,128,128]{4,3,2,1,0:T(8,128)} %collective-permute-done.10.rest_1_), channel_id=1, source_target_pairs={{1,0},{5,4},{9,8},{13,12},{17,16},{21,20},{25,24},{29,28}} | collective-permute-start | bytes 786440 | tf_op jit(solution)/shard_map/ppermute | solution.py:434
  50.0 20.7 %collective-permute-start.8 = (f32[1,2,2,128,128]{4,3,2,1,0:T(8,128)}, f32[1,2,2,128,128]{4,3,2,1,0:T(8,128)}, u32[]{:S(2)}, u32[]{:S(2)}) collective-permute-start(f32[1,2,2,128,128]{4,3,2,1,0:T(8,128)} %collective-permute-done.7.rest_0_), channel_id=1, source_target_pairs={{2,3},{6,7},{10,11},{14,15},{18,19},{22,23},{26,27},{30,31}} | collective-permute-start | bytes 786440 | tf_op jit(solution)/shard_map/ppermute | solution.py:434
  52.1 1.4 %copy-start.1 = (bf16[1024,1024]{1,0:T(8,128)(2,1)}, bf16[1024,1024]{1,0:T(8,128)(2,1)S(1)}, u32[]{:S(2)}) copy-start(bf16[1024,1024]{1,0:T(8,128)(2,1)S(1)} %picks.1.pick_ref) | copy-start | bytes 6291460
  53.6 4.3 %copy-start.6 = (f32[2,32,2048]{2,1,0:T(8,128)S(1)}, f32[2,32,2048]{2,1,0:T(8,128)}, u32[]{:S(2)}) copy-start(f32[2,32,2048]{2,1,0:T(8,128)} %copy-done.5) | copy-start | bytes 1572868
  53.6 11.5 %copy-start.4 = (f32[2,32,2048]{2,1,0:T(8,128)S(1)}, f32[2,32,2048]{2,1,0:T(8,128)}, u32[]{:S(2)}) copy-start(f32[2,32,2048]{2,1,0:T(8,128)} %copy-done.3) | copy-start | bytes 1572868
  57.9 30.4 %collective-permute-start.13 = (f32[2,32,2048]{2,1,0:T(8,128)S(1)}, f32[2,32,2048]{2,1,0:T(8,128)S(1)}, u32[]{:S(2)}, u32[]{:S(2)}) collective-permute-start(f32[2,32,2048]{2,1,0:T(8,128)S(1)} %copy-done.6), channel_id=1, source_target_pairs={{0,1},{1,2},{4,5},{5,6},{8,9},{9,10},{12,13},{13,14},{16,17},{17,1... | collective-permute-start | bytes 1572872 | tf_op jit(solution)/shard_map/ppermute | solution.py:434
  65.1 23.2 %collective-permute-start.14 = (f32[2,32,2048]{2,1,0:T(8,128)S(1)}, f32[2,32,2048]{2,1,0:T(8,128)S(1)}, u32[]{:S(2)}, u32[]{:S(2)}) collective-permute-start(f32[2,32,2048]{2,1,0:T(8,128)S(1)} %copy-done.4), channel_id=1, source_target_pairs={{2,1},{3,2},{6,5},{7,6},{10,9},{11,10},{14,13},{15,14},{18,17},{19... | collective-permute-start | bytes 1572872 | tf_op jit(solution)/shard_map/ppermute | solution.py:434
  70.0 14.6 %collective-permute-start.2 = (f32[1,2,2,128,128]{4,3,2,1,0:T(8,128)}, f32[1,2,2,128,128]{4,3,2,1,0:T(8,128)S(1)}, u32[]{:S(2)}, u32[]{:S(2)}) collective-permute-start(f32[1,2,2,128,128]{4,3,2,1,0:T(8,128)} %collective-permute-done.1.rest_0_), channel_id=1, source_target_pairs={{2,3},{6,7},{10,11},{14,15},{18,19},{22,23},{26,27},{30,31}} | collective-permute-start | bytes 786440 | tf_op jit(solution)/shard_map/ppermute | solution.py:434
  70.7 13.9 %collective-permute-start.5 = (f32[1,2,2,128,128]{4,3,2,1,0:T(8,128)}, f32[1,2,2,128,128]{4,3,2,1,0:T(8,128)S(1)}, u32[]{:S(2)}, u32[]{:S(2)}) collective-permute-start(f32[1,2,2,128,128]{4,3,2,1,0:T(8,128)} %collective-permute-done.4.rest_1_), channel_id=1, source_target_pairs={{1,0},{5,4},{9,8},{13,12},{17,16},{21,20},{25,24},{29,28}} | collective-permute-start | bytes 786440 | tf_op jit(solution)/shard_map/ppermute | solution.py:434
  89.1 6.8 %collective-permute-start.15 = (f32[2,64,128]{2,1,0:T(8,128)S(1)}, f32[2,64,128]{2,1,0:T(8,128)S(1)}, u32[]{:S(2)}, u32[]{:S(2)}) collective-permute-start(f32[2,64,128]{2,1,0:T(8,128)S(1)} %get-tuple-element.57), channel_id=1, source_target_pairs={{0,1},{1,2},{2,3},{4,5},{5,6},{6,7},{8,9},{9,10},{10,11},{12,13},{... | collective-permute-start | bytes 196616 | tf_op jit(solution)/shard_map/ppermute | solution.py:434
  93.9 6.8 %collective-permute-start.16 = (f32[2,64,128]{2,1,0:T(8,128)S(1)}, f32[2,64,128]{2,1,0:T(8,128)S(1)}, u32[]{:S(2)}, u32[]{:S(2)}) collective-permute-start(f32[2,64,128]{2,1,0:T(8,128)S(1)} %get-tuple-element.58), channel_id=1, source_target_pairs={{1,0},{2,1},{3,2},{5,4},{6,5},{7,6},{9,8},{10,9},{11,10},{13,12},{... | collective-permute-start | bytes 196616 | tf_op jit(solution)/shard_map/ppermute | solution.py:434
  102.1 13.5 %all-to-all-start = ((f32[8,2,8,8,128]{4,3,2,1,0:T(8,128)}), f32[8,2,8,8,128]{4,3,2,1,0:T(8,128)S(1)}, u32[]{:S(2)}, u32[]{:S(2)}) async-start(f32[8,2,8,8,128]{4,3,2,1,0:T(8,128)} %band.1), calls=%async_computation | async-start | bytes 1048576 | tf_op jit(solution)/shard_map/all_to_all | solution.py:512
  115.6 1.6 %copy-start.2 = (bf16[1024,1024]{1,0:T(8,128)(2,1)S(1)}, bf16[1024,1024]{1,0:T(8,128)(2,1)}, u32[]{:S(2)}) copy-start(bf16[1024,1024]{1,0:T(8,128)(2,1)} %copy-done.1) | copy-start | bytes 6291460

commit v4 on v3

--- a/solution.py
+++ b/solution.py
@@ -39,47 +39,41 @@
     return 2 if held % 2 == 0 else 1
 
 
-def some_blocks(fields, weights, hi_ref, lo_ref, acc_ref, edges):
-    rows = fields[0][0].shape[0]
+def some_blocks(lane, weights, hi_ref, lo_ref, acc_ref, edges, active):
+    rows = hi_ref.shape[0] - 2 * MARGIN
     wide = 2 * BS
-    hi, lo = halves(jnp.concatenate([x for pair in fields for x in pair], axis=1))
-    hi_ref[MARGIN : MARGIN + rows, :] = hi
-    lo_ref[MARGIN : MARGIN + rows, :] = lo
-    split = []
-    for real, imag in weights:
+    split, products = [], []
+    for n, (real, imag) in enumerate(weights):
         top = jnp.concatenate([real, imag], axis=1)
-        split.append(halves(jnp.concatenate([top, jnp.concatenate([-imag, real], axis=1)], axis=0)))
-    tiles = rows // TILE
-    for t in range(tiles):
-        row, window = MARGIN + t * TILE, t * TILE
+        weight = halves(jnp.concatenate([top, jnp.concatenate([-imag, real], axis=1)], axis=0))
+        cols = pl.ds(lane + n * wide, wide)
+        own = [ref[MARGIN : MARGIN + rows, cols] for ref in (hi_ref, lo_ref)]
+        product = halves(dot3(own, weight, NN))
+        for ref, part in zip(edges, product):
+            ref[n, :MARGIN, :] = part[:MARGIN]
+            ref[n, 3 * MARGIN :, :] = part[rows - MARGIN :]
+        split.append(weight)
+        products.append(product)
+    cols = pl.ds(lane, len(weights) * wide)
+    for t in range(rows // TILE):
         both = []
+        for part in zip(*products):
+            lanes = []
+            for x in part:
+                x = x[t * TILE : (t + 1) * TILE]
+                turned = jnp.concatenate([x[:, BS:], -x[:, :BS]], axis=1)
+                lanes.append(jnp.concatenate([x, turned], axis=0))
+            both.append(jnp.concatenate(lanes, axis=1))
+        near = pl.ds(t * TILE, TILE + 2 * MARGIN)
+        acc_ref[t] = acc_ref[t] + dot3(both, (hi_ref[near, cols], lo_ref[near, cols]), NT)
+
+    @pl.when(active)
+    def _():
         for n, weight in enumerate(split):
-            cols = slice(n * wide, (n + 1) * wide)
-            left = (hi_ref[row : row + TILE, cols], lo_ref[row : row + TILE, cols])
-            product = dot3(left, weight, NN)
-            both.append(
-                [
-                    jnp.concatenate(
-                        [x, jnp.concatenate([x[:, BS:], -x[:, :BS]], axis=1)], axis=0
-                    )
-                    for x in halves(product)
-                ]
-            )
-            if edges is not None:
-                for ref, part in zip(edges, both[-1]):
-                    if t == 0:
-                        ref[n, :MARGIN, :] = part[:MARGIN]
-                    if t == tiles - 1:
-                        ref[n, 3 * MARGIN :, :] = part[TILE - MARGIN : TILE]
-        both = [jnp.concatenate(parts, axis=1) for parts in zip(*both)]
-        upto = window + TILE + 2 * MARGIN
-        acc_ref[t] = acc_ref[t] + dot3(both, (hi_ref[window:upto, :], lo_ref[window:upto, :]), NT)
-    if edges is not None:
-        for n, weight in enumerate(split):
-            cols = slice(n * wide, (n + 1) * wide)
+            one = pl.ds(lane + n * wide, wide)
             outer = [
                 jnp.concatenate(
-                    [ref[MARGIN : 2 * MARGIN, cols], ref[rows : rows + MARGIN, cols]], axis=0
+                    [ref[MARGIN : 2 * MARGIN, one], ref[rows : rows + MARGIN, one]], axis=0
                 )
                 for ref in (hi_ref, lo_ref)
             ]
@@ -87,117 +81,182 @@
                 ref[n, MARGIN : 3 * MARGIN, :] = part
 
 
-def lesser_kernel(shards, first, idx_ref, green_ref, *rest):
-    sigmas, rest = rest[:shards], rest[shards:]
-    if first:
-        acc_ref, keep_hi_ref, keep_lo_ref, *sent, buf, hi_ref, lo_ref, sem, self_ref, self_sem = rest
-    else:
-        before_ref, acc_ref, keep_hi_ref, keep_lo_ref, buf, hi_ref, lo_ref, sem = rest
-    rows, held = green_ref.shape[2], sigmas[0].shape[1]
+def shard_loop(first_block, self_ref, hi_ref, lo_ref, acc_ref, keeps, slot, active):
+    held = self_ref.shape[1]
     once = blocks_at_once(held)
 
-    def fetch(shard, s):
-        col = pl.multiple_of((idx_ref[shard] + s) * BS, BS)
-        at = shard * held + s
+    def step(g, carry):
+        lane = pl.multiple_of((first_block + g * once) * 2 * BS, 2 * BS)
+        weights = [
+            (self_ref[0, g * once + n, 0], self_ref[0, g * once + n, 1]) for n in range(once)
+        ]
+        slots = pl.ds(slot + g * once, once)
+        kept = tuple(ref.at[slots] for ref in keeps)
+        some_blocks(lane, weights, hi_ref, lo_ref, acc_ref, kept, active)
+        return carry
+
+    lax.fori_loop(0, held // once, step, 0)
+
+
+def own_kernel(
+    idx_ref, green_ref, sigma_ref, acc_ref, keep_hi_ref, keep_lo_ref, hi_ref, lo_ref,
+    buf, self_ref, sem,
+):
+    rows, held = green_ref.shape[2], sigma_ref.shape[1]
+    blocks = green_ref.shape[3] // BS
+    begin, active = idx_ref[0], idx_ref[1] == 1
+
+    def block_of(s):
+        return lax.rem(begin + s, blocks)
+
+    def fetch(s):
+        col = pl.multiple_of(block_of(s) * BS, BS)
         return pltpu.make_async_copy(
-            green_ref.at[0, :, :, pl.ds(col, BS)], buf.at[at], sem.at[at]
+            green_ref.at[0, :, :, pl.ds(col, BS)], buf.at[s], sem.at[s]
         )
 
-    def valid(shard):
-        return idx_ref[shards + shard] == 1
-
-    if first:
-        load = pltpu.make_async_copy(sigmas[0], self_ref, self_sem.at[0])
-        load.start()
-        sigmas = [self_ref]
-    for shard in range(shards):
-
-        @pl.when(valid(shard))
-        def _():
-            for s in range(held):
-                fetch(shard, s).start()
-
-    if first:
-        starts = [pl.multiple_of(idx_ref[2], HALF), rows - HALF, 0]
-        copies = [
-            pltpu.make_async_copy(
-                green_ref.at[0, :, pl.ds(row, HALF), :], out, self_sem.at[n + 1]
-            )
-            for n, (row, out) in enumerate(zip(starts, sent))
-        ]
-        for copy in copies:
-            copy.start()
-    acc_ref[...] = jnp.zeros_like(acc_ref) if first else before_ref[...]
+    def store(s, carry):
+        fetch(s).wait()
+        lanes = pl.ds(pl.multiple_of(block_of(s) * 2 * BS, 2 * BS), 2 * BS)
+        parts = halves(jnp.concatenate([buf[s, 0], buf[s, 1]], axis=1))
+        for ref, part in zip((hi_ref, lo_ref), parts):
+            ref[MARGIN : MARGIN + rows, lanes] = part
+        return carry
+
+    load = pltpu.make_async_copy(sigma_ref, self_ref, sem.at[blocks])
+    load.start()
+    for s in range(blocks):
+        fetch(s).start()
+    acc_ref[...] = jnp.zeros_like(acc_ref)
     for ref in (hi_ref, lo_ref):
         ref[:MARGIN, :] = jnp.zeros((MARGIN, ref.shape[1]), BF16)
         ref[MARGIN + rows :, :] = jnp.zeros((MARGIN, ref.shape[1]), BF16)
-    if first:
-        load.wait()
-
-    for shard in range(shards):
-
-        @pl.when(valid(shard))
-        def _():
-            def step(g, carry):
-                fields, weights = [], []
-                for n in range(once):
-                    s = g * once + n
-                    fetch(shard, s).wait()
-                    at = shard * held + s
-                    fields.append((buf[at, 0], buf[at, 1]))
-                    weights.append((sigmas[shard][0, s, 0], sigmas[shard][0, s, 1]))
-                slots = pl.ds(shard * held + g * once, once)
-                some_blocks(
-                    fields, weights, hi_ref, lo_ref, acc_ref,
-                    (keep_hi_ref.at[slots], keep_lo_ref.at[slots]),
-                )
-                return carry
-
-            lax.fori_loop(0, held // once, step, 0)
-
-    if first:
-        for copy in copies:
-            copy.wait()
-
-
-def lesser_part(green, sigmas, index, before):
-    rows, held, shards = green.shape[2], sigmas[0].shape[1], len(sigmas)
-    tiles, count = rows // TILE, held * shards
-    once = blocks_at_once(held)
-    first = before is None
+    lax.fori_loop(0, held, store, 0)
+    load.wait()
+    shard_loop(begin, self_ref, hi_ref, lo_ref, acc_ref, (keep_hi_ref, keep_lo_ref), 0, active)
+    lax.fori_loop(held, blocks, store, 0)
+
+
+def own_part(green, sigma, index):
+    rows, held = green.shape[2], sigma.shape[1]
+    tiles, blocks = rows // TILE, green.shape[3] // BS
     vmem = pl.BlockSpec(memory_space=pltpu.VMEM)
     hbm = pl.BlockSpec(memory_space=pl.ANY)
-    keep = jax.ShapeDtypeStruct((count, 4 * MARGIN, 2 * BS), BF16)
-    sent = jax.ShapeDtypeStruct((2, HALF, green.shape[3]), F32)
-    more = [sent] * 3 if first else []
-    extra = [pltpu.VMEM(sigmas[0].shape, F32), pltpu.SemaphoreType.DMA((4,))] if first else []
-    return pl.pallas_call(
-        functools.partial(lesser_kernel, shards, first),
-        out_shape=[
+    keep = jax.ShapeDtypeStruct((held, 4 * MARGIN, 2 * BS), BF16)
+    whole = jax.ShapeDtypeStruct((rows + 2 * MARGIN, blocks * 2 * BS), BF16)
+    return pl.pallas_call(
+        own_kernel,
+        out_shape=(
             jax.ShapeDtypeStruct((tiles, 2 * TILE, TILE + 2 * MARGIN), F32),
             keep,
             keep,
-        ]
-        + more,
-        in_specs=[pl.BlockSpec(memory_space=pltpu.SMEM), hbm]
-        + ([hbm] * shards if first else [vmem] * (shards + 1)),
-        out_specs=[vmem] * 3 + [hbm] * len(more),
+            whole,
+            whole,
+        ),
+        in_specs=[pl.BlockSpec(memory_space=pltpu.SMEM), hbm, hbm],
+        out_specs=(vmem,) * 5,
         scratch_shapes=[
-            pltpu.VMEM((count, 2, rows, BS), F32),
-            pltpu.VMEM((rows + 2 * MARGIN, once * 2 * BS), BF16),
-            pltpu.VMEM((rows + 2 * MARGIN, once * 2 * BS), BF16),
-            pltpu.SemaphoreType.DMA((count,)),
-        ]
-        + extra,
-        input_output_aliases={} if first else {2 + shards: 0},
-        compiler_params=pltpu.CompilerParams(vmem_limit_bytes=24 << 20),
+            pltpu.VMEM((blocks, 2, rows, BS), F32),
+            pltpu.VMEM(sigma.shape, F32),
+            pltpu.SemaphoreType.DMA((blocks + 1,)),
+        ],
+        compiler_params=pltpu.CompilerParams(vmem_limit_bytes=40 << 20),
         cost_estimate=pl.CostEstimate(
             flops=held * 6 * rows * 2 * BS * (2 * BS + 4 * TILE),
-            bytes_accessed=held * rows * BS * 8 + 8 * tiles * TILE * 512,
+            bytes_accessed=blocks * rows * BS * 8,
             transcendentals=0,
         ),
-        name="lesser_own" if first else "lesser_more",
-    )(index, green, *sigmas, *([] if first else [before]))
+        name="lesser_own",
+    )(index, green, sigma)
+
+
+def lesser_kernel(
+    idx_ref, hi_ref, lo_ref, right_ref, left_ref, before_ref, *rest
+):
+    acc_ref, keep_hi_ref, keep_lo_ref = rest[-3:]
+    held = right_ref.shape[1]
+    acc_ref[...] = before_ref[...]
+    for k, self_ref in enumerate((right_ref, left_ref)):
+
+        @pl.when(idx_ref[2 + k] == 1)
+        def _():
+            shard_loop(
+                idx_ref[k], self_ref, hi_ref, lo_ref, acc_ref,
+                (keep_hi_ref, keep_lo_ref), k * held, idx_ref[4] == 1,
+            )
+
+
+def lesser_part(hi, lo, right, left, index, before, after):
+    held = right.shape[1]
+    vmem = pl.BlockSpec(memory_space=pltpu.VMEM)
+    keep = jax.ShapeDtypeStruct((2 * held, 4 * MARGIN, 2 * BS), BF16)
+    return pl.pallas_call(
+        lesser_kernel,
+        out_shape=(jax.ShapeDtypeStruct(before.shape, F32), keep, keep),
+        in_specs=[pl.BlockSpec(memory_space=pltpu.SMEM)]
+        + [vmem] * 5
+        + [pl.BlockSpec(memory_space=pl.ANY)] * len(after),
+        out_specs=(vmem,) * 3,
+        input_output_aliases={5: 0},
+        compiler_params=pltpu.CompilerParams(vmem_limit_bytes=32 << 20),
+        cost_estimate=pl.CostEstimate(
+            flops=held * 6 * hi.shape[0] * 2 * BS * (2 * BS + 4 * TILE),
+            bytes_accessed=8 * before.size,
+            transcendentals=0,
+        ),
+        name="lesser_more",
+    )(index, hi, lo, right, left, before, *after)
+
+
+def rows_kernel(count, idx_ref, green_ref, *rest):
+    outs, sem = rest[-1 - count : -1], rest[-1]
+    copies = [
+        pltpu.make_async_copy(
+            green_ref.at[0, :, pl.ds(pl.multiple_of(idx_ref[n], HALF), HALF), :],
+            out,
+            sem.at[n],
+        )
+        for n, out in enumerate(outs)
+    ]
+    for copy in copies:
+        copy.start()
+    for copy in copies:
+        copy.wait()
+
+
+def rows_at(green, starts, after):
+    count = len(starts)
+    hbm = pl.BlockSpec(memory_space=pl.ANY)
+    out = jax.ShapeDtypeStruct((2, HALF, green.shape[3]), F32)
+    return pl.pallas_call(
+        functools.partial(rows_kernel, count),
+        out_shape=[out] * count,
+        in_specs=[pl.BlockSpec(memory_space=pltpu.SMEM)] + [hbm] * (1 + len(after)),
+        out_specs=[pl.BlockSpec(memory_space=pltpu.VMEM)] * count,
+        scratch_shapes=[pltpu.SemaphoreType.DMA((count,))],
+        compiler_params=pltpu.CompilerParams(vmem_limit_bytes=8 << 20),
+        cost_estimate=pl.CostEstimate(
+            flops=0, bytes_accessed=4 * count * out.size, transcendentals=0
+        ),
+        name="rows",
+    )(jnp.stack([jnp.asarray(x, jnp.int32) for x in starts]), green, *after)
+
+
+def gate_kernel(right_ref, left_ref, after_ref, *outs):
+    del right_ref, left_ref, after_ref, outs
+
+
+def gate(right, left, after):
+    hbm = pl.BlockSpec(memory_space=pl.ANY)
+    return pl.pallas_call(
+        gate_kernel,
+        out_shape=[jax.ShapeDtypeStruct(x.shape, x.dtype) for x in (right, left)],
+        in_specs=[hbm] * 3,
+        out_specs=[hbm] * 2,
+        input_output_aliases={0: 0, 1: 1},
+        cost_estimate=pl.CostEstimate(flops=0, bytes_accessed=0, transcendentals=0),
+        name="gate",
+    )(right, left, after)
 
 
 def edge_kernel(counts, idx_ref, a_ref, b_ref, c_ref, *rest):
@@ -449,45 +508,50 @@
     far = peers >= 4
     up = [(i, i + 1) for i in range(peers - 1)]
     down = [(i + 1, i) for i in range(peers - 1)]
-    one = jnp.ones((), jnp.int32)
-    sooner = jnp.where(z == 0, rows - MARGIN, HALF)
-    green = pltpu.with_memory_space_constraint(green, pltpu.HBM)
-    acc, *keeps, more, last, leading = lesser_part(
-        green,
-        [pltpu.with_memory_space_constraint(sigma, pltpu.HBM)],
-        jnp.stack([z * held, one, sooner]),
-        None,
-    )
-    near_right = send(last, up[:-1] if far else up)
-    near_left = send(leading, down[1:] if far else down)
     if far:
-        other = send(more, [(0, 1), (peers - 1, peers - 2)])
         from_left, from_right = z == 1, z == peers - 2
         active = (z > 0) & (z < peers - 1)
     else:
-        other = jnp.zeros_like(near_left)
         from_left = from_right = jnp.zeros((), bool)
         active = jnp.ones((), bool)
     limit = jnp.where(from_right, MARGIN, HALF)
-
+    one, inner = jnp.ones((), jnp.int32), active.astype(jnp.int32)
+
+    fixed = pltpu.with_memory_space_constraint(green, pltpu.HBM)
+    acc, keep_hi, keep_lo, hi, lo = own_part(
+        fixed,
+        pltpu.with_memory_space_constraint(sigma, pltpu.HBM),
+        jnp.stack([z * held, inner]),
+    )
+    keeps = [keep_hi, keep_lo]
     counts, listed = [1], [z * held, one]
-    cuts = 2 if held % 2 == 0 else 1
-    piece = held // cuts
-    rightward = [sigma[:, h * piece : (h + 1) * piece] for h in range(cuts)]
-    leftward = list(rightward)
+    rightward = leftward = sigma
+    other = near_right = near_left = None
     for k in range(1, peers):
-        numbers = [jnp.maximum(z - k, 0) * held, jnp.minimum(z + k, peers - 1) * held]
+        rightward = send(rightward, up[k - 1 :])
+        leftward = send(leftward, down[: peers - k])
+        if k < peers - 1:
+            rightward, leftward = gate(rightward, leftward, keeps[-1])
+        after = []
+        if far and k == 1:
+            sooner = jnp.where(z == 0, rows - MARGIN, HALF)
+            (more,) = rows_at(fixed, [sooner], [rightward, leftward])
+            other = send(more, [(0, 1), (peers - 1, peers - 2)])
+            after = [more]
+        if k == min(2, peers - 1):
+            last, leading = rows_at(fixed, [rows - HALF, 0], [rightward, leftward])
+            near_right = send(last, up[:-1] if far else up)
+            near_left = send(leading, down[1:] if far else down)
+        firsts = [jnp.maximum(z - k, 0) * held, jnp.minimum(z + k, peers - 1) * held]
         valid = [(z >= k).astype(jnp.int32), (z + k < peers).astype(jnp.int32)]
-        for h in range(cuts):
-            rightward[h] = send(rightward[h], up[k - 1 :])
-            leftward[h] = send(leftward[h], down[: peers - k])
-            firsts = [x + h * piece for x in numbers]
-            acc, *more_keeps = lesser_part(
-                green, [rightward[h], leftward[h]], jnp.stack(firsts + valid), acc
-            )
-            keeps += more_keeps
-            counts.append(2)
-            listed += [firsts[0], valid[0], firsts[1], valid[1]]
+        acc, *more_keeps = lesser_part(
+            hi, lo, rightward, leftward, jnp.stack(firsts + valid + [inner]), acc, after
+        )
+        keeps += more_keeps
+        counts.append(2)
+        listed += [firsts[0], valid[0], firsts[1], valid[1]]
+    if other is None:
+        other = jnp.zeros_like(near_left)
     listed += [x.astype(jnp.int32) for x in (active, from_left, from_right, limit)]
     to_left, to_right, own = edge_part(
         jnp.stack(listed), other, near_right, near_left, keeps, tuple(counts)

time: 133 us -> 123 us (0.925)
  local copies, waits for them, and re-layouts: 7.85 us -> 29.5 us
  Pallas kernels: 47.5 us -> 26.4 us
  starting transfers between devices: 45.7 us -> 35.7 us
    unnamed x22 -> x66, local copies, waits for them, and re-layouts: 5.43 us -> 28 us
    pallas_call x7 -> x8, Pallas kernels: 42.3 us -> 21.1 us  [the longest x3 11.6 us: lesser_part(): pl.pallas_call(lesser_kernel, out_shape=(jax.ShapeDtypeStruct(before.shap...]
    ppermute x17 -> x11, starting transfers between devices: 42 us -> 32 us  [send(): return lax.ppermute(x, 'orb', pairs)]
    slice x1 -> x0, local copies, waits for them, and re-layouts: 1.94 us -> none  [per_device(): rightward = [sigma[:, h * piece:(h + 1) * piece] for h in range(cuts)]]
    ppermute x17 -> x11, waiting for transfers between devices: 8.7 us -> 8.42 us  [send(): return lax.ppermute(x, 'orb', pairs)]
  transfers between devices with their start and end apart: 18 -> 12, of which waited for: 4 -> 6; matrix products, arithmetic and copies ran while one was open for 1% -> 2% of each run, Pallas kernels for 32% -> 18%
where the time goes in v4:
time: 123 us; the launch traced here: 122 us
  starting transfers between devices  35.7 us (29%)
  local copies, waits for them, and re-layouts  29.5 us (24%)
  Pallas kernels  26.4 us (21%)
  waiting for transfers between devices  17.8 us (14%)
  blocking collectives  12.2 us (10%)
    ppermute x11, starting transfers between devices, send(): return lax.ppermute(x, 'orb', pairs)  32 us
    unnamed x66, local copies, waits for them, and re-layouts  28 us
    all_to_all x1, blocking collectives, per_device(): lax.all_to_all(spread, 'energy', split_axis=0, concat_axis=0, tiled=True)  12.2 us
    pallas_call x3, Pallas kernels, lesser_part(): pl.pallas_call(lesser_kernel, out_shape=(jax.ShapeDtypeStruct(before.shap...  11.6 us
    all_to_all x1, waiting for transfers between devices, per_device(): lax.all_to_all(lesser, 'energy', split_axis=0, concat_axis=0, tiled=True)  9.38 us
    ppermute x11, waiting for transfers between devices, send(): return lax.ppermute(x, 'orb', pairs)  8.42 us
    pallas_call x1, Pallas kernels, own_part(): pl.pallas_call(own_kernel, out_shape=(jax.ShapeDtypeStruct((tiles, 2 * TI...  6.65 us
    all_to_all x1, starting transfers between devices, per_device(): lax.all_to_all(lesser, 'energy', split_axis=0, concat_axis=0, tiled=True)  3.71 us
  transfers between devices with their start and end apart: 12, of which 6 were waited for; matrix products, arithmetic and copies ran while one was open for 2% of the time, Pallas kernels for 18%

profile of v4, /device:TPU:0, one launch (start us, length us, event | category | flops | bytes accessed | tf_op | source)
XLA Modules:
  0.0 122.3 jit_solution(6289129261389095232)
XLA Ops:
  0.0 5.1 %collective-permute-start = (f32[1,4,2,128,128]{4,3,2,1,0:T(8,128)}, f32[1,4,2,128,128]{4,3,2,1,0:T(8,128)S(1)}, u32[]{:S(2)}, u32[]{:S(2)}) collective-permute-start(f32[1,4,2,128,128]{4,3,2,1,0:T(8,128)} %sigma_ref.1), channel_id=1, source_target_pairs={{0,1},{1,2},{2,3},{4,5},{5,6},{6,7},{8,9},{9,10},{10,11},{12,13},{... | collective-permute-start | bytes 1572872 | tf_op jit(solution)/shard_map/ppermute | solution.py:493
  5.1 1.3 %collective-permute-start.1 = (f32[1,4,2,128,128]{4,3,2,1,0:T(8,128)}, f32[1,4,2,128,128]{4,3,2,1,0:T(8,128)S(1)}, u32[]{:S(2)}, u32[]{:S(2)}) collective-permute-start(f32[1,4,2,128,128]{4,3,2,1,0:T(8,128)} %sigma_ref.1), channel_id=1, source_target_pairs={{1,0},{2,1},{3,2},{5,4},{6,5},{7,6},{9,8},{10,9},{11,10},{13,12},{... | collective-permute-start | bytes 1572872 | tf_op jit(solution)/shard_map/ppermute | solution.py:493
  7.3 6.6 %lesser_own.1 = (f32[4,256,256]{2,1,0:T(8,128)S(1)}, bf16[4,256,256]{2,1,0:T(8,128)(2,1)S(1)}, bf16[4,256,256]{2,1,0:T(8,128)(2,1)S(1)}, bf16[640,4096]{1,0:T(8,128)(2,1)S(1)}, bf16[640,4096]{1,0:T(8,128)(2,1)S(1)}) custom-call(s32[2]{0:T(128)S(1)} %pad_add_fusion.idx_ref, f32[1,2,512,2048]{3,2,1,0:T(8,128)} %green_ref.5, f32[1,4,2,128,128]{4,3,2,1,0:T(8,128)} %sigma_ref.1), custom_call_target="tpu_custom_call" | custom-call | flops 2415919104 | bytes 8388608 | tf_op jit(solution)/shard_map/lesser_own/pallas_call | solution.py:147
  13.9 2.3 %copy-done.1 = bf16[640,4096]{1,0:T(8,128)(2,1)} copy-done((bf16[640,4096]{1,0:T(8,128)(2,1)}, bf16[640,4096]{1,0:T(8,128)(2,1)S(1)}, u32[]{:S(2)}) %copy-start.1) | copy-done | bytes 5242904
  16.3 2.4 %copy-done.4 = bf16[640,4096]{1,0:T(8,128)(2,1)} copy-done((bf16[640,4096]{1,0:T(8,128)(2,1)}, bf16[640,4096]{1,0:T(8,128)(2,1)S(1)}, u32[]{:S(2)}) %copy-start.4) | copy-done | bytes 5242904
  22.1 1.3 %collective-permute-start.3 = (f32[1,4,2,128,128]{4,3,2,1,0:T(8,128)}, f32[1,4,2,128,128]{4,3,2,1,0:T(8,128)S(1)}, u32[]{:S(2)}, u32[]{:S(2)}) collective-permute-start(f32[1,4,2,128,128]{4,3,2,1,0:T(8,128)} %get-tuple-element.32.rest_1_.left_ref), channel_id=1, source_target_pairs={{1,0},{2,1},{5,4},{6,5},{9,8},{10,9},{13,12},{14,13},{17,16},{18,1... | collective-permute-start | bytes 1572872 | tf_op jit(solution)/shard_map/ppermute | solution.py:493
  23.6 1.0 copy-done.10
  25.7 1.1 rows.2.rest_0_
  27.1 2.5 %copy-done.2 = bf16[640,4096]{1,0:T(8,128)(2,1)S(1)} copy-done((bf16[640,4096]{1,0:T(8,128)(2,1)S(1)}, bf16[640,4096]{1,0:T(8,128)(2,1)}, u32[]{:S(2)}) %copy-start.2) | copy-done | bytes 5242904
  29.5 2.5 %copy-done.5 = bf16[640,4096]{1,0:T(8,128)(2,1)S(1)} copy-done((bf16[640,4096]{1,0:T(8,128)(2,1)S(1)}, bf16[640,4096]{1,0:T(8,128)(2,1)}, u32[]{:S(2)}) %copy-start.5) | copy-done | bytes 5242904
  32.0 3.5 %lesser_more.3 = (f32[4,256,256]{2,1,0:T(8,128)S(1)}, bf16[8,256,256]{2,1,0:T(8,128)(2,1)S(1)}, bf16[8,256,256]{2,1,0:T(8,128)(2,1)S(1)}) custom-call(s32[5]{0:T(128)S(1)} %stack.130.idx_ref, bf16[640,4096]{1,0:T(8,128)(2,1)S(1)} %copy-done.2, bf16[640,4096]{1,0:T(8,128)(2,1)S(1)} %copy-done.5, ...), custom_call_target="tpu_custom_call", output_to_operand_aliasing={{0}: (5, {})} | custom-call | flops 3019898880 | bytes 2097152 | tf_op jit(solution)/shard_map/lesser_more/pallas_call | solution.py:193
  37.5 3.8 %collective-permute-done.3.left_ref = f32[1,4,2,128,128]{4,3,2,1,0:T(8,128)S(1)} collective-permute-done((f32[1,4,2,128,128]{4,3,2,1,0:T(8,128)}, f32[1,4,2,128,128]{4,3,2,1,0:T(8,128)S(1)}, u32[]{:S(2)}, u32[]{:S(2)}) %collective-permute-start.3) | collective-permute-done | bytes 524320 | tf_op jit(solution)/shard_map/ppermute | solution.py:493
  42.1 1.5 %collective-permute-start.4 = (f32[1,4,2,128,128]{4,3,2,1,0:T(8,128)}, f32[1,4,2,128,128]{4,3,2,1,0:T(8,128)}, u32[]{:S(2)}, u32[]{:S(2)}) collective-permute-start(f32[1,4,2,128,128]{4,3,2,1,0:T(8,128)} %get-tuple-element.35.right_ref.rest_0_), channel_id=1, source_target_pairs={{2,3},{6,7},{10,11},{14,15},{18,19},{22,23},{26,27},{30,31}} | collective-permute-start | bytes 1572872 | tf_op jit(solution)/shard_map/ppermute | solution.py:493
  43.6 1.3 %collective-permute-start.5 = (f32[1,4,2,128,128]{4,3,2,1,0:T(8,128)}, f32[1,4,2,128,128]{4,3,2,1,0:T(8,128)}, u32[]{:S(2)}, u32[]{:S(2)}) collective-permute-start(f32[1,4,2,128,128]{4,3,2,1,0:T(8,128)} %get-tuple-element.36.left_ref.rest_1_), channel_id=1, source_target_pairs={{1,0},{5,4},{9,8},{13,12},{17,16},{21,20},{25,24},{29,28}} | collective-permute-start | bytes 1572872 | tf_op jit(solution)/shard_map/ppermute | solution.py:493
  45.6 1.4 %copy-done.7 = bf16[1024,1024]{1,0:T(8,128)(2,1)} copy-done((bf16[1024,1024]{1,0:T(8,128)(2,1)}, bf16[1024,1024]{1,0:T(8,128)(2,1)S(1)}, u32[]{:S(2)}) %copy-start.7) | copy-done | bytes 2097176
  47.4 10.2 %collective-permute-start.6 = (f32[2,32,2048]{2,1,0:T(8,128)S(1)}, f32[2,32,2048]{2,1,0:T(8,128)S(1)}, u32[]{:S(2)}, u32[]{:S(2)}) collective-permute-start(f32[2,32,2048]{2,1,0:T(8,128)S(1)} %rows.2.rest_0_), channel_id=1, source_target_pairs={{0,1},{3,2},{4,5},{7,6},{8,9},{11,10},{12,13},{15,14},{16,17},{19,... | collective-permute-start | bytes 1572872 | tf_op jit(solution)/shard_map/ppermute | solution.py:493
  59.7 1.8 %rows.3 = (f32[2,32,2048]{2,1,0:T(8,128)S(1)}, f32[2,32,2048]{2,1,0:T(8,128)S(1)}) custom-call(s32[2]{0:T(128)S(1)} %copy-done.29, f32[1,2,512,2048]{3,2,1,0:T(8,128)} %green_ref.5, f32[1,4,2,128,128]{4,3,2,1,0:T(8,128)S(1)} %copy-done.16, f32[1,4,2,128,128]{4,3,2,1,0:T(8,128)S(1)} %copy-done.19), custom_call_target="tpu_custom_call" | custom-call | bytes 1048576 | tf_op jit(solution)/shard_map/rows/pallas_call | solution.py:231
  61.4 1.3 %collective-permute-start.7 = (f32[2,32,2048]{2,1,0:T(8,128)S(1)}, f32[2,32,2048]{2,1,0:T(8,128)S(1)}, u32[]{:S(2)}, u32[]{:S(2)}) collective-permute-start(f32[2,32,2048]{2,1,0:T(8,128)S(1)} %get-tuple-element.40), channel_id=1, source_target_pairs={{0,1},{1,2},{4,5},{5,6},{8,9},{9,10},{12,13},{13,14},{16,17},{17,1... | collective-permute-start | bytes 1572872 | tf_op jit(solution)/shard_map/ppermute | solution.py:493
  63.5 2.5 %copy-done.3 = bf16[640,4096]{1,0:T(8,128)(2,1)S(1)} copy-done((bf16[640,4096]{1,0:T(8,128)(2,1)S(1)}, bf16[640,4096]{1,0:T(8,128)(2,1)}, u32[]{:S(2)}) %copy-start.3) | copy-done | bytes 5242904
  66.0 2.5 %copy-done.6 = bf16[640,4096]{1,0:T(8,128)(2,1)S(1)} copy-done((bf16[640,4096]{1,0:T(8,128)(2,1)S(1)}, bf16[640,4096]{1,0:T(8,128)(2,1)}, u32[]{:S(2)}) %copy-start.6) | copy-done | bytes 5242904
  68.5 3.5 %lesser_more.4 = (f32[4,256,256]{2,1,0:T(8,128)S(1)}, bf16[8,256,256]{2,1,0:T(8,128)(2,1)S(1)}, bf16[8,256,256]{2,1,0:T(8,128)(2,1)S(1)}) custom-call(s32[5]{0:T(128)S(1)} %stack.138.idx_ref, bf16[640,4096]{1,0:T(8,128)(2,1)S(1)} %copy-done.3, bf16[640,4096]{1,0:T(8,128)(2,1)S(1)} %copy-done.6, ...), custom_call_target="tpu_custom_call", output_to_operand_aliasing={{0}: (5, {})} | custom-call | flops 3019898880 | bytes 2097152 | tf_op jit(solution)/shard_map/lesser_more/pallas_call | solution.py:193
  72.1 4.5 %lesser_more.5 = (f32[4,256,256]{2,1,0:T(8,128)S(1)}, bf16[8,256,256]{2,1,0:T(8,128)(2,1)S(1)}, bf16[8,256,256]{2,1,0:T(8,128)(2,1)S(1)}) custom-call(s32[5]{0:T(128)S(1)} %stack.121.idx_ref, bf16[640,4096]{1,0:T(8,128)(2,1)S(1)} %copy-done.3, bf16[640,4096]{1,0:T(8,128)(2,1)S(1)} %copy-done.6, ...), custom_call_target="tpu_custom_call", output_to_operand_aliasing={{0}: (5, {})} | custom-call | flops 3019898880 | bytes 2097152 | tf_op jit(solution)/shard_map/lesser_more/pallas_call | solution.py:193
  76.6 2.5 %collective-permute-done.7.b_ref = f32[2,32,2048]{2,1,0:T(8,128)S(1)} collective-permute-done((f32[2,32,2048]{2,1,0:T(8,128)S(1)}, f32[2,32,2048]{2,1,0:T(8,128)S(1)}, u32[]{:S(2)}, u32[]{:S(2)}) %collective-permute-start.7) | collective-permute-done | bytes 524320 | tf_op jit(solution)/shard_map/ppermute | solution.py:493
  79.8 1.3 %collective-permute-start.10 = (f32[2,64,128]{2,1,0:T(8,128)S(1)}, f32[2,64,128]{2,1,0:T(8,128)S(1)}, u32[]{:S(2)}, u32[]{:S(2)}) collective-permute-start(f32[2,64,128]{2,1,0:T(8,128)S(1)} %get-tuple-element.50), channel_id=1, source_target_pairs={{1,0},{2,1},{3,2},{5,4},{6,5},{7,6},{9,8},{10,9},{11,10},{13,12},{... | collective-permute-start | bytes 196616 | tf_op jit(solution)/shard_map/ppermute | solution.py:493
  81.1 7.4 %collective-permute-start.9 = (f32[2,64,128]{2,1,0:T(8,128)S(1)}, f32[2,64,128]{2,1,0:T(8,128)S(1)}, u32[]{:S(2)}, u32[]{:S(2)}) collective-permute-start(f32[2,64,128]{2,1,0:T(8,128)S(1)} %get-tuple-element.49), channel_id=1, source_target_pairs={{0,1},{1,2},{2,3},{4,5},{5,6},{6,7},{8,9},{9,10},{10,11},{12,13},{... | collective-permute-start | bytes 196616 | tf_op jit(solution)/shard_map/ppermute | solution.py:493
  88.8 1.6 %collective-permute-done.9.from_left_ref = f32[2,64,128]{2,1,0:T(8,128)S(1)} collective-permute-done((f32[2,64,128]{2,1,0:T(8,128)S(1)}, f32[2,64,128]{2,1,0:T(8,128)S(1)}, u32[]{:S(2)}, u32[]{:S(2)}) %collective-permute-start.9) | collective-permute-done | bytes 65568 | tf_op jit(solution)/shard_map/ppermute | solution.py:493
  90.4 1.4 %band.1 = f32[8,2,8,8,128]{4,3,2,1,0:T(8,128)} custom-call(f32[4,256,256]{2,1,0:T(8,128)S(1)} %get-tuple-element.39.acc_ref, f32[2,2,64,128]{3,2,1,0:T(8,128)S(1)} %get-tuple-element.48.own_ref, f32[2,64,128]{2,1,0:T(8,128)S(1)} %collective-permute-done.9.from_left_ref, f32[2,64,128]{2,1,0:T(8,128)S(1)} %collective-permute-done.10.from_right_ref), custom_call_target="tpu_custom_call" | custom-call | tf_op jit(solution)/shard_map/band/pallas_call | solution.py:382
  91.8 3.7 %all-to-all-start = ((f32[8,2,8,8,128]{4,3,2,1,0:T(8,128)}), f32[8,2,8,8,128]{4,3,2,1,0:T(8,128)S(1)}, u32[]{:S(2)}, u32[]{:S(2)}) async-start(f32[8,2,8,8,128]{4,3,2,1,0:T(8,128)} %band.1), calls=%async_computation | async-start | bytes 1048576 | tf_op jit(solution)/shard_map/all_to_all | solution.py:576
  95.9 9.4 %all-to-all-done.recv_ref = f32[8,2,8,8,128]{4,3,2,1,0:T(8,128)S(1)} async-done(((f32[8,2,8,8,128]{4,3,2,1,0:T(8,128)}), f32[8,2,8,8,128]{4,3,2,1,0:T(8,128)S(1)}, u32[]{:S(2)}, u32[]{:S(2)}) %all-to-all-start) | async-done | bytes 524320 | tf_op jit(solution)/shard_map/all_to_all | solution.py:576
  105.3 1.6 %copy-done.8 = bf16[1024,1024]{1,0:T(8,128)(2,1)S(1)} copy-done((bf16[1024,1024]{1,0:T(8,128)(2,1)S(1)}, bf16[1024,1024]{1,0:T(8,128)(2,1)}, u32[]{:S(2)}) %copy-start.8) | copy-done | bytes 2097176
  106.8 2.5 %scatter.1 = f32[8,128,128]{2,1,0:T(8,128)S(1)} custom-call(f32[8,2,8,8,128]{4,3,2,1,0:T(8,128)S(1)} %all-to-all-done.recv_ref, bf16[1024,1024]{1,0:T(8,128)(2,1)S(1)} %copy-done.8, f32[128,128]{1,0:T(8,128)S(1)} %mul.96.mix_ref, f32[192,128]{1,0:T(8,128)S(1)} %constant_dynamic-slice_fusion.dham_ref), custom_call_target="tpu_custom_call" | custom-call | tf_op jit(solution)/shard_map/scatter/pallas_call | solution.py:459
  109.4 12.2 %all_to_all.10 = f32[8,128,128]{2,1,0:T(8,128)S(1)} all-to-all(f32[8,128,128]{2,1,0:T(8,128)S(1)} %scatter.1), channel_id=1, replica_groups=mesh['energy'=8,'orb'=4] {'energy'}, dimensions={0} | all-to-all | bytes 1048576 | tf_op jit(solution)/shard_map/all_to_all | solution.py:578
  (87 shorter events, 14.4 us)
Async XLA Ops:
  0.0 95.8 %copy-start = (f32[1024,3,8,8]{0,3,2,1:T(8,128)S(1)}, f32[1024,3,8,8]{0,3,2,1:T(8,128)}, u32[]{:S(2)}) copy-start(f32[1024,3,8,8]{0,3,2,1:T(8,128)} %param.11) | copy-start | bytes 2359300
  0.0 20.2 %collective-permute-start = (f32[1,4,2,128,128]{4,3,2,1,0:T(8,128)}, f32[1,4,2,128,128]{4,3,2,1,0:T(8,128)S(1)}, u32[]{:S(2)}, u32[]{:S(2)}) collective-permute-start(f32[1,4,2,128,128]{4,3,2,1,0:T(8,128)} %sigma_ref.1), channel_id=1, source_target_pairs={{0,1},{1,2},{2,3},{4,5},{5,6},{6,7},{8,9},{9,10},{10,11},{12,13},{... | collective-permute-start | bytes 1572872 | tf_op jit(solution)/shard_map/ppermute | solution.py:493
  5.1 15.5 %collective-permute-start.1 = (f32[1,4,2,128,128]{4,3,2,1,0:T(8,128)}, f32[1,4,2,128,128]{4,3,2,1,0:T(8,128)S(1)}, u32[]{:S(2)}, u32[]{:S(2)}) collective-permute-start(f32[1,4,2,128,128]{4,3,2,1,0:T(8,128)} %sigma_ref.1), channel_id=1, source_target_pairs={{1,0},{2,1},{3,2},{5,4},{6,5},{7,6},{9,8},{10,9},{11,10},{13,12},{... | collective-permute-start | bytes 1572872 | tf_op jit(solution)/shard_map/ppermute | solution.py:493
  13.9 2.3 %copy-start.1 = (bf16[640,4096]{1,0:T(8,128)(2,1)}, bf16[640,4096]{1,0:T(8,128)(2,1)S(1)}, u32[]{:S(2)}) copy-start(bf16[640,4096]{1,0:T(8,128)(2,1)S(1)} %get-tuple-element.28.hi_ref) | copy-start | bytes 15728644
  16.3 2.4 %copy-start.4 = (bf16[640,4096]{1,0:T(8,128)(2,1)}, bf16[640,4096]{1,0:T(8,128)(2,1)S(1)}, u32[]{:S(2)}) copy-start(bf16[640,4096]{1,0:T(8,128)(2,1)S(1)} %get-tuple-element.29.lo_ref) | copy-start | bytes 15728644
  21.4 16.1 %collective-permute-start.2 = (f32[1,4,2,128,128]{4,3,2,1,0:T(8,128)}, f32[1,4,2,128,128]{4,3,2,1,0:T(8,128)S(1)}, u32[]{:S(2)}, u32[]{:S(2)}) collective-permute-start(f32[1,4,2,128,128]{4,3,2,1,0:T(8,128)} %get-tuple-element.31.rest_0_.right_ref), channel_id=1, source_target_pairs={{1,2},{2,3},{5,6},{6,7},{9,10},{10,11},{13,14},{14,15},{17,18},{18... | collective-permute-start | bytes 1572872 | tf_op jit(solution)/shard_map/ppermute | solution.py:493
  22.1 19.3 %collective-permute-start.3 = (f32[1,4,2,128,128]{4,3,2,1,0:T(8,128)}, f32[1,4,2,128,128]{4,3,2,1,0:T(8,128)S(1)}, u32[]{:S(2)}, u32[]{:S(2)}) collective-permute-start(f32[1,4,2,128,128]{4,3,2,1,0:T(8,128)} %get-tuple-element.32.rest_1_.left_ref), channel_id=1, source_target_pairs={{1,0},{2,1},{5,4},{6,5},{9,8},{10,9},{13,12},{14,13},{17,16},{18,1... | collective-permute-start | bytes 1572872 | tf_op jit(solution)/shard_map/ppermute | solution.py:493
  25.7 1.4 %copy-start.14 = (f32[1,4,2,128,128]{4,3,2,1,0:T(8,128)S(1)}, f32[1,4,2,128,128]{4,3,2,1,0:T(8,128)}, u32[]{:S(2)}) copy-start(f32[1,4,2,128,128]{4,3,2,1,0:T(8,128)} %get-tuple-element.32.rest_1_.left_ref) | copy-start | bytes 1572868
  27.1 2.5 %copy-start.2 = (bf16[640,4096]{1,0:T(8,128)(2,1)S(1)}, bf16[640,4096]{1,0:T(8,128)(2,1)}, u32[]{:S(2)}) copy-start(bf16[640,4096]{1,0:T(8,128)(2,1)} %copy-done.1) | copy-start | bytes 15728644
  29.5 2.5 %copy-start.5 = (bf16[640,4096]{1,0:T(8,128)(2,1)S(1)}, bf16[640,4096]{1,0:T(8,128)(2,1)}, u32[]{:S(2)}) copy-start(bf16[640,4096]{1,0:T(8,128)(2,1)} %copy-done.4) | copy-start | bytes 15728644
  32.0 12.8 %copy-start.30 = (f32[2,6]{1,0:T(2,128)S(1)}, f32[2,6]{1,0:T(2,128)}, u32[]{:S(2)}) copy-start(f32[2,6]{1,0:T(2,128)} %param.10) | copy-start | bytes 148
  32.0 15.2 %copy-start.31 = (s32[6]{0:T(128)S(1)}, s32[6]{0:T(128)}, u32[]{:S(2)}) copy-start(s32[6]{0:T(128)} %param.9) | copy-start | bytes 76
  32.0 25.5 %copy-start.29 = (s32[2]{0:T(128)S(1)}, s32[2]{0:T(128)}, u32[]{:S(2)}) copy-start(s32[2]{0:T(128)} %constant.45.clone.1.idx_ref) | copy-start | bytes 28
  37.5 3.8 %copy-start.15 = (f32[1,4,2,128,128]{4,3,2,1,0:T(8,128)}, f32[1,4,2,128,128]{4,3,2,1,0:T(8,128)S(1)}, u32[]{:S(2)}) copy-start(f32[1,4,2,128,128]{4,3,2,1,0:T(8,128)S(1)} %collective-permute-done.2.right_ref) | copy-start | bytes 1572868
  42.1 29.9 %collective-permute-start.4 = (f32[1,4,2,128,128]{4,3,2,1,0:T(8,128)}, f32[1,4,2,128,128]{4,3,2,1,0:T(8,128)}, u32[]{:S(2)}, u32[]{:S(2)}) collective-permute-start(f32[1,4,2,128,128]{4,3,2,1,0:T(8,128)} %get-tuple-element.35.right_ref.rest_0_), channel_id=1, source_target_pairs={{2,3},{6,7},{10,11},{14,15},{18,19},{22,23},{26,27},{30,31}} | collective-permute-start | bytes 1572872 | tf_op jit(solution)/shard_map/ppermute | solution.py:493
  43.6 28.4 %collective-permute-start.5 = (f32[1,4,2,128,128]{4,3,2,1,0:T(8,128)}, f32[1,4,2,128,128]{4,3,2,1,0:T(8,128)}, u32[]{:S(2)}, u32[]{:S(2)}) collective-permute-start(f32[1,4,2,128,128]{4,3,2,1,0:T(8,128)} %get-tuple-element.36.left_ref.rest_1_), channel_id=1, source_target_pairs={{1,0},{5,4},{9,8},{13,12},{17,16},{21,20},{25,24},{29,28}} | collective-permute-start | bytes 1572872 | tf_op jit(solution)/shard_map/ppermute | solution.py:493
  45.0 18.5 %copy-start.17 = (f32[1,4,2,128,128]{4,3,2,1,0:T(8,128)S(1)}, f32[1,4,2,128,128]{4,3,2,1,0:T(8,128)}, u32[]{:S(2)}) copy-start(f32[1,4,2,128,128]{4,3,2,1,0:T(8,128)} %get-tuple-element.35.right_ref.rest_0_) | copy-start | bytes 1572868
  45.0 18.5 %copy-start.20 = (f32[1,4,2,128,128]{4,3,2,1,0:T(8,128)S(1)}, f32[1,4,2,128,128]{4,3,2,1,0:T(8,128)}, u32[]{:S(2)}) copy-start(f32[1,4,2,128,128]{4,3,2,1,0:T(8,128)} %get-tuple-element.36.left_ref.rest_1_) | copy-start | bytes 1572868
  45.6 1.4 %copy-start.7 = (bf16[1024,1024]{1,0:T(8,128)(2,1)}, bf16[1024,1024]{1,0:T(8,128)(2,1)S(1)}, u32[]{:S(2)}) copy-start(bf16[1024,1024]{1,0:T(8,128)(2,1)S(1)} %picks.1.pick_ref) | copy-start | bytes 6291460
  47.4 29.2 %collective-permute-start.6 = (f32[2,32,2048]{2,1,0:T(8,128)S(1)}, f32[2,32,2048]{2,1,0:T(8,128)S(1)}, u32[]{:S(2)}, u32[]{:S(2)}) collective-permute-start(f32[2,32,2048]{2,1,0:T(8,128)S(1)} %rows.2.rest_0_), channel_id=1, source_target_pairs={{0,1},{3,2},{4,5},{7,6},{8,9},{11,10},{12,13},{15,14},{16,17},{19,... | collective-permute-start | bytes 1572872 | tf_op jit(solution)/shard_map/ppermute | solution.py:493
  61.4 17.7 %collective-permute-start.7 = (f32[2,32,2048]{2,1,0:T(8,128)S(1)}, f32[2,32,2048]{2,1,0:T(8,128)S(1)}, u32[]{:S(2)}, u32[]{:S(2)}) collective-permute-start(f32[2,32,2048]{2,1,0:T(8,128)S(1)} %get-tuple-element.40), channel_id=1, source_target_pairs={{0,1},{1,2},{4,5},{5,6},{8,9},{9,10},{12,13},{13,14},{16,17},{17,1... | collective-permute-start | bytes 1572872 | tf_op jit(solution)/shard_map/ppermute | solution.py:493
  62.8 16.3 %collective-permute-start.8 = (f32[2,32,2048]{2,1,0:T(8,128)S(1)}, f32[2,32,2048]{2,1,0:T(8,128)S(1)}, u32[]{:S(2)}, u32[]{:S(2)}) collective-permute-start(f32[2,32,2048]{2,1,0:T(8,128)S(1)} %get-tuple-element.41), channel_id=1, source_target_pairs={{2,1},{3,2},{6,5},{7,6},{10,9},{11,10},{14,13},{15,14},{18,17},{19... | collective-permute-start | bytes 1572872 | tf_op jit(solution)/shard_map/ppermute | solution.py:493
  63.5 2.5 %copy-start.3 = (bf16[640,4096]{1,0:T(8,128)(2,1)S(1)}, bf16[640,4096]{1,0:T(8,128)(2,1)}, u32[]{:S(2)}) copy-start(bf16[640,4096]{1,0:T(8,128)(2,1)} %copy-done.1) | copy-start | bytes 15728644
  66.0 2.5 %copy-start.6 = (bf16[640,4096]{1,0:T(8,128)(2,1)S(1)}, bf16[640,4096]{1,0:T(8,128)(2,1)}, u32[]{:S(2)}) copy-start(bf16[640,4096]{1,0:T(8,128)(2,1)} %copy-done.4) | copy-start | bytes 15728644
  72.0 7.1 %copy-start.22 = (bf16[8,256,256]{2,1,0:T(8,128)(2,1)S(1)}, bf16[8,256,256]{2,1,0:T(8,128)(2,1)}, u32[]{:S(2)}) copy-start(bf16[8,256,256]{2,1,0:T(8,128)(2,1)} %copy-done.21) | copy-start | bytes 3145732
  72.0 7.1 %copy-start.24 = (bf16[4,256,256]{2,1,0:T(8,128)(2,1)S(1)}, bf16[4,256,256]{2,1,0:T(8,128)(2,1)}, u32[]{:S(2)}) copy-start(bf16[4,256,256]{2,1,0:T(8,128)(2,1)} %copy-done.23) | copy-start | bytes 1572868
  72.0 7.1 %copy-start.26 = (bf16[8,256,256]{2,1,0:T(8,128)(2,1)S(1)}, bf16[8,256,256]{2,1,0:T(8,128)(2,1)}, u32[]{:S(2)}) copy-start(bf16[8,256,256]{2,1,0:T(8,128)(2,1)} %copy-done.25) | copy-start | bytes 3145732
  72.1 7.1 %copy-start.28 = (bf16[4,256,256]{2,1,0:T(8,128)(2,1)S(1)}, bf16[4,256,256]{2,1,0:T(8,128)(2,1)}, u32[]{:S(2)}) copy-start(bf16[4,256,256]{2,1,0:T(8,128)(2,1)} %copy-done.27) | copy-start | bytes 1572868
  79.8 9.0 %collective-permute-start.10 = (f32[2,64,128]{2,1,0:T(8,128)S(1)}, f32[2,64,128]{2,1,0:T(8,128)S(1)}, u32[]{:S(2)}, u32[]{:S(2)}) collective-permute-start(f32[2,64,128]{2,1,0:T(8,128)S(1)} %get-tuple-element.50), channel_id=1, source_target_pairs={{1,0},{2,1},{3,2},{5,4},{6,5},{7,6},{9,8},{10,9},{11,10},{13,12},{... | collective-permute-start | bytes 196616 | tf_op jit(solution)/shard_map/ppermute | solution.py:493
  81.1 9.3 %collective-permute-start.9 = (f32[2,64,128]{2,1,0:T(8,128)S(1)}, f32[2,64,128]{2,1,0:T(8,128)S(1)}, u32[]{:S(2)}, u32[]{:S(2)}) collective-permute-start(f32[2,64,128]{2,1,0:T(8,128)S(1)} %get-tuple-element.49), channel_id=1, source_target_pairs={{0,1},{1,2},{2,3},{4,5},{5,6},{6,7},{8,9},{9,10},{10,11},{12,13},{... | collective-permute-start | bytes 196616 | tf_op jit(solution)/shard_map/ppermute | solution.py:493
  91.8 13.5 %all-to-all-start = ((f32[8,2,8,8,128]{4,3,2,1,0:T(8,128)}), f32[8,2,8,8,128]{4,3,2,1,0:T(8,128)S(1)}, u32[]{:S(2)}, u32[]{:S(2)}) async-start(f32[8,2,8,8,128]{4,3,2,1,0:T(8,128)} %band.1), calls=%async_computation | async-start | bytes 1048576 | tf_op jit(solution)/shard_map/all_to_all | solution.py:576
  105.2 1.6 %copy-start.8 = (bf16[1024,1024]{1,0:T(8,128)(2,1)S(1)}, bf16[1024,1024]{1,0:T(8,128)(2,1)}, u32[]{:S(2)}) copy-start(bf16[1024,1024]{1,0:T(8,128)(2,1)} %copy-done.7) | copy-start | bytes 6291460
  (12 other events, 11.3 us)

commit v5 on v4

--- a/solution.py
+++ b/solution.py
@@ -98,13 +98,30 @@
     lax.fori_loop(0, held // once, step, 0)
 
 
+def is_far(peers):
+    return peers >= 4
+
+
+def is_inner():
+    z, peers = lax.axis_index("orb"), lax.axis_size("orb")
+    if is_far(peers):
+        return jnp.logical_and(z > 0, z < peers - 1)
+    return z >= 0
+
+
+def neighbour(distance):
+    z, peers = lax.axis_index("orb"), lax.axis_size("orb")
+    number = z + distance
+    return jnp.clip(number, 0, peers - 1), jnp.logical_and(number >= 0, number < peers)
+
+
 def own_kernel(
-    idx_ref, green_ref, sigma_ref, acc_ref, keep_hi_ref, keep_lo_ref, hi_ref, lo_ref,
-    buf, self_ref, sem,
+    green_ref, sigma_ref, *rest
 ):
+    acc_ref, keep_hi_ref, keep_lo_ref, hi_ref, lo_ref, buf, self_ref, sem = rest[-8:]
     rows, held = green_ref.shape[2], sigma_ref.shape[1]
     blocks = green_ref.shape[3] // BS
-    begin, active = idx_ref[0], idx_ref[1] == 1
+    begin, active = lax.axis_index("orb") * held, is_inner()
 
     def block_of(s):
         return lax.rem(begin + s, blocks)
@@ -137,7 +154,7 @@
     lax.fori_loop(held, blocks, store, 0)
 
 
-def own_part(green, sigma, index):
+def own_part(green, sigma, after):
     rows, held = green.shape[2], sigma.shape[1]
     tiles, blocks = rows // TILE, green.shape[3] // BS
     vmem = pl.BlockSpec(memory_space=pltpu.VMEM)
@@ -153,7 +170,7 @@
             whole,
             whole,
         ),
-        in_specs=[pl.BlockSpec(memory_space=pltpu.SMEM), hbm, hbm],
+        in_specs=[hbm] * (2 + len(after)),
         out_specs=(vmem,) * 5,
         scratch_shapes=[
             pltpu.VMEM((blocks, 2, rows, BS), F32),
@@ -167,52 +184,54 @@
             transcendentals=0,
         ),
         name="lesser_own",
-    )(index, green, sigma)
-
-
-def lesser_kernel(
-    idx_ref, hi_ref, lo_ref, right_ref, left_ref, before_ref, *rest
-):
-    acc_ref, keep_hi_ref, keep_lo_ref = rest[-3:]
-    held = right_ref.shape[1]
+    )(green, sigma, *after)
+
+
+def lesser_kernel(places, held, hi_ref, lo_ref, before_ref, *rest):
+    sigmas, rest = rest[: len(places)], rest[len(places) :]
+    acc_ref, *keeps = rest[-3:]
     acc_ref[...] = before_ref[...]
-    for k, self_ref in enumerate((right_ref, left_ref)):
-
-        @pl.when(idx_ref[2 + k] == 1)
+    slot = 0
+    for (distance, first), self_ref in zip(places, sigmas):
+        number, valid = neighbour(distance)
+
+        @pl.when(valid)
         def _():
             shard_loop(
-                idx_ref[k], self_ref, hi_ref, lo_ref, acc_ref,
-                (keep_hi_ref, keep_lo_ref), k * held, idx_ref[4] == 1,
+                number * held + first, self_ref, hi_ref, lo_ref, acc_ref, keeps, slot, is_inner()
             )
 
-
-def lesser_part(hi, lo, right, left, index, before, after):
-    held = right.shape[1]
+        slot += self_ref.shape[1]
+
+
+def lesser_part(hi, lo, before, shards, places, held, after=()):
     vmem = pl.BlockSpec(memory_space=pltpu.VMEM)
-    keep = jax.ShapeDtypeStruct((2 * held, 4 * MARGIN, 2 * BS), BF16)
+    count = sum(x.shape[1] for x in shards)
+    kept = jax.ShapeDtypeStruct((count, 4 * MARGIN, 2 * BS), BF16)
+    outs = [jax.ShapeDtypeStruct(before.shape, F32), kept, kept]
     return pl.pallas_call(
-        lesser_kernel,
-        out_shape=(jax.ShapeDtypeStruct(before.shape, F32), keep, keep),
-        in_specs=[pl.BlockSpec(memory_space=pltpu.SMEM)]
-        + [vmem] * 5
-        + [pl.BlockSpec(memory_space=pl.ANY)] * len(after),
-        out_specs=(vmem,) * 3,
-        input_output_aliases={5: 0},
-        compiler_params=pltpu.CompilerParams(vmem_limit_bytes=32 << 20),
+        functools.partial(lesser_kernel, places, held),
+        out_shape=outs,
+        in_specs=[vmem] * (3 + len(shards)) + [pl.BlockSpec(memory_space=pl.ANY)] * len(after),
+        out_specs=[vmem] * len(outs),
+        input_output_aliases={2: 0},
+        compiler_params=pltpu.CompilerParams(vmem_limit_bytes=26 << 20),
         cost_estimate=pl.CostEstimate(
-            flops=held * 6 * hi.shape[0] * 2 * BS * (2 * BS + 4 * TILE),
+            flops=count * 3 * hi.shape[0] * 2 * BS * (2 * BS + 4 * TILE),
             bytes_accessed=8 * before.size,
             transcendentals=0,
         ),
         name="lesser_more",
-    )(index, hi, lo, right, left, before, *after)
-
-
-def rows_kernel(count, idx_ref, green_ref, *rest):
+    )(hi, lo, before, *shards, *after)
+
+
+def rows_kernel(count, green_ref, *rest):
     outs, sem = rest[-1 - count : -1], rest[-1]
+    z, rows = lax.axis_index("orb"), green_ref.shape[2]
+    starts = [rows - HALF, 0, jnp.where(z == 0, rows - MARGIN, HALF)]
     copies = [
         pltpu.make_async_copy(
-            green_ref.at[0, :, pl.ds(pl.multiple_of(idx_ref[n], HALF), HALF), :],
+            green_ref.at[0, :, pl.ds(pl.multiple_of(starts[n], HALF), HALF), :],
             out,
             sem.at[n],
         )
@@ -224,68 +243,148 @@
         copy.wait()
 
 
-def rows_at(green, starts, after):
-    count = len(starts)
-    hbm = pl.BlockSpec(memory_space=pl.ANY)
+def rows_at(green, count):
     out = jax.ShapeDtypeStruct((2, HALF, green.shape[3]), F32)
     return pl.pallas_call(
         functools.partial(rows_kernel, count),
         out_shape=[out] * count,
-        in_specs=[pl.BlockSpec(memory_space=pltpu.SMEM)] + [hbm] * (1 + len(after)),
+        in_specs=[pl.BlockSpec(memory_space=pl.ANY)],
         out_specs=[pl.BlockSpec(memory_space=pltpu.VMEM)] * count,
         scratch_shapes=[pltpu.SemaphoreType.DMA((count,))],
         compiler_params=pltpu.CompilerParams(vmem_limit_bytes=8 << 20),
+        name="rows",
+    )(green)
+
+
+def load_kernel(cases, first, piece, green_ref, right_ref, left_ref, *rest):
+    outs, sem = rest[-1 - 2 * len(first) : -1], rest[-1]
+    per = BS // HALF
+    for side, ((rows, begin), source) in enumerate(zip(cases, (right_ref, left_ref))):
+        row = pl.multiple_of(begin, HALF)
+        taken, passed = [], []
+        for n, block in enumerate(first):
+            out = outs[side * len(first) + n]
+            passed.append(
+                pltpu.make_async_copy(
+                    source.at[:, pl.ds(block - first[0], piece)], out, sem.at[side, n]
+                )
+            )
+            for m in range(piece):
+                for part in range(2):
+                    for q in range(per):
+                        col = ((block + m) * per + q) * BS
+                        taken.append(
+                            pltpu.make_async_copy(
+                                green_ref.at[0, part, pl.ds(row, HALF), pl.ds(col, BS)],
+                                out.at[0, m, part, pl.ds(q * HALF, HALF), :],
+                                sem.at[side, len(taken)],
+                            )
+                        )
+        for want, copies in ((True, taken), (False, passed)):
+
+            @pl.when(rows == want)
+            def _():
+                for copy in copies:
+                    copy.start()
+
+    for side, ((rows, begin), source) in enumerate(zip(cases, (right_ref, left_ref))):
+        row = pl.multiple_of(begin, HALF)
+        for want in (True, False):
+
+            @pl.when(rows == want)
+            def _():
+                count = 0
+                for n, block in enumerate(first):
+                    out = outs[side * len(first) + n]
+                    if not want:
+                        pltpu.make_async_copy(
+                            source.at[:, pl.ds(block - first[0], piece)], out, sem.at[side, n]
+                        ).wait()
+                        continue
+                    for m in range(piece):
+                        for part in range(2):
+                            for q in range(per):
+                                col = ((block + m) * per + q) * BS
+                                pltpu.make_async_copy(
+                                    green_ref.at[0, part, pl.ds(row, HALF), pl.ds(col, BS)],
+                                    out.at[0, m, part, pl.ds(q * HALF, HALF), :],
+                                    sem.at[side, count],
+                                ).wait()
+                                count += 1
+
+
+def load(stage, green, right, left, first, piece, after):
+    rows = green.shape[2]
+
+    def kernel(*refs):
+        z, peers = lax.axis_index("orb"), lax.axis_size("orb")
+        if stage == 0:
+            cases = ((z == 0, rows - MARGIN), (z == peers - 1, HALF))
+        else:
+            cases = ((z < peers - 2, rows - HALF), (z > 1, 0))
+        load_kernel(cases, first, piece, *refs)
+
+    hbm = pl.BlockSpec(memory_space=pl.ANY)
+    out = jax.ShapeDtypeStruct((1, piece) + right.shape[2:], F32)
+    outs = pl.pallas_call(
+        kernel,
+        out_shape=[out] * (2 * len(first)),
+        in_specs=[hbm] * (3 + len(after)),
+        out_specs=[hbm] * (2 * len(first)),
+        scratch_shapes=[
+            pltpu.SemaphoreType.DMA((2, len(first) * piece * 2 * (BS // HALF)))
+        ],
+        compiler_params=pltpu.CompilerParams(vmem_limit_bytes=2 << 20),
         cost_estimate=pl.CostEstimate(
-            flops=0, bytes_accessed=4 * count * out.size, transcendentals=0
+            flops=0, bytes_accessed=8 * out.size * len(first), transcendentals=0
         ),
-        name="rows",
-    )(jnp.stack([jnp.asarray(x, jnp.int32) for x in starts]), green, *after)
-
-
-def gate_kernel(right_ref, left_ref, after_ref, *outs):
-    del right_ref, left_ref, after_ref, outs
-
-
-def gate(right, left, after):
-    hbm = pl.BlockSpec(memory_space=pl.ANY)
-    return pl.pallas_call(
-        gate_kernel,
-        out_shape=[jax.ShapeDtypeStruct(x.shape, x.dtype) for x in (right, left)],
-        in_specs=[hbm] * 3,
-        out_specs=[hbm] * 2,
-        input_output_aliases={0: 0, 1: 1},
-        cost_estimate=pl.CostEstimate(flops=0, bytes_accessed=0, transcendentals=0),
-        name="gate",
-    )(right, left, after)
-
-
-def edge_kernel(counts, idx_ref, a_ref, b_ref, c_ref, *rest):
-    parts = len(counts)
-    keeps, rest = rest[: 2 * parts], rest[2 * parts :]
-    left_ref, right_ref, own_ref, acc_ref = rest
-    base = 2 * sum(counts)
-    active, from_left, from_right = [idx_ref[base + k] == 1 for k in range(3)]
-    limit = idx_ref[base + 3]
-    acc_ref[...] = jnp.zeros_like(acc_ref)
-
-    def add(col, hi, lo, at, held):
-        cols = pl.ds(pl.multiple_of(col * BS, BS), held * BS)
-        wide = [
-            [ref[part, :, cols] for part in range(2)] for ref in (a_ref, b_ref, c_ref)
-        ]
+        name="load",
+    )(green, right, left, *after)
+    return outs[: len(first)], outs[len(first) :]
+
+
+def edge_kernel(places, held, part_of, riding, last, *refs):
+    halos, refs = refs[: 4 if riding else 3], refs[4 if riding else 3 :]
+    keeps, refs = refs[: 2 * len(places)], refs[2 * len(places) :]
+    z, peers = lax.axis_index("orb"), lax.axis_size("orb")
+    if is_far(peers):
+        from_left, from_right = z == 1, z == peers - 2
+    else:
+        from_left = from_right = z < 0
+    limit = jnp.where(from_right, MARGIN, HALF)
+    if part_of[0] > 0:
+        before_ref, refs = refs[0], refs[1:]
+    acc_ref = refs[-1]
+    acc_ref[...] = before_ref[...] if part_of[0] > 0 else jnp.zeros_like(acc_ref)
+    group = peers // part_of[1]
+    begin = part_of[0] * group
+
+    def halo_rows(ref, part, number, s):
+        if riding:
+            return ref[0, number - begin, part, s * HALF : (s + 1) * HALF, :]
+        col = pl.multiple_of((number * held + s) * BS, BS)
+        return ref[part, :, pl.ds(col, BS)]
+
+    def add(number, first, hi, lo, at, count):
         for side in range(2):
             fields = []
             for part in range(2):
-                more = wide[0][part]
-                if side == 0:
-                    rows = [jnp.where(from_left, more, 0.0), wide[1][part]]
-                else:
-                    rows = [wide[2][part], jnp.where(from_right, more, 0.0)]
+                inner, outer = [], []
+                for s in range(first, first + count):
+                    if riding:
+                        near, beyond = halos[2 + side], halos[side]
+                    else:
+                        near, beyond = halos[1 + side], halos[0]
+                    inner.append(halo_rows(near, part, number, s))
+                    outer.append(halo_rows(beyond, part, number, s))
+                inner, outer = jnp.concatenate(inner, axis=1), jnp.concatenate(outer, axis=1)
+                outer = jnp.where(from_left if side == 0 else from_right, outer, 0.0)
+                rows = [outer, inner] if side == 0 else [inner, outer]
                 fields.append(halves(jnp.concatenate(rows, axis=0)))
             halo = []
             for real, imag in zip(*fields):
                 lanes = []
-                for s in range(held):
+                for s in range(count):
                     one = slice(s * BS, (s + 1) * BS)
                     lanes += [
                         jnp.concatenate([real[:, one], -imag[:, one]], axis=0),
@@ -294,25 +393,28 @@
                 halo.append(jnp.concatenate(lanes, axis=1))
             rows = slice(side * TILE, (side + 1) * TILE)
             kept = [
-                jnp.concatenate([ref[at + s, rows, :] for s in range(held)], axis=1)
+                jnp.concatenate([ref[at + s, rows, :] for s in range(count)], axis=1)
                 for ref in (hi, lo)
             ]
             acc_ref[side] = acc_ref[side] + dot3(halo, kept, NT)
 
-    @pl.when(active)
+    @pl.when(is_inner())
     def _():
-        shard = 0
-        for part, count in enumerate(counts):
-            hi, lo = keeps[2 * part], keeps[2 * part + 1]
-            held = hi.shape[0] // count
-            for k in range(count):
-                col, valid = idx_ref[2 * shard], idx_ref[2 * shard + 1]
-                shard += 1
-
-                @pl.when(valid == 1)
+        for k, shards in enumerate(places):
+            at = 0
+            for distance, first, count in shards:
+                number, valid = neighbour(distance)
+                valid = valid & (number >= begin) & (number < begin + group)
+
+                @pl.when(valid)
                 def _():
-                    add(col, hi, lo, k * held, held)
-
+                    add(number, first, keeps[2 * k], keeps[2 * k + 1], at, count)
+
+                at += count
+
+    if not last:
+        return
+    left_ref, right_ref, own_ref = refs[-4:-1]
     lane = lax.broadcasted_iota(jnp.int32, (MARGIN, LANES), 1)
     row = lax.broadcasted_iota(jnp.int32, (MARGIN, LANES), 0)
     low = lane < MARGIN
@@ -329,23 +431,27 @@
     own_ref[1, 1] = jnp.where(mine, turned_right, 0.0)
 
 
-def edge_part(flags, a, b, c, keeps, counts):
+def edge_part(halos, keeps, places, held, part_of, riding, before, after):
     vmem = pl.BlockSpec(memory_space=pltpu.VMEM)
+    last = part_of[0] == part_of[1] - 1
     side = jax.ShapeDtypeStruct((2, MARGIN, LANES), F32)
+    acc = (2, TILE, TILE)
+    ends = [side, side, jax.ShapeDtypeStruct((2, 2, MARGIN, LANES), F32)]
+    args = [*halos, *keeps] + ([] if before is None else [before])
     return pl.pallas_call(
-        functools.partial(edge_kernel, counts),
-        out_shape=(side, side, jax.ShapeDtypeStruct((2, 2, MARGIN, LANES), F32)),
-        in_specs=[pl.BlockSpec(memory_space=pltpu.SMEM)] + [vmem] * (3 + len(keeps)),
-        out_specs=(vmem, vmem, vmem),
-        scratch_shapes=[pltpu.VMEM((2, TILE, TILE), F32)],
-        compiler_params=pltpu.CompilerParams(vmem_limit_bytes=24 << 20),
+        functools.partial(edge_kernel, places, held, part_of, riding, last),
+        out_shape=ends if last else [jax.ShapeDtypeStruct(acc, F32)],
+        in_specs=[vmem] * len(args) + [pl.BlockSpec(memory_space=pl.ANY)] * len(after),
+        out_specs=[vmem] * (3 if last else 1),
+        scratch_shapes=[pltpu.VMEM(acc, F32)] if last else [],
+        compiler_params=pltpu.CompilerParams(vmem_limit_bytes=20 << 20),
         cost_estimate=pl.CostEstimate(
-            flops=a.shape[2] * 2 * 12 * TILE * 2 * TILE,
-            bytes_accessed=a.shape[2] * 2 * 4 * TILE * 4,
+            flops=(1 << 31) // part_of[1],
+            bytes_accessed=(8 << 20) // part_of[1],
             transcendentals=0,
         ),
         name="edges",
-    )(flags, a, b, c, *keeps)
+    )(*args, *after)
 
 
 def band_kernel(acc_ref, own_ref, from_left_ref, from_right_ref, out_ref, rows_ref):
@@ -390,30 +496,7 @@
     )(acc, own, from_left, from_right)
 
 
-def picks_kernel(where_ref, out_ref):
-    rows = out_ref.shape[0]
-    padded = where_ref.shape[1]
-    entry = lax.broadcasted_iota(jnp.int32, (rows, padded), 0)
-    first = where_ref[...] * W
-    for j in range(W):
-        hit = entry == first + j
-        out_ref[:, j * padded : (j + 1) * padded] = jnp.where(hit, 1.0, 0.0).astype(BF16)
-
-
-def picks(where, rows):
-    padded = where.shape[1]
-    vmem = pl.BlockSpec(memory_space=pltpu.VMEM)
-    return pl.pallas_call(
-        picks_kernel,
-        out_shape=jax.ShapeDtypeStruct((rows, W * padded), BF16),
-        in_specs=[vmem],
-        out_specs=vmem,
-        compiler_params=pltpu.CompilerParams(vmem_limit_bytes=16 << 20),
-        name="picks",
-    )(where)
-
-
-def scatter_kernel(recv_ref, pick_ref, mix_ref, dham_ref, out_ref, smeared_ref, result_ref):
+def scatter_kernel(recv_ref, where_ref, mix_ref, dham_ref, out_ref, smeared_ref, result_ref):
     energies, _, group, _, _ = recv_ref.shape
     padded = dham_ref.shape[1]
     pairs = out_ref.shape[1]
@@ -422,7 +505,13 @@
     ]
     received = halves(jnp.concatenate(columns, axis=1))
     mixed = halves(dot3(halves(mix_ref[...]), received, NN))
-    smeared_ref[...] = dot(mixed[0], pick_ref[...], NN) + dot(mixed[1], pick_ref[...], NN)
+    entry = lax.broadcasted_iota(jnp.int32, (group * LANES, padded), 0)
+    first = where_ref[...] * W
+    for j in range(W):
+        pick = jnp.where(entry == first + j, 1.0, 0.0).astype(BF16)
+        smeared_ref[:, j * padded : (j + 1) * padded] = dot(mixed[0], pick, NN) + dot(
+            mixed[1], pick, NN
+        )
 
     def block(part, j, k):
         row = (part * W + j) * energies
@@ -452,7 +541,7 @@
         out_ref[e] = one.T[:pairs, :]
 
 
-def scatter(recv, pick, mix, dham, pairs):
+def scatter(recv, where, mix, dham, pairs):
     energies, _, group, _, _ = recv.shape
     padded = dham.shape[1]
     vmem = pl.BlockSpec(memory_space=pltpu.VMEM)
@@ -467,7 +556,7 @@
         ],
         compiler_params=pltpu.CompilerParams(vmem_limit_bytes=24 << 20),
         name="scatter",
-    )(recv, pick, mix, dham)
+    )(recv, where, mix, dham)
 
 
 def build_kernel(phonon_shift, phonon_weight, energies):
@@ -505,60 +594,12 @@
     padded = -(-pairs // LANES) * LANES
     held = sigma.shape[1]
 
-    far = peers >= 4
+    far = is_far(peers)
+    riding = peers == 4 and held == BS // HALF
     up = [(i, i + 1) for i in range(peers - 1)]
     down = [(i + 1, i) for i in range(peers - 1)]
-    if far:
-        from_left, from_right = z == 1, z == peers - 2
-        active = (z > 0) & (z < peers - 1)
-    else:
-        from_left = from_right = jnp.zeros((), bool)
-        active = jnp.ones((), bool)
-    limit = jnp.where(from_right, MARGIN, HALF)
-    one, inner = jnp.ones((), jnp.int32), active.astype(jnp.int32)
-
     fixed = pltpu.with_memory_space_constraint(green, pltpu.HBM)
-    acc, keep_hi, keep_lo, hi, lo = own_part(
-        fixed,
-        pltpu.with_memory_space_constraint(sigma, pltpu.HBM),
-        jnp.stack([z * held, inner]),
-    )
-    keeps = [keep_hi, keep_lo]
-    counts, listed = [1], [z * held, one]
-    rightward = leftward = sigma
-    other = near_right = near_left = None
-    for k in range(1, peers):
-        rightward = send(rightward, up[k - 1 :])
-        leftward = send(leftward, down[: peers - k])
-        if k < peers - 1:
-            rightward, leftward = gate(rightward, leftward, keeps[-1])
-        after = []
-        if far and k == 1:
-            sooner = jnp.where(z == 0, rows - MARGIN, HALF)
-            (more,) = rows_at(fixed, [sooner], [rightward, leftward])
-            other = send(more, [(0, 1), (peers - 1, peers - 2)])
-            after = [more]
-        if k == min(2, peers - 1):
-            last, leading = rows_at(fixed, [rows - HALF, 0], [rightward, leftward])
-            near_right = send(last, up[:-1] if far else up)
-            near_left = send(leading, down[1:] if far else down)
-        firsts = [jnp.maximum(z - k, 0) * held, jnp.minimum(z + k, peers - 1) * held]
-        valid = [(z >= k).astype(jnp.int32), (z + k < peers).astype(jnp.int32)]
-        acc, *more_keeps = lesser_part(
-            hi, lo, rightward, leftward, jnp.stack(firsts + valid + [inner]), acc, after
-        )
-        keeps += more_keeps
-        counts.append(2)
-        listed += [firsts[0], valid[0], firsts[1], valid[1]]
-    if other is None:
-        other = jnp.zeros_like(near_left)
-    listed += [x.astype(jnp.int32) for x in (active, from_left, from_right, limit)]
-    to_left, to_right, own = edge_part(
-        jnp.stack(listed), other, near_right, near_left, keeps, tuple(counts)
-    )
-    back_right = send(to_left, down)
-    back_left = send(to_right, up)
-    lesser = band(acc, own, back_left, back_right, energies)
+    right, left = send(sigma, up), send(sigma, down)
 
     mine = lax.dynamic_slice_in_dim(neighbours, e * group, group, axis=0)
     first = z * atoms + e * group
@@ -566,15 +607,68 @@
     column = jnp.where(offset < 0, offset + REACH, offset + REACH - 1)
     where = column + 2 * REACH * jnp.arange(group, dtype=jnp.int32)[:, None]
     where = jnp.pad(where.reshape(1, pairs), ((0, 0), (0, padded - pairs)), constant_values=-1)
-    pick = picks(where, group * LANES)
     mix = build_mix(phonon_shift, phonon_weight, energies)
     factors = lax.dynamic_slice_in_dim(
         dham.transpose(1, 2, 3, 0).reshape(3 * W * W, -1), e * pairs, pairs, axis=1
     )
     factors = jnp.pad(factors, ((0, 0), (0, padded - pairs)))
 
+
+    acc, *keeps, hi, lo = own_part(
+        fixed, pltpu.with_memory_space_constraint(sigma, pltpu.HBM), [where, mix, factors]
+    )
+    more = functools.partial(lesser_part, hi, lo, held=held)
+    places = [[(0, 0, held)], [(-1, 0, held), (1, 0, held)]]
+    if riding:
+        piece = held // 2
+        cuts = [0, piece]
+        rights, lefts = load(0, fixed, right, left, cuts, piece, [keeps[-1]])
+        rights, lefts = [send(x, up) for x in rights], [send(x, down) for x in lefts]
+        acc, *kept = more(acc, [right, left], [(-1, 0), (1, 0)])
+        keeps += kept
+        ends = []
+        for h, first in enumerate(cuts):
+            (over,), (under,) = load(
+                1, fixed, rights[h], lefts[h], [first], piece, [kept[-1]]
+            )
+            ends.append((send(over, up), send(under, down)))
+        acc, *kept = more(
+            acc, [*rights, *lefts], [(d, first) for d in (-2, 2) for first in cuts]
+        )
+        keeps += kept
+        places.append([(d, first, piece) for d in (-2, 2) for first in cuts])
+        edge = None
+        for h, first in enumerate(cuts):
+            acc, *kept = more(
+                acc, list(ends[h]), [(-3, first), (3, first)], after=[] if edge is None else [edge]
+            )
+            halos = [rights[h], lefts[h], *ends[h]]
+            edge = edge_part(halos, keeps, places, held, (h, 2), True, edge, kept[:1])
+            edge = edge[0] if h == 0 else edge
+        to_left, to_right, own = edge
+    else:
+        last, leading, *outer = rows_at(fixed, 3 if far else 2)
+        near_right = send(last, up[:-1] if far else up)
+        near_left = send(leading, down[1:] if far else down)
+        if far:
+            other = send(outer[0], [(0, 1), (peers - 1, peers - 2)])
+        else:
+            other = jnp.zeros_like(near_left)
+        for k in range(1, peers):
+            acc, *kept = more(acc, [right, left], [(-k, 0), (k, 0)])
+            keeps += kept
+            if k > 1:
+                places.append([(-k, 0, held), (k, 0, held)])
+            right, left = send(right, up[k:]), send(left, down[: peers - 1 - k])
+        to_left, to_right, own = edge_part(
+            [other, near_right, near_left], keeps, places, held, (0, 1), False, None, []
+        )
+    back_right = send(to_left, down)
+    back_left = send(to_right, up)
+    lesser = band(acc, own, back_left, back_right, energies)
+
     recv = lax.all_to_all(lesser, "energy", split_axis=0, concat_axis=0, tiled=True)
-    spread = scatter(recv, pick, mix, factors, pairs)
+    spread = scatter(recv, where, mix, factors, pairs)
     result = lax.all_to_all(spread, "energy", split_axis=0, concat_axis=0, tiled=True)
     return result.reshape(1, atoms * degree, 2 * W * W)
 

time: 123 us -> 104 us (0.85)
  local copies, waits for them, and re-layouts: 29.5 us -> 2.69 us
  blocking collectives: 12.2 us -> 25.4 us
  waiting for transfers between devices: 17.8 us -> 11.3 us
  starting transfers between devices: 35.7 us -> 37.1 us
    unnamed x66 -> x4, local copies, waits for them, and re-layouts: 28 us -> 0.87 us
    all_to_all x0 -> x1, blocking collectives: none -> 13.3 us  [per_device(): lax.all_to_all(lesser, 'energy', split_axis=0, concat_axis=0, tiled=True)]
    all_to_all x1 -> x0, waiting for transfers between devices: 9.38 us -> none  [per_device(): lax.all_to_all(lesser, 'energy', split_axis=0, concat_axis=0, tiled=True)]
    ppermute x11 -> x12, starting transfers between devices: 32 us -> 37.1 us  [send(): return lax.ppermute(x, 'orb', pairs)]
    all_to_all x1 -> x0, starting transfers between devices: 3.71 us -> none  [per_device(): lax.all_to_all(lesser, 'energy', split_axis=0, concat_axis=0, tiled=True)]
    ppermute x11 -> x12, waiting for transfers between devices: 8.42 us -> 11.3 us  [send(): return lax.ppermute(x, 'orb', pairs)]
  transfers between devices with their start and end apart: 12 -> 12, of which waited for: 6 -> 5; matrix products, arithmetic and copies ran while one was open for 2% -> 3% of each run, Pallas kernels for 18% -> 17%
where the time goes in v5:
time: 104 us; the launch traced here: 103 us
  starting transfers between devices  37.1 us (36%)
  Pallas kernels  25.4 us (24%)
  blocking collectives  25.4 us (24%)
  waiting for transfers between devices  11.3 us (11%)
  local copies, waits for them, and re-layouts  2.69 us (3%)
    ppermute x12, starting transfers between devices, send(): return lax.ppermute(x, 'orb', pairs)  37.1 us
    all_to_all x1, blocking collectives, per_device(): lax.all_to_all(lesser, 'energy', split_axis=0, concat_axis=0, tiled=True)  13.3 us
    all_to_all x1, blocking collectives, per_device(): lax.all_to_all(spread, 'energy', split_axis=0, concat_axis=0, tiled=True)  12.2 us
    ppermute x12, waiting for transfers between devices, send(): return lax.ppermute(x, 'orb', pairs)  11.3 us
    pallas_call x4, Pallas kernels, lesser_part(): pl.pallas_call(functools.partial(lesser_kernel, places, held), out_shape=...  10.9 us
    pallas_call x1, Pallas kernels, own_part(): pl.pallas_call(own_kernel, out_shape=(jax.ShapeDtypeStruct((tiles, 2 * TI...  6.11 us
    pallas_call x3, Pallas kernels, load(): pl.pallas_call(kernel, out_shape=[out] * (2 * len(first)), in_specs=[hbm]...  3.96 us
    pallas_call x1, Pallas kernels, scatter(): pl.pallas_call(scatter_kernel, out_shape=jax.ShapeDtypeStruct((energies,...  3.67 us
  transfers between devices with their start and end apart: 12, of which 5 were waited for; matrix products, arithmetic and copies ran while one was open for 3% of the time, Pallas kernels for 17%

profile of v5, /device:TPU:0, one launch (start us, length us, event | category | flops | bytes accessed | tf_op | source)
XLA Modules:
  0.0 103.3 jit_solution(3219269405035275754)
XLA Ops:
  0.0 5.1 %collective-permute-start = (f32[1,4,2,128,128]{4,3,2,1,0:T(8,128)}, f32[1,4,2,128,128]{4,3,2,1,0:T(8,128)S(1)}, u32[]{:S(2)}, u32[]{:S(2)}) collective-permute-start(f32[1,4,2,128,128]{4,3,2,1,0:T(8,128)} %sigma_ref.1), channel_id=1, source_target_pairs={{0,1},{1,2},{2,3},{4,5},{5,6},{6,7},{8,9},{9,10},{10,11},{12,13},{... | collective-permute-start | bytes 1572872 | tf_op jit(solution)/shard_map/ppermute | solution.py:582
  5.1 1.3 %collective-permute-start.1 = (f32[1,4,2,128,128]{4,3,2,1,0:T(8,128)}, f32[1,4,2,128,128]{4,3,2,1,0:T(8,128)S(1)}, u32[]{:S(2)}, u32[]{:S(2)}) collective-permute-start(f32[1,4,2,128,128]{4,3,2,1,0:T(8,128)} %sigma_ref.1), channel_id=1, source_target_pairs={{1,0},{2,1},{3,2},{5,4},{6,5},{7,6},{9,8},{10,9},{11,10},{13,12},{... | collective-permute-start | bytes 1572872 | tf_op jit(solution)/shard_map/ppermute | solution.py:582
  6.4 0.8 constant_dynamic-slice_fusion.1
  7.4 0.7 iota_add_fusion
  8.2 0.8 slice_bitcast_fusion.1
  9.4 6.1 %lesser_own.1 = (f32[4,256,256]{2,1,0:T(8,128)S(1)}, bf16[4,256,256]{2,1,0:T(8,128)(2,1)S(1)}, bf16[4,256,256]{2,1,0:T(8,128)(2,1)S(1)}, bf16[640,4096]{1,0:T(8,128)(2,1)S(1)}, bf16[640,4096]{1,0:T(8,128)(2,1)S(1)}) custom-call(f32[1,2,512,2048]{3,2,1,0:T(8,128)} %refs_0_.5, f32[1,4,2,128,128]{4,3,2,1,0:T(8,128)} %sigma_ref.1, ...), custom_call_target="tpu_custom_call" | custom-call | flops 2415919104 | bytes 8388608 | tf_op jit(solution)/shard_map/lesser_own/pallas_call | solution.py:164
  15.5 1.0 %collective-permute-done.rest_0_.refs_1_ = f32[1,4,2,128,128]{4,3,2,1,0:T(8,128)S(1)} collective-permute-done((f32[1,4,2,128,128]{4,3,2,1,0:T(8,128)}, f32[1,4,2,128,128]{4,3,2,1,0:T(8,128)S(1)}, u32[]{:S(2)}, u32[]{:S(2)}) %collective-permute-start) | collective-permute-done | bytes 524320 | tf_op jit(solution)/shard_map/ppermute | solution.py:582
  16.5 4.0 %collective-permute-done.1.rest_1_.refs_2_ = f32[1,4,2,128,128]{4,3,2,1,0:T(8,128)S(1)} collective-permute-done((f32[1,4,2,128,128]{4,3,2,1,0:T(8,128)}, f32[1,4,2,128,128]{4,3,2,1,0:T(8,128)S(1)}, u32[]{:S(2)}, u32[]{:S(2)}) %collective-permute-start.1) | collective-permute-done | bytes 524320 | tf_op jit(solution)/shard_map/ppermute | solution.py:582
  20.6 1.6 %load.3 = (f32[1,2,2,128,128]{4,3,2,1,0:T(8,128)S(1)}, f32[1,2,2,128,128]{4,3,2,1,0:T(8,128)S(1)}, f32[1,2,2,128,128]{4,3,2,1,0:T(8,128)S(1)}, f32[1,2,2,128,128]{4,3,2,1,0:T(8,128)S(1)}) custom-call(f32[1,2,512,2048]{3,2,1,0:T(8,128)} %refs_0_.5, f32[1,4,2,128,128]{4,3,2,1,0:T(8,128)S(1)} %collective-permute-done.rest_0_.refs_1_, ...), custom_call_target="tpu_custom_call" | custom-call | bytes 1048576 | tf_op jit(solution)/shard_map/load/pallas_call | solution.py:329
  22.2 2.6 %collective-permute-start.2 = (f32[1,2,2,128,128]{4,3,2,1,0:T(8,128)S(1)}, f32[1,2,2,128,128]{4,3,2,1,0:T(8,128)S(1)}, u32[]{:S(2)}, u32[]{:S(2)}) collective-permute-start(f32[1,2,2,128,128]{4,3,2,1,0:T(8,128)S(1)} %get-tuple-element.36), channel_id=1, source_target_pairs={{0,1},{1,2},{2,3},{4,5},{5,6},{6,7},{8,9},{9,10},{10,11},{12,13},{... | collective-permute-start | bytes 786440 | tf_op jit(solution)/shard_map/ppermute | solution.py:582
  24.8 1.3 %collective-permute-start.4 = (f32[1,2,2,128,128]{4,3,2,1,0:T(8,128)S(1)}, f32[1,2,2,128,128]{4,3,2,1,0:T(8,128)S(1)}, u32[]{:S(2)}, u32[]{:S(2)}) collective-permute-start(f32[1,2,2,128,128]{4,3,2,1,0:T(8,128)S(1)} %get-tuple-element.38), channel_id=1, source_target_pairs={{1,0},{2,1},{3,2},{5,4},{6,5},{7,6},{9,8},{10,9},{11,10},{13,12},{... | collective-permute-start | bytes 786440 | tf_op jit(solution)/shard_map/ppermute | solution.py:582
  26.1 4.6 %collective-permute-start.3 = (f32[1,2,2,128,128]{4,3,2,1,0:T(8,128)S(1)}, f32[1,2,2,128,128]{4,3,2,1,0:T(8,128)S(1)}, u32[]{:S(2)}, u32[]{:S(2)}) collective-permute-start(f32[1,2,2,128,128]{4,3,2,1,0:T(8,128)S(1)} %get-tuple-element.37), channel_id=1, source_target_pairs={{0,1},{1,2},{2,3},{4,5},{5,6},{6,7},{8,9},{9,10},{10,11},{12,13},{... | collective-permute-start | bytes 786440 | tf_op jit(solution)/shard_map/ppermute | solution.py:582
  30.7 1.3 %collective-permute-start.5 = (f32[1,2,2,128,128]{4,3,2,1,0:T(8,128)S(1)}, f32[1,2,2,128,128]{4,3,2,1,0:T(8,128)S(1)}, u32[]{:S(2)}, u32[]{:S(2)}) collective-permute-start(f32[1,2,2,128,128]{4,3,2,1,0:T(8,128)S(1)} %get-tuple-element.39), channel_id=1, source_target_pairs={{1,0},{2,1},{3,2},{5,4},{6,5},{7,6},{9,8},{10,9},{11,10},{13,12},{... | collective-permute-start | bytes 786440 | tf_op jit(solution)/shard_map/ppermute | solution.py:582
  32.0 3.0 %lesser_more.4 = (f32[4,256,256]{2,1,0:T(8,128)S(1)}, bf16[8,256,256]{2,1,0:T(8,128)(2,1)S(1)}, bf16[8,256,256]{2,1,0:T(8,128)(2,1)S(1)}) custom-call(bf16[640,4096]{1,0:T(8,128)(2,1)S(1)} %get-tuple-element.31.hi_ref, bf16[640,4096]{1,0:T(8,128)(2,1)S(1)} %get-tuple-element.32.lo_ref, ...), custom_call_target="tpu_custom_call", output_to_operand_aliasing={{0}: (2, {})} | custom-call | flops 3019898880 | bytes 2097152 | tf_op jit(solution)/shard_map/lesser_more/pallas_call | solution.py:212
  35.0 1.2 %load.4 = (f32[1,2,2,128,128]{4,3,2,1,0:T(8,128)S(1)}, f32[1,2,2,128,128]{4,3,2,1,0:T(8,128)S(1)}) custom-call(f32[1,2,512,2048]{3,2,1,0:T(8,128)} %refs_0_.5, f32[1,2,2,128,128]{4,3,2,1,0:T(8,128)S(1)} %collective-permute-done.2.rest_0_.refs_1_.refs_0_, f32[1,2,2,128,128]{4,3,2,1,0:T(8,128)S(1)} %collective-permute-done.4.rest_2_.refs_2_.refs_1_, ...), custom_call_target="tpu_custom_call" | custom-call | bytes 524288 | tf_op jit(solution)/shard_map/load/pallas_call | solution.py:329
  36.2 9.0 %collective-permute-start.6 = (f32[1,2,2,128,128]{4,3,2,1,0:T(8,128)S(1)}, f32[1,2,2,128,128]{4,3,2,1,0:T(8,128)S(1)}, u32[]{:S(2)}, u32[]{:S(2)}) collective-permute-start(f32[1,2,2,128,128]{4,3,2,1,0:T(8,128)S(1)} %get-tuple-element.42), channel_id=1, source_target_pairs={{0,1},{1,2},{2,3},{4,5},{5,6},{6,7},{8,9},{9,10},{10,11},{12,13},{... | collective-permute-start | bytes 786440 | tf_op jit(solution)/shard_map/ppermute | solution.py:582
  45.2 1.3 %collective-permute-start.7 = (f32[1,2,2,128,128]{4,3,2,1,0:T(8,128)S(1)}, f32[1,2,2,128,128]{4,3,2,1,0:T(8,128)S(1)}, u32[]{:S(2)}, u32[]{:S(2)}) collective-permute-start(f32[1,2,2,128,128]{4,3,2,1,0:T(8,128)S(1)} %get-tuple-element.43), channel_id=1, source_target_pairs={{1,0},{2,1},{3,2},{5,4},{6,5},{7,6},{9,8},{10,9},{11,10},{13,12},{... | collective-permute-start | bytes 786440 | tf_op jit(solution)/shard_map/ppermute | solution.py:582
  46.5 1.2 %load.5 = (f32[1,2,2,128,128]{4,3,2,1,0:T(8,128)S(1)}, f32[1,2,2,128,128]{4,3,2,1,0:T(8,128)S(1)}) custom-call(f32[1,2,512,2048]{3,2,1,0:T(8,128)} %refs_0_.5, f32[1,2,2,128,128]{4,3,2,1,0:T(8,128)S(1)} %collective-permute-done.3.rest_1_.refs_1_.refs_0_, f32[1,2,2,128,128]{4,3,2,1,0:T(8,128)S(1)} %collective-permute-done.5.rest_3_.refs_2_.refs_1_, ...), custom_call_target="tpu_custom_call" | custom-call | bytes 524288 | tf_op jit(solution)/shard_map/load/pallas_call | solution.py:329
  47.7 4.6 %collective-permute-start.8 = (f32[1,2,2,128,128]{4,3,2,1,0:T(8,128)S(1)}, f32[1,2,2,128,128]{4,3,2,1,0:T(8,128)S(1)}, u32[]{:S(2)}, u32[]{:S(2)}) collective-permute-start(f32[1,2,2,128,128]{4,3,2,1,0:T(8,128)S(1)} %get-tuple-element.45), channel_id=1, source_target_pairs={{0,1},{1,2},{2,3},{4,5},{5,6},{6,7},{8,9},{9,10},{10,11},{12,13},{... | collective-permute-start | bytes 786440 | tf_op jit(solution)/shard_map/ppermute | solution.py:582
  52.3 1.3 %collective-permute-start.9 = (f32[1,2,2,128,128]{4,3,2,1,0:T(8,128)S(1)}, f32[1,2,2,128,128]{4,3,2,1,0:T(8,128)S(1)}, u32[]{:S(2)}, u32[]{:S(2)}) collective-permute-start(f32[1,2,2,128,128]{4,3,2,1,0:T(8,128)S(1)} %get-tuple-element.46), channel_id=1, source_target_pairs={{1,0},{2,1},{3,2},{5,4},{6,5},{7,6},{9,8},{10,9},{11,10},{13,12},{... | collective-permute-start | bytes 786440 | tf_op jit(solution)/shard_map/ppermute | solution.py:582
  53.6 3.2 %lesser_more.5 = (f32[4,256,256]{2,1,0:T(8,128)S(1)}, bf16[8,256,256]{2,1,0:T(8,128)(2,1)S(1)}, bf16[8,256,256]{2,1,0:T(8,128)(2,1)S(1)}) custom-call(bf16[640,4096]{1,0:T(8,128)(2,1)S(1)} %get-tuple-element.31.hi_ref, bf16[640,4096]{1,0:T(8,128)(2,1)S(1)} %get-tuple-element.32.lo_ref, ...), custom_call_target="tpu_custom_call", output_to_operand_aliasing={{0}: (2, {})} | custom-call | flops 3019898880 | bytes 2097152 | tf_op jit(solution)/shard_map/lesser_more/pallas_call | solution.py:212
  56.8 2.4 %lesser_more.6 = (f32[4,256,256]{2,1,0:T(8,128)S(1)}, bf16[4,256,256]{2,1,0:T(8,128)(2,1)S(1)}, bf16[4,256,256]{2,1,0:T(8,128)(2,1)}) custom-call(bf16[640,4096]{1,0:T(8,128)(2,1)S(1)} %get-tuple-element.31.hi_ref, bf16[640,4096]{1,0:T(8,128)(2,1)S(1)} %get-tuple-element.32.lo_ref, ...), custom_call_target="tpu_custom_call", output_to_operand_aliasing={{0}: (2, {})} | custom-call | flops 1509949440 | bytes 2097152 | tf_op jit(solution)/shard_map/lesser_more/pallas_call | solution.py:212
  59.2 1.4 %collective-permute-done.9.rest_1_.refs_3_ = f32[1,2,2,128,128]{4,3,2,1,0:T(8,128)S(1)} collective-permute-done((f32[1,2,2,128,128]{4,3,2,1,0:T(8,128)S(1)}, f32[1,2,2,128,128]{4,3,2,1,0:T(8,128)S(1)}, u32[]{:S(2)}, u32[]{:S(2)}) %collective-permute-start.9) | collective-permute-done | bytes 262176 | tf_op jit(solution)/shard_map/ppermute | solution.py:582
  60.6 2.4 %lesser_more.7 = (f32[4,256,256]{2,1,0:T(8,128)S(1)}, bf16[4,256,256]{2,1,0:T(8,128)(2,1)S(1)}, bf16[4,256,256]{2,1,0:T(8,128)(2,1)}) custom-call(bf16[640,4096]{1,0:T(8,128)(2,1)S(1)} %get-tuple-element.31.hi_ref, bf16[640,4096]{1,0:T(8,128)(2,1)S(1)} %get-tuple-element.32.lo_ref, ...), custom_call_target="tpu_custom_call", output_to_operand_aliasing={{0}: (2, {})} | custom-call | flops 1509949440 | bytes 2097152 | tf_op jit(solution)/shard_map/lesser_more/pallas_call | solution.py:212
  63.1 3.5 %collective-permute-start.10 = (f32[2,64,128]{2,1,0:T(8,128)S(1)}, f32[2,64,128]{2,1,0:T(8,128)S(1)}, u32[]{:S(2)}, u32[]{:S(2)}) collective-permute-start(f32[2,64,128]{2,1,0:T(8,128)S(1)} %get-tuple-element.55), channel_id=1, source_target_pairs={{0,1},{1,2},{2,3},{4,5},{5,6},{6,7},{8,9},{9,10},{10,11},{12,13},{... | collective-permute-start | bytes 196616 | tf_op jit(solution)/shard_map/ppermute | solution.py:582
  66.6 1.3 %collective-permute-start.11 = (f32[2,64,128]{2,1,0:T(8,128)S(1)}, f32[2,64,128]{2,1,0:T(8,128)S(1)}, u32[]{:S(2)}, u32[]{:S(2)}) collective-permute-start(f32[2,64,128]{2,1,0:T(8,128)S(1)} %get-tuple-element.56), channel_id=1, source_target_pairs={{1,0},{2,1},{3,2},{5,4},{6,5},{7,6},{9,8},{10,9},{11,10},{13,12},{... | collective-permute-start | bytes 196616 | tf_op jit(solution)/shard_map/ppermute | solution.py:582
  67.9 0.6 collective-permute-done.10.from_left_ref
  68.5 4.3 %collective-permute-done.11.from_right_ref = f32[2,64,128]{2,1,0:T(8,128)S(1)} collective-permute-done((f32[2,64,128]{2,1,0:T(8,128)S(1)}, f32[2,64,128]{2,1,0:T(8,128)S(1)}, u32[]{:S(2)}, u32[]{:S(2)}) %collective-permute-start.11) | collective-permute-done | bytes 65568 | tf_op jit(solution)/shard_map/ppermute | solution.py:582
  73.4 13.3 %all_to_all.10.recv_ref = f32[8,2,8,8,128]{4,3,2,1,0:T(8,128)S(1)} all-to-all(f32[8,2,8,8,128]{4,3,2,1,0:T(8,128)S(1)} %band.1), channel_id=1, replica_groups=mesh['energy'=8,'orb'=4] {'energy'}, dimensions={0} | all-to-all | bytes 1048576 | tf_op jit(solution)/shard_map/all_to_all | solution.py:670
  86.7 3.7 %scatter.1 = f32[8,128,128]{2,1,0:T(8,128)S(1)} custom-call(f32[8,2,8,8,128]{4,3,2,1,0:T(8,128)S(1)} %all_to_all.10.recv_ref, s32[1,128]{1,0:T(1,128)S(1)} %reshape.79.rest_0_.where_ref, f32[128,128]{1,0:T(8,128)S(1)} %mul.67.rest_1_.mix_ref, f32[192,128]{1,0:T(8,128)S(1)} %constant_dynamic-slice_fusion.rest_2_.dham_ref), custom_call_target="tpu_custom_call" | custom-call | tf_op jit(solution)/shard_map/scatter/pallas_call | solution.py:548
  90.3 12.2 %all_to_all.11 = f32[8,128,128]{2,1,0:T(8,128)S(1)} all-to-all(f32[8,128,128]{2,1,0:T(8,128)S(1)} %scatter.1), channel_id=1, replica_groups=mesh['energy'=8,'orb'=4] {'energy'}, dimensions={0} | all-to-all | bytes 1048576 | tf_op jit(solution)/shard_map/all_to_all | solution.py:672
  102.5 0.8 copy.20
  (21 shorter events, 1.4 us)
Async XLA Ops:
  0.0 9.3 %copy-start = (f32[1024,3,8,8]{0,3,2,1:T(8,128)S(1)}, f32[1024,3,8,8]{0,3,2,1:T(8,128)}, u32[]{:S(2)}) copy-start(f32[1024,3,8,8]{0,3,2,1:T(8,128)} %param.11) | copy-start | bytes 2359300
  0.0 16.5 %collective-permute-start = (f32[1,4,2,128,128]{4,3,2,1,0:T(8,128)}, f32[1,4,2,128,128]{4,3,2,1,0:T(8,128)S(1)}, u32[]{:S(2)}, u32[]{:S(2)}) collective-permute-start(f32[1,4,2,128,128]{4,3,2,1,0:T(8,128)} %sigma_ref.1), channel_id=1, source_target_pairs={{0,1},{1,2},{2,3},{4,5},{5,6},{6,7},{8,9},{9,10},{10,11},{12,13},{... | collective-permute-start | bytes 1572872 | tf_op jit(solution)/shard_map/ppermute | solution.py:582
  5.1 15.5 %collective-permute-start.1 = (f32[1,4,2,128,128]{4,3,2,1,0:T(8,128)}, f32[1,4,2,128,128]{4,3,2,1,0:T(8,128)S(1)}, u32[]{:S(2)}, u32[]{:S(2)}) collective-permute-start(f32[1,4,2,128,128]{4,3,2,1,0:T(8,128)} %sigma_ref.1), channel_id=1, source_target_pairs={{1,0},{2,1},{3,2},{5,4},{6,5},{7,6},{9,8},{10,9},{11,10},{13,12},{... | collective-permute-start | bytes 1572872 | tf_op jit(solution)/shard_map/ppermute | solution.py:582
  22.2 12.8 %collective-permute-start.2 = (f32[1,2,2,128,128]{4,3,2,1,0:T(8,128)S(1)}, f32[1,2,2,128,128]{4,3,2,1,0:T(8,128)S(1)}, u32[]{:S(2)}, u32[]{:S(2)}) collective-permute-start(f32[1,2,2,128,128]{4,3,2,1,0:T(8,128)S(1)} %get-tuple-element.36), channel_id=1, source_target_pairs={{0,1},{1,2},{2,3},{4,5},{5,6},{6,7},{8,9},{9,10},{10,11},{12,13},{... | collective-permute-start | bytes 786440 | tf_op jit(solution)/shard_map/ppermute | solution.py:582
  24.8 10.2 %collective-permute-start.4 = (f32[1,2,2,128,128]{4,3,2,1,0:T(8,128)S(1)}, f32[1,2,2,128,128]{4,3,2,1,0:T(8,128)S(1)}, u32[]{:S(2)}, u32[]{:S(2)}) collective-permute-start(f32[1,2,2,128,128]{4,3,2,1,0:T(8,128)S(1)} %get-tuple-element.38), channel_id=1, source_target_pairs={{1,0},{2,1},{3,2},{5,4},{6,5},{7,6},{9,8},{10,9},{11,10},{13,12},{... | collective-permute-start | bytes 786440 | tf_op jit(solution)/shard_map/ppermute | solution.py:582
  26.1 20.4 %collective-permute-start.3 = (f32[1,2,2,128,128]{4,3,2,1,0:T(8,128)S(1)}, f32[1,2,2,128,128]{4,3,2,1,0:T(8,128)S(1)}, u32[]{:S(2)}, u32[]{:S(2)}) collective-permute-start(f32[1,2,2,128,128]{4,3,2,1,0:T(8,128)S(1)} %get-tuple-element.37), channel_id=1, source_target_pairs={{0,1},{1,2},{2,3},{4,5},{5,6},{6,7},{8,9},{9,10},{10,11},{12,13},{... | collective-permute-start | bytes 786440 | tf_op jit(solution)/shard_map/ppermute | solution.py:582
  30.7 15.9 %collective-permute-start.5 = (f32[1,2,2,128,128]{4,3,2,1,0:T(8,128)S(1)}, f32[1,2,2,128,128]{4,3,2,1,0:T(8,128)S(1)}, u32[]{:S(2)}, u32[]{:S(2)}) collective-permute-start(f32[1,2,2,128,128]{4,3,2,1,0:T(8,128)S(1)} %get-tuple-element.39), channel_id=1, source_target_pairs={{1,0},{2,1},{3,2},{5,4},{6,5},{7,6},{9,8},{10,9},{11,10},{13,12},{... | collective-permute-start | bytes 786440 | tf_op jit(solution)/shard_map/ppermute | solution.py:582
  36.2 20.6 %collective-permute-start.6 = (f32[1,2,2,128,128]{4,3,2,1,0:T(8,128)S(1)}, f32[1,2,2,128,128]{4,3,2,1,0:T(8,128)S(1)}, u32[]{:S(2)}, u32[]{:S(2)}) collective-permute-start(f32[1,2,2,128,128]{4,3,2,1,0:T(8,128)S(1)} %get-tuple-element.42), channel_id=1, source_target_pairs={{0,1},{1,2},{2,3},{4,5},{5,6},{6,7},{8,9},{9,10},{10,11},{12,13},{... | collective-permute-start | bytes 786440 | tf_op jit(solution)/shard_map/ppermute | solution.py:582
  45.2 11.6 %collective-permute-start.7 = (f32[1,2,2,128,128]{4,3,2,1,0:T(8,128)S(1)}, f32[1,2,2,128,128]{4,3,2,1,0:T(8,128)S(1)}, u32[]{:S(2)}, u32[]{:S(2)}) collective-permute-start(f32[1,2,2,128,128]{4,3,2,1,0:T(8,128)S(1)} %get-tuple-element.43), channel_id=1, source_target_pairs={{1,0},{2,1},{3,2},{5,4},{6,5},{7,6},{9,8},{10,9},{11,10},{13,12},{... | collective-permute-start | bytes 786440 | tf_op jit(solution)/shard_map/ppermute | solution.py:582
  47.7 11.5 %collective-permute-start.8 = (f32[1,2,2,128,128]{4,3,2,1,0:T(8,128)S(1)}, f32[1,2,2,128,128]{4,3,2,1,0:T(8,128)S(1)}, u32[]{:S(2)}, u32[]{:S(2)}) collective-permute-start(f32[1,2,2,128,128]{4,3,2,1,0:T(8,128)S(1)} %get-tuple-element.45), channel_id=1, source_target_pairs={{0,1},{1,2},{2,3},{4,5},{5,6},{6,7},{8,9},{9,10},{10,11},{12,13},{... | collective-permute-start | bytes 786440 | tf_op jit(solution)/shard_map/ppermute | solution.py:582
  52.3 8.3 %collective-permute-start.9 = (f32[1,2,2,128,128]{4,3,2,1,0:T(8,128)S(1)}, f32[1,2,2,128,128]{4,3,2,1,0:T(8,128)S(1)}, u32[]{:S(2)}, u32[]{:S(2)}) collective-permute-start(f32[1,2,2,128,128]{4,3,2,1,0:T(8,128)S(1)} %get-tuple-element.46), channel_id=1, source_target_pairs={{1,0},{2,1},{3,2},{5,4},{6,5},{7,6},{9,8},{10,9},{11,10},{13,12},{... | collective-permute-start | bytes 786440 | tf_op jit(solution)/shard_map/ppermute | solution.py:582
  63.1 5.4 %collective-permute-start.10 = (f32[2,64,128]{2,1,0:T(8,128)S(1)}, f32[2,64,128]{2,1,0:T(8,128)S(1)}, u32[]{:S(2)}, u32[]{:S(2)}) collective-permute-start(f32[2,64,128]{2,1,0:T(8,128)S(1)} %get-tuple-element.55), channel_id=1, source_target_pairs={{0,1},{1,2},{2,3},{4,5},{5,6},{6,7},{8,9},{9,10},{10,11},{12,13},{... | collective-permute-start | bytes 196616 | tf_op jit(solution)/shard_map/ppermute | solution.py:582
  66.6 6.2 %collective-permute-start.11 = (f32[2,64,128]{2,1,0:T(8,128)S(1)}, f32[2,64,128]{2,1,0:T(8,128)S(1)}, u32[]{:S(2)}, u32[]{:S(2)}) collective-permute-start(f32[2,64,128]{2,1,0:T(8,128)S(1)} %get-tuple-element.56), channel_id=1, source_target_pairs={{1,0},{2,1},{3,2},{5,4},{6,5},{7,6},{9,8},{10,9},{11,10},{13,12},{... | collective-permute-start | bytes 196616 | tf_op jit(solution)/shard_map/ppermute | solution.py:582

commit v6 on v5

--- a/solution.py
+++ b/solution.py
@@ -192,13 +192,13 @@
     acc_ref, *keeps = rest[-3:]
     acc_ref[...] = before_ref[...]
     slot = 0
-    for (distance, first), self_ref in zip(places, sigmas):
+    for distance, self_ref in zip(places, sigmas):
         number, valid = neighbour(distance)
 
         @pl.when(valid)
         def _():
             shard_loop(
-                number * held + first, self_ref, hi_ref, lo_ref, acc_ref, keeps, slot, is_inner()
+                number * held, self_ref, hi_ref, lo_ref, acc_ref, keeps, slot, is_inner()
             )
 
         slot += self_ref.shape[1]
@@ -256,135 +256,50 @@
     )(green)
 
 
-def load_kernel(cases, first, piece, green_ref, right_ref, left_ref, *rest):
-    outs, sem = rest[-1 - 2 * len(first) : -1], rest[-1]
-    per = BS // HALF
-    for side, ((rows, begin), source) in enumerate(zip(cases, (right_ref, left_ref))):
-        row = pl.multiple_of(begin, HALF)
-        taken, passed = [], []
-        for n, block in enumerate(first):
-            out = outs[side * len(first) + n]
-            passed.append(
-                pltpu.make_async_copy(
-                    source.at[:, pl.ds(block - first[0], piece)], out, sem.at[side, n]
-                )
-            )
-            for m in range(piece):
-                for part in range(2):
-                    for q in range(per):
-                        col = ((block + m) * per + q) * BS
-                        taken.append(
-                            pltpu.make_async_copy(
-                                green_ref.at[0, part, pl.ds(row, HALF), pl.ds(col, BS)],
-                                out.at[0, m, part, pl.ds(q * HALF, HALF), :],
-                                sem.at[side, len(taken)],
-                            )
-                        )
-        for want, copies in ((True, taken), (False, passed)):
-
-            @pl.when(rows == want)
-            def _():
-                for copy in copies:
-                    copy.start()
-
-    for side, ((rows, begin), source) in enumerate(zip(cases, (right_ref, left_ref))):
-        row = pl.multiple_of(begin, HALF)
-        for want in (True, False):
-
-            @pl.when(rows == want)
-            def _():
-                count = 0
-                for n, block in enumerate(first):
-                    out = outs[side * len(first) + n]
-                    if not want:
-                        pltpu.make_async_copy(
-                            source.at[:, pl.ds(block - first[0], piece)], out, sem.at[side, n]
-                        ).wait()
-                        continue
-                    for m in range(piece):
-                        for part in range(2):
-                            for q in range(per):
-                                col = ((block + m) * per + q) * BS
-                                pltpu.make_async_copy(
-                                    green_ref.at[0, part, pl.ds(row, HALF), pl.ds(col, BS)],
-                                    out.at[0, m, part, pl.ds(q * HALF, HALF), :],
-                                    sem.at[side, count],
-                                ).wait()
-                                count += 1
-
-
-def load(stage, green, right, left, first, piece, after):
-    rows = green.shape[2]
-
-    def kernel(*refs):
-        z, peers = lax.axis_index("orb"), lax.axis_size("orb")
-        if stage == 0:
-            cases = ((z == 0, rows - MARGIN), (z == peers - 1, HALF))
-        else:
-            cases = ((z < peers - 2, rows - HALF), (z > 1, 0))
-        load_kernel(cases, first, piece, *refs)
-
+def gate_kernel(*refs):
+    del refs
+
+
+def gate(right, left, after):
     hbm = pl.BlockSpec(memory_space=pl.ANY)
-    out = jax.ShapeDtypeStruct((1, piece) + right.shape[2:], F32)
-    outs = pl.pallas_call(
-        kernel,
-        out_shape=[out] * (2 * len(first)),
-        in_specs=[hbm] * (3 + len(after)),
-        out_specs=[hbm] * (2 * len(first)),
-        scratch_shapes=[
-            pltpu.SemaphoreType.DMA((2, len(first) * piece * 2 * (BS // HALF)))
-        ],
-        compiler_params=pltpu.CompilerParams(vmem_limit_bytes=2 << 20),
-        cost_estimate=pl.CostEstimate(
-            flops=0, bytes_accessed=8 * out.size * len(first), transcendentals=0
-        ),
-        name="load",
-    )(green, right, left, *after)
-    return outs[: len(first)], outs[len(first) :]
-
-
-def edge_kernel(places, held, part_of, riding, last, *refs):
-    halos, refs = refs[: 4 if riding else 3], refs[4 if riding else 3 :]
-    keeps, refs = refs[: 2 * len(places)], refs[2 * len(places) :]
+    return pl.pallas_call(
+        gate_kernel,
+        out_shape=[jax.ShapeDtypeStruct(x.shape, x.dtype) for x in (right, left)],
+        in_specs=[hbm] * 3,
+        out_specs=[hbm] * 2,
+        input_output_aliases={0: 0, 1: 1},
+        compiler_params=pltpu.CompilerParams(vmem_limit_bytes=1 << 20),
+        cost_estimate=pl.CostEstimate(flops=0, bytes_accessed=0, transcendentals=0),
+        name="gate",
+    )(right, left, after)
+
+
+def edge_kernel(places, held, a_ref, b_ref, c_ref, *refs):
+    keeps = refs[: 2 * len(places)]
+    left_ref, right_ref, own_ref, acc_ref = refs[2 * len(places) :]
     z, peers = lax.axis_index("orb"), lax.axis_size("orb")
     if is_far(peers):
         from_left, from_right = z == 1, z == peers - 2
     else:
         from_left = from_right = z < 0
     limit = jnp.where(from_right, MARGIN, HALF)
-    if part_of[0] > 0:
-        before_ref, refs = refs[0], refs[1:]
-    acc_ref = refs[-1]
-    acc_ref[...] = before_ref[...] if part_of[0] > 0 else jnp.zeros_like(acc_ref)
-    group = peers // part_of[1]
-    begin = part_of[0] * group
-
-    def halo_rows(ref, part, number, s):
-        if riding:
-            return ref[0, number - begin, part, s * HALF : (s + 1) * HALF, :]
-        col = pl.multiple_of((number * held + s) * BS, BS)
-        return ref[part, :, pl.ds(col, BS)]
-
-    def add(number, first, hi, lo, at, count):
+    acc_ref[...] = jnp.zeros_like(acc_ref)
+
+    def add(number, hi, lo, at):
+        cols = pl.ds(pl.multiple_of(number * held * BS, BS), held * BS)
         for side in range(2):
             fields = []
             for part in range(2):
-                inner, outer = [], []
-                for s in range(first, first + count):
-                    if riding:
-                        near, beyond = halos[2 + side], halos[side]
-                    else:
-                        near, beyond = halos[1 + side], halos[0]
-                    inner.append(halo_rows(near, part, number, s))
-                    outer.append(halo_rows(beyond, part, number, s))
-                inner, outer = jnp.concatenate(inner, axis=1), jnp.concatenate(outer, axis=1)
-                outer = jnp.where(from_left if side == 0 else from_right, outer, 0.0)
+                outer = jnp.where(
+                    from_left if side == 0 else from_right, a_ref[part, :, cols], 0.0
+                )
+                inner = (b_ref if side == 0 else c_ref)[part, :, cols]
                 rows = [outer, inner] if side == 0 else [inner, outer]
                 fields.append(halves(jnp.concatenate(rows, axis=0)))
             halo = []
             for real, imag in zip(*fields):
                 lanes = []
-                for s in range(count):
+                for s in range(held):
                     one = slice(s * BS, (s + 1) * BS)
                     lanes += [
                         jnp.concatenate([real[:, one], -imag[:, one]], axis=0),
@@ -393,7 +308,7 @@
                 halo.append(jnp.concatenate(lanes, axis=1))
             rows = slice(side * TILE, (side + 1) * TILE)
             kept = [
-                jnp.concatenate([ref[at + s, rows, :] for s in range(count)], axis=1)
+                jnp.concatenate([ref[at + s, rows, :] for s in range(held)], axis=1)
                 for ref in (hi, lo)
             ]
             acc_ref[side] = acc_ref[side] + dot3(halo, kept, NT)
@@ -401,20 +316,13 @@
     @pl.when(is_inner())
     def _():
         for k, shards in enumerate(places):
-            at = 0
-            for distance, first, count in shards:
+            for n, distance in enumerate(shards):
                 number, valid = neighbour(distance)
-                valid = valid & (number >= begin) & (number < begin + group)
 
                 @pl.when(valid)
                 def _():
-                    add(number, first, keeps[2 * k], keeps[2 * k + 1], at, count)
-
-                at += count
-
-    if not last:
-        return
-    left_ref, right_ref, own_ref = refs[-4:-1]
+                    add(number, keeps[2 * k], keeps[2 * k + 1], n * held)
+
     lane = lax.broadcasted_iota(jnp.int32, (MARGIN, LANES), 1)
     row = lax.broadcasted_iota(jnp.int32, (MARGIN, LANES), 0)
     low = lane < MARGIN
@@ -431,27 +339,21 @@
     own_ref[1, 1] = jnp.where(mine, turned_right, 0.0)
 
 
-def edge_part(halos, keeps, places, held, part_of, riding, before, after):
+def edge_part(halos, keeps, places, held):
     vmem = pl.BlockSpec(memory_space=pltpu.VMEM)
-    last = part_of[0] == part_of[1] - 1
     side = jax.ShapeDtypeStruct((2, MARGIN, LANES), F32)
-    acc = (2, TILE, TILE)
-    ends = [side, side, jax.ShapeDtypeStruct((2, 2, MARGIN, LANES), F32)]
-    args = [*halos, *keeps] + ([] if before is None else [before])
-    return pl.pallas_call(
-        functools.partial(edge_kernel, places, held, part_of, riding, last),
-        out_shape=ends if last else [jax.ShapeDtypeStruct(acc, F32)],
-        in_specs=[vmem] * len(args) + [pl.BlockSpec(memory_space=pl.ANY)] * len(after),
-        out_specs=[vmem] * (3 if last else 1),
-        scratch_shapes=[pltpu.VMEM(acc, F32)] if last else [],
+    return pl.pallas_call(
+        functools.partial(edge_kernel, places, held),
+        out_shape=(side, side, jax.ShapeDtypeStruct((2, 2, MARGIN, LANES), F32)),
+        in_specs=[vmem] * (len(halos) + len(keeps)),
+        out_specs=(vmem, vmem, vmem),
+        scratch_shapes=[pltpu.VMEM((2, TILE, TILE), F32)],
         compiler_params=pltpu.CompilerParams(vmem_limit_bytes=20 << 20),
         cost_estimate=pl.CostEstimate(
-            flops=(1 << 31) // part_of[1],
-            bytes_accessed=(8 << 20) // part_of[1],
-            transcendentals=0,
+            flops=1 << 31, bytes_accessed=8 << 20, transcendentals=0
         ),
         name="edges",
-    )(*args, *after)
+    )(*halos, *keeps)
 
 
 def band_kernel(acc_ref, own_ref, from_left_ref, from_right_ref, out_ref, rows_ref):
@@ -595,11 +497,17 @@
     held = sigma.shape[1]
 
     far = is_far(peers)
-    riding = peers == 4 and held == BS // HALF
     up = [(i, i + 1) for i in range(peers - 1)]
     down = [(i + 1, i) for i in range(peers - 1)]
     fixed = pltpu.with_memory_space_constraint(green, pltpu.HBM)
     right, left = send(sigma, up), send(sigma, down)
+    last, leading, *outer = rows_at(fixed, 3 if far else 2)
+    near_right = send(last, up[:-1] if far else up)
+    near_left = send(leading, down[1:] if far else down)
+    if far:
+        other = send(outer[0], [(0, 1), (peers - 1, peers - 2)])
+    else:
+        other = jnp.zeros_like(near_left)
 
     mine = lax.dynamic_slice_in_dim(neighbours, e * group, group, axis=0)
     first = z * atoms + e * group
@@ -615,56 +523,31 @@
 
 
     acc, *keeps, hi, lo = own_part(
-        fixed, pltpu.with_memory_space_constraint(sigma, pltpu.HBM), [where, mix, factors]
+        fixed, pltpu.with_memory_space_constraint(sigma, pltpu.HBM), [where, mix, factors, last]
     )
-    more = functools.partial(lesser_part, hi, lo, held=held)
-    places = [[(0, 0, held)], [(-1, 0, held), (1, 0, held)]]
-    if riding:
-        piece = held // 2
-        cuts = [0, piece]
-        rights, lefts = load(0, fixed, right, left, cuts, piece, [keeps[-1]])
-        rights, lefts = [send(x, up) for x in rights], [send(x, down) for x in lefts]
-        acc, *kept = more(acc, [right, left], [(-1, 0), (1, 0)])
+    places = [[0]]
+    for k in range(1, peers):
+        if k < peers - 1:
+            right, left = gate(right, left, keeps[-1])
+            following = send(right, up[k:]), send(left, down[: peers - 1 - k])
+            after = []
+        else:
+            if not far:
+                acc, *kept = lesser_part(hi, lo, acc, [right, left], [-k, k], held)
+                keeps += kept
+                places.append([-k, k])
+            to_left, to_right, own = edge_part(
+                [other, near_right, near_left], keeps, places, held
+            )
+            back_right, back_left = send(to_left, down), send(to_right, up)
+            after = [to_left]
+            if not far:
+                break
+        acc, *kept = lesser_part(hi, lo, acc, [right, left], [-k, k], held, after)
         keeps += kept
-        ends = []
-        for h, first in enumerate(cuts):
-            (over,), (under,) = load(
-                1, fixed, rights[h], lefts[h], [first], piece, [kept[-1]]
-            )
-            ends.append((send(over, up), send(under, down)))
-        acc, *kept = more(
-            acc, [*rights, *lefts], [(d, first) for d in (-2, 2) for first in cuts]
-        )
-        keeps += kept
-        places.append([(d, first, piece) for d in (-2, 2) for first in cuts])
-        edge = None
-        for h, first in enumerate(cuts):
-            acc, *kept = more(
-                acc, list(ends[h]), [(-3, first), (3, first)], after=[] if edge is None else [edge]
-            )
-            halos = [rights[h], lefts[h], *ends[h]]
-            edge = edge_part(halos, keeps, places, held, (h, 2), True, edge, kept[:1])
-            edge = edge[0] if h == 0 else edge
-        to_left, to_right, own = edge
-    else:
-        last, leading, *outer = rows_at(fixed, 3 if far else 2)
-        near_right = send(last, up[:-1] if far else up)
-        near_left = send(leading, down[1:] if far else down)
-        if far:
-            other = send(outer[0], [(0, 1), (peers - 1, peers - 2)])
-        else:
-            other = jnp.zeros_like(near_left)
-        for k in range(1, peers):
-            acc, *kept = more(acc, [right, left], [(-k, 0), (k, 0)])
-            keeps += kept
-            if k > 1:
-                places.append([(-k, 0, held), (k, 0, held)])
-            right, left = send(right, up[k:]), send(left, down[: peers - 1 - k])
-        to_left, to_right, own = edge_part(
-            [other, near_right, near_left], keeps, places, held, (0, 1), False, None, []
-        )
-    back_right = send(to_left, down)
-    back_left = send(to_right, up)
+        places.append([-k, k])
+        if k < peers - 1:
+            right, left = following
     lesser = band(acc, own, back_left, back_right, energies)
 
     recv = lax.all_to_all(lesser, "energy", split_axis=0, concat_axis=0, tiled=True)

time: 104 us -> 94.8 us (0.912)
  starting transfers between devices: 37.1 us -> 30.5 us
  Pallas kernels: 25.4 us -> 22.4 us
    ppermute x12 -> x11, starting transfers between devices: 37.1 us -> 30.5 us  [send(): return lax.ppermute(x, 'orb', pairs)]
    pallas_call x5 -> x4, Pallas kernels: 4.14 us -> 1.56 us  [the longest x1 1.39 us: rows_at(): pl.pallas_call(functools.partial(rows_kernel, count), out_shape=[out] * c...]
    ppermute x12 -> x11, waiting for transfers between devices: 11.3 us -> 11.9 us  [send(): return lax.ppermute(x, 'orb', pairs)]
    pallas_call x4 -> x3, Pallas kernels: 10.9 us -> 10.5 us  [lesser_part(): pl.pallas_call(functools.partial(lesser_kernel, places, held), out_shape=...]
  transfers between devices with their start and end apart: 12 -> 11, of which waited for: 5 -> 3; matrix products, arithmetic and copies ran while one was open for 3% -> 3% of each run, Pallas kernels for 17% -> 19%
where the time goes in v6:
time: 94.8 us; the launch traced here: 94.3 us
  starting transfers between devices  30.5 us (32%)
  blocking collectives  25.4 us (27%)
  Pallas kernels  22.4 us (24%)
  waiting for transfers between devices  11.9 us (13%)
  local copies, waits for them, and re-layouts  2.69 us (3%)
  other arithmetic  1.02 us (1%)
    ppermute x11, starting transfers between devices, send(): return lax.ppermute(x, 'orb', pairs)  30.5 us
    all_to_all x1, blocking collectives, per_device(): lax.all_to_all(lesser, 'energy', split_axis=0, concat_axis=0, tiled=True)  13.3 us
    all_to_all x1, blocking collectives, per_device(): lax.all_to_all(spread, 'energy', split_axis=0, concat_axis=0, tiled=True)  12.2 us
    ppermute x11, waiting for transfers between devices, send(): return lax.ppermute(x, 'orb', pairs)  11.9 us
    pallas_call x3, Pallas kernels, lesser_part(): pl.pallas_call(functools.partial(lesser_kernel, places, held), out_shape=...  10.5 us
    pallas_call x1, Pallas kernels, own_part(): pl.pallas_call(own_kernel, out_shape=(jax.ShapeDtypeStruct((tiles, 2 * TI...  6.12 us
    pallas_call x1, Pallas kernels, scatter(): pl.pallas_call(scatter_kernel, out_shape=jax.ShapeDtypeStruct((energies,...  3.65 us
  transfers between devices with their start and end apart: 11, of which 3 were waited for; matrix products, arithmetic and copies ran while one was open for 3% of the time, Pallas kernels for 19%

profile of v6, /device:TPU:0, one launch (start us, length us, event | category | flops | bytes accessed | tf_op | source)
XLA Modules:
  0.0 94.3 jit_solution(10164306039512606186)
XLA Ops:
  0.0 5.1 %collective-permute-start = (f32[1,4,2,128,128]{4,3,2,1,0:T(8,128)}, f32[1,4,2,128,128]{4,3,2,1,0:T(8,128)S(1)}, u32[]{:S(2)}, u32[]{:S(2)}) collective-permute-start(f32[1,4,2,128,128]{4,3,2,1,0:T(8,128)} %sigma_ref.1), channel_id=1, source_target_pairs={{0,1},{1,2},{2,3},{4,5},{5,6},{6,7},{8,9},{9,10},{10,11},{12,13},{... | collective-permute-start | bytes 1572872 | tf_op jit(solution)/shard_map/ppermute | solution.py:484
  5.1 1.3 %collective-permute-start.1 = (f32[1,4,2,128,128]{4,3,2,1,0:T(8,128)}, f32[1,4,2,128,128]{4,3,2,1,0:T(8,128)S(1)}, u32[]{:S(2)}, u32[]{:S(2)}) collective-permute-start(f32[1,4,2,128,128]{4,3,2,1,0:T(8,128)} %sigma_ref.1), channel_id=1, source_target_pairs={{1,0},{2,1},{3,2},{5,4},{6,5},{7,6},{9,8},{10,9},{11,10},{13,12},{... | collective-permute-start | bytes 1572872 | tf_op jit(solution)/shard_map/ppermute | solution.py:484
  6.4 0.8 constant_dynamic-slice_fusion.1
  7.3 0.1 reshape.79.rest_0_.where_ref
  7.4 0.7 iota_add_fusion
  8.2 0.8 slice_bitcast_fusion.1
  8.9 0.1 add_reduce_fusion
  9.0 0.1 broadcast_multiply_fusion
  9.1 0.2 mul.67.rest_1_.mix_ref
  9.3 1.4 %rows.1 = (f32[2,32,2048]{2,1,0:T(8,128)S(1)}, f32[2,32,2048]{2,1,0:T(8,128)S(1)}, f32[2,32,2048]{2,1,0:T(8,128)S(1)}) custom-call(f32[1,2,512,2048]{3,2,1,0:T(8,128)} %green_ref.3), custom_call_target="tpu_custom_call" | custom-call | tf_op jit(solution)/shard_map/rows/pallas_call | solution.py:248
  10.8 6.1 %lesser_own.1 = (f32[4,256,256]{2,1,0:T(8,128)S(1)}, bf16[4,256,256]{2,1,0:T(8,128)(2,1)S(1)}, bf16[4,256,256]{2,1,0:T(8,128)(2,1)S(1)}, bf16[640,4096]{1,0:T(8,128)(2,1)S(1)}, bf16[640,4096]{1,0:T(8,128)(2,1)S(1)}) custom-call(f32[1,2,512,2048]{3,2,1,0:T(8,128)} %green_ref.3, f32[1,4,2,128,128]{4,3,2,1,0:T(8,128)} %sigma_ref.1, ...), custom_call_target="tpu_custom_call" | custom-call | flops 2415919104 | bytes 8388608 | tf_op jit(solution)/shard_map/lesser_own/pallas_call | solution.py:164
  16.9 3.7 %collective-permute-done.1.refs_1_ = f32[1,4,2,128,128]{4,3,2,1,0:T(8,128)S(1)} collective-permute-done((f32[1,4,2,128,128]{4,3,2,1,0:T(8,128)}, f32[1,4,2,128,128]{4,3,2,1,0:T(8,128)S(1)}, u32[]{:S(2)}, u32[]{:S(2)}) %collective-permute-start.1) | collective-permute-done | bytes 524320 | tf_op jit(solution)/shard_map/ppermute | solution.py:484
  20.6 0.7 collective-permute-start.2
  21.3 1.3 %collective-permute-start.3 = (f32[1,4,2,128,128]{4,3,2,1,0:T(8,128)S(1)}, f32[1,4,2,128,128]{4,3,2,1,0:T(8,128)S(1)}, u32[]{:S(2)}, u32[]{:S(2)}) collective-permute-start(f32[1,4,2,128,128]{4,3,2,1,0:T(8,128)S(1)} %get-tuple-element.33.rest_1_), channel_id=1, source_target_pairs={{1,0},{2,1},{5,4},{6,5},{9,8},{10,9},{13,12},{14,13},{17,16},{18,1... | collective-permute-start | bytes 1572872 | tf_op jit(solution)/shard_map/ppermute | solution.py:484
  22.6 6.9 %collective-permute-start.7 = (f32[2,32,2048]{2,1,0:T(8,128)S(1)}, f32[2,32,2048]{2,1,0:T(8,128)S(1)}, u32[]{:S(2)}, u32[]{:S(2)}) collective-permute-start(f32[2,32,2048]{2,1,0:T(8,128)S(1)} %get-tuple-element.27.rest_3_), channel_id=1, source_target_pairs={{0,1},{1,2},{4,5},{5,6},{8,9},{9,10},{12,13},{13,14},{16,17},{17,1... | collective-permute-start | bytes 1572872 | tf_op jit(solution)/shard_map/ppermute | solution.py:484
  29.5 4.0 %collective-permute-start.6 = (f32[2,32,2048]{2,1,0:T(8,128)S(1)}, f32[2,32,2048]{2,1,0:T(8,128)S(1)}, u32[]{:S(2)}, u32[]{:S(2)}) collective-permute-start(f32[2,32,2048]{2,1,0:T(8,128)S(1)} %get-tuple-element.39), channel_id=1, source_target_pairs={{0,1},{3,2},{4,5},{7,6},{8,9},{11,10},{12,13},{15,14},{16,17},{19,... | collective-permute-start | bytes 1572872 | tf_op jit(solution)/shard_map/ppermute | solution.py:484
  33.5 0.7 collective-permute-start.8
  34.2 3.0 %lesser_more.3 = (f32[4,256,256]{2,1,0:T(8,128)S(1)}, bf16[8,256,256]{2,1,0:T(8,128)(2,1)S(1)}, bf16[8,256,256]{2,1,0:T(8,128)(2,1)S(1)}) custom-call(bf16[640,4096]{1,0:T(8,128)(2,1)S(1)} %get-tuple-element.28.hi_ref, bf16[640,4096]{1,0:T(8,128)(2,1)S(1)} %get-tuple-element.29.lo_ref, ...), custom_call_target="tpu_custom_call", output_to_operand_aliasing={{0}: (2, {})} | custom-call | flops 3019898880 | bytes 2097152 | tf_op jit(solution)/shard_map/lesser_more/pallas_call | solution.py:212
  37.2 0.8 collective-permute-done.3.refs_1_
  38.0 0.7 collective-permute-start.4
  38.7 1.3 %collective-permute-start.5 = (f32[1,4,2,128,128]{4,3,2,1,0:T(8,128)S(1)}, f32[1,4,2,128,128]{4,3,2,1,0:T(8,128)S(1)}, u32[]{:S(2)}, u32[]{:S(2)}) collective-permute-start(f32[1,4,2,128,128]{4,3,2,1,0:T(8,128)S(1)} %get-tuple-element.37.rest_1_), channel_id=1, source_target_pairs={{1,0},{5,4},{9,8},{13,12},{17,16},{21,20},{25,24},{29,28}} | collective-permute-start | bytes 1572872 | tf_op jit(solution)/shard_map/ppermute | solution.py:484
  40.0 3.0 %lesser_more.4 = (f32[4,256,256]{2,1,0:T(8,128)S(1)}, bf16[8,256,256]{2,1,0:T(8,128)(2,1)S(1)}, bf16[8,256,256]{2,1,0:T(8,128)(2,1)S(1)}) custom-call(bf16[640,4096]{1,0:T(8,128)(2,1)S(1)} %get-tuple-element.28.hi_ref, bf16[640,4096]{1,0:T(8,128)(2,1)S(1)} %get-tuple-element.29.lo_ref, ...), custom_call_target="tpu_custom_call", output_to_operand_aliasing={{0}: (2, {})} | custom-call | flops 3019898880 | bytes 2097152 | tf_op jit(solution)/shard_map/lesser_more/pallas_call | solution.py:212
  43.0 7.4 %collective-permute-done.6.a_ref = f32[2,32,2048]{2,1,0:T(8,128)S(1)} collective-permute-done((f32[2,32,2048]{2,1,0:T(8,128)S(1)}, f32[2,32,2048]{2,1,0:T(8,128)S(1)}, u32[]{:S(2)}, u32[]{:S(2)}) %collective-permute-start.6) | collective-permute-done | bytes 524320 | tf_op jit(solution)/shard_map/ppermute | solution.py:484
  50.4 0.2 edges.1
  50.6 1.3 %collective-permute-start.10 = (f32[2,64,128]{2,1,0:T(8,128)S(1)}, f32[2,64,128]{2,1,0:T(8,128)S(1)}, u32[]{:S(2)}, u32[]{:S(2)}) collective-permute-start(f32[2,64,128]{2,1,0:T(8,128)S(1)} %get-tuple-element.45.rest_2_), channel_id=1, source_target_pairs={{1,0},{2,1},{3,2},{5,4},{6,5},{7,6},{9,8},{10,9},{11,10},{13,12},{... | collective-permute-start | bytes 196616 | tf_op jit(solution)/shard_map/ppermute | solution.py:484
  51.9 7.4 %collective-permute-start.9 = (f32[2,64,128]{2,1,0:T(8,128)S(1)}, f32[2,64,128]{2,1,0:T(8,128)S(1)}, u32[]{:S(2)}, u32[]{:S(2)}) collective-permute-start(f32[2,64,128]{2,1,0:T(8,128)S(1)} %get-tuple-element.48), channel_id=1, source_target_pairs={{0,1},{1,2},{2,3},{4,5},{5,6},{6,7},{8,9},{9,10},{10,11},{12,13},{... | collective-permute-start | bytes 196616 | tf_op jit(solution)/shard_map/ppermute | solution.py:484
  59.3 4.5 %lesser_more.5 = (f32[4,256,256]{2,1,0:T(8,128)S(1)}, bf16[8,256,256]{2,1,0:T(8,128)(2,1)}, bf16[8,256,256]{2,1,0:T(8,128)(2,1)}) custom-call(bf16[640,4096]{1,0:T(8,128)(2,1)S(1)} %get-tuple-element.28.hi_ref, bf16[640,4096]{1,0:T(8,128)(2,1)S(1)} %get-tuple-element.29.lo_ref, ...), custom_call_target="tpu_custom_call", output_to_operand_aliasing={{0}: (2, {})} | custom-call | flops 3019898880 | bytes 2097152 | tf_op jit(solution)/shard_map/lesser_more/pallas_call | solution.py:212
  63.8 0.6 band.1
  64.4 13.3 %all_to_all.10.recv_ref = f32[8,2,8,8,128]{4,3,2,1,0:T(8,128)S(1)} all-to-all(f32[8,2,8,8,128]{4,3,2,1,0:T(8,128)S(1)} %band.1), channel_id=1, replica_groups=mesh['energy'=8,'orb'=4] {'energy'}, dimensions={0} | all-to-all | bytes 1048576 | tf_op jit(solution)/shard_map/all_to_all | solution.py:553
  77.7 3.7 %scatter.1 = f32[8,128,128]{2,1,0:T(8,128)S(1)} custom-call(f32[8,2,8,8,128]{4,3,2,1,0:T(8,128)S(1)} %all_to_all.10.recv_ref, s32[1,128]{1,0:T(1,128)S(1)} %reshape.79.rest_0_.where_ref, f32[128,128]{1,0:T(8,128)S(1)} %mul.67.rest_1_.mix_ref, f32[192,128]{1,0:T(8,128)S(1)} %constant_dynamic-slice_fusion.rest_2_.dham_ref), custom_call_target="tpu_custom_call" | custom-call | tf_op jit(solution)/shard_map/scatter/pallas_call | solution.py:450
  81.3 12.2 %all_to_all.11 = f32[8,128,128]{2,1,0:T(8,128)S(1)} all-to-all(f32[8,128,128]{2,1,0:T(8,128)S(1)} %scatter.1), channel_id=1, replica_groups=mesh['energy'=8,'orb'=4] {'energy'}, dimensions={0} | all-to-all | bytes 1048576 | tf_op jit(solution)/shard_map/all_to_all | solution.py:555
  93.5 0.8 copy.26
  (17 shorter events, 0.2 us)
Async XLA Ops:
  0.0 10.7 %copy-start = (f32[1024,3,8,8]{0,3,2,1:T(8,128)S(1)}, f32[1024,3,8,8]{0,3,2,1:T(8,128)}, u32[]{:S(2)}) copy-start(f32[1024,3,8,8]{0,3,2,1:T(8,128)} %param.11) | copy-start | bytes 2359300
  0.0 16.9 %collective-permute-start = (f32[1,4,2,128,128]{4,3,2,1,0:T(8,128)}, f32[1,4,2,128,128]{4,3,2,1,0:T(8,128)S(1)}, u32[]{:S(2)}, u32[]{:S(2)}) collective-permute-start(f32[1,4,2,128,128]{4,3,2,1,0:T(8,128)} %sigma_ref.1), channel_id=1, source_target_pairs={{0,1},{1,2},{2,3},{4,5},{5,6},{6,7},{8,9},{9,10},{10,11},{12,13},{... | collective-permute-start | bytes 1572872 | tf_op jit(solution)/shard_map/ppermute | solution.py:484
  5.1 15.5 %collective-permute-start.1 = (f32[1,4,2,128,128]{4,3,2,1,0:T(8,128)}, f32[1,4,2,128,128]{4,3,2,1,0:T(8,128)S(1)}, u32[]{:S(2)}, u32[]{:S(2)}) collective-permute-start(f32[1,4,2,128,128]{4,3,2,1,0:T(8,128)} %sigma_ref.1), channel_id=1, source_target_pairs={{1,0},{2,1},{3,2},{5,4},{6,5},{7,6},{9,8},{10,9},{11,10},{13,12},{... | collective-permute-start | bytes 1572872 | tf_op jit(solution)/shard_map/ppermute | solution.py:484
  20.6 16.6 %collective-permute-start.2 = (f32[1,4,2,128,128]{4,3,2,1,0:T(8,128)S(1)}, f32[1,4,2,128,128]{4,3,2,1,0:T(8,128)S(1)}, u32[]{:S(2)}, u32[]{:S(2)}) collective-permute-start(f32[1,4,2,128,128]{4,3,2,1,0:T(8,128)S(1)} %get-tuple-element.32.rest_0_), channel_id=1, source_target_pairs={{1,2},{2,3},{5,6},{6,7},{9,10},{10,11},{13,14},{14,15},{17,18},{18... | collective-permute-start | bytes 1572872 | tf_op jit(solution)/shard_map/ppermute | solution.py:484
  21.3 16.7 %collective-permute-start.3 = (f32[1,4,2,128,128]{4,3,2,1,0:T(8,128)S(1)}, f32[1,4,2,128,128]{4,3,2,1,0:T(8,128)S(1)}, u32[]{:S(2)}, u32[]{:S(2)}) collective-permute-start(f32[1,4,2,128,128]{4,3,2,1,0:T(8,128)S(1)} %get-tuple-element.33.rest_1_), channel_id=1, source_target_pairs={{1,0},{2,1},{5,4},{6,5},{9,8},{10,9},{13,12},{14,13},{17,16},{18,1... | collective-permute-start | bytes 1572872 | tf_op jit(solution)/shard_map/ppermute | solution.py:484
  22.6 20.4 %collective-permute-start.7 = (f32[2,32,2048]{2,1,0:T(8,128)S(1)}, f32[2,32,2048]{2,1,0:T(8,128)S(1)}, u32[]{:S(2)}, u32[]{:S(2)}) collective-permute-start(f32[2,32,2048]{2,1,0:T(8,128)S(1)} %get-tuple-element.27.rest_3_), channel_id=1, source_target_pairs={{0,1},{1,2},{4,5},{5,6},{8,9},{9,10},{12,13},{13,14},{16,17},{17,1... | collective-permute-start | bytes 1572872 | tf_op jit(solution)/shard_map/ppermute | solution.py:484
  29.5 20.9 %collective-permute-start.6 = (f32[2,32,2048]{2,1,0:T(8,128)S(1)}, f32[2,32,2048]{2,1,0:T(8,128)S(1)}, u32[]{:S(2)}, u32[]{:S(2)}) collective-permute-start(f32[2,32,2048]{2,1,0:T(8,128)S(1)} %get-tuple-element.39), channel_id=1, source_target_pairs={{0,1},{3,2},{4,5},{7,6},{8,9},{11,10},{12,13},{15,14},{16,17},{19,... | collective-permute-start | bytes 1572872 | tf_op jit(solution)/shard_map/ppermute | solution.py:484
  33.5 16.9 %collective-permute-start.8 = (f32[2,32,2048]{2,1,0:T(8,128)S(1)}, f32[2,32,2048]{2,1,0:T(8,128)S(1)}, u32[]{:S(2)}, u32[]{:S(2)}) collective-permute-start(f32[2,32,2048]{2,1,0:T(8,128)S(1)} %get-tuple-element.40), channel_id=1, source_target_pairs={{2,1},{3,2},{6,5},{7,6},{10,9},{11,10},{14,13},{15,14},{18,17},{19... | collective-permute-start | bytes 1572872 | tf_op jit(solution)/shard_map/ppermute | solution.py:484
  38.0 21.3 %collective-permute-start.4 = (f32[1,4,2,128,128]{4,3,2,1,0:T(8,128)S(1)}, f32[1,4,2,128,128]{4,3,2,1,0:T(8,128)S(1)}, u32[]{:S(2)}, u32[]{:S(2)}) collective-permute-start(f32[1,4,2,128,128]{4,3,2,1,0:T(8,128)S(1)} %get-tuple-element.36.rest_0_), channel_id=1, source_target_pairs={{2,3},{6,7},{10,11},{14,15},{18,19},{22,23},{26,27},{30,31}} | collective-permute-start | bytes 1572872 | tf_op jit(solution)/shard_map/ppermute | solution.py:484
  38.7 20.6 %collective-permute-start.5 = (f32[1,4,2,128,128]{4,3,2,1,0:T(8,128)S(1)}, f32[1,4,2,128,128]{4,3,2,1,0:T(8,128)S(1)}, u32[]{:S(2)}, u32[]{:S(2)}) collective-permute-start(f32[1,4,2,128,128]{4,3,2,1,0:T(8,128)S(1)} %get-tuple-element.37.rest_1_), channel_id=1, source_target_pairs={{1,0},{5,4},{9,8},{13,12},{17,16},{21,20},{25,24},{29,28}} | collective-permute-start | bytes 1572872 | tf_op jit(solution)/shard_map/ppermute | solution.py:484
  50.6 13.2 %collective-permute-start.10 = (f32[2,64,128]{2,1,0:T(8,128)S(1)}, f32[2,64,128]{2,1,0:T(8,128)S(1)}, u32[]{:S(2)}, u32[]{:S(2)}) collective-permute-start(f32[2,64,128]{2,1,0:T(8,128)S(1)} %get-tuple-element.45.rest_2_), channel_id=1, source_target_pairs={{1,0},{2,1},{3,2},{5,4},{6,5},{7,6},{9,8},{10,9},{11,10},{13,12},{... | collective-permute-start | bytes 196616 | tf_op jit(solution)/shard_map/ppermute | solution.py:484
  51.9 11.9 %collective-permute-start.9 = (f32[2,64,128]{2,1,0:T(8,128)S(1)}, f32[2,64,128]{2,1,0:T(8,128)S(1)}, u32[]{:S(2)}, u32[]{:S(2)}) collective-permute-start(f32[2,64,128]{2,1,0:T(8,128)S(1)} %get-tuple-element.48), channel_id=1, source_target_pairs={{0,1},{1,2},{2,3},{4,5},{5,6},{6,7},{8,9},{9,10},{10,11},{12,13},{... | collective-permute-start | bytes 196616 | tf_op jit(solution)/shard_map/ppermute | solution.py:484

commit v7 on v6

--- a/solution.py
+++ b/solution.py
@@ -67,6 +67,9 @@
         near = pl.ds(t * TILE, TILE + 2 * MARGIN)
         acc_ref[t] = acc_ref[t] + dot3(both, (hi_ref[near, cols], lo_ref[near, cols]), NT)
 
+    if not edges:
+        return
+
     @pl.when(active)
     def _():
         for n, weight in enumerate(split):
@@ -179,17 +182,18 @@
         ],
         compiler_params=pltpu.CompilerParams(vmem_limit_bytes=40 << 20),
         cost_estimate=pl.CostEstimate(
-            flops=held * 6 * rows * 2 * BS * (2 * BS + 4 * TILE),
-            bytes_accessed=blocks * rows * BS * 8,
+            flops=held * rows * BS * BS,
+            bytes_accessed=blocks * rows * BS,
             transcendentals=0,
         ),
         name="lesser_own",
     )(green, sigma, *after)
 
 
-def lesser_kernel(places, held, hi_ref, lo_ref, before_ref, *rest):
+def lesser_kernel(places, held, extra, hi_ref, lo_ref, before_ref, *rest):
     sigmas, rest = rest[: len(places)], rest[len(places) :]
-    acc_ref, *keeps = rest[-3:]
+    rest = rest[extra:]
+    acc_ref, keeps = rest[0], rest[1:]
     acc_ref[...] = before_ref[...]
     slot = 0
     for distance, self_ref in zip(places, sigmas):
@@ -204,31 +208,32 @@
         slot += self_ref.shape[1]
 
 
-def lesser_part(hi, lo, before, shards, places, held, after=()):
+def lesser_part(hi, lo, before, shards, places, held, after=(), keep=True):
     vmem = pl.BlockSpec(memory_space=pltpu.VMEM)
     count = sum(x.shape[1] for x in shards)
     kept = jax.ShapeDtypeStruct((count, 4 * MARGIN, 2 * BS), BF16)
-    outs = [jax.ShapeDtypeStruct(before.shape, F32), kept, kept]
-    return pl.pallas_call(
-        functools.partial(lesser_kernel, places, held),
+    outs = [jax.ShapeDtypeStruct(before.shape, F32)] + ([kept, kept] if keep else [])
+    return pl.pallas_call(
+        functools.partial(lesser_kernel, places, held, len(after)),
         out_shape=outs,
         in_specs=[vmem] * (3 + len(shards)) + [pl.BlockSpec(memory_space=pl.ANY)] * len(after),
         out_specs=[vmem] * len(outs),
         input_output_aliases={2: 0},
         compiler_params=pltpu.CompilerParams(vmem_limit_bytes=26 << 20),
         cost_estimate=pl.CostEstimate(
-            flops=count * 3 * hi.shape[0] * 2 * BS * (2 * BS + 4 * TILE),
-            bytes_accessed=8 * before.size,
+            flops=count * hi.shape[0] * BS * BS,
+            bytes_accessed=before.size,
             transcendentals=0,
         ),
         name="lesser_more",
     )(hi, lo, before, *shards, *after)
 
 
-def rows_kernel(count, green_ref, *rest):
+def rows_kernel(near, green_ref, *rest):
+    count = 2 if near else 1
     outs, sem = rest[-1 - count : -1], rest[-1]
     z, rows = lax.axis_index("orb"), green_ref.shape[2]
-    starts = [rows - HALF, 0, jnp.where(z == 0, rows - MARGIN, HALF)]
+    starts = [rows - HALF, 0] if near else [jnp.where(z == 0, rows - MARGIN, HALF)]
     copies = [
         pltpu.make_async_copy(
             green_ref.at[0, :, pl.ds(pl.multiple_of(starts[n], HALF), HALF), :],
@@ -243,35 +248,36 @@
         copy.wait()
 
 
-def rows_at(green, count):
+def rows_at(green, near, after=()):
+    count = 2 if near else 1
     out = jax.ShapeDtypeStruct((2, HALF, green.shape[3]), F32)
     return pl.pallas_call(
-        functools.partial(rows_kernel, count),
+        functools.partial(rows_kernel, near),
         out_shape=[out] * count,
-        in_specs=[pl.BlockSpec(memory_space=pl.ANY)],
+        in_specs=[pl.BlockSpec(memory_space=pl.ANY)] * (1 + len(after)),
         out_specs=[pl.BlockSpec(memory_space=pltpu.VMEM)] * count,
         scratch_shapes=[pltpu.SemaphoreType.DMA((count,))],
         compiler_params=pltpu.CompilerParams(vmem_limit_bytes=8 << 20),
         name="rows",
-    )(green)
+    )(green, *after)
 
 
 def gate_kernel(*refs):
     del refs
 
 
-def gate(right, left, after):
+def gate(right, left, *after):
     hbm = pl.BlockSpec(memory_space=pl.ANY)
     return pl.pallas_call(
         gate_kernel,
         out_shape=[jax.ShapeDtypeStruct(x.shape, x.dtype) for x in (right, left)],
-        in_specs=[hbm] * 3,
+        in_specs=[hbm] * (2 + len(after)),
         out_specs=[hbm] * 2,
         input_output_aliases={0: 0, 1: 1},
         compiler_params=pltpu.CompilerParams(vmem_limit_bytes=1 << 20),
         cost_estimate=pl.CostEstimate(flops=0, bytes_accessed=0, transcendentals=0),
         name="gate",
-    )(right, left, after)
+    )(right, left, *after)
 
 
 def edge_kernel(places, held, a_ref, b_ref, c_ref, *refs):
@@ -501,14 +507,9 @@
     down = [(i + 1, i) for i in range(peers - 1)]
     fixed = pltpu.with_memory_space_constraint(green, pltpu.HBM)
     right, left = send(sigma, up), send(sigma, down)
-    last, leading, *outer = rows_at(fixed, 3 if far else 2)
+    last, leading = rows_at(fixed, True)
     near_right = send(last, up[:-1] if far else up)
     near_left = send(leading, down[1:] if far else down)
-    if far:
-        other = send(outer[0], [(0, 1), (peers - 1, peers - 2)])
-    else:
-        other = jnp.zeros_like(near_left)
-
     mine = lax.dynamic_slice_in_dim(neighbours, e * group, group, axis=0)
     first = z * atoms + e * group
     offset = mine - (first + jnp.arange(group, dtype=jnp.int32))[:, None]
@@ -526,9 +527,14 @@
         fixed, pltpu.with_memory_space_constraint(sigma, pltpu.HBM), [where, mix, factors, last]
     )
     places = [[0]]
+    if far:
+        (outer,) = rows_at(fixed, False, [keeps[-1]])
+        other = send(outer, [(0, 1), (peers - 1, peers - 2)])
+    else:
+        outer = other = jnp.zeros_like(near_left)
     for k in range(1, peers):
         if k < peers - 1:
-            right, left = gate(right, left, keeps[-1])
+            right, left = gate(right, left, keeps[-1], outer if k == 1 else other)
             following = send(right, up[k:]), send(left, down[: peers - 1 - k])
             after = []
         else:
@@ -539,11 +545,12 @@
             to_left, to_right, own = edge_part(
                 [other, near_right, near_left], keeps, places, held
             )
-            back_right, back_left = send(to_left, down), send(to_right, up)
+            back_right = send(to_left, down[:-1] if far else down)
+            back_left = send(to_right, up[1:] if far else up)
             after = [to_left]
             if not far:
                 break
-        acc, *kept = lesser_part(hi, lo, acc, [right, left], [-k, k], held, after)
+        acc, *kept = lesser_part(hi, lo, acc, [right, left], [-k, k], held, after, k < peers - 1)
         keeps += kept
         places.append([-k, k])
         if k < peers - 1:

time: 94.8 us -> 91 us (0.960)
  the two profiles are of different devices: /device:TPU:0 before, /device:TPU:16 now
where the time goes in v7:
time: 91 us; the launch traced here: 90.5 us
  Pallas kernels  27.5 us (30%)
  starting transfers between devices  27.3 us (30%)
  blocking collectives  25.4 us (28%)
  waiting for transfers between devices  6.19 us (7%)
  local copies, waits for them, and re-layouts  2.69 us (3%)
  other arithmetic  1.02 us (1%)
    ppermute x11, starting transfers between devices, send(): return lax.ppermute(x, 'orb', pairs)  27.3 us
    all_to_all x1, blocking collectives, per_device(): lax.all_to_all(lesser, 'energy', split_axis=0, concat_axis=0, tiled=True)  13.3 us
    all_to_all x1, blocking collectives, per_device(): lax.all_to_all(spread, 'energy', split_axis=0, concat_axis=0, tiled=True)  12.2 us
    pallas_call x3, Pallas kernels, lesser_part(): pl.pallas_call(functools.partial(lesser_kernel, places, held, len(after))...  11.6 us
    pallas_call x1, Pallas kernels, own_part(): pl.pallas_call(own_kernel, out_shape=(jax.ShapeDtypeStruct((tiles, 2 * TI...  6.91 us
    ppermute x11, waiting for transfers between devices, send(): return lax.ppermute(x, 'orb', pairs)  6.19 us
    pallas_call x1, Pallas kernels, scatter(): pl.pallas_call(scatter_kernel, out_shape=jax.ShapeDtypeStruct((energies,...  3.65 us
    pallas_call x1, Pallas kernels, edge_part(): pl.pallas_call(functools.partial(edge_kernel, places, held), out_shape=(s...  2.5 us
  transfers between devices with their start and end apart: 11, of which 3 were waited for; matrix products, arithmetic and copies ran while one was open for 3% of the time, Pallas kernels for 26%

profile of v7, /device:TPU:16, one launch (start us, length us, event | category | flops | bytes accessed | tf_op | source)
XLA Modules:
  0.0 90.5 jit_solution(4592493147743622842)
XLA Ops:
  0.0 3.6 %collective-permute-start = (f32[1,4,2,128,128]{4,3,2,1,0:T(8,128)}, f32[1,4,2,128,128]{4,3,2,1,0:T(8,128)S(1)}, u32[]{:S(2)}, u32[]{:S(2)}) collective-permute-start(f32[1,4,2,128,128]{4,3,2,1,0:T(8,128)} %sigma_ref.1), channel_id=1, source_target_pairs={{0,1},{1,2},{2,3},{4,5},{5,6},{6,7},{8,9},{9,10},{10,11},{12,13},{... | collective-permute-start | bytes 1572872 | tf_op jit(solution)/shard_map/ppermute | solution.py:490
  3.6 2.4 %collective-permute-start.1 = (f32[1,4,2,128,128]{4,3,2,1,0:T(8,128)}, f32[1,4,2,128,128]{4,3,2,1,0:T(8,128)S(1)}, u32[]{:S(2)}, u32[]{:S(2)}) collective-permute-start(f32[1,4,2,128,128]{4,3,2,1,0:T(8,128)} %sigma_ref.1), channel_id=1, source_target_pairs={{1,0},{2,1},{3,2},{5,4},{6,5},{7,6},{9,8},{10,9},{11,10},{13,12},{... | collective-permute-start | bytes 1572872 | tf_op jit(solution)/shard_map/ppermute | solution.py:490
  6.0 0.8 constant_dynamic-slice_fusion.1
  6.8 0.7 iota_add_fusion
  7.6 0.8 slice_bitcast_fusion.1
  8.5 0.1 add_reduce_fusion
  8.6 0.1 broadcast_multiply_fusion
  8.7 0.2 mul.67.rest_1_.mix_ref
  8.9 1.2 %rows.2 = (f32[2,32,2048]{2,1,0:T(8,128)S(1)}, f32[2,32,2048]{2,1,0:T(8,128)S(1)}) custom-call(f32[1,2,512,2048]{3,2,1,0:T(8,128)} %green_ref.5), custom_call_target="tpu_custom_call" | custom-call | tf_op jit(solution)/shard_map/rows/pallas_call | solution.py:254
  10.2 6.9 %lesser_own.1 = (f32[4,256,256]{2,1,0:T(8,128)S(1)}, bf16[4,256,256]{2,1,0:T(8,128)(2,1)S(1)}, bf16[4,256,256]{2,1,0:T(8,128)(2,1)S(1)}, bf16[640,4096]{1,0:T(8,128)(2,1)S(1)}, bf16[640,4096]{1,0:T(8,128)(2,1)S(1)}) custom-call(f32[1,2,512,2048]{3,2,1,0:T(8,128)} %green_ref.5, f32[1,4,2,128,128]{4,3,2,1,0:T(8,128)} %sigma_ref.1, ...), custom_call_target="tpu_custom_call" | custom-call | flops 33554432 | bytes 1048576 | tf_op jit(solution)/shard_map/lesser_own/pallas_call | solution.py:167
  17.1 1.1 %rows.3.refs_3_ = f32[2,32,2048]{2,1,0:T(8,128)S(1)} custom-call(f32[1,2,512,2048]{3,2,1,0:T(8,128)} %green_ref.5, bf16[4,256,256]{2,1,0:T(8,128)(2,1)S(1)} %get-tuple-element.29.rest_0_.refs_2_.refs_1_), custom_call_target="tpu_custom_call" | custom-call | tf_op jit(solution)/shard_map/rows/pallas_call | solution.py:254
  18.2 1.3 %collective-permute-start.4 = (f32[2,32,2048]{2,1,0:T(8,128)S(1)}, f32[2,32,2048]{2,1,0:T(8,128)S(1)}, u32[]{:S(2)}, u32[]{:S(2)}) collective-permute-start(f32[2,32,2048]{2,1,0:T(8,128)S(1)} %rows.3.refs_3_), channel_id=1, source_target_pairs={{0,1},{3,2},{4,5},{7,6},{8,9},{11,10},{12,13},{15,14},{16,17},{19,... | collective-permute-start | bytes 1572872 | tf_op jit(solution)/shard_map/ppermute | solution.py:490
  19.5 4.6 %collective-permute-start.2 = (f32[1,4,2,128,128]{4,3,2,1,0:T(8,128)S(1)}, f32[1,4,2,128,128]{4,3,2,1,0:T(8,128)S(1)}, u32[]{:S(2)}, u32[]{:S(2)}) collective-permute-start(f32[1,4,2,128,128]{4,3,2,1,0:T(8,128)S(1)} %get-tuple-element.30.rest_0_), channel_id=1, source_target_pairs={{1,2},{2,3},{5,6},{6,7},{9,10},{10,11},{13,14},{14,15},{17,18},{18... | collective-permute-start | bytes 1572872 | tf_op jit(solution)/shard_map/ppermute | solution.py:490
  24.1 1.3 %collective-permute-start.3 = (f32[1,4,2,128,128]{4,3,2,1,0:T(8,128)S(1)}, f32[1,4,2,128,128]{4,3,2,1,0:T(8,128)S(1)}, u32[]{:S(2)}, u32[]{:S(2)}) collective-permute-start(f32[1,4,2,128,128]{4,3,2,1,0:T(8,128)S(1)} %get-tuple-element.31.rest_1_), channel_id=1, source_target_pairs={{1,0},{2,1},{5,4},{6,5},{9,8},{10,9},{13,12},{14,13},{17,16},{18,1... | collective-permute-start | bytes 1572872 | tf_op jit(solution)/shard_map/ppermute | solution.py:490
  25.4 1.3 %collective-permute-start.7 = (f32[2,32,2048]{2,1,0:T(8,128)S(1)}, f32[2,32,2048]{2,1,0:T(8,128)S(1)}, u32[]{:S(2)}, u32[]{:S(2)}) collective-permute-start(f32[2,32,2048]{2,1,0:T(8,128)S(1)} %get-tuple-element.25.rest_3_), channel_id=1, source_target_pairs={{0,1},{1,2},{4,5},{5,6},{8,9},{9,10},{12,13},{13,14},{16,17},{17,1... | collective-permute-start | bytes 1572872 | tf_op jit(solution)/shard_map/ppermute | solution.py:490
  26.7 4.6 %collective-permute-start.8 = (f32[2,32,2048]{2,1,0:T(8,128)S(1)}, f32[2,32,2048]{2,1,0:T(8,128)S(1)}, u32[]{:S(2)}, u32[]{:S(2)}) collective-permute-start(f32[2,32,2048]{2,1,0:T(8,128)S(1)} %get-tuple-element.37), channel_id=1, source_target_pairs={{2,1},{3,2},{6,5},{7,6},{10,9},{11,10},{14,13},{15,14},{18,17},{19... | collective-permute-start | bytes 1572872 | tf_op jit(solution)/shard_map/ppermute | solution.py:490
  31.3 7.5 %lesser_more.3 = (f32[4,256,256]{2,1,0:T(8,128)S(1)}, bf16[8,256,256]{2,1,0:T(8,128)(2,1)S(1)}, bf16[8,256,256]{2,1,0:T(8,128)(2,1)S(1)}) custom-call(bf16[640,4096]{1,0:T(8,128)(2,1)S(1)} %get-tuple-element.26.hi_ref, bf16[640,4096]{1,0:T(8,128)(2,1)S(1)} %get-tuple-element.27.lo_ref, ...), custom_call_target="tpu_custom_call", output_to_operand_aliasing={{0}: (2, {})} | custom-call | flops 83886080 | bytes 262144 | tf_op jit(solution)/shard_map/lesser_more/pallas_call | solution.py:216
  38.8 1.3 %collective-permute-start.5 = (f32[1,4,2,128,128]{4,3,2,1,0:T(8,128)S(1)}, f32[1,4,2,128,128]{4,3,2,1,0:T(8,128)S(1)}, u32[]{:S(2)}, u32[]{:S(2)}) collective-permute-start(f32[1,4,2,128,128]{4,3,2,1,0:T(8,128)S(1)} %get-tuple-element.34.rest_0_), channel_id=1, source_target_pairs={{2,3},{6,7},{10,11},{14,15},{18,19},{22,23},{26,27},{30,31}} | collective-permute-start | bytes 1572872 | tf_op jit(solution)/shard_map/ppermute | solution.py:490
  40.1 0.7 collective-permute-start.6
  40.8 3.8 %lesser_more.4 = (f32[4,256,256]{2,1,0:T(8,128)S(1)}, bf16[8,256,256]{2,1,0:T(8,128)(2,1)S(1)}, bf16[8,256,256]{2,1,0:T(8,128)(2,1)S(1)}) custom-call(bf16[640,4096]{1,0:T(8,128)(2,1)S(1)} %get-tuple-element.26.hi_ref, bf16[640,4096]{1,0:T(8,128)(2,1)S(1)} %get-tuple-element.27.lo_ref, ...), custom_call_target="tpu_custom_call", output_to_operand_aliasing={{0}: (2, {})} | custom-call | flops 83886080 | bytes 262144 | tf_op jit(solution)/shard_map/lesser_more/pallas_call | solution.py:216
  44.6 1.1 %collective-permute-done.7.b_ref = f32[2,32,2048]{2,1,0:T(8,128)S(1)} collective-permute-done((f32[2,32,2048]{2,1,0:T(8,128)S(1)}, f32[2,32,2048]{2,1,0:T(8,128)S(1)}, u32[]{:S(2)}, u32[]{:S(2)}) %collective-permute-start.7) | collective-permute-done | bytes 524320 | tf_op jit(solution)/shard_map/ppermute | solution.py:490
  45.7 1.2 %collective-permute-done.8.c_ref = f32[2,32,2048]{2,1,0:T(8,128)S(1)} collective-permute-done((f32[2,32,2048]{2,1,0:T(8,128)S(1)}, f32[2,32,2048]{2,1,0:T(8,128)S(1)}, u32[]{:S(2)}, u32[]{:S(2)}) %collective-permute-start.8) | collective-permute-done | bytes 524320 | tf_op jit(solution)/shard_map/ppermute | solution.py:490
  46.9 2.5 %edges.1 = (f32[2,64,128]{2,1,0:T(8,128)S(1)}, f32[2,64,128]{2,1,0:T(8,128)S(1)}, f32[2,2,64,128]{3,2,1,0:T(8,128)S(1)}) custom-call(f32[2,32,2048]{2,1,0:T(8,128)S(1)} %collective-permute-done.4.refs_3_.a_ref, f32[2,32,2048]{2,1,0:T(8,128)S(1)} %collective-permute-done.7.b_ref, f32[2,32,2048]{2,1,0:T(8,128)S(1)} %collective-permute-done.8.c_ref, ...), custom_call_target="tpu_custom_call" | custom-call | flops 2147483648 | bytes 8388608 | tf_op jit(solution)/shard_map/edges/pallas_call | solution.py:351
  49.4 4.4 %collective-permute-start.10 = (f32[2,64,128]{2,1,0:T(8,128)S(1)}, f32[2,64,128]{2,1,0:T(8,128)S(1)}, u32[]{:S(2)}, u32[]{:S(2)}) collective-permute-start(f32[2,64,128]{2,1,0:T(8,128)S(1)} %get-tuple-element.42.rest_2_), channel_id=1, source_target_pairs={{1,0},{2,1},{5,4},{6,5},{9,8},{10,9},{13,12},{14,13},{17,16},{18,1... | collective-permute-start | bytes 196616 | tf_op jit(solution)/shard_map/ppermute | solution.py:490
  53.8 1.9 %collective-permute-start.9 = (f32[2,64,128]{2,1,0:T(8,128)S(1)}, f32[2,64,128]{2,1,0:T(8,128)S(1)}, u32[]{:S(2)}, u32[]{:S(2)}) collective-permute-start(f32[2,64,128]{2,1,0:T(8,128)S(1)} %get-tuple-element.44), channel_id=1, source_target_pairs={{1,2},{2,3},{5,6},{6,7},{9,10},{10,11},{13,14},{14,15},{17,18},{18... | collective-permute-start | bytes 196616 | tf_op jit(solution)/shard_map/ppermute | solution.py:490
  55.8 0.3 lesser_more.5.acc_ref
  56.1 3.9 %collective-permute-done.9.from_left_ref = f32[2,64,128]{2,1,0:T(8,128)S(1)} collective-permute-done((f32[2,64,128]{2,1,0:T(8,128)S(1)}, f32[2,64,128]{2,1,0:T(8,128)S(1)}, u32[]{:S(2)}, u32[]{:S(2)}) %collective-permute-start.9) | collective-permute-done | bytes 65568 | tf_op jit(solution)/shard_map/ppermute | solution.py:490
  60.0 0.6 band.1
  60.6 13.3 %all_to_all.10.recv_ref = f32[8,2,8,8,128]{4,3,2,1,0:T(8,128)S(1)} all-to-all(f32[8,2,8,8,128]{4,3,2,1,0:T(8,128)S(1)} %band.1), channel_id=1, replica_groups=mesh['energy'=8,'orb'=4] {'energy'}, dimensions={0} | all-to-all | bytes 1048576 | tf_op jit(solution)/shard_map/all_to_all | solution.py:560
  73.9 3.7 %scatter.1 = f32[8,128,128]{2,1,0:T(8,128)S(1)} custom-call(f32[8,2,8,8,128]{4,3,2,1,0:T(8,128)S(1)} %all_to_all.10.recv_ref, s32[1,128]{1,0:T(1,128)S(1)} %reshape.79.rest_0_.where_ref, f32[128,128]{1,0:T(8,128)S(1)} %mul.67.rest_1_.mix_ref, f32[192,128]{1,0:T(8,128)S(1)} %constant_dynamic-slice_fusion.rest_2_.dham_ref), custom_call_target="tpu_custom_call" | custom-call | tf_op jit(solution)/shard_map/scatter/pallas_call | solution.py:456
  77.5 12.2 %all_to_all.11 = f32[8,128,128]{2,1,0:T(8,128)S(1)} all-to-all(f32[8,128,128]{2,1,0:T(8,128)S(1)} %scatter.1), channel_id=1, replica_groups=mesh['energy'=8,'orb'=4] {'energy'}, dimensions={0} | all-to-all | bytes 1048576 | tf_op jit(solution)/shard_map/all_to_all | solution.py:562
  89.7 0.8 copy.26
  (18 shorter events, 0.3 us)
Async XLA Ops:
  0.0 10.1 %copy-start = (f32[1024,3,8,8]{0,3,2,1:T(8,128)S(1)}, f32[1024,3,8,8]{0,3,2,1:T(8,128)}, u32[]{:S(2)}) copy-start(f32[1024,3,8,8]{0,3,2,1:T(8,128)} %param.11) | copy-start | bytes 2359300
  0.0 19.5 %collective-permute-start = (f32[1,4,2,128,128]{4,3,2,1,0:T(8,128)}, f32[1,4,2,128,128]{4,3,2,1,0:T(8,128)S(1)}, u32[]{:S(2)}, u32[]{:S(2)}) collective-permute-start(f32[1,4,2,128,128]{4,3,2,1,0:T(8,128)} %sigma_ref.1), channel_id=1, source_target_pairs={{0,1},{1,2},{2,3},{4,5},{5,6},{6,7},{8,9},{9,10},{10,11},{12,13},{... | collective-permute-start | bytes 1572872 | tf_op jit(solution)/shard_map/ppermute | solution.py:490
  3.6 15.9 %collective-permute-start.1 = (f32[1,4,2,128,128]{4,3,2,1,0:T(8,128)}, f32[1,4,2,128,128]{4,3,2,1,0:T(8,128)S(1)}, u32[]{:S(2)}, u32[]{:S(2)}) collective-permute-start(f32[1,4,2,128,128]{4,3,2,1,0:T(8,128)} %sigma_ref.1), channel_id=1, source_target_pairs={{1,0},{2,1},{3,2},{5,4},{6,5},{7,6},{9,8},{10,9},{11,10},{13,12},{... | collective-permute-start | bytes 1572872 | tf_op jit(solution)/shard_map/ppermute | solution.py:490
  18.2 20.6 %collective-permute-start.4 = (f32[2,32,2048]{2,1,0:T(8,128)S(1)}, f32[2,32,2048]{2,1,0:T(8,128)S(1)}, u32[]{:S(2)}, u32[]{:S(2)}) collective-permute-start(f32[2,32,2048]{2,1,0:T(8,128)S(1)} %rows.3.refs_3_), channel_id=1, source_target_pairs={{0,1},{3,2},{4,5},{7,6},{8,9},{11,10},{12,13},{15,14},{16,17},{19,... | collective-permute-start | bytes 1572872 | tf_op jit(solution)/shard_map/ppermute | solution.py:490
  19.5 19.2 %collective-permute-start.2 = (f32[1,4,2,128,128]{4,3,2,1,0:T(8,128)S(1)}, f32[1,4,2,128,128]{4,3,2,1,0:T(8,128)S(1)}, u32[]{:S(2)}, u32[]{:S(2)}) collective-permute-start(f32[1,4,2,128,128]{4,3,2,1,0:T(8,128)S(1)} %get-tuple-element.30.rest_0_), channel_id=1, source_target_pairs={{1,2},{2,3},{5,6},{6,7},{9,10},{10,11},{13,14},{14,15},{17,18},{18... | collective-permute-start | bytes 1572872 | tf_op jit(solution)/shard_map/ppermute | solution.py:490
  24.1 14.7 %collective-permute-start.3 = (f32[1,4,2,128,128]{4,3,2,1,0:T(8,128)S(1)}, f32[1,4,2,128,128]{4,3,2,1,0:T(8,128)S(1)}, u32[]{:S(2)}, u32[]{:S(2)}) collective-permute-start(f32[1,4,2,128,128]{4,3,2,1,0:T(8,128)S(1)} %get-tuple-element.31.rest_1_), channel_id=1, source_target_pairs={{1,0},{2,1},{5,4},{6,5},{9,8},{10,9},{13,12},{14,13},{17,16},{18,1... | collective-permute-start | bytes 1572872 | tf_op jit(solution)/shard_map/ppermute | solution.py:490
  25.4 20.3 %collective-permute-start.7 = (f32[2,32,2048]{2,1,0:T(8,128)S(1)}, f32[2,32,2048]{2,1,0:T(8,128)S(1)}, u32[]{:S(2)}, u32[]{:S(2)}) collective-permute-start(f32[2,32,2048]{2,1,0:T(8,128)S(1)} %get-tuple-element.25.rest_3_), channel_id=1, source_target_pairs={{0,1},{1,2},{4,5},{5,6},{8,9},{9,10},{12,13},{13,14},{16,17},{17,1... | collective-permute-start | bytes 1572872 | tf_op jit(solution)/shard_map/ppermute | solution.py:490
  26.7 20.2 %collective-permute-start.8 = (f32[2,32,2048]{2,1,0:T(8,128)S(1)}, f32[2,32,2048]{2,1,0:T(8,128)S(1)}, u32[]{:S(2)}, u32[]{:S(2)}) collective-permute-start(f32[2,32,2048]{2,1,0:T(8,128)S(1)} %get-tuple-element.37), channel_id=1, source_target_pairs={{2,1},{3,2},{6,5},{7,6},{10,9},{11,10},{14,13},{15,14},{18,17},{19... | collective-permute-start | bytes 1572872 | tf_op jit(solution)/shard_map/ppermute | solution.py:490
  38.8 17.0 %collective-permute-start.5 = (f32[1,4,2,128,128]{4,3,2,1,0:T(8,128)S(1)}, f32[1,4,2,128,128]{4,3,2,1,0:T(8,128)S(1)}, u32[]{:S(2)}, u32[]{:S(2)}) collective-permute-start(f32[1,4,2,128,128]{4,3,2,1,0:T(8,128)S(1)} %get-tuple-element.34.rest_0_), channel_id=1, source_target_pairs={{2,3},{6,7},{10,11},{14,15},{18,19},{22,23},{26,27},{30,31}} | collective-permute-start | bytes 1572872 | tf_op jit(solution)/shard_map/ppermute | solution.py:490
  40.1 15.7 %collective-permute-start.6 = (f32[1,4,2,128,128]{4,3,2,1,0:T(8,128)S(1)}, f32[1,4,2,128,128]{4,3,2,1,0:T(8,128)S(1)}, u32[]{:S(2)}, u32[]{:S(2)}) collective-permute-start(f32[1,4,2,128,128]{4,3,2,1,0:T(8,128)S(1)} %get-tuple-element.35.rest_1_), channel_id=1, source_target_pairs={{1,0},{5,4},{9,8},{13,12},{17,16},{21,20},{25,24},{29,28}} | collective-permute-start | bytes 1572872 | tf_op jit(solution)/shard_map/ppermute | solution.py:490
  49.4 6.7 %collective-permute-start.10 = (f32[2,64,128]{2,1,0:T(8,128)S(1)}, f32[2,64,128]{2,1,0:T(8,128)S(1)}, u32[]{:S(2)}, u32[]{:S(2)}) collective-permute-start(f32[2,64,128]{2,1,0:T(8,128)S(1)} %get-tuple-element.42.rest_2_), channel_id=1, source_target_pairs={{1,0},{2,1},{5,4},{6,5},{9,8},{10,9},{13,12},{14,13},{17,16},{18,1... | collective-permute-start | bytes 196616 | tf_op jit(solution)/shard_map/ppermute | solution.py:490
  53.8 6.2 %collective-permute-start.9 = (f32[2,64,128]{2,1,0:T(8,128)S(1)}, f32[2,64,128]{2,1,0:T(8,128)S(1)}, u32[]{:S(2)}, u32[]{:S(2)}) collective-permute-start(f32[2,64,128]{2,1,0:T(8,128)S(1)} %get-tuple-element.44), channel_id=1, source_target_pairs={{1,2},{2,3},{5,6},{6,7},{9,10},{10,11},{13,14},{14,15},{17,18},{18... | collective-permute-start | bytes 196616 | tf_op jit(solution)/shard_map/ppermute | solution.py:490

commit v8 on v7

--- a/solution.py
+++ b/solution.py
@@ -113,9 +113,35 @@
 
 
 def neighbour(distance):
-    z, peers = lax.axis_index("orb"), lax.axis_size("orb")
-    number = z + distance
-    return jnp.clip(number, 0, peers - 1), jnp.logical_and(number >= 0, number < peers)
+    def place():
+        z, peers = lax.axis_index("orb"), lax.axis_size("orb")
+        number = z + distance
+        return jnp.clip(number, 0, peers - 1), jnp.logical_and(number >= 0, number < peers)
+
+    return place
+
+
+def reflected(offset, inner):
+    def place():
+        z = lax.axis_index("orb")
+        is_inner_one = jnp.logical_or(z == 1, z == 2)
+        valid = z >= 0 if inner is None else is_inner_one == inner
+        return lax.rem(offset + 4 - z, 4), valid
+
+    return place
+
+
+def beside():
+    z = lax.axis_index("orb")
+    return jnp.where(lax.rem(z, 2) == 0, z + 1, z - 1), z >= 0
+
+
+def two_off(inner):
+    def place():
+        z = lax.axis_index("orb")
+        return lax.rem(z + 2, 4), jnp.logical_or(z == 1, z == 2) == inner
+
+    return place
 
 
 def own_kernel(
@@ -196,8 +222,8 @@
     acc_ref, keeps = rest[0], rest[1:]
     acc_ref[...] = before_ref[...]
     slot = 0
-    for distance, self_ref in zip(places, sigmas):
-        number, valid = neighbour(distance)
+    for place, self_ref in zip(places, sigmas):
+        number, valid = place()
 
         @pl.when(valid)
         def _():
@@ -229,35 +255,33 @@
     )(hi, lo, before, *shards, *after)
 
 
-def rows_kernel(near, green_ref, *rest):
-    count = 2 if near else 1
-    outs, sem = rest[-1 - count : -1], rest[-1]
-    z, rows = lax.axis_index("orb"), green_ref.shape[2]
-    starts = [rows - HALF, 0] if near else [jnp.where(z == 0, rows - MARGIN, HALF)]
-    copies = [
-        pltpu.make_async_copy(
-            green_ref.at[0, :, pl.ds(pl.multiple_of(starts[n], HALF), HALF), :],
-            out,
-            sem.at[n],
+def rows_kernel(wanted, green_ref, *rest):
+    outs, sem = rest[-1 - len(wanted) : -1], rest[-1]
+    copies = []
+    for n, ((size, start), out) in enumerate(zip(wanted, outs)):
+        row = pl.multiple_of(start(lax.axis_index("orb"), green_ref.shape[2]), HALF)
+        copies.append(
+            pltpu.make_async_copy(green_ref.at[0, :, pl.ds(row, size), :], out, sem.at[n])
         )
-        for n, out in enumerate(outs)
-    ]
     for copy in copies:
         copy.start()
     for copy in copies:
         copy.wait()
 
 
-def rows_at(green, near, after=()):
-    count = 2 if near else 1
-    out = jax.ShapeDtypeStruct((2, HALF, green.shape[3]), F32)
+def rows_at(green, wanted, after=()):
+    count = len(wanted)
+    outs = [jax.ShapeDtypeStruct((2, size, green.shape[3]), F32) for size, _ in wanted]
     return pl.pallas_call(
-        functools.partial(rows_kernel, near),
-        out_shape=[out] * count,
+        functools.partial(rows_kernel, wanted),
+        out_shape=outs,
         in_specs=[pl.BlockSpec(memory_space=pl.ANY)] * (1 + len(after)),
         out_specs=[pl.BlockSpec(memory_space=pltpu.VMEM)] * count,
         scratch_shapes=[pltpu.SemaphoreType.DMA((count,))],
         compiler_params=pltpu.CompilerParams(vmem_limit_bytes=8 << 20),
+        cost_estimate=pl.CostEstimate(
+            flops=0, bytes_accessed=4 * sum(x.size for x in outs), transcendentals=0
+        ),
         name="rows",
     )(green, *after)
 
@@ -266,21 +290,22 @@
     del refs
 
 
-def gate(right, left, *after):
+def gate(arrays, after):
     hbm = pl.BlockSpec(memory_space=pl.ANY)
     return pl.pallas_call(
         gate_kernel,
-        out_shape=[jax.ShapeDtypeStruct(x.shape, x.dtype) for x in (right, left)],
-        in_specs=[hbm] * (2 + len(after)),
-        out_specs=[hbm] * 2,
-        input_output_aliases={0: 0, 1: 1},
+        out_shape=[jax.ShapeDtypeStruct(x.shape, x.dtype) for x in arrays],
+        in_specs=[hbm] * (len(arrays) + len(after)),
+        out_specs=[hbm] * len(arrays),
+        input_output_aliases={n: n for n in range(len(arrays))},
         compiler_params=pltpu.CompilerParams(vmem_limit_bytes=1 << 20),
         cost_estimate=pl.CostEstimate(flops=0, bytes_accessed=0, transcendentals=0),
         name="gate",
-    )(right, left, *after)
-
-
-def edge_kernel(places, held, a_ref, b_ref, c_ref, *refs):
+    )(*arrays, *after)
+
+
+def edge_kernel(places, held, paired, *refs):
+    halos, refs = refs[: 2 if paired else 3], refs[2 if paired else 3 :]
     keeps = refs[: 2 * len(places)]
     left_ref, right_ref, own_ref, acc_ref = refs[2 * len(places) :]
     z, peers = lax.axis_index("orb"), lax.axis_size("orb")
@@ -291,15 +316,25 @@
     limit = jnp.where(from_right, MARGIN, HALF)
     acc_ref[...] = jnp.zeros_like(acc_ref)
 
+    def rows_of(part, cols):
+        if not paired:
+            return [ref[part, :, cols] for ref in halos]
+        first, second = halos[0][part, :HALF, cols], halos[0][part, HALF:, cols]
+        middle = halos[1][part, :, cols]
+        return (
+            jnp.where(from_left, first, second),
+            jnp.where(from_left, second, middle),
+            jnp.where(from_left, middle, first),
+        )
+
     def add(number, hi, lo, at):
         cols = pl.ds(pl.multiple_of(number * held * BS, BS), held * BS)
+        wide = [rows_of(part, cols) for part in range(2)]
         for side in range(2):
             fields = []
             for part in range(2):
-                outer = jnp.where(
-                    from_left if side == 0 else from_right, a_ref[part, :, cols], 0.0
-                )
-                inner = (b_ref if side == 0 else c_ref)[part, :, cols]
+                outer = jnp.where(from_left if side == 0 else from_right, wide[part][0], 0.0)
+                inner = wide[part][1 + side]
                 rows = [outer, inner] if side == 0 else [inner, outer]
                 fields.append(halves(jnp.concatenate(rows, axis=0)))
             halo = []
@@ -322,8 +357,8 @@
     @pl.when(is_inner())
     def _():
         for k, shards in enumerate(places):
-            for n, distance in enumerate(shards):
-                number, valid = neighbour(distance)
+            for n, place in enumerate(shards):
+                number, valid = place()
 
                 @pl.when(valid)
                 def _():
@@ -334,10 +369,18 @@
     low = lane < MARGIN
     left, right = acc_ref[0], acc_ref[1]
     turned_left, turned_right = left.T[:MARGIN], right.T[MARGIN:]
-    left_ref[0] = jnp.where(low, 0.0, left[:MARGIN])
-    left_ref[1] = jnp.where(low, 0.0, -left[MARGIN:])
-    right_ref[0] = jnp.where(lane < limit, right[:MARGIN], 0.0)
-    right_ref[1] = jnp.where(lane < limit, -right[MARGIN:], 0.0)
+    for part in range(2):
+        rows = slice(part * MARGIN, (part + 1) * MARGIN)
+        sign = 1.0 - 2.0 * part
+        to_left = jnp.where(low, 0.0, sign * left[rows])
+        to_right = jnp.where(lane < limit, sign * right[rows], 0.0)
+        if paired:
+            to_left, to_right = (
+                jnp.where(from_left, to_left, to_right),
+                jnp.where(from_left, to_right, to_left),
+            )
+        left_ref[part] = to_left
+        right_ref[part] = to_right
     own_ref[0, 0] = jnp.where(low, turned_left, 0.0)
     own_ref[0, 1] = jnp.where(low, pltpu.roll(turned_left, MARGIN, 1), 0.0)
     mine = jnp.logical_and(row < limit, lane >= MARGIN)
@@ -345,11 +388,11 @@
     own_ref[1, 1] = jnp.where(mine, turned_right, 0.0)
 
 
-def edge_part(halos, keeps, places, held):
+def edge_part(halos, keeps, places, held, paired=False):
     vmem = pl.BlockSpec(memory_space=pltpu.VMEM)
     side = jax.ShapeDtypeStruct((2, MARGIN, LANES), F32)
     return pl.pallas_call(
-        functools.partial(edge_kernel, places, held),
+        functools.partial(edge_kernel, places, held, paired),
         out_shape=(side, side, jax.ShapeDtypeStruct((2, 2, MARGIN, LANES), F32)),
         in_specs=[vmem] * (len(halos) + len(keeps)),
         out_specs=(vmem, vmem, vmem),
@@ -362,8 +405,16 @@
     )(*halos, *keeps)
 
 
-def band_kernel(acc_ref, own_ref, from_left_ref, from_right_ref, out_ref, rows_ref):
+def band_kernel(paired, acc_ref, own_ref, from_left_ref, from_right_ref, out_ref, rows_ref):
     tiles = acc_ref.shape[0]
+    returned = [[ref[part] for part in range(2)] for ref in (from_left_ref, from_right_ref)]
+    if paired:
+        either = [x + y for x, y in zip(*returned)]
+        high = lax.axis_index("orb") >= 2
+        returned = [
+            [jnp.where(high, x, 0.0) for x in either],
+            [jnp.where(high, 0.0, x) for x in either],
+        ]
     group = out_ref.shape[2]
     per_tile = TILE // W
     for t in range(tiles):
@@ -372,10 +423,10 @@
             x = acc_ref[t, base : base + TILE, :]
             rows_ref[t, part] = x
             if t == 0:
-                extra = own_ref[0, part] + from_left_ref[part]
+                extra = own_ref[0, part] + returned[0][part]
                 rows_ref[t, part, :MARGIN, :LANES] = x[:MARGIN, :LANES] + extra
             if t == tiles - 1:
-                extra = own_ref[1, part] + from_right_ref[part]
+                extra = own_ref[1, part] + returned[1][part]
                 rows_ref[t, part, MARGIN:, LANES:] = x[MARGIN:, LANES:] + extra
     low = lax.broadcasted_iota(jnp.int32, (W, LANES), 1) < MARGIN
     width = TILE + 2 * MARGIN
@@ -389,12 +440,12 @@
                 out_ref[atom // group, part, atom % group] = jnp.where(low, before, after)
 
 
-def band(acc, own, from_left, from_right, energies):
+def band(acc, own, from_left, from_right, energies, paired):
     tiles = acc.shape[0]
     atoms = tiles * TILE // W
     vmem = pl.BlockSpec(memory_space=pltpu.VMEM)
     return pl.pallas_call(
-        band_kernel,
+        functools.partial(band_kernel, paired),
         out_shape=jax.ShapeDtypeStruct((energies, 2, atoms // energies, W, LANES), F32),
         in_specs=[vmem] * 4,
         out_specs=vmem,
@@ -502,14 +553,18 @@
     padded = -(-pairs // LANES) * LANES
     held = sigma.shape[1]
 
-    far = is_far(peers)
+    far, paired = is_far(peers), peers == 4
     up = [(i, i + 1) for i in range(peers - 1)]
     down = [(i + 1, i) for i in range(peers - 1)]
     fixed = pltpu.with_memory_space_constraint(green, pltpu.HBM)
-    right, left = send(sigma, up), send(sigma, down)
-    last, leading = rows_at(fixed, True)
-    near_right = send(last, up[:-1] if far else up)
-    near_left = send(leading, down[1:] if far else down)
+    if paired:
+        ends, middle, outward = [(0, 1), (3, 2)], [(1, 2), (2, 1)], [(1, 0), (2, 3)]
+        aside, across = send(sigma, ends + outward), send(sigma, middle)
+        near = rows_at(fixed, [(HALF, lambda z, rows: jnp.where(z == 1, rows - HALF, 0))])
+    else:
+        right, left = send(sigma, up), send(sigma, down)
+        near = rows_at(fixed, [(HALF, lambda z, rows: rows - HALF), (HALF, lambda z, rows: 0 * z)])
+
     mine = lax.dynamic_slice_in_dim(neighbours, e * group, group, axis=0)
     first = z * atoms + e * group
     offset = mine - (first + jnp.arange(group, dtype=jnp.int32))[:, None]
@@ -524,38 +579,67 @@
 
 
     acc, *keeps, hi, lo = own_part(
-        fixed, pltpu.with_memory_space_constraint(sigma, pltpu.HBM), [where, mix, factors, last]
+        fixed,
+        pltpu.with_memory_space_constraint(sigma, pltpu.HBM),
+        [where, mix, factors, near[0]],
     )
-    places = [[0]]
-    if far:
-        (outer,) = rows_at(fixed, False, [keeps[-1]])
-        other = send(outer, [(0, 1), (peers - 1, peers - 2)])
+    more = functools.partial(lesser_part, hi, lo, held=held)
+    places = [[neighbour(0)]]
+    if paired:
+        (outer,) = rows_at(
+            fixed, [(MARGIN, lambda z, rows: jnp.where(z == 0, rows - MARGIN, 0))], [keeps[-1]]
+        )
+        aside, across = gate([aside, across], [keeps[-1], outer])
+        second_across, second_aside = send(aside, middle), send(across, outward)
+        halos = [send(outer, ends), send(near[0], middle)]
+        places.append([beside, reflected(3, True)])
+        acc, *kept = more(acc, [aside, across], places[-1])
+        keeps += kept
+        (second_across,) = gate([second_across], [kept[-1]])
+        third_aside = send(second_across, outward)
+        places.append([two_off(True), two_off(False)])
+        acc, *kept = more(acc, [second_across, second_aside], places[-1])
+        keeps += kept
+        to_end, to_middle, own = edge_part(halos, keeps, places, held, True)
+        back_left, back_right = send(to_end, outward), send(to_middle, middle)
+        (acc,) = more(acc, [third_aside], [reflected(3, False)], after=[to_end], keep=False)
     else:
-        outer = other = jnp.zeros_like(near_left)
-    for k in range(1, peers):
-        if k < peers - 1:
-            right, left = gate(right, left, keeps[-1], outer if k == 1 else other)
-            following = send(right, up[k:]), send(left, down[: peers - 1 - k])
-            after = []
+        near_right = send(near[0], up[:-1] if far else up)
+        near_left = send(near[1], down[1:] if far else down)
+        if far:
+            (outer,) = rows_at(
+                fixed,
+                [(HALF, lambda z, rows: jnp.where(z == 0, rows - MARGIN, HALF))],
+                [keeps[-1]],
+            )
+            other = send(outer, [(0, 1), (peers - 1, peers - 2)])
         else:
-            if not far:
-                acc, *kept = lesser_part(hi, lo, acc, [right, left], [-k, k], held)
-                keeps += kept
-                places.append([-k, k])
-            to_left, to_right, own = edge_part(
-                [other, near_right, near_left], keeps, places, held
-            )
-            back_right = send(to_left, down[:-1] if far else down)
-            back_left = send(to_right, up[1:] if far else up)
-            after = [to_left]
-            if not far:
-                break
-        acc, *kept = lesser_part(hi, lo, acc, [right, left], [-k, k], held, after, k < peers - 1)
-        keeps += kept
-        places.append([-k, k])
-        if k < peers - 1:
-            right, left = following
-    lesser = band(acc, own, back_left, back_right, energies)
+            outer = other = jnp.zeros_like(near_left)
+        for k in range(1, peers):
+            around = [neighbour(-k), neighbour(k)]
+            if k < peers - 1:
+                right, left = gate([right, left], [keeps[-1], outer if k == 1 else other])
+                following = send(right, up[k:]), send(left, down[: peers - 1 - k])
+                after = []
+            else:
+                if not far:
+                    acc, *kept = more(acc, [right, left], around)
+                    keeps += kept
+                    places.append(around)
+                to_left, to_right, own = edge_part(
+                    [other, near_right, near_left], keeps, places, held
+                )
+                back_right = send(to_left, down[:-1] if far else down)
+                back_left = send(to_right, up[1:] if far else up)
+                after = [to_left]
+                if not far:
+                    break
+            acc, *kept = more(acc, [right, left], around, after=after, keep=k < peers - 1)
+            keeps += kept
+            places.append(around)
+            if k < peers - 1:
+                right, left = following
+    lesser = band(acc, own, back_left, back_right, energies, paired)
 
     recv = lax.all_to_all(lesser, "energy", split_axis=0, concat_axis=0, tiled=True)
     spread = scatter(recv, where, mix, factors, pairs)

time: 91 us -> 85.8 us (0.943)
  the two profiles are of different devices: /device:TPU:16 before, /device:TPU:0 now
where the time goes in v8:
time: 85.8 us; the launch traced here: 84.4 us
  blocking collectives  25.4 us (30%)
  Pallas kernels  22 us (26%)
  starting transfers between devices  16.8 us (20%)
  waiting for transfers between devices  16.2 us (19%)
  local copies, waits for them, and re-layouts  2.69 us (3%)
  other arithmetic  1.02 us (1%)
    ppermute x9, starting transfers between devices, send(): return lax.ppermute(x, 'orb', pairs)  16.8 us
    ppermute x9, waiting for transfers between devices, send(): return lax.ppermute(x, 'orb', pairs)  16.2 us
    all_to_all x1, blocking collectives, per_device(): lax.all_to_all(lesser, 'energy', split_axis=0, concat_axis=0, tiled=True)  13.3 us
    all_to_all x1, blocking collectives, per_device(): lax.all_to_all(spread, 'energy', split_axis=0, concat_axis=0, tiled=True)  12.2 us
    pallas_call x3, Pallas kernels, lesser_part(): pl.pallas_call(functools.partial(lesser_kernel, places, held, len(after))...  9.17 us
    pallas_call x1, Pallas kernels, own_part(): pl.pallas_call(own_kernel, out_shape=(jax.ShapeDtypeStruct((tiles, 2 * TI...  6.11 us
    pallas_call x1, Pallas kernels, scatter(): pl.pallas_call(scatter_kernel, out_shape=jax.ShapeDtypeStruct((energies,...  3.65 us
    pallas_call x2, Pallas kernels, rows_at(): pl.pallas_call(functools.partial(rows_kernel, wanted), out_shape=outs, in...  2.3 us
  transfers between devices with their start and end apart: 9, of which 4 were waited for; matrix products, arithmetic and copies ran while one was open for 3% of the time, Pallas kernels for 21%

profile of v8, /device:TPU:0, one launch (start us, length us, event | category | flops | bytes accessed | tf_op | source)
XLA Modules:
  0.0 84.4 jit_solution(10485210581893667402)
XLA Ops:
  0.0 3.0 %collective-permute-start = (f32[1,4,2,128,128]{4,3,2,1,0:T(8,128)}, f32[1,4,2,128,128]{4,3,2,1,0:T(8,128)S(1)}, u32[]{:S(2)}, u32[]{:S(2)}) collective-permute-start(f32[1,4,2,128,128]{4,3,2,1,0:T(8,128)} %sigma_ref.1), channel_id=1, source_target_pairs={{0,1},{3,2},{1,0},{2,3},{4,5},{7,6},{5,4},{6,7},{8,9},{11,10},{9,8... | collective-permute-start | bytes 1572872 | tf_op jit(solution)/shard_map/ppermute | solution.py:541
  3.0 0.7 collective-permute-start.1
  3.7 0.8 constant_dynamic-slice_fusion.1
  4.7 0.1 reshape.79.rest_0_.where_ref
  4.7 0.7 iota_add_fusion
  5.5 0.8 slice_bitcast_fusion.1
  6.2 0.1 add_reduce_fusion
  6.3 0.1 broadcast_multiply_fusion
  6.5 0.2 mul.67.rest_1_.mix_ref
  6.7 1.1 %rows.2.rest_3_ = f32[2,32,2048]{2,1,0:T(8,128)S(1)} custom-call(f32[1,2,512,2048]{3,2,1,0:T(8,128)} %green_ref.5), custom_call_target="tpu_custom_call" | custom-call | bytes 524288 | tf_op jit(solution)/shard_map/rows/pallas_call | solution.py:275
  7.8 6.1 %lesser_own.1 = (f32[4,256,256]{2,1,0:T(8,128)S(1)}, bf16[4,256,256]{2,1,0:T(8,128)(2,1)S(1)}, bf16[4,256,256]{2,1,0:T(8,128)(2,1)S(1)}, bf16[640,4096]{1,0:T(8,128)(2,1)S(1)}, bf16[640,4096]{1,0:T(8,128)(2,1)S(1)}) custom-call(f32[1,2,512,2048]{3,2,1,0:T(8,128)} %green_ref.5, f32[1,4,2,128,128]{4,3,2,1,0:T(8,128)} %sigma_ref.1, ...), custom_call_target="tpu_custom_call" | custom-call | flops 33554432 | bytes 1048576 | tf_op jit(solution)/shard_map/lesser_own/pallas_call | solution.py:193
  13.9 1.2 %rows.3.refs_3_ = f32[2,64,2048]{2,1,0:T(8,128)S(1)} custom-call(f32[1,2,512,2048]{3,2,1,0:T(8,128)} %green_ref.5, bf16[4,256,256]{2,1,0:T(8,128)(2,1)S(1)} %get-tuple-element.24.rest_0_.refs_2_.refs_3_), custom_call_target="tpu_custom_call" | custom-call | bytes 1048576 | tf_op jit(solution)/shard_map/rows/pallas_call | solution.py:275
  15.1 7.1 %collective-permute-start.5 = (f32[2,64,2048]{2,1,0:T(8,128)S(1)}, f32[2,64,2048]{2,1,0:T(8,128)S(1)}, u32[]{:S(2)}, u32[]{:S(2)}) collective-permute-start(f32[2,64,2048]{2,1,0:T(8,128)S(1)} %rows.3.refs_3_), channel_id=1, source_target_pairs={{0,1},{3,2},{4,5},{7,6},{8,9},{11,10},{12,13},{15,14},{16,17},{19,... | collective-permute-start | bytes 3145736 | tf_op jit(solution)/shard_map/ppermute | solution.py:541
  22.3 0.7 collective-permute-start.2
  23.0 1.3 %collective-permute-start.3 = (f32[1,4,2,128,128]{4,3,2,1,0:T(8,128)S(1)}, f32[1,4,2,128,128]{4,3,2,1,0:T(8,128)S(1)}, u32[]{:S(2)}, u32[]{:S(2)}) collective-permute-start(f32[1,4,2,128,128]{4,3,2,1,0:T(8,128)S(1)} %get-tuple-element.26.rest_1_), channel_id=1, source_target_pairs={{1,0},{2,3},{5,4},{6,7},{9,8},{10,11},{13,12},{14,15},{17,16},{18,... | collective-permute-start | bytes 1572872 | tf_op jit(solution)/shard_map/ppermute | solution.py:541
  24.3 0.7 collective-permute-start.6
  25.0 3.0 %lesser_more.3 = (f32[4,256,256]{2,1,0:T(8,128)S(1)}, bf16[8,256,256]{2,1,0:T(8,128)(2,1)S(1)}, bf16[8,256,256]{2,1,0:T(8,128)(2,1)S(1)}) custom-call(bf16[640,4096]{1,0:T(8,128)(2,1)S(1)} %get-tuple-element.21.hi_ref, bf16[640,4096]{1,0:T(8,128)(2,1)S(1)} %get-tuple-element.22.lo_ref, ...), custom_call_target="tpu_custom_call", output_to_operand_aliasing={{0}: (2, {})} | custom-call | flops 83886080 | bytes 262144 | tf_op jit(solution)/shard_map/lesser_more/pallas_call | solution.py:242
  28.0 1.3 %collective-permute-start.4 = (f32[1,4,2,128,128]{4,3,2,1,0:T(8,128)S(1)}, f32[1,4,2,128,128]{4,3,2,1,0:T(8,128)S(1)}, u32[]{:S(2)}, u32[]{:S(2)}) collective-permute-start(f32[1,4,2,128,128]{4,3,2,1,0:T(8,128)S(1)} %gate.3.rest_0_), channel_id=1, source_target_pairs={{1,0},{2,3},{5,4},{6,7},{9,8},{10,11},{13,12},{14,15},{17,16},{18,... | collective-permute-start | bytes 1572872 | tf_op jit(solution)/shard_map/ppermute | solution.py:541
  29.3 8.8 %collective-permute-done.3.rest_1_ = f32[1,4,2,128,128]{4,3,2,1,0:T(8,128)S(1)} collective-permute-done((f32[1,4,2,128,128]{4,3,2,1,0:T(8,128)S(1)}, f32[1,4,2,128,128]{4,3,2,1,0:T(8,128)S(1)}, u32[]{:S(2)}, u32[]{:S(2)}) %collective-permute-start.3) | collective-permute-done | bytes 524320 | tf_op jit(solution)/shard_map/ppermute | solution.py:541
  38.2 3.0 %lesser_more.4 = (f32[4,256,256]{2,1,0:T(8,128)S(1)}, bf16[8,256,256]{2,1,0:T(8,128)(2,1)S(1)}, bf16[8,256,256]{2,1,0:T(8,128)(2,1)S(1)}) custom-call(bf16[640,4096]{1,0:T(8,128)(2,1)S(1)} %get-tuple-element.21.hi_ref, bf16[640,4096]{1,0:T(8,128)(2,1)S(1)} %get-tuple-element.22.lo_ref, ...), custom_call_target="tpu_custom_call", output_to_operand_aliasing={{0}: (2, {})} | custom-call | flops 83886080 | bytes 262144 | tf_op jit(solution)/shard_map/lesser_more/pallas_call | solution.py:242
  41.2 2.9 %collective-permute-done.5.refs_0_ = f32[2,64,2048]{2,1,0:T(8,128)S(1)} collective-permute-done((f32[2,64,2048]{2,1,0:T(8,128)S(1)}, f32[2,64,2048]{2,1,0:T(8,128)S(1)}, u32[]{:S(2)}, u32[]{:S(2)}) %collective-permute-start.5) | collective-permute-done | bytes 1048608 | tf_op jit(solution)/shard_map/ppermute | solution.py:541
  44.1 0.2 edges.1
  44.2 1.3 %collective-permute-start.7 = (f32[2,64,128]{2,1,0:T(8,128)S(1)}, f32[2,64,128]{2,1,0:T(8,128)S(1)}, u32[]{:S(2)}, u32[]{:S(2)}) collective-permute-start(f32[2,64,128]{2,1,0:T(8,128)S(1)} %get-tuple-element.34.rest_1_), channel_id=1, source_target_pairs={{1,0},{2,3},{5,4},{6,7},{9,8},{10,11},{13,12},{14,15},{17,16},{18,... | collective-permute-start | bytes 196616 | tf_op jit(solution)/shard_map/ppermute | solution.py:541
  45.5 0.7 collective-permute-start.8
  46.2 2.8 %collective-permute-done.4.rest_0_ = f32[1,4,2,128,128]{4,3,2,1,0:T(8,128)S(1)} collective-permute-done((f32[1,4,2,128,128]{4,3,2,1,0:T(8,128)S(1)}, f32[1,4,2,128,128]{4,3,2,1,0:T(8,128)S(1)}, u32[]{:S(2)}, u32[]{:S(2)}) %collective-permute-start.4) | collective-permute-done | bytes 524320 | tf_op jit(solution)/shard_map/ppermute | solution.py:541
  49.0 3.2 %lesser_more.5.acc_ref = f32[4,256,256]{2,1,0:T(8,128)S(1)} custom-call(bf16[640,4096]{1,0:T(8,128)(2,1)S(1)} %get-tuple-element.21.hi_ref, bf16[640,4096]{1,0:T(8,128)(2,1)S(1)} %get-tuple-element.22.lo_ref, f32[4,256,256]{2,1,0:T(8,128)S(1)} %get-tuple-element.29.before_ref, ...), custom_call_target="tpu_custom_call", output_to_operand_aliasing={{}: (2, {})} | custom-call | flops 41943040 | bytes 262144 | tf_op jit(solution)/shard_map/lesser_more/pallas_call | solution.py:242
  52.1 1.8 %collective-permute-done.7.from_left_ref = f32[2,64,128]{2,1,0:T(8,128)S(1)} collective-permute-done((f32[2,64,128]{2,1,0:T(8,128)S(1)}, f32[2,64,128]{2,1,0:T(8,128)S(1)}, u32[]{:S(2)}, u32[]{:S(2)}) %collective-permute-start.7) | collective-permute-done | bytes 65568 | tf_op jit(solution)/shard_map/ppermute | solution.py:541
  53.9 0.6 band.1
  54.5 13.3 %all_to_all.10.recv_ref = f32[8,2,8,8,128]{4,3,2,1,0:T(8,128)S(1)} all-to-all(f32[8,2,8,8,128]{4,3,2,1,0:T(8,128)S(1)} %band.1), channel_id=1, replica_groups=mesh['energy'=8,'orb'=4] {'energy'}, dimensions={0} | all-to-all | bytes 1048576 | tf_op jit(solution)/shard_map/all_to_all | solution.py:644
  67.8 3.7 %scatter.1 = f32[8,128,128]{2,1,0:T(8,128)S(1)} custom-call(f32[8,2,8,8,128]{4,3,2,1,0:T(8,128)S(1)} %all_to_all.10.recv_ref, s32[1,128]{1,0:T(1,128)S(1)} %reshape.79.rest_0_.where_ref, f32[128,128]{1,0:T(8,128)S(1)} %mul.67.rest_1_.mix_ref, f32[192,128]{1,0:T(8,128)S(1)} %constant_dynamic-slice_fusion.rest_2_.dham_ref), custom_call_target="tpu_custom_call" | custom-call | tf_op jit(solution)/shard_map/scatter/pallas_call | solution.py:507
  71.4 12.2 %all_to_all.11 = f32[8,128,128]{2,1,0:T(8,128)S(1)} all-to-all(f32[8,128,128]{2,1,0:T(8,128)S(1)} %scatter.1), channel_id=1, replica_groups=mesh['energy'=8,'orb'=4] {'energy'}, dimensions={0} | all-to-all | bytes 1048576 | tf_op jit(solution)/shard_map/all_to_all | solution.py:646
  83.6 0.8 copy.24
  (14 shorter events, 0.2 us)
Async XLA Ops:
  0.0 7.7 %copy-start = (f32[1024,3,8,8]{0,3,2,1:T(8,128)S(1)}, f32[1024,3,8,8]{0,3,2,1:T(8,128)}, u32[]{:S(2)}) copy-start(f32[1024,3,8,8]{0,3,2,1:T(8,128)} %param.11) | copy-start | bytes 2359300
  0.0 22.3 %collective-permute-start = (f32[1,4,2,128,128]{4,3,2,1,0:T(8,128)}, f32[1,4,2,128,128]{4,3,2,1,0:T(8,128)S(1)}, u32[]{:S(2)}, u32[]{:S(2)}) collective-permute-start(f32[1,4,2,128,128]{4,3,2,1,0:T(8,128)} %sigma_ref.1), channel_id=1, source_target_pairs={{0,1},{3,2},{1,0},{2,3},{4,5},{7,6},{5,4},{6,7},{8,9},{11,10},{9,8... | collective-permute-start | bytes 1572872 | tf_op jit(solution)/shard_map/ppermute | solution.py:541
  3.0 19.3 %collective-permute-start.1 = (f32[1,4,2,128,128]{4,3,2,1,0:T(8,128)}, f32[1,4,2,128,128]{4,3,2,1,0:T(8,128)S(1)}, u32[]{:S(2)}, u32[]{:S(2)}) collective-permute-start(f32[1,4,2,128,128]{4,3,2,1,0:T(8,128)} %sigma_ref.1), channel_id=1, source_target_pairs={{1,2},{2,1},{5,6},{6,5},{9,10},{10,9},{13,14},{14,13},{17,18},{18,... | collective-permute-start | bytes 1572872 | tf_op jit(solution)/shard_map/ppermute | solution.py:541
  15.1 28.9 %collective-permute-start.5 = (f32[2,64,2048]{2,1,0:T(8,128)S(1)}, f32[2,64,2048]{2,1,0:T(8,128)S(1)}, u32[]{:S(2)}, u32[]{:S(2)}) collective-permute-start(f32[2,64,2048]{2,1,0:T(8,128)S(1)} %rows.3.refs_3_), channel_id=1, source_target_pairs={{0,1},{3,2},{4,5},{7,6},{8,9},{11,10},{12,13},{15,14},{16,17},{19,... | collective-permute-start | bytes 3145736 | tf_op jit(solution)/shard_map/ppermute | solution.py:541
  22.3 5.7 %collective-permute-start.2 = (f32[1,4,2,128,128]{4,3,2,1,0:T(8,128)S(1)}, f32[1,4,2,128,128]{4,3,2,1,0:T(8,128)S(1)}, u32[]{:S(2)}, u32[]{:S(2)}) collective-permute-start(f32[1,4,2,128,128]{4,3,2,1,0:T(8,128)S(1)} %get-tuple-element.25.rest_0_), channel_id=1, source_target_pairs={{1,2},{2,1},{5,6},{6,5},{9,10},{10,9},{13,14},{14,13},{17,18},{18,... | collective-permute-start | bytes 1572872 | tf_op jit(solution)/shard_map/ppermute | solution.py:541
  23.0 15.1 %collective-permute-start.3 = (f32[1,4,2,128,128]{4,3,2,1,0:T(8,128)S(1)}, f32[1,4,2,128,128]{4,3,2,1,0:T(8,128)S(1)}, u32[]{:S(2)}, u32[]{:S(2)}) collective-permute-start(f32[1,4,2,128,128]{4,3,2,1,0:T(8,128)S(1)} %get-tuple-element.26.rest_1_), channel_id=1, source_target_pairs={{1,0},{2,3},{5,4},{6,7},{9,8},{10,11},{13,12},{14,15},{17,16},{18,... | collective-permute-start | bytes 1572872 | tf_op jit(solution)/shard_map/ppermute | solution.py:541
  24.3 16.8 %collective-permute-start.6 = (f32[2,32,2048]{2,1,0:T(8,128)S(1)}, f32[2,32,2048]{2,1,0:T(8,128)S(1)}, u32[]{:S(2)}, u32[]{:S(2)}) collective-permute-start(f32[2,32,2048]{2,1,0:T(8,128)S(1)} %rows.2.rest_3_), channel_id=1, source_target_pairs={{1,2},{2,1},{5,6},{6,5},{9,10},{10,9},{13,14},{14,13},{17,18},{18,... | collective-permute-start | bytes 1572872 | tf_op jit(solution)/shard_map/ppermute | solution.py:541
  28.0 20.9 %collective-permute-start.4 = (f32[1,4,2,128,128]{4,3,2,1,0:T(8,128)S(1)}, f32[1,4,2,128,128]{4,3,2,1,0:T(8,128)S(1)}, u32[]{:S(2)}, u32[]{:S(2)}) collective-permute-start(f32[1,4,2,128,128]{4,3,2,1,0:T(8,128)S(1)} %gate.3.rest_0_), channel_id=1, source_target_pairs={{1,0},{2,3},{5,4},{6,7},{9,8},{10,11},{13,12},{14,15},{17,16},{18,... | collective-permute-start | bytes 1572872 | tf_op jit(solution)/shard_map/ppermute | solution.py:541
  44.2 9.7 %collective-permute-start.7 = (f32[2,64,128]{2,1,0:T(8,128)S(1)}, f32[2,64,128]{2,1,0:T(8,128)S(1)}, u32[]{:S(2)}, u32[]{:S(2)}) collective-permute-start(f32[2,64,128]{2,1,0:T(8,128)S(1)} %get-tuple-element.34.rest_1_), channel_id=1, source_target_pairs={{1,0},{2,3},{5,4},{6,7},{9,8},{10,11},{13,12},{14,15},{17,16},{18,... | collective-permute-start | bytes 196616 | tf_op jit(solution)/shard_map/ppermute | solution.py:541
  45.5 8.4 %collective-permute-start.8 = (f32[2,64,128]{2,1,0:T(8,128)S(1)}, f32[2,64,128]{2,1,0:T(8,128)S(1)}, u32[]{:S(2)}, u32[]{:S(2)}) collective-permute-start(f32[2,64,128]{2,1,0:T(8,128)S(1)} %get-tuple-element.36), channel_id=1, source_target_pairs={{1,2},{2,1},{5,6},{6,5},{9,10},{10,9},{13,14},{14,13},{17,18},{18,... | collective-permute-start | bytes 196616 | tf_op jit(solution)/shard_map/ppermute | solution.py:541

commit v9 on v8

--- a/solution.py
+++ b/solution.py
@@ -144,10 +144,9 @@
     return place
 
 
-def own_kernel(
-    green_ref, sigma_ref, *rest
-):
-    acc_ref, keep_hi_ref, keep_lo_ref, hi_ref, lo_ref, buf, self_ref, sem = rest[-8:]
+def own_kernel(wanted, extra, green_ref, sigma_ref, *rest):
+    acc_ref, keep_hi_ref, keep_lo_ref, hi_ref, lo_ref, *rest = rest[extra:]
+    *sent, buf, self_ref, sem, sent_sem = rest
     rows, held = green_ref.shape[2], sigma_ref.shape[1]
     blocks = green_ref.shape[3] // BS
     begin, active = lax.axis_index("orb") * held, is_inner()
@@ -173,6 +172,14 @@
     load.start()
     for s in range(blocks):
         fetch(s).start()
+    copies = []
+    for n, ((size, start), out) in enumerate(zip(wanted, sent)):
+        row = pl.multiple_of(start(lax.axis_index("orb"), rows), HALF)
+        copies.append(
+            pltpu.make_async_copy(green_ref.at[0, :, pl.ds(row, size), :], out, sent_sem.at[n])
+        )
+    for copy in copies:
+        copy.start()
     acc_ref[...] = jnp.zeros_like(acc_ref)
     for ref in (hi_ref, lo_ref):
         ref[:MARGIN, :] = jnp.zeros((MARGIN, ref.shape[1]), BF16)
@@ -181,9 +188,11 @@
     load.wait()
     shard_loop(begin, self_ref, hi_ref, lo_ref, acc_ref, (keep_hi_ref, keep_lo_ref), 0, active)
     lax.fori_loop(held, blocks, store, 0)
-
-
-def own_part(green, sigma, after):
+    for copy in copies:
+        copy.wait()
+
+
+def own_part(green, sigma, wanted, after):
     rows, held = green.shape[2], sigma.shape[1]
     tiles, blocks = rows // TILE, green.shape[3] // BS
     vmem = pl.BlockSpec(memory_space=pltpu.VMEM)
@@ -191,20 +200,22 @@
     keep = jax.ShapeDtypeStruct((held, 4 * MARGIN, 2 * BS), BF16)
     whole = jax.ShapeDtypeStruct((rows + 2 * MARGIN, blocks * 2 * BS), BF16)
     return pl.pallas_call(
-        own_kernel,
+        functools.partial(own_kernel, wanted, len(after)),
         out_shape=(
             jax.ShapeDtypeStruct((tiles, 2 * TILE, TILE + 2 * MARGIN), F32),
             keep,
             keep,
             whole,
             whole,
+            *[jax.ShapeDtypeStruct((2, size, green.shape[3]), F32) for size, _ in wanted],
         ),
         in_specs=[hbm] * (2 + len(after)),
-        out_specs=(vmem,) * 5,
+        out_specs=(vmem,) * (5 + len(wanted)),
         scratch_shapes=[
             pltpu.VMEM((blocks, 2, rows, BS), F32),
             pltpu.VMEM(sigma.shape, F32),
             pltpu.SemaphoreType.DMA((blocks + 1,)),
+            pltpu.SemaphoreType.DMA((len(wanted),)),
         ],
         compiler_params=pltpu.CompilerParams(vmem_limit_bytes=40 << 20),
         cost_estimate=pl.CostEstimate(
@@ -253,37 +264,6 @@
         ),
         name="lesser_more",
     )(hi, lo, before, *shards, *after)
-
-
-def rows_kernel(wanted, green_ref, *rest):
-    outs, sem = rest[-1 - len(wanted) : -1], rest[-1]
-    copies = []
-    for n, ((size, start), out) in enumerate(zip(wanted, outs)):
-        row = pl.multiple_of(start(lax.axis_index("orb"), green_ref.shape[2]), HALF)
-        copies.append(
-            pltpu.make_async_copy(green_ref.at[0, :, pl.ds(row, size), :], out, sem.at[n])
-        )
-    for copy in copies:
-        copy.start()
-    for copy in copies:
-        copy.wait()
-
-
-def rows_at(green, wanted, after=()):
-    count = len(wanted)
-    outs = [jax.ShapeDtypeStruct((2, size, green.shape[3]), F32) for size, _ in wanted]
-    return pl.pallas_call(
-        functools.partial(rows_kernel, wanted),
-        out_shape=outs,
-        in_specs=[pl.BlockSpec(memory_space=pl.ANY)] * (1 + len(after)),
-        out_specs=[pl.BlockSpec(memory_space=pltpu.VMEM)] * count,
-        scratch_shapes=[pltpu.SemaphoreType.DMA((count,))],
-        compiler_params=pltpu.CompilerParams(vmem_limit_bytes=8 << 20),
-        cost_estimate=pl.CostEstimate(
-            flops=0, bytes_accessed=4 * sum(x.size for x in outs), transcendentals=0
-        ),
-        name="rows",
-    )(green, *after)
 
 
 def gate_kernel(*refs):
@@ -560,10 +540,17 @@
     if paired:
         ends, middle, outward = [(0, 1), (3, 2)], [(1, 2), (2, 1)], [(1, 0), (2, 3)]
         aside, across = send(sigma, ends + outward), send(sigma, middle)
-        near = rows_at(fixed, [(HALF, lambda z, rows: jnp.where(z == 1, rows - HALF, 0))])
+        wanted = [
+            (MARGIN, lambda z, rows: jnp.where(z == 0, rows - MARGIN, 0)),
+            (HALF, lambda z, rows: jnp.where(z == 1, rows - HALF, 0)),
+        ]
     else:
         right, left = send(sigma, up), send(sigma, down)
-        near = rows_at(fixed, [(HALF, lambda z, rows: rows - HALF), (HALF, lambda z, rows: 0 * z)])
+        wanted = [
+            (HALF, lambda z, rows: jnp.where(z == 0, rows - MARGIN, HALF)),
+            (HALF, lambda z, rows: rows - HALF),
+            (HALF, lambda z, rows: 0 * z),
+        ]
 
     mine = lax.dynamic_slice_in_dim(neighbours, e * group, group, axis=0)
     first = z * atoms + e * group
@@ -578,20 +565,19 @@
     factors = jnp.pad(factors, ((0, 0), (0, padded - pairs)))
 
 
-    acc, *keeps, hi, lo = own_part(
+    acc, keep_hi, keep_lo, hi, lo, outer, near, *nearer = own_part(
         fixed,
         pltpu.with_memory_space_constraint(sigma, pltpu.HBM),
-        [where, mix, factors, near[0]],
+        wanted,
+        [where, mix, factors],
     )
+    keeps = [keep_hi, keep_lo]
     more = functools.partial(lesser_part, hi, lo, held=held)
     places = [[neighbour(0)]]
     if paired:
-        (outer,) = rows_at(
-            fixed, [(MARGIN, lambda z, rows: jnp.where(z == 0, rows - MARGIN, 0))], [keeps[-1]]
-        )
-        aside, across = gate([aside, across], [keeps[-1], outer])
+        aside, across = gate([aside, across], [keeps[-1]])
         second_across, second_aside = send(aside, middle), send(across, outward)
-        halos = [send(outer, ends), send(near[0], middle)]
+        halos = [send(outer, ends), send(near, middle)]
         places.append([beside, reflected(3, True)])
         acc, *kept = more(acc, [aside, across], places[-1])
         keeps += kept
@@ -604,17 +590,12 @@
         back_left, back_right = send(to_end, outward), send(to_middle, middle)
         (acc,) = more(acc, [third_aside], [reflected(3, False)], after=[to_end], keep=False)
     else:
-        near_right = send(near[0], up[:-1] if far else up)
-        near_left = send(near[1], down[1:] if far else down)
+        near_right = send(near, up[:-1] if far else up)
+        near_left = send(nearer[0], down[1:] if far else down)
         if far:
-            (outer,) = rows_at(
-                fixed,
-                [(HALF, lambda z, rows: jnp.where(z == 0, rows - MARGIN, HALF))],
-                [keeps[-1]],
-            )
             other = send(outer, [(0, 1), (peers - 1, peers - 2)])
         else:
-            outer = other = jnp.zeros_like(near_left)
+            other = jnp.zeros_like(near_left)
         for k in range(1, peers):
             around = [neighbour(-k), neighbour(k)]
             if k < peers - 1:

time: 85.8 us -> 83.7 us (0.976)
  Pallas kernels: 22 us -> 19.7 us
    pallas_call x3 -> x1, Pallas kernels: 8.41 us -> 6.13 us  [own_part(): pl.pallas_call(functools.partial(own_kernel, wanted, len(after)), out_sha...]
  transfers between devices with their start and end apart: 9 -> 9, of which waited for: 4 -> 4; matrix products, arithmetic and copies ran while one was open for 3% -> 4% of each run, Pallas kernels for 21% -> 19%
where the time goes in v9:
time: 83.7 us; the launch traced here: 82.4 us
  blocking collectives  25.4 us (30%)
  Pallas kernels  19.7 us (24%)
  starting transfers between devices  16.8 us (20%)
  waiting for transfers between devices  16.5 us (20%)
  local copies, waits for them, and re-layouts  2.69 us (3%)
  other arithmetic  1.02 us (1%)
    ppermute x9, starting transfers between devices, send(): return lax.ppermute(x, 'orb', pairs)  16.8 us
    ppermute x9, waiting for transfers between devices, send(): return lax.ppermute(x, 'orb', pairs)  16.5 us
    all_to_all x1, blocking collectives, per_device(): lax.all_to_all(lesser, 'energy', split_axis=0, concat_axis=0, tiled=True)  13.3 us
    all_to_all x1, blocking collectives, per_device(): lax.all_to_all(spread, 'energy', split_axis=0, concat_axis=0, tiled=True)  12.2 us
    pallas_call x3, Pallas kernels, lesser_part(): pl.pallas_call(functools.partial(lesser_kernel, places, held, len(after))...  9.16 us
    pallas_call x1, Pallas kernels, own_part(): pl.pallas_call(functools.partial(own_kernel, wanted, len(after)), out_sha...  6.13 us
    pallas_call x1, Pallas kernels, scatter(): pl.pallas_call(scatter_kernel, out_shape=jax.ShapeDtypeStruct((energies,...  3.66 us
  transfers between devices with their start and end apart: 9, of which 4 were waited for; matrix products, arithmetic and copies ran while one was open for 4% of the time, Pallas kernels for 19%

profile of v9, /device:TPU:0, one launch (start us, length us, event | category | flops | bytes accessed | tf_op | source)
XLA Modules:
  0.0 82.4 jit_solution(15722782440521994296)
XLA Ops:
  0.0 3.0 %collective-permute-start = (f32[1,4,2,128,128]{4,3,2,1,0:T(8,128)}, f32[1,4,2,128,128]{4,3,2,1,0:T(8,128)S(1)}, u32[]{:S(2)}, u32[]{:S(2)}) collective-permute-start(f32[1,4,2,128,128]{4,3,2,1,0:T(8,128)} %sigma_ref.1), channel_id=1, source_target_pairs={{0,1},{3,2},{1,0},{2,3},{4,5},{7,6},{5,4},{6,7},{8,9},{11,10},{9,8... | collective-permute-start | bytes 1572872 | tf_op jit(solution)/shard_map/ppermute | solution.py:521
  3.0 0.7 collective-permute-start.1
  3.7 0.8 constant_dynamic-slice_fusion.1
  4.5 0.1 copy.16
  4.6 0.1 select_add_fusion
  4.7 0.1 reshape.79.rest_0_.where_ref
  4.7 0.7 iota_add_fusion
  5.5 0.8 slice_bitcast_fusion.1
  6.2 0.1 add_reduce_fusion
  6.3 0.1 broadcast_multiply_fusion
  6.5 0.2 mul.67.rest_1_.mix_ref
  6.7 6.1 %lesser_own.1 = (f32[4,256,256]{2,1,0:T(8,128)S(1)}, bf16[4,256,256]{2,1,0:T(8,128)(2,1)S(1)}, bf16[4,256,256]{2,1,0:T(8,128)(2,1)S(1)}, bf16[640,4096]{1,0:T(8,...) custom-call(f32[1,2,512,2048]{3,2,1,0:T(8,128)} %green_ref.1, ...), custom_call_target="tpu_custom_call" | custom-call | flops 33554432 | bytes 1048576 | tf_op jit(solution)/shard_map/lesser_own/pallas_call | solution.py:202
  12.8 7.1 %collective-permute-start.5 = (f32[2,64,2048]{2,1,0:T(8,128)S(1)}, f32[2,64,2048]{2,1,0:T(8,128)S(1)}, u32[]{:S(2)}, u32[]{:S(2)}) collective-permute-start(f32[2,64,2048]{2,1,0:T(8,128)S(1)} %get-tuple-element.32), channel_id=1, source_target_pairs={{0,1},{3,2},{4,5},{7,6},{8,9},{11,10},{12,13},{15,14},{16,17},{19,... | collective-permute-start | bytes 3145736 | tf_op jit(solution)/shard_map/ppermute | solution.py:521
  20.0 0.7 collective-permute-start.2
  20.7 1.3 %collective-permute-start.3 = (f32[1,4,2,128,128]{4,3,2,1,0:T(8,128)S(1)}, f32[1,4,2,128,128]{4,3,2,1,0:T(8,128)S(1)}, u32[]{:S(2)}, u32[]{:S(2)}) collective-permute-start(f32[1,4,2,128,128]{4,3,2,1,0:T(8,128)S(1)} %get-tuple-element.28.rest_1_), channel_id=1, source_target_pairs={{1,0},{2,3},{5,4},{6,7},{9,8},{10,11},{13,12},{14,15},{17,16},{18,... | collective-permute-start | bytes 1572872 | tf_op jit(solution)/shard_map/ppermute | solution.py:521
  22.0 0.7 collective-permute-start.6
  22.7 3.0 %lesser_more.3 = (f32[4,256,256]{2,1,0:T(8,128)S(1)}, bf16[8,256,256]{2,1,0:T(8,128)(2,1)S(1)}, bf16[8,256,256]{2,1,0:T(8,128)(2,1)S(1)}) custom-call(bf16[640,4096]{1,0:T(8,128)(2,1)S(1)} %get-tuple-element.23.hi_ref, bf16[640,4096]{1,0:T(8,128)(2,1)S(1)} %get-tuple-element.24.lo_ref, ...), custom_call_target="tpu_custom_call", output_to_operand_aliasing={{0}: (2, {})} | custom-call | flops 83886080 | bytes 262144 | tf_op jit(solution)/shard_map/lesser_more/pallas_call | solution.py:253
  25.7 1.3 %collective-permute-start.4 = (f32[1,4,2,128,128]{4,3,2,1,0:T(8,128)S(1)}, f32[1,4,2,128,128]{4,3,2,1,0:T(8,128)S(1)}, u32[]{:S(2)}, u32[]{:S(2)}) collective-permute-start(f32[1,4,2,128,128]{4,3,2,1,0:T(8,128)S(1)} %gate.3.rest_0_), channel_id=1, source_target_pairs={{1,0},{2,3},{5,4},{6,7},{9,8},{10,11},{13,12},{14,15},{17,16},{18,... | collective-permute-start | bytes 1572872 | tf_op jit(solution)/shard_map/ppermute | solution.py:521
  27.0 8.6 %collective-permute-done.3.rest_1_ = f32[1,4,2,128,128]{4,3,2,1,0:T(8,128)S(1)} collective-permute-done((f32[1,4,2,128,128]{4,3,2,1,0:T(8,128)S(1)}, f32[1,4,2,128,128]{4,3,2,1,0:T(8,128)S(1)}, u32[]{:S(2)}, u32[]{:S(2)}) %collective-permute-start.3) | collective-permute-done | bytes 524320 | tf_op jit(solution)/shard_map/ppermute | solution.py:521
  35.7 3.0 %lesser_more.4 = (f32[4,256,256]{2,1,0:T(8,128)S(1)}, bf16[8,256,256]{2,1,0:T(8,128)(2,1)S(1)}, bf16[8,256,256]{2,1,0:T(8,128)(2,1)S(1)}) custom-call(bf16[640,4096]{1,0:T(8,128)(2,1)S(1)} %get-tuple-element.23.hi_ref, bf16[640,4096]{1,0:T(8,128)(2,1)S(1)} %get-tuple-element.24.lo_ref, ...), custom_call_target="tpu_custom_call", output_to_operand_aliasing={{0}: (2, {})} | custom-call | flops 83886080 | bytes 262144 | tf_op jit(solution)/shard_map/lesser_more/pallas_call | solution.py:253
  38.7 3.1 %collective-permute-done.5.refs_0_ = f32[2,64,2048]{2,1,0:T(8,128)S(1)} collective-permute-done((f32[2,64,2048]{2,1,0:T(8,128)S(1)}, f32[2,64,2048]{2,1,0:T(8,128)S(1)}, u32[]{:S(2)}, u32[]{:S(2)}) %collective-permute-start.5) | collective-permute-done | bytes 1048608 | tf_op jit(solution)/shard_map/ppermute | solution.py:521
  41.7 0.2 edges.1
  41.9 1.3 %collective-permute-start.7 = (f32[2,64,128]{2,1,0:T(8,128)S(1)}, f32[2,64,128]{2,1,0:T(8,128)S(1)}, u32[]{:S(2)}, u32[]{:S(2)}) collective-permute-start(f32[2,64,128]{2,1,0:T(8,128)S(1)} %get-tuple-element.38.rest_1_), channel_id=1, source_target_pairs={{1,0},{2,3},{5,4},{6,7},{9,8},{10,11},{13,12},{14,15},{17,16},{18,... | collective-permute-start | bytes 196616 | tf_op jit(solution)/shard_map/ppermute | solution.py:521
  43.2 0.7 collective-permute-start.8
  43.9 2.8 %collective-permute-done.4.rest_0_ = f32[1,4,2,128,128]{4,3,2,1,0:T(8,128)S(1)} collective-permute-done((f32[1,4,2,128,128]{4,3,2,1,0:T(8,128)S(1)}, f32[1,4,2,128,128]{4,3,2,1,0:T(8,128)S(1)}, u32[]{:S(2)}, u32[]{:S(2)}) %collective-permute-start.4) | collective-permute-done | bytes 524320 | tf_op jit(solution)/shard_map/ppermute | solution.py:521
  46.7 3.2 %lesser_more.5.acc_ref = f32[4,256,256]{2,1,0:T(8,128)S(1)} custom-call(bf16[640,4096]{1,0:T(8,128)(2,1)S(1)} %get-tuple-element.23.hi_ref, bf16[640,4096]{1,0:T(8,128)(2,1)S(1)} %get-tuple-element.24.lo_ref, f32[4,256,256]{2,1,0:T(8,128)S(1)} %get-tuple-element.31.before_ref, ...), custom_call_target="tpu_custom_call", output_to_operand_aliasing={{}: (2, {})} | custom-call | flops 41943040 | bytes 262144 | tf_op jit(solution)/shard_map/lesser_more/pallas_call | solution.py:253
  49.8 2.1 %collective-permute-done.7.from_left_ref = f32[2,64,128]{2,1,0:T(8,128)S(1)} collective-permute-done((f32[2,64,128]{2,1,0:T(8,128)S(1)}, f32[2,64,128]{2,1,0:T(8,128)S(1)}, u32[]{:S(2)}, u32[]{:S(2)}) %collective-permute-start.7) | collective-permute-done | bytes 65568 | tf_op jit(solution)/shard_map/ppermute | solution.py:521
  51.9 0.6 band.1
  52.5 13.3 %all_to_all.10.recv_ref = f32[8,2,8,8,128]{4,3,2,1,0:T(8,128)S(1)} all-to-all(f32[8,2,8,8,128]{4,3,2,1,0:T(8,128)S(1)} %band.1), channel_id=1, replica_groups=mesh['energy'=8,'orb'=4] {'energy'}, dimensions={0} | all-to-all | bytes 1048576 | tf_op jit(solution)/shard_map/all_to_all | solution.py:625
  65.7 3.7 %scatter.1 = f32[8,128,128]{2,1,0:T(8,128)S(1)} custom-call(f32[8,2,8,8,128]{4,3,2,1,0:T(8,128)S(1)} %all_to_all.10.recv_ref, s32[1,128]{1,0:T(1,128)S(1)} %reshape.79.rest_0_.where_ref, f32[128,128]{1,0:T(8,128)S(1)} %mul.67.rest_1_.mix_ref, f32[192,128]{1,0:T(8,128)S(1)} %constant_dynamic-slice_fusion.rest_2_.dham_ref), custom_call_target="tpu_custom_call" | custom-call | tf_op jit(solution)/shard_map/scatter/pallas_call | solution.py:487
  69.4 12.2 %all_to_all.11 = f32[8,128,128]{2,1,0:T(8,128)S(1)} all-to-all(f32[8,128,128]{2,1,0:T(8,128)S(1)} %scatter.1), channel_id=1, replica_groups=mesh['energy'=8,'orb'=4] {'energy'}, dimensions={0} | all-to-all | bytes 1048576 | tf_op jit(solution)/shard_map/all_to_all | solution.py:627
  81.6 0.8 copy.24
  (12 shorter events, 0.1 us)
Async XLA Ops:
  0.0 6.7 %copy-start = (f32[1024,3,8,8]{0,3,2,1:T(8,128)S(1)}, f32[1024,3,8,8]{0,3,2,1:T(8,128)}, u32[]{:S(2)}) copy-start(f32[1024,3,8,8]{0,3,2,1:T(8,128)} %param.11) | copy-start | bytes 2359300
  0.0 20.0 %collective-permute-start = (f32[1,4,2,128,128]{4,3,2,1,0:T(8,128)}, f32[1,4,2,128,128]{4,3,2,1,0:T(8,128)S(1)}, u32[]{:S(2)}, u32[]{:S(2)}) collective-permute-start(f32[1,4,2,128,128]{4,3,2,1,0:T(8,128)} %sigma_ref.1), channel_id=1, source_target_pairs={{0,1},{3,2},{1,0},{2,3},{4,5},{7,6},{5,4},{6,7},{8,9},{11,10},{9,8... | collective-permute-start | bytes 1572872 | tf_op jit(solution)/shard_map/ppermute | solution.py:521
  3.0 17.0 %collective-permute-start.1 = (f32[1,4,2,128,128]{4,3,2,1,0:T(8,128)}, f32[1,4,2,128,128]{4,3,2,1,0:T(8,128)S(1)}, u32[]{:S(2)}, u32[]{:S(2)}) collective-permute-start(f32[1,4,2,128,128]{4,3,2,1,0:T(8,128)} %sigma_ref.1), channel_id=1, source_target_pairs={{1,2},{2,1},{5,6},{6,5},{9,10},{10,9},{13,14},{14,13},{17,18},{18,... | collective-permute-start | bytes 1572872 | tf_op jit(solution)/shard_map/ppermute | solution.py:521
  12.8 28.9 %collective-permute-start.5 = (f32[2,64,2048]{2,1,0:T(8,128)S(1)}, f32[2,64,2048]{2,1,0:T(8,128)S(1)}, u32[]{:S(2)}, u32[]{:S(2)}) collective-permute-start(f32[2,64,2048]{2,1,0:T(8,128)S(1)} %get-tuple-element.32), channel_id=1, source_target_pairs={{0,1},{3,2},{4,5},{7,6},{8,9},{11,10},{12,13},{15,14},{16,17},{19,... | collective-permute-start | bytes 3145736 | tf_op jit(solution)/shard_map/ppermute | solution.py:521
  20.0 5.7 %collective-permute-start.2 = (f32[1,4,2,128,128]{4,3,2,1,0:T(8,128)S(1)}, f32[1,4,2,128,128]{4,3,2,1,0:T(8,128)S(1)}, u32[]{:S(2)}, u32[]{:S(2)}) collective-permute-start(f32[1,4,2,128,128]{4,3,2,1,0:T(8,128)S(1)} %get-tuple-element.27.rest_0_), channel_id=1, source_target_pairs={{1,2},{2,1},{5,6},{6,5},{9,10},{10,9},{13,14},{14,13},{17,18},{18,... | collective-permute-start | bytes 1572872 | tf_op jit(solution)/shard_map/ppermute | solution.py:521
  20.7 15.0 %collective-permute-start.3 = (f32[1,4,2,128,128]{4,3,2,1,0:T(8,128)S(1)}, f32[1,4,2,128,128]{4,3,2,1,0:T(8,128)S(1)}, u32[]{:S(2)}, u32[]{:S(2)}) collective-permute-start(f32[1,4,2,128,128]{4,3,2,1,0:T(8,128)S(1)} %get-tuple-element.28.rest_1_), channel_id=1, source_target_pairs={{1,0},{2,3},{5,4},{6,7},{9,8},{10,11},{13,12},{14,15},{17,16},{18,... | collective-permute-start | bytes 1572872 | tf_op jit(solution)/shard_map/ppermute | solution.py:521
  22.0 16.7 %collective-permute-start.6 = (f32[2,32,2048]{2,1,0:T(8,128)S(1)}, f32[2,32,2048]{2,1,0:T(8,128)S(1)}, u32[]{:S(2)}, u32[]{:S(2)}) collective-permute-start(f32[2,32,2048]{2,1,0:T(8,128)S(1)} %get-tuple-element.33), channel_id=1, source_target_pairs={{1,2},{2,1},{5,6},{6,5},{9,10},{10,9},{13,14},{14,13},{17,18},{18,... | collective-permute-start | bytes 1572872 | tf_op jit(solution)/shard_map/ppermute | solution.py:521
  25.7 20.9 %collective-permute-start.4 = (f32[1,4,2,128,128]{4,3,2,1,0:T(8,128)S(1)}, f32[1,4,2,128,128]{4,3,2,1,0:T(8,128)S(1)}, u32[]{:S(2)}, u32[]{:S(2)}) collective-permute-start(f32[1,4,2,128,128]{4,3,2,1,0:T(8,128)S(1)} %gate.3.rest_0_), channel_id=1, source_target_pairs={{1,0},{2,3},{5,4},{6,7},{9,8},{10,11},{13,12},{14,15},{17,16},{18,... | collective-permute-start | bytes 1572872 | tf_op jit(solution)/shard_map/ppermute | solution.py:521
  41.9 10.0 %collective-permute-start.7 = (f32[2,64,128]{2,1,0:T(8,128)S(1)}, f32[2,64,128]{2,1,0:T(8,128)S(1)}, u32[]{:S(2)}, u32[]{:S(2)}) collective-permute-start(f32[2,64,128]{2,1,0:T(8,128)S(1)} %get-tuple-element.38.rest_1_), channel_id=1, source_target_pairs={{1,0},{2,3},{5,4},{6,7},{9,8},{10,11},{13,12},{14,15},{17,16},{18,... | collective-permute-start | bytes 196616 | tf_op jit(solution)/shard_map/ppermute | solution.py:521
  43.2 8.7 %collective-permute-start.8 = (f32[2,64,128]{2,1,0:T(8,128)S(1)}, f32[2,64,128]{2,1,0:T(8,128)S(1)}, u32[]{:S(2)}, u32[]{:S(2)}) collective-permute-start(f32[2,64,128]{2,1,0:T(8,128)S(1)} %get-tuple-element.40), channel_id=1, source_target_pairs={{1,2},{2,1},{5,6},{6,5},{9,10},{10,9},{13,14},{14,13},{17,18},{18,... | collective-permute-start | bytes 196616 | tf_op jit(solution)/shard_map/ppermute | solution.py:521

commit v10 on v9

--- a/solution.py
+++ b/solution.py
@@ -339,6 +339,9 @@
         for k, shards in enumerate(places):
             for n, place in enumerate(shards):
                 number, valid = place()
+                if paired:
+                    add(number, keeps[2 * k], keeps[2 * k + 1], n * held)
+                    continue
 
                 @pl.when(valid)
                 def _():
@@ -435,7 +438,9 @@
     )(acc, own, from_left, from_right)
 
 
-def scatter_kernel(recv_ref, where_ref, mix_ref, dham_ref, out_ref, smeared_ref, result_ref):
+def scatter_kernel(
+    recv_ref, where_ref, mix_ref, dham_ref, out_ref, smeared_ref, result_ref, factor_ref
+):
     energies, _, group, _, _ = recv_ref.shape
     padded = dham_ref.shape[1]
     pairs = out_ref.shape[1]
@@ -443,34 +448,35 @@
         recv_ref[:, :, a, :, :].reshape(energies * 2 * W, LANES) for a in range(group)
     ]
     received = halves(jnp.concatenate(columns, axis=1))
-    mixed = halves(dot3(halves(mix_ref[...]), received, NN))
+    mixed = jnp.concatenate(halves(dot3(halves(mix_ref[...]), received, NN)), axis=0)
+    rows = smeared_ref.shape[0]
     entry = lax.broadcasted_iota(jnp.int32, (group * LANES, padded), 0)
-    first = where_ref[...] * W
-    for j in range(W):
-        pick = jnp.where(entry == first + j, 1.0, 0.0).astype(BF16)
-        smeared_ref[:, j * padded : (j + 1) * padded] = dot(mixed[0], pick, NN) + dot(
-            mixed[1], pick, NN
+    offset = entry - where_ref[...] * W
+    for j in range(0, W, 2):
+        pick = jnp.concatenate(
+            [jnp.where(offset == j + n, 1.0, 0.0).astype(BF16) for n in range(2)], axis=1
         )
+        both = dot(mixed, pick, NN)
+        smeared_ref[:, j * padded : (j + 2) * padded] = both[:rows] + both[rows:]
+    for row in range(dham_ref.shape[0]):
+        factor_ref[row] = jnp.broadcast_to(dham_ref[row : row + 1, :], (energies, padded))
 
     def block(part, j, k):
         row = (part * W + j) * energies
         return smeared_ref[row : row + energies, k * padded : (k + 1) * padded]
-
-    def factor(c, i, j):
-        row = (c * W + i) * W + j
-        return dham_ref[row : row + 1, :]
 
     for part in range(2):
         for i in range(W):
             total = [None] * W
             for c in range(3):
+                factors = [factor_ref[(c * W + i) * W + j] for j in range(W)]
                 for k in range(W):
                     t = None
                     for j in range(W):
-                        term = factor(c, i, j) * block(part, j, k)
+                        term = factors[j] * block(part, j, k)
                         t = term if t is None else t + term
                     for l in range(W):
-                        term = t * factor(c, l, k)
+                        term = t * factor_ref[(c * W + l) * W + k]
                         total[l] = term if total[l] is None else total[l] + term
             for l in range(W):
                 row = ((part * W + i) * W + l) * energies
@@ -492,6 +498,7 @@
         scratch_shapes=[
             pltpu.VMEM((2 * W * energies, W * padded), F32),
             pltpu.VMEM((2 * W * W * energies, padded), F32),
+            pltpu.VMEM((dham.shape[0], energies, padded), F32),
         ],
         compiler_params=pltpu.CompilerParams(vmem_limit_bytes=24 << 20),
         name="scatter",
@@ -586,7 +593,9 @@
         places.append([two_off(True), two_off(False)])
         acc, *kept = more(acc, [second_across, second_aside], places[-1])
         keeps += kept
-        to_end, to_middle, own = edge_part(halos, keeps, places, held, True)
+        to_end, to_middle, own = edge_part(
+            halos, keeps, [*places[:-1], places[-1][:1]], held, True
+        )
         back_left, back_right = send(to_end, outward), send(to_middle, middle)
         (acc,) = more(acc, [third_aside], [reflected(3, False)], after=[to_end], keep=False)
     else:

time: 83.7 us -> 82.2 us (0.982)
  Pallas kernels: 19.7 us -> 18.7 us
    pallas_call x1, Pallas kernels: 3.66 us -> 2.67 us  [scatter(): pl.pallas_call(scatter_kernel, out_shape=jax.ShapeDtypeStruct((energies,...]
where the time goes in v10:
time: 82.2 us; the launch traced here: 80.8 us
  blocking collectives  25.4 us (31%)
  Pallas kernels  18.7 us (23%)
  starting transfers between devices  16.8 us (20%)
  waiting for transfers between devices  16 us (19%)
  local copies, waits for them, and re-layouts  2.69 us (3%)
  other arithmetic  1.02 us (1%)
    ppermute x9, starting transfers between devices, send(): return lax.ppermute(x, 'orb', pairs)  16.8 us
    ppermute x9, waiting for transfers between devices, send(): return lax.ppermute(x, 'orb', pairs)  16 us
    all_to_all x1, blocking collectives, per_device(): lax.all_to_all(lesser, 'energy', split_axis=0, concat_axis=0, tiled=True)  13.3 us
    all_to_all x1, blocking collectives, per_device(): lax.all_to_all(spread, 'energy', split_axis=0, concat_axis=0, tiled=True)  12.2 us
    pallas_call x3, Pallas kernels, lesser_part(): pl.pallas_call(functools.partial(lesser_kernel, places, held, len(after))...  9.16 us
    pallas_call x1, Pallas kernels, own_part(): pl.pallas_call(functools.partial(own_kernel, wanted, len(after)), out_sha...  6.13 us
    pallas_call x1, Pallas kernels, scatter(): pl.pallas_call(scatter_kernel, out_shape=jax.ShapeDtypeStruct((energies,...  2.67 us
  transfers between devices with their start and end apart: 9, of which 4 were waited for; matrix products, arithmetic and copies ran while one was open for 4% of the time, Pallas kernels for 19%

profile of v10, /device:TPU:0, one launch (start us, length us, event | category | flops | bytes accessed | tf_op | source)
XLA Modules:
  0.0 80.8 jit_solution(16768921178282985500)
XLA Ops:
  0.0 3.0 %collective-permute-start = (f32[1,4,2,128,128]{4,3,2,1,0:T(8,128)}, f32[1,4,2,128,128]{4,3,2,1,0:T(8,128)S(1)}, u32[]{:S(2)}, u32[]{:S(2)}) collective-permute-start(f32[1,4,2,128,128]{4,3,2,1,0:T(8,128)} %sigma_ref.1), channel_id=1, source_target_pairs={{0,1},{3,2},{1,0},{2,3},{4,5},{7,6},{5,4},{6,7},{8,9},{11,10},{9,8... | collective-permute-start | bytes 1572872 | tf_op jit(solution)/shard_map/ppermute | solution.py:528
  3.0 0.7 collective-permute-start.1
  3.7 0.8 constant_dynamic-slice_fusion.1
  4.5 0.1 copy.16
  4.6 0.1 select_add_fusion
  4.7 0.1 reshape.79.rest_0_.where_ref
  4.7 0.7 iota_add_fusion
  5.5 0.8 slice_bitcast_fusion.1
  6.2 0.1 add_reduce_fusion
  6.3 0.1 broadcast_multiply_fusion
  6.5 0.2 mul.67.rest_1_.mix_ref
  6.7 6.1 %lesser_own.1 = (f32[4,256,256]{2,1,0:T(8,128)S(1)}, bf16[4,256,256]{2,1,0:T(8,128)(2,1)S(1)}, bf16[4,256,256]{2,1,0:T(8,128)(2,1)S(1)}, bf16[640,4096]{1,0:T(8,...) custom-call(f32[1,2,512,2048]{3,2,1,0:T(8,128)} %green_ref.1, ...), custom_call_target="tpu_custom_call" | custom-call | flops 33554432 | bytes 1048576 | tf_op jit(solution)/shard_map/lesser_own/pallas_call | solution.py:202
  12.8 7.1 %collective-permute-start.5 = (f32[2,64,2048]{2,1,0:T(8,128)S(1)}, f32[2,64,2048]{2,1,0:T(8,128)S(1)}, u32[]{:S(2)}, u32[]{:S(2)}) collective-permute-start(f32[2,64,2048]{2,1,0:T(8,128)S(1)} %get-tuple-element.32), channel_id=1, source_target_pairs={{0,1},{3,2},{4,5},{7,6},{8,9},{11,10},{12,13},{15,14},{16,17},{19,... | collective-permute-start | bytes 3145736 | tf_op jit(solution)/shard_map/ppermute | solution.py:528
  20.0 0.7 collective-permute-start.2
  20.7 1.3 %collective-permute-start.3 = (f32[1,4,2,128,128]{4,3,2,1,0:T(8,128)S(1)}, f32[1,4,2,128,128]{4,3,2,1,0:T(8,128)S(1)}, u32[]{:S(2)}, u32[]{:S(2)}) collective-permute-start(f32[1,4,2,128,128]{4,3,2,1,0:T(8,128)S(1)} %get-tuple-element.28.rest_1_), channel_id=1, source_target_pairs={{1,0},{2,3},{5,4},{6,7},{9,8},{10,11},{13,12},{14,15},{17,16},{18,... | collective-permute-start | bytes 1572872 | tf_op jit(solution)/shard_map/ppermute | solution.py:528
  22.0 0.7 collective-permute-start.6
  22.7 3.0 %lesser_more.3 = (f32[4,256,256]{2,1,0:T(8,128)S(1)}, bf16[8,256,256]{2,1,0:T(8,128)(2,1)S(1)}, bf16[8,256,256]{2,1,0:T(8,128)(2,1)S(1)}) custom-call(bf16[640,4096]{1,0:T(8,128)(2,1)S(1)} %get-tuple-element.23.hi_ref, bf16[640,4096]{1,0:T(8,128)(2,1)S(1)} %get-tuple-element.24.lo_ref, ...), custom_call_target="tpu_custom_call", output_to_operand_aliasing={{0}: (2, {})} | custom-call | flops 83886080 | bytes 262144 | tf_op jit(solution)/shard_map/lesser_more/pallas_call | solution.py:253
  25.7 1.3 %collective-permute-start.4 = (f32[1,4,2,128,128]{4,3,2,1,0:T(8,128)S(1)}, f32[1,4,2,128,128]{4,3,2,1,0:T(8,128)S(1)}, u32[]{:S(2)}, u32[]{:S(2)}) collective-permute-start(f32[1,4,2,128,128]{4,3,2,1,0:T(8,128)S(1)} %gate.3.rest_0_), channel_id=1, source_target_pairs={{1,0},{2,3},{5,4},{6,7},{9,8},{10,11},{13,12},{14,15},{17,16},{18,... | collective-permute-start | bytes 1572872 | tf_op jit(solution)/shard_map/ppermute | solution.py:528
  27.0 8.6 %collective-permute-done.3.rest_1_ = f32[1,4,2,128,128]{4,3,2,1,0:T(8,128)S(1)} collective-permute-done((f32[1,4,2,128,128]{4,3,2,1,0:T(8,128)S(1)}, f32[1,4,2,128,128]{4,3,2,1,0:T(8,128)S(1)}, u32[]{:S(2)}, u32[]{:S(2)}) %collective-permute-start.3) | collective-permute-done | bytes 524320 | tf_op jit(solution)/shard_map/ppermute | solution.py:528
  35.7 3.0 %lesser_more.4 = (f32[4,256,256]{2,1,0:T(8,128)S(1)}, bf16[8,256,256]{2,1,0:T(8,128)(2,1)S(1)}, bf16[8,256,256]{2,1,0:T(8,128)(2,1)S(1)}) custom-call(bf16[640,4096]{1,0:T(8,128)(2,1)S(1)} %get-tuple-element.23.hi_ref, bf16[640,4096]{1,0:T(8,128)(2,1)S(1)} %get-tuple-element.24.lo_ref, ...), custom_call_target="tpu_custom_call", output_to_operand_aliasing={{0}: (2, {})} | custom-call | flops 83886080 | bytes 262144 | tf_op jit(solution)/shard_map/lesser_more/pallas_call | solution.py:253
  38.7 3.1 %collective-permute-done.5.refs_0_ = f32[2,64,2048]{2,1,0:T(8,128)S(1)} collective-permute-done((f32[2,64,2048]{2,1,0:T(8,128)S(1)}, f32[2,64,2048]{2,1,0:T(8,128)S(1)}, u32[]{:S(2)}, u32[]{:S(2)}) %collective-permute-start.5) | collective-permute-done | bytes 1048608 | tf_op jit(solution)/shard_map/ppermute | solution.py:528
  41.7 0.2 edges.1
  41.9 1.3 %collective-permute-start.7 = (f32[2,64,128]{2,1,0:T(8,128)S(1)}, f32[2,64,128]{2,1,0:T(8,128)S(1)}, u32[]{:S(2)}, u32[]{:S(2)}) collective-permute-start(f32[2,64,128]{2,1,0:T(8,128)S(1)} %get-tuple-element.38.rest_1_), channel_id=1, source_target_pairs={{1,0},{2,3},{5,4},{6,7},{9,8},{10,11},{13,12},{14,15},{17,16},{18,... | collective-permute-start | bytes 196616 | tf_op jit(solution)/shard_map/ppermute | solution.py:528
  43.2 0.7 collective-permute-start.8
  43.9 2.8 %collective-permute-done.4.rest_0_ = f32[1,4,2,128,128]{4,3,2,1,0:T(8,128)S(1)} collective-permute-done((f32[1,4,2,128,128]{4,3,2,1,0:T(8,128)S(1)}, f32[1,4,2,128,128]{4,3,2,1,0:T(8,128)S(1)}, u32[]{:S(2)}, u32[]{:S(2)}) %collective-permute-start.4) | collective-permute-done | bytes 524320 | tf_op jit(solution)/shard_map/ppermute | solution.py:528
  46.7 3.2 %lesser_more.5.acc_ref = f32[4,256,256]{2,1,0:T(8,128)S(1)} custom-call(bf16[640,4096]{1,0:T(8,128)(2,1)S(1)} %get-tuple-element.23.hi_ref, bf16[640,4096]{1,0:T(8,128)(2,1)S(1)} %get-tuple-element.24.lo_ref, f32[4,256,256]{2,1,0:T(8,128)S(1)} %get-tuple-element.31.before_ref, ...), custom_call_target="tpu_custom_call", output_to_operand_aliasing={{}: (2, {})} | custom-call | flops 41943040 | bytes 262144 | tf_op jit(solution)/shard_map/lesser_more/pallas_call | solution.py:253
  49.8 1.5 %collective-permute-done.7.from_left_ref = f32[2,64,128]{2,1,0:T(8,128)S(1)} collective-permute-done((f32[2,64,128]{2,1,0:T(8,128)S(1)}, f32[2,64,128]{2,1,0:T(8,128)S(1)}, u32[]{:S(2)}, u32[]{:S(2)}) %collective-permute-start.7) | collective-permute-done | bytes 65568 | tf_op jit(solution)/shard_map/ppermute | solution.py:528
  51.4 0.6 band.1
  51.9 13.3 %all_to_all.10.recv_ref = f32[8,2,8,8,128]{4,3,2,1,0:T(8,128)S(1)} all-to-all(f32[8,2,8,8,128]{4,3,2,1,0:T(8,128)S(1)} %band.1), channel_id=1, replica_groups=mesh['energy'=8,'orb'=4] {'energy'}, dimensions={0} | all-to-all | bytes 1048576 | tf_op jit(solution)/shard_map/all_to_all | solution.py:634
  65.2 2.7 %scatter.1 = f32[8,128,128]{2,1,0:T(8,128)S(1)} custom-call(f32[8,2,8,8,128]{4,3,2,1,0:T(8,128)S(1)} %all_to_all.10.recv_ref, s32[1,128]{1,0:T(1,128)S(1)} %reshape.79.rest_0_.where_ref, f32[128,128]{1,0:T(8,128)S(1)} %mul.67.rest_1_.mix_ref, f32[192,128]{1,0:T(8,128)S(1)} %constant_dynamic-slice_fusion.rest_2_.dham_ref), custom_call_target="tpu_custom_call" | custom-call | tf_op jit(solution)/shard_map/scatter/pallas_call | solution.py:493
  67.9 12.2 %all_to_all.11 = f32[8,128,128]{2,1,0:T(8,128)S(1)} all-to-all(f32[8,128,128]{2,1,0:T(8,128)S(1)} %scatter.1), channel_id=1, replica_groups=mesh['energy'=8,'orb'=4] {'energy'}, dimensions={0} | all-to-all | bytes 1048576 | tf_op jit(solution)/shard_map/all_to_all | solution.py:636
  80.1 0.8 copy.24
  (12 shorter events, 0.1 us)
Async XLA Ops:
  0.0 6.7 %copy-start = (f32[1024,3,8,8]{0,3,2,1:T(8,128)S(1)}, f32[1024,3,8,8]{0,3,2,1:T(8,128)}, u32[]{:S(2)}) copy-start(f32[1024,3,8,8]{0,3,2,1:T(8,128)} %param.11) | copy-start | bytes 2359300
  0.0 20.0 %collective-permute-start = (f32[1,4,2,128,128]{4,3,2,1,0:T(8,128)}, f32[1,4,2,128,128]{4,3,2,1,0:T(8,128)S(1)}, u32[]{:S(2)}, u32[]{:S(2)}) collective-permute-start(f32[1,4,2,128,128]{4,3,2,1,0:T(8,128)} %sigma_ref.1), channel_id=1, source_target_pairs={{0,1},{3,2},{1,0},{2,3},{4,5},{7,6},{5,4},{6,7},{8,9},{11,10},{9,8... | collective-permute-start | bytes 1572872 | tf_op jit(solution)/shard_map/ppermute | solution.py:528
  3.0 17.0 %collective-permute-start.1 = (f32[1,4,2,128,128]{4,3,2,1,0:T(8,128)}, f32[1,4,2,128,128]{4,3,2,1,0:T(8,128)S(1)}, u32[]{:S(2)}, u32[]{:S(2)}) collective-permute-start(f32[1,4,2,128,128]{4,3,2,1,0:T(8,128)} %sigma_ref.1), channel_id=1, source_target_pairs={{1,2},{2,1},{5,6},{6,5},{9,10},{10,9},{13,14},{14,13},{17,18},{18,... | collective-permute-start | bytes 1572872 | tf_op jit(solution)/shard_map/ppermute | solution.py:528
  12.8 28.9 %collective-permute-start.5 = (f32[2,64,2048]{2,1,0:T(8,128)S(1)}, f32[2,64,2048]{2,1,0:T(8,128)S(1)}, u32[]{:S(2)}, u32[]{:S(2)}) collective-permute-start(f32[2,64,2048]{2,1,0:T(8,128)S(1)} %get-tuple-element.32), channel_id=1, source_target_pairs={{0,1},{3,2},{4,5},{7,6},{8,9},{11,10},{12,13},{15,14},{16,17},{19,... | collective-permute-start | bytes 3145736 | tf_op jit(solution)/shard_map/ppermute | solution.py:528
  20.0 5.7 %collective-permute-start.2 = (f32[1,4,2,128,128]{4,3,2,1,0:T(8,128)S(1)}, f32[1,4,2,128,128]{4,3,2,1,0:T(8,128)S(1)}, u32[]{:S(2)}, u32[]{:S(2)}) collective-permute-start(f32[1,4,2,128,128]{4,3,2,1,0:T(8,128)S(1)} %get-tuple-element.27.rest_0_), channel_id=1, source_target_pairs={{1,2},{2,1},{5,6},{6,5},{9,10},{10,9},{13,14},{14,13},{17,18},{18,... | collective-permute-start | bytes 1572872 | tf_op jit(solution)/shard_map/ppermute | solution.py:528
  20.7 15.0 %collective-permute-start.3 = (f32[1,4,2,128,128]{4,3,2,1,0:T(8,128)S(1)}, f32[1,4,2,128,128]{4,3,2,1,0:T(8,128)S(1)}, u32[]{:S(2)}, u32[]{:S(2)}) collective-permute-start(f32[1,4,2,128,128]{4,3,2,1,0:T(8,128)S(1)} %get-tuple-element.28.rest_1_), channel_id=1, source_target_pairs={{1,0},{2,3},{5,4},{6,7},{9,8},{10,11},{13,12},{14,15},{17,16},{18,... | collective-permute-start | bytes 1572872 | tf_op jit(solution)/shard_map/ppermute | solution.py:528
  22.0 16.7 %collective-permute-start.6 = (f32[2,32,2048]{2,1,0:T(8,128)S(1)}, f32[2,32,2048]{2,1,0:T(8,128)S(1)}, u32[]{:S(2)}, u32[]{:S(2)}) collective-permute-start(f32[2,32,2048]{2,1,0:T(8,128)S(1)} %get-tuple-element.33), channel_id=1, source_target_pairs={{1,2},{2,1},{5,6},{6,5},{9,10},{10,9},{13,14},{14,13},{17,18},{18,... | collective-permute-start | bytes 1572872 | tf_op jit(solution)/shard_map/ppermute | solution.py:528
  25.7 20.9 %collective-permute-start.4 = (f32[1,4,2,128,128]{4,3,2,1,0:T(8,128)S(1)}, f32[1,4,2,128,128]{4,3,2,1,0:T(8,128)S(1)}, u32[]{:S(2)}, u32[]{:S(2)}) collective-permute-start(f32[1,4,2,128,128]{4,3,2,1,0:T(8,128)S(1)} %gate.3.rest_0_), channel_id=1, source_target_pairs={{1,0},{2,3},{5,4},{6,7},{9,8},{10,11},{13,12},{14,15},{17,16},{18,... | collective-permute-start | bytes 1572872 | tf_op jit(solution)/shard_map/ppermute | solution.py:528
  41.9 9.4 %collective-permute-start.7 = (f32[2,64,128]{2,1,0:T(8,128)S(1)}, f32[2,64,128]{2,1,0:T(8,128)S(1)}, u32[]{:S(2)}, u32[]{:S(2)}) collective-permute-start(f32[2,64,128]{2,1,0:T(8,128)S(1)} %get-tuple-element.38.rest_1_), channel_id=1, source_target_pairs={{1,0},{2,3},{5,4},{6,7},{9,8},{10,11},{13,12},{14,15},{17,16},{18,... | collective-permute-start | bytes 196616 | tf_op jit(solution)/shard_map/ppermute | solution.py:528
  43.2 8.1 %collective-permute-start.8 = (f32[2,64,128]{2,1,0:T(8,128)S(1)}, f32[2,64,128]{2,1,0:T(8,128)S(1)}, u32[]{:S(2)}, u32[]{:S(2)}) collective-permute-start(f32[2,64,128]{2,1,0:T(8,128)S(1)} %get-tuple-element.40), channel_id=1, source_target_pairs={{1,2},{2,1},{5,6},{6,5},{9,10},{10,9},{13,14},{14,13},{17,18},{18,... | collective-permute-start | bytes 196616 | tf_op jit(solution)/shard_map/ppermute | solution.py:528

commit v11 on v10

--- a/solution.py
+++ b/solution.py
@@ -284,8 +284,8 @@
     )(*arrays, *after)
 
 
-def edge_kernel(places, held, paired, *refs):
-    halos, refs = refs[: 2 if paired else 3], refs[2 if paired else 3 :]
+def edge_kernel(places, held, *refs):
+    halos, refs = refs[:3], refs[3:]
     keeps = refs[: 2 * len(places)]
     left_ref, right_ref, own_ref, acc_ref = refs[2 * len(places) :]
     z, peers = lax.axis_index("orb"), lax.axis_size("orb")
@@ -297,15 +297,7 @@
     acc_ref[...] = jnp.zeros_like(acc_ref)
 
     def rows_of(part, cols):
-        if not paired:
-            return [ref[part, :, cols] for ref in halos]
-        first, second = halos[0][part, :HALF, cols], halos[0][part, HALF:, cols]
-        middle = halos[1][part, :, cols]
-        return (
-            jnp.where(from_left, first, second),
-            jnp.where(from_left, second, middle),
-            jnp.where(from_left, middle, first),
-        )
+        return [ref[part, :, cols] for ref in halos]
 
     def add(number, hi, lo, at):
         cols = pl.ds(pl.multiple_of(number * held * BS, BS), held * BS)
@@ -339,9 +331,6 @@
         for k, shards in enumerate(places):
             for n, place in enumerate(shards):
                 number, valid = place()
-                if paired:
-                    add(number, keeps[2 * k], keeps[2 * k + 1], n * held)
-                    continue
 
                 @pl.when(valid)
                 def _():
@@ -357,11 +346,6 @@
         sign = 1.0 - 2.0 * part
         to_left = jnp.where(low, 0.0, sign * left[rows])
         to_right = jnp.where(lane < limit, sign * right[rows], 0.0)
-        if paired:
-            to_left, to_right = (
-                jnp.where(from_left, to_left, to_right),
-                jnp.where(from_left, to_right, to_left),
-            )
         left_ref[part] = to_left
         right_ref[part] = to_right
     own_ref[0, 0] = jnp.where(low, turned_left, 0.0)
@@ -371,11 +355,11 @@
     own_ref[1, 1] = jnp.where(mine, turned_right, 0.0)
 
 
-def edge_part(halos, keeps, places, held, paired=False):
+def edge_part(halos, keeps, places, held):
     vmem = pl.BlockSpec(memory_space=pltpu.VMEM)
     side = jax.ShapeDtypeStruct((2, MARGIN, LANES), F32)
     return pl.pallas_call(
-        functools.partial(edge_kernel, places, held, paired),
+        functools.partial(edge_kernel, places, held),
         out_shape=(side, side, jax.ShapeDtypeStruct((2, 2, MARGIN, LANES), F32)),
         in_specs=[vmem] * (len(halos) + len(keeps)),
         out_specs=(vmem, vmem, vmem),
@@ -386,6 +370,95 @@
         ),
         name="edges",
     )(*halos, *keeps)
+
+
+def pair_edge_kernel(middle, shards, held, *refs):
+    halo_ref, keeps, refs = refs[0], refs[1 : 1 + 2 * len(shards)], refs[1 + 2 * len(shards) :]
+    if middle:
+        before_ref, refs = refs[0], refs[1:]
+    send_ref, own_ref, acc_ref = refs
+    z = lax.axis_index("orb")
+    on_left = (z == 2) if middle else (z == 1)
+    count = halo_ref.shape[1]
+    begin = pl.multiple_of(jnp.where(on_left, 0, TILE), TILE)
+    acc_ref[...] = jnp.zeros_like(acc_ref)
+
+    @pl.when(is_inner())
+    def _():
+        for k, group in enumerate(shards):
+            for n, place in enumerate(group):
+                number, _ = place()
+                cols = pl.ds(pl.multiple_of(number * held * BS, BS), held * BS)
+                fields = [halves(halo_ref[part, :, cols]) for part in range(2)]
+                halo = []
+                for real, imag in zip(*fields):
+                    lanes = []
+                    for s in range(held):
+                        one = slice(s * BS, (s + 1) * BS)
+                        lanes += [
+                            jnp.concatenate([real[:, one], -imag[:, one]], axis=0),
+                            jnp.concatenate([imag[:, one], real[:, one]], axis=0),
+                        ]
+                    halo.append(jnp.concatenate(lanes, axis=1))
+                kept = [
+                    jnp.concatenate(
+                        [ref[n * held + s, pl.ds(begin, TILE), :] for s in range(held)], axis=1
+                    )
+                    for ref in keeps[2 * k : 2 * k + 2]
+                ]
+                acc_ref[...] = acc_ref[...] + dot3(halo, kept, NT)
+
+    limit = HALF if middle else MARGIN
+    lane = lax.broadcasted_iota(jnp.int32, (MARGIN, LANES), 1)
+    row = lax.broadcasted_iota(jnp.int32, (MARGIN, LANES), 0)
+    low = lane < MARGIN
+    mine = jnp.logical_and(row < limit, lane >= MARGIN)
+    parts = [acc_ref[part * count : (part + 1) * count, :] for part in range(2)]
+    if middle:
+        none = jnp.zeros((MARGIN - count, LANES), F32)
+        parts = [
+            jnp.where(
+                on_left,
+                jnp.concatenate([none, x], axis=0),
+                jnp.concatenate([x, none], axis=0),
+            )
+            for x in parts
+        ]
+    for part, sign in enumerate((1.0, -1.0)):
+        x = sign * parts[part]
+        send_ref[part] = jnp.where(
+            on_left, jnp.where(low, 0.0, x), jnp.where(lane < limit, x, 0.0)
+        )
+    turned = jnp.concatenate(parts, axis=0).T
+    left, right = turned[:MARGIN], turned[MARGIN:]
+    lefts = left, pltpu.roll(left, MARGIN, 1)
+    rights = pltpu.roll(right, MARGIN, 1), right
+    for part in range(2):
+        own = [
+            jnp.where(on_left, jnp.where(low, lefts[part], 0.0), 0.0),
+            jnp.where(on_left, 0.0, jnp.where(mine, rights[part], 0.0)),
+        ]
+        for side in range(2):
+            own_ref[side, part] = own[side] + (before_ref[side, part] if middle else 0.0)
+
+
+def pair_edge_part(halo, keeps, shards, held, before=None):
+    vmem = pl.BlockSpec(memory_space=pltpu.VMEM)
+    middle = before is not None
+    args = [halo, *keeps] + ([before] if middle else [])
+    return pl.pallas_call(
+        functools.partial(pair_edge_kernel, middle, shards, held),
+        out_shape=(
+            jax.ShapeDtypeStruct((2, MARGIN, LANES), F32),
+            jax.ShapeDtypeStruct((2, 2, MARGIN, LANES), F32),
+        ),
+        in_specs=[vmem] * len(args),
+        out_specs=(vmem, vmem),
+        scratch_shapes=[pltpu.VMEM((2 * halo.shape[1], TILE), F32)],
+        compiler_params=pltpu.CompilerParams(vmem_limit_bytes=20 << 20),
+        cost_estimate=pl.CostEstimate(flops=1 << 30, bytes_accessed=4 << 20, transcendentals=0),
+        name="edge_middle" if middle else "edge_end",
+    )(*args)
 
 
 def band_kernel(paired, acc_ref, own_ref, from_left_ref, from_right_ref, out_ref, rows_ref):
@@ -582,7 +655,8 @@
     more = functools.partial(lesser_part, hi, lo, held=held)
     places = [[neighbour(0)]]
     if paired:
-        aside, across = gate([aside, across], [keeps[-1]])
+        (aside,) = gate([aside], [keeps[-1]])
+        (across,) = gate([across], [aside])
         second_across, second_aside = send(aside, middle), send(across, outward)
         halos = [send(outer, ends), send(near, middle)]
         places.append([beside, reflected(3, True)])
@@ -593,11 +667,12 @@
         places.append([two_off(True), two_off(False)])
         acc, *kept = more(acc, [second_across, second_aside], places[-1])
         keeps += kept
-        to_end, to_middle, own = edge_part(
-            halos, keeps, [*places[:-1], places[-1][:1]], held, True
-        )
-        back_left, back_right = send(to_end, outward), send(to_middle, middle)
-        (acc,) = more(acc, [third_aside], [reflected(3, False)], after=[to_end], keep=False)
+        shards = [*places[:-1], places[-1][:1]]
+        to_end, own = pair_edge_part(halos[0], keeps, shards, held)
+        back_left = send(to_end, outward)
+        to_middle, own = pair_edge_part(halos[1], keeps, shards, held, own)
+        back_right = send(to_middle, middle)
+        (acc,) = more(acc, [third_aside], [reflected(3, False)], after=[to_middle], keep=False)
     else:
         near_right = send(near, up[:-1] if far else up)
         near_left = send(nearer[0], down[1:] if far else down)

time: 82.2 us -> 82.3 us (level); the launches traced: 80.8 us -> 81.9 us
  waiting for transfers between devices: 16 us -> 17.1 us
    ppermute x9, waiting for transfers between devices: 16 us -> 17.1 us  [send(): return lax.ppermute(x, 'orb', pairs)]
where the time goes in v11:
time: 82.3 us; the launch traced here: 81.9 us
  blocking collectives  25.4 us (31%)
  Pallas kernels  18.7 us (23%)
  waiting for transfers between devices  17.1 us (21%)
  starting transfers between devices  16.8 us (20%)
  local copies, waits for them, and re-layouts  2.68 us (3%)
  other arithmetic  1.02 us (1%)
    ppermute x9, waiting for transfers between devices, send(): return lax.ppermute(x, 'orb', pairs)  17.1 us
    ppermute x9, starting transfers between devices, send(): return lax.ppermute(x, 'orb', pairs)  16.8 us
    all_to_all x1, blocking collectives, per_device(): lax.all_to_all(lesser, 'energy', split_axis=0, concat_axis=0, tiled=True)  13.3 us
    all_to_all x1, blocking collectives, per_device(): lax.all_to_all(spread, 'energy', split_axis=0, concat_axis=0, tiled=True)  12.2 us
    pallas_call x3, Pallas kernels, lesser_part(): pl.pallas_call(functools.partial(lesser_kernel, places, held, len(after))...  9.16 us
    pallas_call x1, Pallas kernels, own_part(): pl.pallas_call(functools.partial(own_kernel, wanted, len(after)), out_sha...  6.13 us
    pallas_call x1, Pallas kernels, scatter(): pl.pallas_call(scatter_kernel, out_shape=jax.ShapeDtypeStruct((energies,...  2.44 us
  transfers between devices with their start and end apart: 9, of which 4 were waited for; matrix products, arithmetic and copies ran while one was open for 4% of the time, Pallas kernels for 19%

profile of v11, /device:TPU:0, one launch (start us, length us, event | category | flops | bytes accessed | tf_op | source)
XLA Modules:
  0.0 81.9 jit_solution(14128010439871105972)
XLA Ops:
  0.0 3.0 %collective-permute-start = (f32[1,4,2,128,128]{4,3,2,1,0:T(8,128)}, f32[1,4,2,128,128]{4,3,2,1,0:T(8,128)S(1)}, u32[]{:S(2)}, u32[]{:S(2)}) collective-permute-start(f32[1,4,2,128,128]{4,3,2,1,0:T(8,128)} %sigma_ref.1), channel_id=1, source_target_pairs={{0,1},{3,2},{1,0},{2,3},{4,5},{7,6},{5,4},{6,7},{8,9},{11,10},{9,8... | collective-permute-start | bytes 1572872 | tf_op jit(solution)/shard_map/ppermute | solution.py:601
  3.0 0.7 collective-permute-start.1
  3.7 0.8 constant_dynamic-slice_fusion.1
  4.6 0.7 iota_add_fusion
  5.3 0.8 slice_bitcast_fusion.1
  6.1 0.1 add_reduce_fusion
  6.2 0.1 broadcast_multiply_fusion
  6.3 0.1 select_add_fusion
  6.4 0.1 reshape.79.rest_0_.where_ref
  6.5 0.2 mul.67.rest_1_.mix_ref
  6.7 6.1 %lesser_own.1 = (f32[4,256,256]{2,1,0:T(8,128)S(1)}, bf16[4,256,256]{2,1,0:T(8,128)(2,1)S(1)}, bf16[4,256,256]{2,1,0:T(8,128)(2,1)S(1)}, bf16[640,4096]{1,0:T(8,...) custom-call(f32[1,2,512,2048]{3,2,1,0:T(8,128)} %green_ref.1, ...), custom_call_target="tpu_custom_call" | custom-call | flops 33554432 | bytes 1048576 | tf_op jit(solution)/shard_map/lesser_own/pallas_call | solution.py:202
  12.8 7.1 %collective-permute-start.6 = (f32[2,64,2048]{2,1,0:T(8,128)S(1)}, f32[2,64,2048]{2,1,0:T(8,128)S(1)}, u32[]{:S(2)}, u32[]{:S(2)}) collective-permute-start(f32[2,64,2048]{2,1,0:T(8,128)S(1)} %get-tuple-element.34), channel_id=1, source_target_pairs={{0,1},{3,2},{4,5},{7,6},{8,9},{11,10},{12,13},{15,14},{16,17},{19,... | collective-permute-start | bytes 3145736 | tf_op jit(solution)/shard_map/ppermute | solution.py:601
  20.0 0.7 collective-permute-start.2
  20.7 1.3 %collective-permute-start.3 = (f32[1,4,2,128,128]{4,3,2,1,0:T(8,128)S(1)}, f32[1,4,2,128,128]{4,3,2,1,0:T(8,128)S(1)}, u32[]{:S(2)}, u32[]{:S(2)}) collective-permute-start(f32[1,4,2,128,128]{4,3,2,1,0:T(8,128)S(1)} %gate.4.rest_1_), channel_id=1, source_target_pairs={{1,0},{2,3},{5,4},{6,7},{9,8},{10,11},{13,12},{14,15},{17,16},{18,... | collective-permute-start | bytes 1572872 | tf_op jit(solution)/shard_map/ppermute | solution.py:601
  22.0 0.7 collective-permute-start.5
  22.7 3.0 %lesser_more.3 = (f32[4,256,256]{2,1,0:T(8,128)S(1)}, bf16[8,256,256]{2,1,0:T(8,128)(2,1)S(1)}, bf16[8,256,256]{2,1,0:T(8,128)(2,1)S(1)}) custom-call(bf16[640,4096]{1,0:T(8,128)(2,1)S(1)} %get-tuple-element.22.hi_ref, bf16[640,4096]{1,0:T(8,128)(2,1)S(1)} %get-tuple-element.23.lo_ref, ...), custom_call_target="tpu_custom_call", output_to_operand_aliasing={{0}: (2, {})} | custom-call | flops 83886080 | bytes 262144 | tf_op jit(solution)/shard_map/lesser_more/pallas_call | solution.py:253
  25.7 1.3 %collective-permute-start.4 = (f32[1,4,2,128,128]{4,3,2,1,0:T(8,128)S(1)}, f32[1,4,2,128,128]{4,3,2,1,0:T(8,128)S(1)}, u32[]{:S(2)}, u32[]{:S(2)}) collective-permute-start(f32[1,4,2,128,128]{4,3,2,1,0:T(8,128)S(1)} %gate.5.rest_0_), channel_id=1, source_target_pairs={{1,0},{2,3},{5,4},{6,7},{9,8},{10,11},{13,12},{14,15},{17,16},{18,... | collective-permute-start | bytes 1572872 | tf_op jit(solution)/shard_map/ppermute | solution.py:601
  27.0 8.8 %collective-permute-done.3.rest_1_ = f32[1,4,2,128,128]{4,3,2,1,0:T(8,128)S(1)} collective-permute-done((f32[1,4,2,128,128]{4,3,2,1,0:T(8,128)S(1)}, f32[1,4,2,128,128]{4,3,2,1,0:T(8,128)S(1)}, u32[]{:S(2)}, u32[]{:S(2)}) %collective-permute-start.3) | collective-permute-done | bytes 524320 | tf_op jit(solution)/shard_map/ppermute | solution.py:601
  35.8 3.0 %lesser_more.4 = (f32[4,256,256]{2,1,0:T(8,128)S(1)}, bf16[8,256,256]{2,1,0:T(8,128)(2,1)S(1)}, bf16[8,256,256]{2,1,0:T(8,128)(2,1)S(1)}) custom-call(bf16[640,4096]{1,0:T(8,128)(2,1)S(1)} %get-tuple-element.22.hi_ref, bf16[640,4096]{1,0:T(8,128)(2,1)S(1)} %get-tuple-element.23.lo_ref, ...), custom_call_target="tpu_custom_call", output_to_operand_aliasing={{0}: (2, {})} | custom-call | flops 83886080 | bytes 262144 | tf_op jit(solution)/shard_map/lesser_more/pallas_call | solution.py:253
  38.8 2.9 %collective-permute-done.6.refs_0_ = f32[2,64,2048]{2,1,0:T(8,128)S(1)} collective-permute-done((f32[2,64,2048]{2,1,0:T(8,128)S(1)}, f32[2,64,2048]{2,1,0:T(8,128)S(1)}, u32[]{:S(2)}, u32[]{:S(2)}) %collective-permute-start.6) | collective-permute-done | bytes 1048608 | tf_op jit(solution)/shard_map/ppermute | solution.py:601
  41.7 0.2 edge_end.1
  41.9 0.2 edge_middle.1
  42.1 0.7 collective-permute-start.8
  42.8 1.3 %collective-permute-start.7 = (f32[2,64,128]{2,1,0:T(8,128)S(1)}, f32[2,64,128]{2,1,0:T(8,128)S(1)}, u32[]{:S(2)}, u32[]{:S(2)}) collective-permute-start(f32[2,64,128]{2,1,0:T(8,128)S(1)} %get-tuple-element.38), channel_id=1, source_target_pairs={{1,0},{2,3},{5,4},{6,7},{9,8},{10,11},{13,12},{14,15},{17,16},{18,... | collective-permute-start | bytes 196616 | tf_op jit(solution)/shard_map/ppermute | solution.py:601
  44.1 2.6 %collective-permute-done.4.rest_0_ = f32[1,4,2,128,128]{4,3,2,1,0:T(8,128)S(1)} collective-permute-done((f32[1,4,2,128,128]{4,3,2,1,0:T(8,128)S(1)}, f32[1,4,2,128,128]{4,3,2,1,0:T(8,128)S(1)}, u32[]{:S(2)}, u32[]{:S(2)}) %collective-permute-start.4) | collective-permute-done | bytes 524320 | tf_op jit(solution)/shard_map/ppermute | solution.py:601
  46.6 3.2 %lesser_more.5.acc_ref = f32[4,256,256]{2,1,0:T(8,128)S(1)} custom-call(bf16[640,4096]{1,0:T(8,128)(2,1)S(1)} %get-tuple-element.22.hi_ref, bf16[640,4096]{1,0:T(8,128)(2,1)S(1)} %get-tuple-element.23.lo_ref, f32[4,256,256]{2,1,0:T(8,128)S(1)} %get-tuple-element.28.before_ref, ...), custom_call_target="tpu_custom_call", output_to_operand_aliasing={{}: (2, {})} | custom-call | flops 41943040 | bytes 262144 | tf_op jit(solution)/shard_map/lesser_more/pallas_call | solution.py:253
  49.8 2.8 %collective-permute-done.7.from_left_ref = f32[2,64,128]{2,1,0:T(8,128)S(1)} collective-permute-done((f32[2,64,128]{2,1,0:T(8,128)S(1)}, f32[2,64,128]{2,1,0:T(8,128)S(1)}, u32[]{:S(2)}, u32[]{:S(2)}) %collective-permute-start.7) | collective-permute-done | bytes 65568 | tf_op jit(solution)/shard_map/ppermute | solution.py:601
  52.6 0.6 band.1
  53.2 13.3 %all_to_all.10.recv_ref = f32[8,2,8,8,128]{4,3,2,1,0:T(8,128)S(1)} all-to-all(f32[8,2,8,8,128]{4,3,2,1,0:T(8,128)S(1)} %band.1), channel_id=1, replica_groups=mesh['energy'=8,'orb'=4] {'energy'}, dimensions={0} | all-to-all | bytes 1048576 | tf_op jit(solution)/shard_map/all_to_all | solution.py:709
  66.5 2.4 %scatter.1 = f32[8,128,128]{2,1,0:T(8,128)S(1)} custom-call(f32[8,2,8,8,128]{4,3,2,1,0:T(8,128)S(1)} %all_to_all.10.recv_ref, s32[1,128]{1,0:T(1,128)S(1)} %reshape.79.rest_0_.where_ref, f32[128,128]{1,0:T(8,128)S(1)} %mul.67.rest_1_.mix_ref, f32[192,128]{1,0:T(8,128)S(1)} %constant_dynamic-slice_fusion.rest_2_.dham_ref), custom_call_target="tpu_custom_call" | custom-call | tf_op jit(solution)/shard_map/scatter/pallas_call | solution.py:566
  68.9 12.2 %all_to_all.11 = f32[8,128,128]{2,1,0:T(8,128)S(1)} all-to-all(f32[8,128,128]{2,1,0:T(8,128)S(1)} %scatter.1), channel_id=1, replica_groups=mesh['energy'=8,'orb'=4] {'energy'}, dimensions={0} | all-to-all | bytes 1048576 | tf_op jit(solution)/shard_map/all_to_all | solution.py:711
  81.1 0.8 copy.24
  (14 shorter events, 0.1 us)
Async XLA Ops:
  0.0 6.4 %copy-start = (f32[1024,3,8,8]{0,3,2,1:T(8,128)S(1)}, f32[1024,3,8,8]{0,3,2,1:T(8,128)}, u32[]{:S(2)}) copy-start(f32[1024,3,8,8]{0,3,2,1:T(8,128)} %param.11) | copy-start | bytes 2359300
  0.0 19.9 %collective-permute-start = (f32[1,4,2,128,128]{4,3,2,1,0:T(8,128)}, f32[1,4,2,128,128]{4,3,2,1,0:T(8,128)S(1)}, u32[]{:S(2)}, u32[]{:S(2)}) collective-permute-start(f32[1,4,2,128,128]{4,3,2,1,0:T(8,128)} %sigma_ref.1), channel_id=1, source_target_pairs={{0,1},{3,2},{1,0},{2,3},{4,5},{7,6},{5,4},{6,7},{8,9},{11,10},{9,8... | collective-permute-start | bytes 1572872 | tf_op jit(solution)/shard_map/ppermute | solution.py:601
  3.0 17.6 %collective-permute-start.1 = (f32[1,4,2,128,128]{4,3,2,1,0:T(8,128)}, f32[1,4,2,128,128]{4,3,2,1,0:T(8,128)S(1)}, u32[]{:S(2)}, u32[]{:S(2)}) collective-permute-start(f32[1,4,2,128,128]{4,3,2,1,0:T(8,128)} %sigma_ref.1), channel_id=1, source_target_pairs={{1,2},{2,1},{5,6},{6,5},{9,10},{10,9},{13,14},{14,13},{17,18},{18,... | collective-permute-start | bytes 1572872 | tf_op jit(solution)/shard_map/ppermute | solution.py:601
  12.8 28.9 %collective-permute-start.6 = (f32[2,64,2048]{2,1,0:T(8,128)S(1)}, f32[2,64,2048]{2,1,0:T(8,128)S(1)}, u32[]{:S(2)}, u32[]{:S(2)}) collective-permute-start(f32[2,64,2048]{2,1,0:T(8,128)S(1)} %get-tuple-element.34), channel_id=1, source_target_pairs={{0,1},{3,2},{4,5},{7,6},{8,9},{11,10},{12,13},{15,14},{16,17},{19,... | collective-permute-start | bytes 3145736 | tf_op jit(solution)/shard_map/ppermute | solution.py:601
  20.0 5.7 %collective-permute-start.2 = (f32[1,4,2,128,128]{4,3,2,1,0:T(8,128)S(1)}, f32[1,4,2,128,128]{4,3,2,1,0:T(8,128)S(1)}, u32[]{:S(2)}, u32[]{:S(2)}) collective-permute-start(f32[1,4,2,128,128]{4,3,2,1,0:T(8,128)S(1)} %gate.3.refs_1_.rest_0_), channel_id=1, source_target_pairs={{1,2},{2,1},{5,6},{6,5},{9,10},{10,9},{13,14},{14,13},{17,18},{18,... | collective-permute-start | bytes 1572872 | tf_op jit(solution)/shard_map/ppermute | solution.py:601
  20.7 15.1 %collective-permute-start.3 = (f32[1,4,2,128,128]{4,3,2,1,0:T(8,128)S(1)}, f32[1,4,2,128,128]{4,3,2,1,0:T(8,128)S(1)}, u32[]{:S(2)}, u32[]{:S(2)}) collective-permute-start(f32[1,4,2,128,128]{4,3,2,1,0:T(8,128)S(1)} %gate.4.rest_1_), channel_id=1, source_target_pairs={{1,0},{2,3},{5,4},{6,7},{9,8},{10,11},{13,12},{14,15},{17,16},{18,... | collective-permute-start | bytes 1572872 | tf_op jit(solution)/shard_map/ppermute | solution.py:601
  22.0 19.9 %collective-permute-start.5 = (f32[2,32,2048]{2,1,0:T(8,128)S(1)}, f32[2,32,2048]{2,1,0:T(8,128)S(1)}, u32[]{:S(2)}, u32[]{:S(2)}) collective-permute-start(f32[2,32,2048]{2,1,0:T(8,128)S(1)} %get-tuple-element.29), channel_id=1, source_target_pairs={{1,2},{2,1},{5,6},{6,5},{9,10},{10,9},{13,14},{14,13},{17,18},{18,... | collective-permute-start | bytes 1572872 | tf_op jit(solution)/shard_map/ppermute | solution.py:601
  25.7 20.9 %collective-permute-start.4 = (f32[1,4,2,128,128]{4,3,2,1,0:T(8,128)S(1)}, f32[1,4,2,128,128]{4,3,2,1,0:T(8,128)S(1)}, u32[]{:S(2)}, u32[]{:S(2)}) collective-permute-start(f32[1,4,2,128,128]{4,3,2,1,0:T(8,128)S(1)} %gate.5.rest_0_), channel_id=1, source_target_pairs={{1,0},{2,3},{5,4},{6,7},{9,8},{10,11},{13,12},{14,15},{17,16},{18,... | collective-permute-start | bytes 1572872 | tf_op jit(solution)/shard_map/ppermute | solution.py:601
  42.1 7.7 %collective-permute-start.8 = (f32[2,64,128]{2,1,0:T(8,128)S(1)}, f32[2,64,128]{2,1,0:T(8,128)S(1)}, u32[]{:S(2)}, u32[]{:S(2)}) collective-permute-start(f32[2,64,128]{2,1,0:T(8,128)S(1)} %get-tuple-element.36.rest_1_), channel_id=1, source_target_pairs={{1,2},{2,1},{5,6},{6,5},{9,10},{10,9},{13,14},{14,13},{17,18},{18,... | collective-permute-start | bytes 196616 | tf_op jit(solution)/shard_map/ppermute | solution.py:601
  42.8 9.8 %collective-permute-start.7 = (f32[2,64,128]{2,1,0:T(8,128)S(1)}, f32[2,64,128]{2,1,0:T(8,128)S(1)}, u32[]{:S(2)}, u32[]{:S(2)}) collective-permute-start(f32[2,64,128]{2,1,0:T(8,128)S(1)} %get-tuple-element.38), channel_id=1, source_target_pairs={{1,0},{2,3},{5,4},{6,7},{9,8},{10,11},{13,12},{14,15},{17,16},{18,... | collective-permute-start | bytes 196616 | tf_op jit(solution)/shard_map/ppermute | solution.py:601

commit v12 on v11

--- a/solution.py
+++ b/solution.py
@@ -672,7 +672,7 @@
         back_left = send(to_end, outward)
         to_middle, own = pair_edge_part(halos[1], keeps, shards, held, own)
         back_right = send(to_middle, middle)
-        (acc,) = more(acc, [third_aside], [reflected(3, False)], after=[to_middle], keep=False)
+        (acc,) = more(acc, [third_aside], [reflected(3, False)], after=[to_middle, back_left], keep=False)
     else:
         near_right = send(near, up[:-1] if far else up)
         near_left = send(nearer[0], down[1:] if far else down)

time: 82.3 us -> 81.7 us (level)
  transfers between devices with their start and end apart: 9 -> 9, of which waited for: 4 -> 3; matrix products, arithmetic and copies ran while one was open for 4% -> 4% of each run, Pallas kernels for 19% -> 19%
where the time goes in v12:
time: 81.7 us; the launch traced here: 81.3 us
  blocking collectives  25.4 us (31%)
  Pallas kernels  18.7 us (23%)
  starting transfers between devices  16.8 us (21%)
  waiting for transfers between devices  16.5 us (20%)
  local copies, waits for them, and re-layouts  2.68 us (3%)
  other arithmetic  1.02 us (1%)
    ppermute x9, starting transfers between devices, send(): return lax.ppermute(x, 'orb', pairs)  16.8 us
    ppermute x9, waiting for transfers between devices, send(): return lax.ppermute(x, 'orb', pairs)  16.5 us
    all_to_all x1, blocking collectives, per_device(): lax.all_to_all(lesser, 'energy', split_axis=0, concat_axis=0, tiled=True)  13.3 us
    all_to_all x1, blocking collectives, per_device(): lax.all_to_all(spread, 'energy', split_axis=0, concat_axis=0, tiled=True)  12.2 us
    pallas_call x3, Pallas kernels, lesser_part(): pl.pallas_call(functools.partial(lesser_kernel, places, held, len(after))...  9.17 us
    pallas_call x1, Pallas kernels, own_part(): pl.pallas_call(functools.partial(own_kernel, wanted, len(after)), out_sha...  6.13 us
    pallas_call x1, Pallas kernels, scatter(): pl.pallas_call(scatter_kernel, out_shape=jax.ShapeDtypeStruct((energies,...  2.44 us
  transfers between devices with their start and end apart: 9, of which 3 were waited for; matrix products, arithmetic and copies ran while one was open for 4% of the time, Pallas kernels for 19%

profile of v12, /device:TPU:0, one launch (start us, length us, event | category | flops | bytes accessed | tf_op | source)
XLA Modules:
  0.0 81.3 jit_solution(8931758964119707226)
XLA Ops:
  0.0 3.0 %collective-permute-start = (f32[1,4,2,128,128]{4,3,2,1,0:T(8,128)}, f32[1,4,2,128,128]{4,3,2,1,0:T(8,128)S(1)}, u32[]{:S(2)}, u32[]{:S(2)}) collective-permute-start(f32[1,4,2,128,128]{4,3,2,1,0:T(8,128)} %sigma_ref.1), channel_id=1, source_target_pairs={{0,1},{3,2},{1,0},{2,3},{4,5},{7,6},{5,4},{6,7},{8,9},{11,10},{9,8... | collective-permute-start | bytes 1572872 | tf_op jit(solution)/shard_map/ppermute | solution.py:601
  3.0 0.7 collective-permute-start.1
  3.7 0.8 constant_dynamic-slice_fusion.1
  4.5 0.1 copy.16
  4.6 0.7 iota_add_fusion
  5.3 0.8 slice_bitcast_fusion.1
  6.1 0.1 add_reduce_fusion
  6.2 0.1 broadcast_multiply_fusion
  6.3 0.1 select_add_fusion
  6.4 0.1 reshape.79.rest_0_.where_ref
  6.5 0.2 mul.67.rest_1_.mix_ref
  6.7 6.1 %lesser_own.1 = (f32[4,256,256]{2,1,0:T(8,128)S(1)}, bf16[4,256,256]{2,1,0:T(8,128)(2,1)S(1)}, bf16[4,256,256]{2,1,0:T(8,128)(2,1)S(1)}, bf16[640,4096]{1,0:T(8,...) custom-call(f32[1,2,512,2048]{3,2,1,0:T(8,128)} %green_ref.1, ...), custom_call_target="tpu_custom_call" | custom-call | flops 33554432 | bytes 1048576 | tf_op jit(solution)/shard_map/lesser_own/pallas_call | solution.py:202
  12.8 7.1 %collective-permute-start.6 = (f32[2,64,2048]{2,1,0:T(8,128)S(1)}, f32[2,64,2048]{2,1,0:T(8,128)S(1)}, u32[]{:S(2)}, u32[]{:S(2)}) collective-permute-start(f32[2,64,2048]{2,1,0:T(8,128)S(1)} %get-tuple-element.34), channel_id=1, source_target_pairs={{0,1},{3,2},{4,5},{7,6},{8,9},{11,10},{12,13},{15,14},{16,17},{19,... | collective-permute-start | bytes 3145736 | tf_op jit(solution)/shard_map/ppermute | solution.py:601
  20.0 0.7 collective-permute-start.2
  20.7 1.3 %collective-permute-start.3 = (f32[1,4,2,128,128]{4,3,2,1,0:T(8,128)S(1)}, f32[1,4,2,128,128]{4,3,2,1,0:T(8,128)S(1)}, u32[]{:S(2)}, u32[]{:S(2)}) collective-permute-start(f32[1,4,2,128,128]{4,3,2,1,0:T(8,128)S(1)} %gate.4.rest_1_), channel_id=1, source_target_pairs={{1,0},{2,3},{5,4},{6,7},{9,8},{10,11},{13,12},{14,15},{17,16},{18,... | collective-permute-start | bytes 1572872 | tf_op jit(solution)/shard_map/ppermute | solution.py:601
  22.0 0.7 collective-permute-start.5
  22.7 3.0 %lesser_more.3 = (f32[4,256,256]{2,1,0:T(8,128)S(1)}, bf16[8,256,256]{2,1,0:T(8,128)(2,1)S(1)}, bf16[8,256,256]{2,1,0:T(8,128)(2,1)S(1)}) custom-call(bf16[640,4096]{1,0:T(8,128)(2,1)S(1)} %get-tuple-element.22.hi_ref, bf16[640,4096]{1,0:T(8,128)(2,1)S(1)} %get-tuple-element.23.lo_ref, ...), custom_call_target="tpu_custom_call", output_to_operand_aliasing={{0}: (2, {})} | custom-call | flops 83886080 | bytes 262144 | tf_op jit(solution)/shard_map/lesser_more/pallas_call | solution.py:253
  25.7 1.3 %collective-permute-start.4 = (f32[1,4,2,128,128]{4,3,2,1,0:T(8,128)S(1)}, f32[1,4,2,128,128]{4,3,2,1,0:T(8,128)S(1)}, u32[]{:S(2)}, u32[]{:S(2)}) collective-permute-start(f32[1,4,2,128,128]{4,3,2,1,0:T(8,128)S(1)} %gate.5.rest_0_), channel_id=1, source_target_pairs={{1,0},{2,3},{5,4},{6,7},{9,8},{10,11},{13,12},{14,15},{17,16},{18,... | collective-permute-start | bytes 1572872 | tf_op jit(solution)/shard_map/ppermute | solution.py:601
  27.0 8.8 %collective-permute-done.3.rest_1_ = f32[1,4,2,128,128]{4,3,2,1,0:T(8,128)S(1)} collective-permute-done((f32[1,4,2,128,128]{4,3,2,1,0:T(8,128)S(1)}, f32[1,4,2,128,128]{4,3,2,1,0:T(8,128)S(1)}, u32[]{:S(2)}, u32[]{:S(2)}) %collective-permute-start.3) | collective-permute-done | bytes 524320 | tf_op jit(solution)/shard_map/ppermute | solution.py:601
  35.8 3.0 %lesser_more.4 = (f32[4,256,256]{2,1,0:T(8,128)S(1)}, bf16[8,256,256]{2,1,0:T(8,128)(2,1)S(1)}, bf16[8,256,256]{2,1,0:T(8,128)(2,1)S(1)}) custom-call(bf16[640,4096]{1,0:T(8,128)(2,1)S(1)} %get-tuple-element.22.hi_ref, bf16[640,4096]{1,0:T(8,128)(2,1)S(1)} %get-tuple-element.23.lo_ref, ...), custom_call_target="tpu_custom_call", output_to_operand_aliasing={{0}: (2, {})} | custom-call | flops 83886080 | bytes 262144 | tf_op jit(solution)/shard_map/lesser_more/pallas_call | solution.py:253
  38.8 2.9 %collective-permute-done.6.refs_0_ = f32[2,64,2048]{2,1,0:T(8,128)S(1)} collective-permute-done((f32[2,64,2048]{2,1,0:T(8,128)S(1)}, f32[2,64,2048]{2,1,0:T(8,128)S(1)}, u32[]{:S(2)}, u32[]{:S(2)}) %collective-permute-start.6) | collective-permute-done | bytes 1048608 | tf_op jit(solution)/shard_map/ppermute | solution.py:601
  41.7 0.2 edge_end.1
  41.9 1.3 %collective-permute-start.7 = (f32[2,64,128]{2,1,0:T(8,128)S(1)}, f32[2,64,128]{2,1,0:T(8,128)S(1)}, u32[]{:S(2)}, u32[]{:S(2)}) collective-permute-start(f32[2,64,128]{2,1,0:T(8,128)S(1)} %get-tuple-element.37), channel_id=1, source_target_pairs={{1,0},{2,3},{5,4},{6,7},{9,8},{10,11},{13,12},{14,15},{17,16},{18,... | collective-permute-start | bytes 196616 | tf_op jit(solution)/shard_map/ppermute | solution.py:601
  43.2 0.2 edge_middle.1
  43.4 0.7 collective-permute-start.8
  44.1 4.8 %collective-permute-done.7.rest_2_.from_left_ref = f32[2,64,128]{2,1,0:T(8,128)S(1)} collective-permute-done((f32[2,64,128]{2,1,0:T(8,128)S(1)}, f32[2,64,128]{2,1,0:T(8,128)S(1)}, u32[]{:S(2)}, u32[]{:S(2)}) %collective-permute-start.7) | collective-permute-done | bytes 65568 | tf_op jit(solution)/shard_map/ppermute | solution.py:601
  48.9 3.2 %lesser_more.5.acc_ref = f32[4,256,256]{2,1,0:T(8,128)S(1)} custom-call(bf16[640,4096]{1,0:T(8,128)(2,1)S(1)} %get-tuple-element.22.hi_ref, bf16[640,4096]{1,0:T(8,128)(2,1)S(1)} %get-tuple-element.23.lo_ref, f32[4,256,256]{2,1,0:T(8,128)S(1)} %get-tuple-element.28.before_ref, ...), custom_call_target="tpu_custom_call", output_to_operand_aliasing={{}: (2, {})} | custom-call | flops 41943040 | bytes 262144 | tf_op jit(solution)/shard_map/lesser_more/pallas_call | solution.py:253
  52.1 0.6 band.1
  52.7 13.3 %all_to_all.10.recv_ref = f32[8,2,8,8,128]{4,3,2,1,0:T(8,128)S(1)} all-to-all(f32[8,2,8,8,128]{4,3,2,1,0:T(8,128)S(1)} %band.1), channel_id=1, replica_groups=mesh['energy'=8,'orb'=4] {'energy'}, dimensions={0} | all-to-all | bytes 1048576 | tf_op jit(solution)/shard_map/all_to_all | solution.py:709
  65.9 2.4 %scatter.1 = f32[8,128,128]{2,1,0:T(8,128)S(1)} custom-call(f32[8,2,8,8,128]{4,3,2,1,0:T(8,128)S(1)} %all_to_all.10.recv_ref, s32[1,128]{1,0:T(1,128)S(1)} %reshape.79.rest_0_.where_ref, f32[128,128]{1,0:T(8,128)S(1)} %mul.67.rest_1_.mix_ref, f32[192,128]{1,0:T(8,128)S(1)} %constant_dynamic-slice_fusion.rest_2_.dham_ref), custom_call_target="tpu_custom_call" | custom-call | tf_op jit(solution)/shard_map/scatter/pallas_call | solution.py:566
  68.4 12.2 %all_to_all.11 = f32[8,128,128]{2,1,0:T(8,128)S(1)} all-to-all(f32[8,128,128]{2,1,0:T(8,128)S(1)} %scatter.1), channel_id=1, replica_groups=mesh['energy'=8,'orb'=4] {'energy'}, dimensions={0} | all-to-all | bytes 1048576 | tf_op jit(solution)/shard_map/all_to_all | solution.py:711
  80.5 0.8 copy.24
  (14 shorter events, 0.0 us)
Async XLA Ops:
  0.0 6.4 %copy-start = (f32[1024,3,8,8]{0,3,2,1:T(8,128)S(1)}, f32[1024,3,8,8]{0,3,2,1:T(8,128)}, u32[]{:S(2)}) copy-start(f32[1024,3,8,8]{0,3,2,1:T(8,128)} %param.11) | copy-start | bytes 2359300
  0.0 19.9 %collective-permute-start = (f32[1,4,2,128,128]{4,3,2,1,0:T(8,128)}, f32[1,4,2,128,128]{4,3,2,1,0:T(8,128)S(1)}, u32[]{:S(2)}, u32[]{:S(2)}) collective-permute-start(f32[1,4,2,128,128]{4,3,2,1,0:T(8,128)} %sigma_ref.1), channel_id=1, source_target_pairs={{0,1},{3,2},{1,0},{2,3},{4,5},{7,6},{5,4},{6,7},{8,9},{11,10},{9,8... | collective-permute-start | bytes 1572872 | tf_op jit(solution)/shard_map/ppermute | solution.py:601
  3.0 17.6 %collective-permute-start.1 = (f32[1,4,2,128,128]{4,3,2,1,0:T(8,128)}, f32[1,4,2,128,128]{4,3,2,1,0:T(8,128)S(1)}, u32[]{:S(2)}, u32[]{:S(2)}) collective-permute-start(f32[1,4,2,128,128]{4,3,2,1,0:T(8,128)} %sigma_ref.1), channel_id=1, source_target_pairs={{1,2},{2,1},{5,6},{6,5},{9,10},{10,9},{13,14},{14,13},{17,18},{18,... | collective-permute-start | bytes 1572872 | tf_op jit(solution)/shard_map/ppermute | solution.py:601
  12.8 28.9 %collective-permute-start.6 = (f32[2,64,2048]{2,1,0:T(8,128)S(1)}, f32[2,64,2048]{2,1,0:T(8,128)S(1)}, u32[]{:S(2)}, u32[]{:S(2)}) collective-permute-start(f32[2,64,2048]{2,1,0:T(8,128)S(1)} %get-tuple-element.34), channel_id=1, source_target_pairs={{0,1},{3,2},{4,5},{7,6},{8,9},{11,10},{12,13},{15,14},{16,17},{19,... | collective-permute-start | bytes 3145736 | tf_op jit(solution)/shard_map/ppermute | solution.py:601
  20.0 5.7 %collective-permute-start.2 = (f32[1,4,2,128,128]{4,3,2,1,0:T(8,128)S(1)}, f32[1,4,2,128,128]{4,3,2,1,0:T(8,128)S(1)}, u32[]{:S(2)}, u32[]{:S(2)}) collective-permute-start(f32[1,4,2,128,128]{4,3,2,1,0:T(8,128)S(1)} %gate.3.refs_1_.rest_0_), channel_id=1, source_target_pairs={{1,2},{2,1},{5,6},{6,5},{9,10},{10,9},{13,14},{14,13},{17,18},{18,... | collective-permute-start | bytes 1572872 | tf_op jit(solution)/shard_map/ppermute | solution.py:601
  20.7 15.1 %collective-permute-start.3 = (f32[1,4,2,128,128]{4,3,2,1,0:T(8,128)S(1)}, f32[1,4,2,128,128]{4,3,2,1,0:T(8,128)S(1)}, u32[]{:S(2)}, u32[]{:S(2)}) collective-permute-start(f32[1,4,2,128,128]{4,3,2,1,0:T(8,128)S(1)} %gate.4.rest_1_), channel_id=1, source_target_pairs={{1,0},{2,3},{5,4},{6,7},{9,8},{10,11},{13,12},{14,15},{17,16},{18,... | collective-permute-start | bytes 1572872 | tf_op jit(solution)/shard_map/ppermute | solution.py:601
  22.0 21.2 %collective-permute-start.5 = (f32[2,32,2048]{2,1,0:T(8,128)S(1)}, f32[2,32,2048]{2,1,0:T(8,128)S(1)}, u32[]{:S(2)}, u32[]{:S(2)}) collective-permute-start(f32[2,32,2048]{2,1,0:T(8,128)S(1)} %get-tuple-element.29), channel_id=1, source_target_pairs={{1,2},{2,1},{5,6},{6,5},{9,10},{10,9},{13,14},{14,13},{17,18},{18,... | collective-permute-start | bytes 1572872 | tf_op jit(solution)/shard_map/ppermute | solution.py:601
  25.7 23.2 %collective-permute-start.4 = (f32[1,4,2,128,128]{4,3,2,1,0:T(8,128)S(1)}, f32[1,4,2,128,128]{4,3,2,1,0:T(8,128)S(1)}, u32[]{:S(2)}, u32[]{:S(2)}) collective-permute-start(f32[1,4,2,128,128]{4,3,2,1,0:T(8,128)S(1)} %gate.5.rest_0_), channel_id=1, source_target_pairs={{1,0},{2,3},{5,4},{6,7},{9,8},{10,11},{13,12},{14,15},{17,16},{18,... | collective-permute-start | bytes 1572872 | tf_op jit(solution)/shard_map/ppermute | solution.py:601
  41.9 7.0 %collective-permute-start.7 = (f32[2,64,128]{2,1,0:T(8,128)S(1)}, f32[2,64,128]{2,1,0:T(8,128)S(1)}, u32[]{:S(2)}, u32[]{:S(2)}) collective-permute-start(f32[2,64,128]{2,1,0:T(8,128)S(1)} %get-tuple-element.37), channel_id=1, source_target_pairs={{1,0},{2,3},{5,4},{6,7},{9,8},{10,11},{13,12},{14,15},{17,16},{18,... | collective-permute-start | bytes 196616 | tf_op jit(solution)/shard_map/ppermute | solution.py:601
  43.4 8.7 %collective-permute-start.8 = (f32[2,64,128]{2,1,0:T(8,128)S(1)}, f32[2,64,128]{2,1,0:T(8,128)S(1)}, u32[]{:S(2)}, u32[]{:S(2)}) collective-permute-start(f32[2,64,128]{2,1,0:T(8,128)S(1)} %get-tuple-element.36.rest_1_), channel_id=1, source_target_pairs={{1,2},{2,1},{5,6},{6,5},{9,10},{10,9},{13,14},{14,13},{17,18},{18,... | collective-permute-start | bytes 196616 | tf_op jit(solution)/shard_map/ppermute | solution.py:601

commit v13 on v11

--- a/solution.py
+++ b/solution.py
@@ -669,10 +669,11 @@
         keeps += kept
         shards = [*places[:-1], places[-1][:1]]
         to_end, own = pair_edge_part(halos[0], keeps, shards, held)
-        back_left = send(to_end, outward)
+        back_right = send(to_end, outward)
         to_middle, own = pair_edge_part(halos[1], keeps, shards, held, own)
-        back_right = send(to_middle, middle)
+        back_left = send(to_middle, middle)
         (acc,) = more(acc, [third_aside], [reflected(3, False)], after=[to_middle], keep=False)
+        (back_right,) = gate([back_right], [acc])
     else:
         near_right = send(near, up[:-1] if far else up)
         near_left = send(nearer[0], down[1:] if far else down)

time: 82.3 us -> 80.8 us (0.982)
  waiting for transfers between devices: 17.1 us -> 15 us
    ppermute x9, waiting for transfers between devices: 17.1 us -> 15 us  [send(): return lax.ppermute(x, 'orb', pairs)]
  transfers between devices with their start and end apart: 9 -> 9, of which waited for: 4 -> 3; matrix products, arithmetic and copies ran while one was open for 4% -> 4% of each run, Pallas kernels for 19% -> 20%
where the time goes in v13:
time: 80.8 us; the launch traced here: 79.8 us
  blocking collectives  25.4 us (31%)
  Pallas kernels  18.7 us (23%)
  starting transfers between devices  16.8 us (21%)
  waiting for transfers between devices  15 us (19%)
  local copies, waits for them, and re-layouts  2.68 us (3%)
  other arithmetic  1.02 us (1%)
    ppermute x9, starting transfers between devices, send(): return lax.ppermute(x, 'orb', pairs)  16.8 us
    ppermute x9, waiting for transfers between devices, send(): return lax.ppermute(x, 'orb', pairs)  15 us
    all_to_all x1, blocking collectives, per_device(): lax.all_to_all(lesser, 'energy', split_axis=0, concat_axis=0, tiled=True)  13.3 us
    all_to_all x1, blocking collectives, per_device(): lax.all_to_all(spread, 'energy', split_axis=0, concat_axis=0, tiled=True)  12.2 us
    pallas_call x3, Pallas kernels, lesser_part(): pl.pallas_call(functools.partial(lesser_kernel, places, held, len(after))...  9.17 us
    pallas_call x1, Pallas kernels, own_part(): pl.pallas_call(functools.partial(own_kernel, wanted, len(after)), out_sha...  6.13 us
    pallas_call x1, Pallas kernels, scatter(): pl.pallas_call(scatter_kernel, out_shape=jax.ShapeDtypeStruct((energies,...  2.44 us
  transfers between devices with their start and end apart: 9, of which 3 were waited for; matrix products, arithmetic and copies ran while one was open for 4% of the time, Pallas kernels for 20%

profile of v13, /device:TPU:0, one launch (start us, length us, event | category | flops | bytes accessed | tf_op | source)
XLA Modules:
  0.0 79.8 jit_solution(8743199802232652006)
XLA Ops:
  0.0 3.0 %collective-permute-start = (f32[1,4,2,128,128]{4,3,2,1,0:T(8,128)}, f32[1,4,2,128,128]{4,3,2,1,0:T(8,128)S(1)}, u32[]{:S(2)}, u32[]{:S(2)}) collective-permute-start(f32[1,4,2,128,128]{4,3,2,1,0:T(8,128)} %sigma_ref.1), channel_id=1, source_target_pairs={{0,1},{3,2},{1,0},{2,3},{4,5},{7,6},{5,4},{6,7},{8,9},{11,10},{9,8... | collective-permute-start | bytes 1572872 | tf_op jit(solution)/shard_map/ppermute | solution.py:601
  3.0 0.7 collective-permute-start.1
  3.7 0.8 constant_dynamic-slice_fusion.1
  4.5 0.1 copy.17
  4.6 0.7 iota_add_fusion
  5.3 0.8 slice_bitcast_fusion.1
  6.1 0.1 add_reduce_fusion
  6.2 0.1 broadcast_multiply_fusion
  6.3 0.1 select_add_fusion
  6.4 0.1 reshape.79.rest_0_.where_ref
  6.5 0.2 mul.67.rest_1_.mix_ref
  6.7 6.1 %lesser_own.1 = (f32[4,256,256]{2,1,0:T(8,128)S(1)}, bf16[4,256,256]{2,1,0:T(8,128)(2,1)S(1)}, bf16[4,256,256]{2,1,0:T(8,128)(2,1)S(1)}, bf16[640,4096]{1,0:T(8,...) custom-call(f32[1,2,512,2048]{3,2,1,0:T(8,128)} %green_ref.1, ...), custom_call_target="tpu_custom_call" | custom-call | flops 33554432 | bytes 1048576 | tf_op jit(solution)/shard_map/lesser_own/pallas_call | solution.py:202
  12.8 7.1 %collective-permute-start.6 = (f32[2,64,2048]{2,1,0:T(8,128)S(1)}, f32[2,64,2048]{2,1,0:T(8,128)S(1)}, u32[]{:S(2)}, u32[]{:S(2)}) collective-permute-start(f32[2,64,2048]{2,1,0:T(8,128)S(1)} %get-tuple-element.34), channel_id=1, source_target_pairs={{0,1},{3,2},{4,5},{7,6},{8,9},{11,10},{12,13},{15,14},{16,17},{19,... | collective-permute-start | bytes 3145736 | tf_op jit(solution)/shard_map/ppermute | solution.py:601
  20.0 0.7 collective-permute-start.2
  20.7 1.3 %collective-permute-start.3 = (f32[1,4,2,128,128]{4,3,2,1,0:T(8,128)S(1)}, f32[1,4,2,128,128]{4,3,2,1,0:T(8,128)S(1)}, u32[]{:S(2)}, u32[]{:S(2)}) collective-permute-start(f32[1,4,2,128,128]{4,3,2,1,0:T(8,128)S(1)} %gate.5.rest_1_), channel_id=1, source_target_pairs={{1,0},{2,3},{5,4},{6,7},{9,8},{10,11},{13,12},{14,15},{17,16},{18,... | collective-permute-start | bytes 1572872 | tf_op jit(solution)/shard_map/ppermute | solution.py:601
  22.0 0.7 collective-permute-start.5
  22.7 3.0 %lesser_more.3 = (f32[4,256,256]{2,1,0:T(8,128)S(1)}, bf16[8,256,256]{2,1,0:T(8,128)(2,1)S(1)}, bf16[8,256,256]{2,1,0:T(8,128)(2,1)S(1)}) custom-call(bf16[640,4096]{1,0:T(8,128)(2,1)S(1)} %get-tuple-element.22.hi_ref, bf16[640,4096]{1,0:T(8,128)(2,1)S(1)} %get-tuple-element.23.lo_ref, ...), custom_call_target="tpu_custom_call", output_to_operand_aliasing={{0}: (2, {})} | custom-call | flops 83886080 | bytes 262144 | tf_op jit(solution)/shard_map/lesser_more/pallas_call | solution.py:253
  25.7 1.3 %collective-permute-start.4 = (f32[1,4,2,128,128]{4,3,2,1,0:T(8,128)S(1)}, f32[1,4,2,128,128]{4,3,2,1,0:T(8,128)S(1)}, u32[]{:S(2)}, u32[]{:S(2)}) collective-permute-start(f32[1,4,2,128,128]{4,3,2,1,0:T(8,128)S(1)} %gate.6.rest_0_), channel_id=1, source_target_pairs={{1,0},{2,3},{5,4},{6,7},{9,8},{10,11},{13,12},{14,15},{17,16},{18,... | collective-permute-start | bytes 1572872 | tf_op jit(solution)/shard_map/ppermute | solution.py:601
  27.0 8.8 %collective-permute-done.3.rest_1_ = f32[1,4,2,128,128]{4,3,2,1,0:T(8,128)S(1)} collective-permute-done((f32[1,4,2,128,128]{4,3,2,1,0:T(8,128)S(1)}, f32[1,4,2,128,128]{4,3,2,1,0:T(8,128)S(1)}, u32[]{:S(2)}, u32[]{:S(2)}) %collective-permute-start.3) | collective-permute-done | bytes 524320 | tf_op jit(solution)/shard_map/ppermute | solution.py:601
  35.8 3.0 %lesser_more.4 = (f32[4,256,256]{2,1,0:T(8,128)S(1)}, bf16[8,256,256]{2,1,0:T(8,128)(2,1)S(1)}, bf16[8,256,256]{2,1,0:T(8,128)(2,1)S(1)}) custom-call(bf16[640,4096]{1,0:T(8,128)(2,1)S(1)} %get-tuple-element.22.hi_ref, bf16[640,4096]{1,0:T(8,128)(2,1)S(1)} %get-tuple-element.23.lo_ref, ...), custom_call_target="tpu_custom_call", output_to_operand_aliasing={{0}: (2, {})} | custom-call | flops 83886080 | bytes 262144 | tf_op jit(solution)/shard_map/lesser_more/pallas_call | solution.py:253
  38.8 2.9 %collective-permute-done.6.refs_0_ = f32[2,64,2048]{2,1,0:T(8,128)S(1)} collective-permute-done((f32[2,64,2048]{2,1,0:T(8,128)S(1)}, f32[2,64,2048]{2,1,0:T(8,128)S(1)}, u32[]{:S(2)}, u32[]{:S(2)}) %collective-permute-start.6) | collective-permute-done | bytes 1048608 | tf_op jit(solution)/shard_map/ppermute | solution.py:601
  41.7 0.2 edge_end.1
  41.9 1.3 %collective-permute-start.8 = (f32[2,64,128]{2,1,0:T(8,128)S(1)}, f32[2,64,128]{2,1,0:T(8,128)S(1)}, u32[]{:S(2)}, u32[]{:S(2)}) collective-permute-start(f32[2,64,128]{2,1,0:T(8,128)S(1)} %get-tuple-element.38), channel_id=1, source_target_pairs={{1,0},{2,3},{5,4},{6,7},{9,8},{10,11},{13,12},{14,15},{17,16},{18,... | collective-permute-start | bytes 196616 | tf_op jit(solution)/shard_map/ppermute | solution.py:601
  43.2 0.2 edge_middle.1
  43.4 0.7 collective-permute-start.7
  44.1 3.3 %collective-permute-done.4.rest_0_ = f32[1,4,2,128,128]{4,3,2,1,0:T(8,128)S(1)} collective-permute-done((f32[1,4,2,128,128]{4,3,2,1,0:T(8,128)S(1)}, f32[1,4,2,128,128]{4,3,2,1,0:T(8,128)S(1)}, u32[]{:S(2)}, u32[]{:S(2)}) %collective-permute-start.4) | collective-permute-done | bytes 524320 | tf_op jit(solution)/shard_map/ppermute | solution.py:601
  47.4 3.2 %lesser_more.5.refs_1_.acc_ref = f32[4,256,256]{2,1,0:T(8,128)S(1)} custom-call(bf16[640,4096]{1,0:T(8,128)(2,1)S(1)} %get-tuple-element.22.hi_ref, bf16[640,4096]{1,0:T(8,128)(2,1)S(1)} %get-tuple-element.23.lo_ref, f32[4,256,256]{2,1,0:T(8,128)S(1)} %get-tuple-element.28.before_ref, ...), custom_call_target="tpu_custom_call", output_to_operand_aliasing={{}: (2, {})} | custom-call | flops 41943040 | bytes 262144 | tf_op jit(solution)/shard_map/lesser_more/pallas_call | solution.py:253
  50.6 0.6 band.1
  51.2 13.3 %all_to_all.10.recv_ref = f32[8,2,8,8,128]{4,3,2,1,0:T(8,128)S(1)} all-to-all(f32[8,2,8,8,128]{4,3,2,1,0:T(8,128)S(1)} %band.1), channel_id=1, replica_groups=mesh['energy'=8,'orb'=4] {'energy'}, dimensions={0} | all-to-all | bytes 1048576 | tf_op jit(solution)/shard_map/all_to_all | solution.py:710
  64.4 2.4 %scatter.1 = f32[8,128,128]{2,1,0:T(8,128)S(1)} custom-call(f32[8,2,8,8,128]{4,3,2,1,0:T(8,128)S(1)} %all_to_all.10.recv_ref, s32[1,128]{1,0:T(1,128)S(1)} %reshape.79.rest_0_.where_ref, f32[128,128]{1,0:T(8,128)S(1)} %mul.67.rest_1_.mix_ref, f32[192,128]{1,0:T(8,128)S(1)} %constant_dynamic-slice_fusion.rest_2_.dham_ref), custom_call_target="tpu_custom_call" | custom-call | tf_op jit(solution)/shard_map/scatter/pallas_call | solution.py:566
  66.9 12.2 %all_to_all.11 = f32[8,128,128]{2,1,0:T(8,128)S(1)} all-to-all(f32[8,128,128]{2,1,0:T(8,128)S(1)} %scatter.1), channel_id=1, replica_groups=mesh['energy'=8,'orb'=4] {'energy'}, dimensions={0} | all-to-all | bytes 1048576 | tf_op jit(solution)/shard_map/all_to_all | solution.py:712
  79.0 0.8 copy.26
  (15 shorter events, 0.1 us)
Async XLA Ops:
  0.0 6.4 %copy-start = (f32[1024,3,8,8]{0,3,2,1:T(8,128)S(1)}, f32[1024,3,8,8]{0,3,2,1:T(8,128)}, u32[]{:S(2)}) copy-start(f32[1024,3,8,8]{0,3,2,1:T(8,128)} %param.11) | copy-start | bytes 2359300
  0.0 19.9 %collective-permute-start = (f32[1,4,2,128,128]{4,3,2,1,0:T(8,128)}, f32[1,4,2,128,128]{4,3,2,1,0:T(8,128)S(1)}, u32[]{:S(2)}, u32[]{:S(2)}) collective-permute-start(f32[1,4,2,128,128]{4,3,2,1,0:T(8,128)} %sigma_ref.1), channel_id=1, source_target_pairs={{0,1},{3,2},{1,0},{2,3},{4,5},{7,6},{5,4},{6,7},{8,9},{11,10},{9,8... | collective-permute-start | bytes 1572872 | tf_op jit(solution)/shard_map/ppermute | solution.py:601
  3.0 17.6 %collective-permute-start.1 = (f32[1,4,2,128,128]{4,3,2,1,0:T(8,128)}, f32[1,4,2,128,128]{4,3,2,1,0:T(8,128)S(1)}, u32[]{:S(2)}, u32[]{:S(2)}) collective-permute-start(f32[1,4,2,128,128]{4,3,2,1,0:T(8,128)} %sigma_ref.1), channel_id=1, source_target_pairs={{1,2},{2,1},{5,6},{6,5},{9,10},{10,9},{13,14},{14,13},{17,18},{18,... | collective-permute-start | bytes 1572872 | tf_op jit(solution)/shard_map/ppermute | solution.py:601
  12.8 28.9 %collective-permute-start.6 = (f32[2,64,2048]{2,1,0:T(8,128)S(1)}, f32[2,64,2048]{2,1,0:T(8,128)S(1)}, u32[]{:S(2)}, u32[]{:S(2)}) collective-permute-start(f32[2,64,2048]{2,1,0:T(8,128)S(1)} %get-tuple-element.34), channel_id=1, source_target_pairs={{0,1},{3,2},{4,5},{7,6},{8,9},{11,10},{12,13},{15,14},{16,17},{19,... | collective-permute-start | bytes 3145736 | tf_op jit(solution)/shard_map/ppermute | solution.py:601
  20.0 5.7 %collective-permute-start.2 = (f32[1,4,2,128,128]{4,3,2,1,0:T(8,128)S(1)}, f32[1,4,2,128,128]{4,3,2,1,0:T(8,128)S(1)}, u32[]{:S(2)}, u32[]{:S(2)}) collective-permute-start(f32[1,4,2,128,128]{4,3,2,1,0:T(8,128)S(1)} %gate.4.refs_1_.rest_0_), channel_id=1, source_target_pairs={{1,2},{2,1},{5,6},{6,5},{9,10},{10,9},{13,14},{14,13},{17,18},{18,... | collective-permute-start | bytes 1572872 | tf_op jit(solution)/shard_map/ppermute | solution.py:601
  20.7 15.1 %collective-permute-start.3 = (f32[1,4,2,128,128]{4,3,2,1,0:T(8,128)S(1)}, f32[1,4,2,128,128]{4,3,2,1,0:T(8,128)S(1)}, u32[]{:S(2)}, u32[]{:S(2)}) collective-permute-start(f32[1,4,2,128,128]{4,3,2,1,0:T(8,128)S(1)} %gate.5.rest_1_), channel_id=1, source_target_pairs={{1,0},{2,3},{5,4},{6,7},{9,8},{10,11},{13,12},{14,15},{17,16},{18,... | collective-permute-start | bytes 1572872 | tf_op jit(solution)/shard_map/ppermute | solution.py:601
  22.0 21.2 %collective-permute-start.5 = (f32[2,32,2048]{2,1,0:T(8,128)S(1)}, f32[2,32,2048]{2,1,0:T(8,128)S(1)}, u32[]{:S(2)}, u32[]{:S(2)}) collective-permute-start(f32[2,32,2048]{2,1,0:T(8,128)S(1)} %get-tuple-element.29), channel_id=1, source_target_pairs={{1,2},{2,1},{5,6},{6,5},{9,10},{10,9},{13,14},{14,13},{17,18},{18,... | collective-permute-start | bytes 1572872 | tf_op jit(solution)/shard_map/ppermute | solution.py:601
  25.7 21.6 %collective-permute-start.4 = (f32[1,4,2,128,128]{4,3,2,1,0:T(8,128)S(1)}, f32[1,4,2,128,128]{4,3,2,1,0:T(8,128)S(1)}, u32[]{:S(2)}, u32[]{:S(2)}) collective-permute-start(f32[1,4,2,128,128]{4,3,2,1,0:T(8,128)S(1)} %gate.6.rest_0_), channel_id=1, source_target_pairs={{1,0},{2,3},{5,4},{6,7},{9,8},{10,11},{13,12},{14,15},{17,16},{18,... | collective-permute-start | bytes 1572872 | tf_op jit(solution)/shard_map/ppermute | solution.py:601
  41.9 8.6 %collective-permute-start.8 = (f32[2,64,128]{2,1,0:T(8,128)S(1)}, f32[2,64,128]{2,1,0:T(8,128)S(1)}, u32[]{:S(2)}, u32[]{:S(2)}) collective-permute-start(f32[2,64,128]{2,1,0:T(8,128)S(1)} %get-tuple-element.38), channel_id=1, source_target_pairs={{1,0},{2,3},{5,4},{6,7},{9,8},{10,11},{13,12},{14,15},{17,16},{18,... | collective-permute-start | bytes 196616 | tf_op jit(solution)/shard_map/ppermute | solution.py:601
  43.4 7.2 %collective-permute-start.7 = (f32[2,64,128]{2,1,0:T(8,128)S(1)}, f32[2,64,128]{2,1,0:T(8,128)S(1)}, u32[]{:S(2)}, u32[]{:S(2)}) collective-permute-start(f32[2,64,128]{2,1,0:T(8,128)S(1)} %get-tuple-element.36.rest_1_), channel_id=1, source_target_pairs={{1,2},{2,1},{5,6},{6,5},{9,10},{10,9},{13,14},{14,13},{17,18},{18,... | collective-permute-start | bytes 196616 | tf_op jit(solution)/shard_map/ppermute | solution.py:601
